TPU v7x, 32 devices: a whole 2x2x4 slice. The times are simulated.
32 devices in a mesh: parts: 2 (over x), seq: 8 (over z, y), head: 2 (over core).
Axes of the slice: x: 2, y: 2, z: 4, core: 2. Of those that a mesh axis runs over, the one named last changes fastest.
Arguments:
- latents: bfloat16 [8192, 2112], P(('parts', 'seq', 'head')), parts along dimension 0, may hold values from -400 to 400
- q_gain: float32 [1536], replicated, may hold values from 0.25 to 1.75
- kv_gain: float32 [512], replicated, may hold values from 0.25 to 1.75
- q_weight: bfloat16 [2, 1536, 32, 192], P('head', None, 'seq'), may hold values from -0.15625 to 0.15625
- kv_weight: bfloat16 [2, 512, 32, 256], P('head', None, 'seq'), may hold values from -0.25 to 0.25
- lengths: int32 [16, 8], P('parts'), parts along dimension 0, may hold values from 0 to 512, as said below
Outputs:
- attended: bfloat16 [8192, 8192], P(('parts', 'seq'), 'head'), parts along dimension 0
There are 2 independent parts, one for each index of `parts`. A program takes and returns all parts, laid end to end along the dimension named above; an argument that names none is the same for every part. Nothing has to cross between parts.
Inputs may be any that keep to these rules, and one draw needn't show every extreme that they name: Row g lists the lengths of the sequences packed in order in group g: they sum to 512, each is a multiple of 64, the nonzero ones come first. Some group holds a single sequence of 512 tokens; the group after it holds two sequences of 256 tokens, and the group 8 / 2 after that one holds 8 sequences of 64 tokens.
All inputs are finite; a program needn't handle non-finite values.
Results may differ from a plain program's by a relative error of at most 0.011.
Values may be sent and summed in bfloat16 or wider, within the bound.
No kernel may reach another device: no remote copies, remote signals or barrier semaphores. Data moves between devices by JAX's collectives and lax.ppermute only.
A program may use at most 128 MiB of HBM per device.

v0:
```python
from functools import partial
import math

import jax
import jax.numpy as jnp
from jax import lax
from jax.sharding import PartitionSpec as P

epsilon = 1e-06


def rotary(values, positions):
    half_width = values.shape[-1] // 2
    freq_table = jnp.exp(
        jnp.arange(half_width, dtype=jnp.float32) * (-2.0 * jnp.log(10000.0) / values.shape[-1])
    )
    angles = positions.astype(jnp.float32)[:, None] * freq_table[None, :]
    if values.ndim == 3:
        angles = angles[:, None, :]
    cosine = jnp.cos(angles)
    sine_part = jnp.sin(angles)
    first_half = values[..., :half_width]
    second_half = values[..., half_width:]
    return jnp.concatenate(
        [
            first_half * cosine - second_half * sine_part,
            second_half * cosine + first_half * sine_part,
        ],
        axis=-1,
    )


def normalize(part_values, gain_vec):
    squares = jnp.mean(part_values * part_values, axis=-1, keepdims=True)
    return (part_values * lax.rsqrt(squares + epsilon) * gain_vec).astype(jnp.bfloat16)


def seq_starts(length_row, token_count):
    seq_ends = jnp.cumsum(length_row)
    begins = seq_ends - length_row
    token_ids = jnp.arange(token_count, dtype=jnp.int32)
    inside = (token_ids[:, None] >= begins[None, :]) & (token_ids[:, None] < seq_ends[None, :])
    return jnp.sum(jnp.where(inside, begins[None, :], 0), axis=1)


def prepare(block_rows, q_gain, kv_gain, positions):
    q_width = q_gain.shape[0]
    kv_width = kv_gain.shape[0]
    q_part = block_rows[:, :q_width].astype(jnp.float32)
    kv_part = block_rows[:, q_width : q_width + kv_width].astype(jnp.float32)
    rope_part = block_rows[:, q_width + kv_width :].astype(jnp.float32)
    return (
        normalize(q_part, q_gain),
        normalize(kv_part, kv_gain),
        rotary(rope_part, positions).astype(jnp.bfloat16),
    )


def rotate_tail(projected, positions, rope_width):
    nope_width = projected.shape[2] - rope_width
    return jnp.concatenate(
        [projected[:, :, :nope_width], rotary(projected[:, :, nope_width:], positions)], axis=-1
    )


def tile_scores(
    query_nope, query_rope, key_nope, rope_keys, begins, score_scale, row_span, col_span
):
    row_low, row_high = row_span
    col_low, col_high = col_span
    part_scores = jnp.einsum(
        "qhd,khd->hqk", query_nope, key_nope, preferred_element_type=jnp.float32
    )
    part_scores = part_scores + jnp.einsum(
        "qhd,kd->hqk", query_rope, rope_keys, preferred_element_type=jnp.float32
    )
    row_ids = jnp.arange(row_low, row_high, dtype=jnp.int32)
    col_ids = jnp.arange(col_low, col_high, dtype=jnp.int32)
    allowed = (begins[row_low:row_high, None] <= col_ids[None, :]) & (
        col_ids[None, :] <= row_ids[:, None]
    )
    return jnp.where(allowed[None], part_scores * score_scale, -jnp.inf)


def softmax_parts(scores):
    maxima = jnp.max(scores, axis=-1, keepdims=True)
    exp_terms = jnp.exp(scores - maxima)
    return (exp_terms.astype(jnp.bfloat16), jnp.sum(exp_terms, axis=-1))


def head_block(queries, key_values, rope_keys, begins):
    token_count = queries.shape[0]
    rope_width = rope_keys.shape[1]
    nope_width = queries.shape[2] - rope_width
    score_scale = queries.shape[2] ** (-0.5)
    value_part = key_values[:, :, nope_width:]
    scorer = partial(
        tile_scores,
        queries[:, :, :nope_width],
        queries[:, :, nope_width:],
        key_values[:, :, :nope_width],
        rope_keys,
        begins,
        score_scale,
    )
    softmax_num, totals = softmax_parts(scorer((0, token_count), (0, token_count)))
    mixed_out = jnp.einsum(
        "hqk,khd->qhd", softmax_num, value_part, preferred_element_type=jnp.float32
    )
    return (mixed_out / totals.T[:, :, None]).astype(jnp.bfloat16)


def heads_attention(queries, key_values, rope_keys, begins):
    token_count = queries.shape[0]
    head_count = queries.shape[1]
    block_heads = math.gcd(4, head_count)
    value_width = key_values.shape[2] - (queries.shape[2] - rope_keys.shape[1])

    def block_step(block_index, collected):
        mixed_out = head_block(queries, key_values, rope_keys, begins)
        return mixed_out

    collected = lax.fori_loop(
        0,
        head_count // block_heads,
        block_step,
        jnp.zeros((token_count, head_count, value_width), jnp.bfloat16),
    )
    return collected.reshape(token_count, head_count * value_width)


def shards(latents, q_gain, kv_gain, q_weight, kv_weight, lengths):
    rope_width = latents.shape[1] - q_gain.shape[0] - kv_gain.shape[0]
    group_count = lengths.shape[0]
    token_count = latents.shape[0] * lax.axis_size("head")
    total_tokens = token_count * group_count
    local_heads = q_weight.shape[2]
    begins_all = jax.vmap(partial(seq_starts, token_count=token_count))(lengths)
    positions_all = (jnp.arange(token_count, dtype=jnp.int32)[None, :] - begins_all).reshape(
        total_tokens
    )
    q_normed, kv_normed, rope_keys = prepare(
        lax.all_gather(latents, ("seq", "head"), axis=0, tiled=True), q_gain, kv_gain, positions_all
    )
    projected = jnp.einsum("tc,chd->thd", q_normed, q_weight[0], preferred_element_type=jnp.float32)
    queries = rotate_tail(projected, positions_all, rope_width).astype(jnp.bfloat16)
    key_values = jnp.einsum(
        "tc,chd->thd", kv_normed, kv_weight[0], preferred_element_type=jnp.float32
    ).astype(jnp.bfloat16)
    value_width = kv_weight.shape[3] - (q_weight.shape[3] - rope_width)

    def group_step(group_index, collected):
        row_low = group_index * token_count
        query_rows = lax.dynamic_slice_in_dim(queries, row_low, token_count, 0)
        pair_rows = lax.dynamic_slice_in_dim(key_values, row_low, token_count, 0)
        rope_rows = lax.dynamic_slice_in_dim(rope_keys, row_low, token_count, 0)
        begin_row = lax.dynamic_index_in_dim(begins_all, group_index, 0, keepdims=False)
        mixed_out = heads_attention(query_rows, pair_rows, rope_rows, begin_row)
        return lax.dynamic_update_slice_in_dim(collected, mixed_out, row_low, 0)

    mixed_all = lax.fori_loop(
        0,
        group_count,
        group_step,
        jnp.zeros((total_tokens, local_heads * value_width), jnp.bfloat16),
    )
    return lax.all_to_all(mixed_all, "seq", split_axis=0, concat_axis=1, tiled=True)


def solution(mesh):
    return jax.shard_map(
        shards,
        mesh=mesh,
        in_specs=(
            P(("parts", "seq", "head"), None),
            P(),
            P(),
            P("head", None, "seq", None),
            P("head", None, "seq", None),
            P("parts", None),
        ),
        out_specs=P(("parts", "seq"), "head"),
        check_vma=False,
    )
```

profile of v0, /device:TPU:0, one launch (start us, length us, event | category | flops | bytes accessed | tf_op | source)
XLA Modules:
  0.0 367.9 jit_solution(16817115893242284728)
XLA Ops:
  9.0 102.0 %all-gather.2.cloned.1.call-done = bf16[4096,2112]{0,1:T(8,128)(2,1)} async-done(((bf16[256,2112]{0,1:T(8,128)(2,1)}), bf16[4096,2112]{0,1:T(8,128)(2,1)}) %all-gather.2.cloned.1.call-update) | async-done | bytes 17301520 | tf_op jit(solution)/shard_map/all_gather | solution.py:143
  111.0 7.2 %fusion.27 = f32[4096]{0:T(1024)S(1)} fusion(bf16[4096,2112]{0,1:T(8,128)(2,1)} %all-gather.2.cloned.1.call-done), kind=kLoop, calls=%fused_computation.28 | loop fusion | flops 18870272 | bytes 12599296 | tf_op jit(solution)/shard_map/reduce_sum | solution.py:34
  118.3 16.1 %fusion.30 = f32[4096,768]{0,1} fusion(bf16[1536,768]{0,1:T(8,128)(2,1)S(1)} %bitcast.46, f32[1536]{0:T(1024)S(1)} %copy-done.3, f32[4096]{0:T(1024)S(1)} %add_rsqrt_fusion, bf16[4096,2112]{0,1:T(8,128)(2,1)} %all-gather.2.cloned.1.call-done), kind=kOutput, calls=%fused_computation.31 | convolution fusion | flops 9688842240 | bytes 27547648
  134.3 6.0 %slice.96 = bf16[4096,4,128]{0,2,1:T(8,128)(2,1)} slice(f32[4096,4,192]{0,2,1:T(8,128)} %bitcast.52), slice={[0:4096], [0:4], [0:128]} | slice | bytes 8388608 | tf_op jit(solution)/shard_map/slice | solution.py:62
  147.0 5.5 %pad_maximum_fusion = bf16[4096,4,192]{0,2,1:T(8,128)(2,1)} fusion(bf16[4096,4,32]{0,2,1:T(8,128)(2,1)S(1)} %get-tuple-element.181, bf16[4096,4,32]{0,2,1:T(8,128)(2,1)S(1)} %get-tuple-element.180, bf16[4096,4,128]{0,2,1:T(8,128)(2,1)S(1)} %copy-done.2), kind=kLoop, calls=%fused_computation.42 | loop fusion | flops 18874368 | bytes 12582912 | tf_op jit(solution)/shard_map/concatenate | solution.py:61
  152.5 8.2 %convolution_convert_fusion = bf16[4096,4,256]{2,0,1:T(8,128)(2,1)} fusion(f32[512]{0:T(512)S(1)} %copy-done.4, f32[4096]{0:T(1024)S(1)} %add_rsqrt_fusion.1, bf16[4096,2112]{0,1:T(8,128)(2,1)S(1)} %bitcast.48, bf16[512,4,256]{2,1,0:T(4,128)(2,1)} %bitcast.57), kind=kOutput, calls=%fused_computation.41 | convolution fusion | flops 4307550208 | bytes 13649920 | tf_op jit(solution)/shard_map/tc,chd->thd/dot_general | solution.py:147
  163.0 86.8 %while.21 = (s32[]{:T(128)}, bf16[4096,512]{1,0:T(8,128)(2,1)}, bf16[4096,4,256]{2,0,1:T(8,128)(2,1)}, s32[8,512]{1,0:T(8,128)S(1)}, bf16[4096,4,192]{0,2,1:T(8,...) while((s32[]{:T(128)}, bf16[4096,512]{1,0:T(8,128)(2,1)}, ...), condition=%wide.region_7.8_spmd, body=%wide.region_4.7_spmd.sunk | while | flops 680783872 | bytes 26067640 | solution.py:161
  163.0 3.9 %fusion.60 = f32[4,512,512]{1,2,0:T(8,128)} fusion(bf16[4096,4,192]{0,2,1:T(8,128)(2,1)} %get-tuple-element.253, s32[]{:T(128)S(6)} %select_n.33, bf16[4096,4,256]{2,0,1:T(8,128)(2,1)} %get-tuple-element.251), kind=kOutput, calls=%fused_computation.14.clone.1 | convolution fusion | flops 268435456 | bytes 5243904 | tf_op jit(solution)/shard_map/while/body/eval_jaxpr/while/body/eval_jaxpr/qhd,khd->hqk/dot_general | solution.py:71
  167.0 3.4 fusion.62
  173.8 3.9 %fusion.60 = f32[4,512,512]{1,2,0:T(8,128)} fusion(bf16[4096,4,192]{0,2,1:T(8,128)(2,1)} %get-tuple-element.253, s32[]{:T(128)S(6)} %select_n.33, bf16[4096,4,256]{2,0,1:T(8,128)(2,1)} %get-tuple-element.251), kind=kOutput, calls=%fused_computation.14.clone.1 | convolution fusion | flops 268435456 | bytes 5243904 | tf_op jit(solution)/shard_map/while/body/eval_jaxpr/while/body/eval_jaxpr/qhd,khd->hqk/dot_general | solution.py:71
  184.7 3.8 %fusion.60 = f32[4,512,512]{1,2,0:T(8,128)} fusion(bf16[4096,4,192]{0,2,1:T(8,128)(2,1)} %get-tuple-element.253, s32[]{:T(128)S(6)} %select_n.33, bf16[4096,4,256]{2,0,1:T(8,128)(2,1)} %get-tuple-element.251), kind=kOutput, calls=%fused_computation.14.clone.1 | convolution fusion | flops 268435456 | bytes 5243904 | tf_op jit(solution)/shard_map/while/body/eval_jaxpr/while/body/eval_jaxpr/qhd,khd->hqk/dot_general | solution.py:71
  188.7 3.4 fusion.62
  195.5 3.8 %fusion.60 = f32[4,512,512]{1,2,0:T(8,128)} fusion(bf16[4096,4,192]{0,2,1:T(8,128)(2,1)} %get-tuple-element.253, s32[]{:T(128)S(6)} %select_n.33, bf16[4096,4,256]{2,0,1:T(8,128)(2,1)} %get-tuple-element.251), kind=kOutput, calls=%fused_computation.14.clone.1 | convolution fusion | flops 268435456 | bytes 5243904 | tf_op jit(solution)/shard_map/while/body/eval_jaxpr/while/body/eval_jaxpr/qhd,khd->hqk/dot_general | solution.py:71
  199.5 3.4 fusion.62
  206.3 3.8 %fusion.60 = f32[4,512,512]{1,2,0:T(8,128)} fusion(bf16[4096,4,192]{0,2,1:T(8,128)(2,1)} %get-tuple-element.253, s32[]{:T(128)S(6)} %select_n.33, bf16[4096,4,256]{2,0,1:T(8,128)(2,1)} %get-tuple-element.251), kind=kOutput, calls=%fused_computation.14.clone.1 | convolution fusion | flops 268435456 | bytes 5243904 | tf_op jit(solution)/shard_map/while/body/eval_jaxpr/while/body/eval_jaxpr/qhd,khd->hqk/dot_general | solution.py:71
  210.3 3.4 fusion.62
  217.2 3.8 %fusion.60 = f32[4,512,512]{1,2,0:T(8,128)} fusion(bf16[4096,4,192]{0,2,1:T(8,128)(2,1)} %get-tuple-element.253, s32[]{:T(128)S(6)} %select_n.33, bf16[4096,4,256]{2,0,1:T(8,128)(2,1)} %get-tuple-element.251), kind=kOutput, calls=%fused_computation.14.clone.1 | convolution fusion | flops 268435456 | bytes 5243904 | tf_op jit(solution)/shard_map/while/body/eval_jaxpr/while/body/eval_jaxpr/qhd,khd->hqk/dot_general | solution.py:71
  221.2 3.4 fusion.62
  228.0 3.8 %fusion.60 = f32[4,512,512]{1,2,0:T(8,128)} fusion(bf16[4096,4,192]{0,2,1:T(8,128)(2,1)} %get-tuple-element.253, s32[]{:T(128)S(6)} %select_n.33, bf16[4096,4,256]{2,0,1:T(8,128)(2,1)} %get-tuple-element.251), kind=kOutput, calls=%fused_computation.14.clone.1 | convolution fusion | flops 268435456 | bytes 5243904 | tf_op jit(solution)/shard_map/while/body/eval_jaxpr/while/body/eval_jaxpr/qhd,khd->hqk/dot_general | solution.py:71
  232.0 3.4 fusion.62
  238.9 3.8 %fusion.60 = f32[4,512,512]{1,2,0:T(8,128)} fusion(bf16[4096,4,192]{0,2,1:T(8,128)(2,1)} %get-tuple-element.253, s32[]{:T(128)S(6)} %select_n.33, bf16[4096,4,256]{2,0,1:T(8,128)(2,1)} %get-tuple-element.251), kind=kOutput, calls=%fused_computation.14.clone.1 | convolution fusion | flops 268435456 | bytes 5243904 | tf_op jit(solution)/shard_map/while/body/eval_jaxpr/while/body/eval_jaxpr/qhd,khd->hqk/dot_general | solution.py:71
  249.7 98.3 %all_to_all.19 = bf16[8,512,512]{2,1,0:T(8,128)(2,1)} all-to-all(bf16[8,512,512]{2,1,0:T(8,128)(2,1)} %bitcast.49), channel_id=1, replica_groups=mesh['parts'=2,'seq'=8,'head'=2] {'seq'}, dimensions={0} | all-to-all | bytes 8388608 | tf_op jit(solution)/shard_map/all_to_all | solution.py:167
  348.0 6.5 %copy.41 = bf16[8,512,512]{1,2,0:T(8,128)(2,1)} copy(bf16[8,512,512]{2,1,0:T(8,128)(2,1)} %all_to_all.19) | data formatting | bytes 8388608 | tf_op jit(solution)/shard_map/all_to_all | solution.py:167
  354.6 6.5 %copy.42 = bf16[512,4096]{1,0:T(8,128)(2,1)} copy(bf16[512,4096]{0,1:T(8,128)(2,1)} %bitcast.50) | data formatting | bytes 8388608 | tf_op jit(solution)/shard_map/all_to_all | solution.py:167
  (87 shorter events, 46.8 us)
Async XLA Ops:
  6.5 111.7 %copy-start = (bf16[1,1536,4,192]{1,3,2,0:T(8,128)(2,1)S(1)}, bf16[1,1536,4,192]{1,3,2,0:T(8,128)(2,1)}, u32[]{:S(2)}) copy-start(bf16[1,1536,4,192]{1,3,2,0:T(8,128)(2,1)} %param.11) | copy-start | bytes 7077892
  6.5 104.5 %all-gather.2.cloned.1.call-start = ((), (), s32[]{:S(2)}) async-start(), calls=%async_computation.1 | async-start | bytes 18382848 | tf_op jit(solution)/shard_map/all_gather | solution.py:143
  9.0 109.2 %copy-start.3 = (f32[1536]{0:T(1024)S(1)}, f32[1536]{0:T(1024)}, u32[]{:S(2)}) copy-start(f32[1536]{0:T(1024)} %param.9) | copy-start | bytes 18436
  111.0 29.4 %slice-start = ((s8[17301504]{0:T(1024)(128)(4,1)}), s8[524288]{0:T(1024)(128)(4,1)S(1)}, s32[]{:S(2)}) async-start(s8[17301504]{0:T(1024)(128)(4,1)} %bitcast.47), calls=%async_computation.2 | async-start | bytes 1048576
  118.2 22.1 %slice-start.1 = ((s8[17301504]{0:T(1024)(128)(4,1)}), s8[4194304]{0:T(1024)(128)(4,1)S(1)}, s32[]{:S(2)}) async-start(s8[17301504]{0:T(1024)(128)(4,1)} %bitcast.47), calls=%async_computation.3 | async-start | bytes 8388608
  118.2 22.1 %slice-start.2 = ((s8[17301504]{0:T(1024)(128)(4,1)}), s8[4194304]{0:T(1024)(128)(4,1)S(1)}, s32[]{:S(2)}) async-start(s8[17301504]{0:T(1024)(128)(4,1)} %bitcast.47), calls=%async_computation.4 | async-start | bytes 8388608
  118.2 22.1 %slice-start.3 = ((s8[17301504]{0:T(1024)(128)(4,1)}), s8[4194304]{0:T(1024)(128)(4,1)S(1)}, s32[]{:S(2)}) async-start(s8[17301504]{0:T(1024)(128)(4,1)} %bitcast.47), calls=%async_computation.5 | async-start | bytes 8388608
  118.3 22.1 %slice-start.4 = ((s8[17301504]{0:T(1024)(128)(4,1)}), s8[4194304]{0:T(1024)(128)(4,1)S(1)}, s32[]{:S(2)}) async-start(s8[17301504]{0:T(1024)(128)(4,1)} %bitcast.47), calls=%async_computation.6 | async-start | bytes 8388608
  143.5 3.5 copy-start.2
  147.0 5.5 %copy-start.4 = (f32[512]{0:T(512)S(1)}, f32[512]{0:T(512)}, u32[]{:S(2)}) copy-start(f32[512]{0:T(512)} %param.10) | copy-start | bytes 6148
  354.6 6.5 %copy-start.1 = (bf16[1,1536,4,192]{1,3,2,0:T(8,128)(2,1)S(1)}, bf16[1,1536,4,192]{1,3,2,0:T(8,128)(2,1)}, u32[]{:S(2)}) copy-start(bf16[1,1536,4,192]{1,3,2,0:T(8,128)(2,1)} %param.11) | copy-start | bytes 7077892
Sparse Core Ops, SparseCore 0:
  8.9 102.0 all-gather.1
where the time goes:
time: 369 us; the launch traced here: 368 us
  waiting for transfers between devices  103 us (28%)
  blocking collectives  98.3 us (27%)
  matrix products  96.7 us (26%)
  local copies, waits for them, and re-layouts  30.2 us (8%)
  other arithmetic  26.1 us (7%)
  between operations  13.6 us (4%)
    all_gather x1, waiting for transfers between devices, shards(): lax.all_gather(latents, ('seq', 'head'), axis=0, tiled=True)  102 us
    all_to_all x1, blocking collectives, shards(): lax.all_to_all(mixed_all, 'seq', split_axis=0, concat_axis=1, tiled=True)  98.3 us
    dot_general x8, matrix products, tile_scores(): jnp.einsum('qhd,khd->hqk', query_nope, key_nope, preferred_element_type=j...  30.8 us
    dot_general x8, matrix products, tile_scores(): jnp.einsum('qhd,kd->hqk', query_rope, rope_keys, preferred_element_type=j...  27 us
    unnamed x1, matrix products  16.1 us
    dot_general x8, matrix products, head_block(): jnp.einsum('hqk,khd->qhd', softmax_num, value_part, preferred_element_typ...  14.7 us
    all_to_all x2, local copies, waits for them, and re-layouts, shards(): lax.all_to_all(mixed_all, 'seq', split_axis=0, concat_axis=1, tiled=True)  13 us
    dynamic_update_slice x16, local copies, waits for them, and re-layouts, group_step(): return lax.dynamic_update_slice_in_dim(collected, mixed_out, row_low, 0)  8.37 us
  transfers between devices with their start and end apart: 1, of which 1 were waited for; matrix products, arithmetic and copies ran while one was open for 0% of the time, Pallas kernels for 0%

commit v1 on v0

v1 whole, which is shorter than its diff:
```python
from functools import partial
import math

import jax
import jax.numpy as jnp
from jax import lax
from jax.experimental import pallas as pl
from jax.experimental.pallas import tpu as pltpu
from jax.sharding import PartitionSpec as P

epsilon = 1e-06
VMEM_LIMIT = 48 * 1024 * 1024
NT = (((1,), (1,)), ((), ()))
NN = (((1,), (0,)), ((), ()))


def frequencies(lane, half_width):
    steps = lax.rem(lane, half_width).astype(jnp.float32)
    return jnp.exp(steps * (-math.log(10000.0) / half_width))


def begins_of(lengths_ref, group, token_ids):
    begin = jnp.zeros_like(token_ids)
    start = jnp.int32(0)
    for slot in range(lengths_ref.shape[1]):
        begin = jnp.where(token_ids >= start, start, begin)
        start = start + lengths_ref[group, slot]
    return begin


def prepare_kernel(q_width, kv_width, place_ref, lengths_ref, latents_ref, q_gain_ref, kv_gain_ref, out_ref):
    rows = latents_ref.shape[1]
    rope_width = latents_ref.shape[0] - q_width - kv_width
    half_width = rope_width // 2

    def normalized(low, width, gain_ref):
        part = latents_ref[low : low + width, :].astype(jnp.float32)
        scale = lax.rsqrt(jnp.mean(part * part, axis=0, keepdims=True) + epsilon)
        return (jnp.transpose(part * scale) * gain_ref[...]).astype(jnp.bfloat16)

    out_ref[:, :q_width] = normalized(0, q_width, q_gain_ref)
    out_ref[:, q_width : q_width + kv_width] = normalized(q_width, kv_width, kv_gain_ref)
    token_ids = lax.broadcasted_iota(jnp.int32, (1, rows), 1) + place_ref[1] * rows
    position = (token_ids - begins_of(lengths_ref, place_ref[0], token_ids)).astype(jnp.float32)
    angle = position * frequencies(lax.broadcasted_iota(jnp.int32, (half_width, rows), 0), half_width)
    cosine, sine = jnp.cos(angle), jnp.sin(angle)
    rope = latents_ref[q_width + kv_width :, :].astype(jnp.float32)
    first, second = rope[:half_width], rope[half_width:]
    turned = jnp.concatenate([first * cosine - second * sine, second * cosine + first * sine], axis=0)
    spare = out_ref.shape[1] - q_width - kv_width - rope_width
    if spare:
        turned = jnp.concatenate([turned, jnp.zeros((spare, rows), jnp.float32)], axis=0)
    out_ref[:, q_width + kv_width :] = jnp.transpose(turned).astype(jnp.bfloat16)


def prepare(latents, q_gain, kv_gain, lengths, place):
    rows = latents.shape[0]
    width = -(-latents.shape[1] // 128) * 128
    smem = pl.BlockSpec(memory_space=pltpu.SMEM)
    vmem = pl.BlockSpec(memory_space=pltpu.VMEM)
    return pl.pallas_call(
        partial(prepare_kernel, q_gain.shape[0], kv_gain.shape[0]),
        out_shape=jax.ShapeDtypeStruct((rows, width), jnp.bfloat16),
        in_specs=[smem, smem, vmem, vmem, vmem],
        out_specs=vmem,
        compiler_params=pltpu.CompilerParams(vmem_limit_bytes=VMEM_LIMIT),
        cost_estimate=pl.CostEstimate(flops=8 * rows * width, bytes_accessed=4 * rows * width, transcendentals=rows * 64),
        name="prepare",
    )(place, lengths, jnp.transpose(latents), q_gain[None, :], kv_gain[None, :])


def attend_kernel(sizes, place_ref, lengths_ref, table_ref, q_weight_ref, kv_weight_ref, *refs):
    slots, heads, q_width, kv_width, nope_width, rope_width, value_width = sizes
    same_refs, other_refs, out_refs = refs[:slots], refs[slots : 2 * slots], refs[2 * slots : 3 * slots]
    query_ref, key_ref, value_ref, turn_ref, bias_ref = refs[3 * slots :]
    core = place_ref[0]
    rows = same_refs[0].shape[0]
    half_width = rope_width // 2
    score_scale = (nope_width + rope_width) ** -0.5
    slot_count = lengths_ref.shape[1]
    block = 2 * rows // slot_count
    for slot in range(slots):
        group = place_ref[1 + slot]
        starts, start = [], jnp.int32(0)
        for index in range(slot_count):
            starts.append(start)
            start = start + lengths_ref[group, index]
        for index in range(slot_count):
            begin = jnp.int32(0)
            for entry in starts:
                begin = jnp.where(entry <= index * block, entry, begin)
            position = pl.multiple_of(index * block - begin, block)
            turn_ref[index * block : (index + 1) * block, :] = table_ref[pl.ds(position, block), :]
        row_ids = lax.broadcasted_iota(jnp.int32, (2 * rows, 1), 0)
        begins = begins_of(lengths_ref, group, row_ids)
        col_ids = lax.broadcasted_iota(jnp.int32, (2 * rows, 2 * rows), 1)
        allowed = (col_ids <= row_ids) & (col_ids >= begins)
        bias_ref[...] = jnp.where(allowed, 0.0, -jnp.inf)
        for head in range(heads):
            for tokens_ref, half in ((same_refs[slot], core), (other_refs[slot], 1 - core)):
                span = pl.ds(pl.multiple_of(half * rows, rows), rows)
                projected = lax.dot_general(
                    tokens_ref[:, :q_width], q_weight_ref[head], NT, preferred_element_type=jnp.float32
                )
                rope = projected[:, nope_width:]
                swapped = jnp.concatenate([rope[:, half_width:], rope[:, :half_width]], axis=1)
                turned = rope * turn_ref[span, :rope_width] + swapped * turn_ref[span, rope_width : 2 * rope_width]
                query_ref[head, span, :nope_width] = projected[:, :nope_width].astype(jnp.bfloat16)
                query_ref[head, span, nope_width:] = turned.astype(jnp.bfloat16)
                pair = lax.dot_general(
                    tokens_ref[:, q_width : q_width + kv_width],
                    kv_weight_ref[head],
                    NN,
                    preferred_element_type=jnp.float32,
                ).astype(jnp.bfloat16)
                key_ref[head, span, :nope_width] = pair[:, :nope_width]
                key_ref[head, span, nope_width:] = tokens_ref[:, q_width + kv_width : q_width + kv_width + rope_width]
                value_ref[head, span, :] = pair[:, nope_width:]
            for half in range(2):
                low, high = half * rows, (half + 1) * rows
                scores = lax.dot_general(
                    query_ref[head, low:high], key_ref[head, :high], NT, preferred_element_type=jnp.float32
                )
                scores = scores * score_scale + bias_ref[low:high, :high]
                terms = jnp.exp(scores - jnp.max(scores, axis=1, keepdims=True))
                totals = jnp.sum(terms, axis=1, keepdims=True)
                mixed = lax.dot_general(
                    terms.astype(jnp.bfloat16), value_ref[head, :high], NN, preferred_element_type=jnp.float32
                )
                out_refs[slot][low:high, head * value_width : (head + 1) * value_width] = (mixed / totals).astype(
                    jnp.bfloat16
                )


def attend(same, other, groups, core, q_weight, kv_weight, table, lengths, rope_width):
    slots = len(same)
    rows = same[0].shape[0]
    heads, query_width, q_width = q_weight.shape
    kv_width, pair_width = kv_weight.shape[1:]
    nope_width = query_width - rope_width
    value_width = pair_width - nope_width
    smem = pl.BlockSpec(memory_space=pltpu.SMEM)
    vmem = pl.BlockSpec(memory_space=pltpu.VMEM)
    place = jnp.stack([core] + groups).astype(jnp.int32)
    sizes = (slots, heads, q_width, kv_width, nope_width, rope_width, value_width)
    tokens = 2 * rows
    flops = 2 * slots * heads * tokens * (q_width * query_width + kv_width * pair_width + tokens * (query_width + value_width))
    out_shape = jax.ShapeDtypeStruct((tokens, heads * value_width), jnp.bfloat16)
    return pl.pallas_call(
        partial(attend_kernel, sizes),
        out_shape=[out_shape] * slots,
        in_specs=[smem, smem] + [vmem] * (3 + 2 * slots),
        out_specs=[vmem] * slots,
        scratch_shapes=[
            pltpu.VMEM((heads, tokens, query_width), jnp.bfloat16),
            pltpu.VMEM((heads, tokens, query_width), jnp.bfloat16),
            pltpu.VMEM((heads, tokens, value_width), jnp.bfloat16),
            pltpu.VMEM((tokens, 2 * rope_width), jnp.float32),
            pltpu.VMEM((tokens, tokens), jnp.float32),
        ],
        compiler_params=pltpu.CompilerParams(vmem_limit_bytes=VMEM_LIMIT),
        cost_estimate=pl.CostEstimate(
            flops=flops,
            bytes_accessed=2 * slots * rows * (q_width + kv_width) * 2 + 2 * heads * (query_width * q_width + kv_width * pair_width),
            transcendentals=slots * heads * tokens * tokens,
        ),
        name="attend",
    )(place, lengths, table, q_weight, kv_weight, *same, *other)


def place_kernel(count, offsets_ref, *refs):
    pieces, out_ref, sems = refs[:count], refs[-2], refs[-1]
    copies = []
    for index, piece in enumerate(pieces):
        width = piece.shape[1]
        columns = pl.ds(pl.multiple_of(offsets_ref[index], 128), width)
        copies.append(pltpu.make_async_copy(piece, out_ref.at[:, columns], sems.at[index]))
        copies[-1].start()
    for copy in copies:
        copy.wait()


def place_pieces(pieces, offsets, width, held=None):
    count = len(pieces)
    any_space = pl.BlockSpec(memory_space=pl.ANY)
    operands = [jnp.stack(offsets).astype(jnp.int32), *pieces]
    aliases = {}
    if held is not None:
        aliases = {len(operands): 0}
        operands.append(held)
    return pl.pallas_call(
        partial(place_kernel, count),
        out_shape=jax.ShapeDtypeStruct((pieces[0].shape[0], width), pieces[0].dtype),
        in_specs=[pl.BlockSpec(memory_space=pltpu.SMEM)] + [any_space] * (len(operands) - 1),
        out_specs=any_space,
        scratch_shapes=[pltpu.SemaphoreType.DMA((count,))],
        input_output_aliases=aliases,
        name="place_pieces",
    )(*operands)


def shards(latents, q_gain, kv_gain, q_weight, kv_weight, lengths):
    rope_width = latents.shape[1] - q_gain.shape[0] - kv_gain.shape[0]
    places = lax.axis_size("seq")
    parts = lax.axis_size("parts")
    half_places = places // 2
    place = lax.axis_index("seq")
    core = lax.axis_index("head")
    part = lax.axis_index("parts")
    tokens = 2 * latents.shape[0]
    local_heads = q_weight.shape[2]
    value_width = kv_weight.shape[3] - (q_weight.shape[3] - rope_width)
    block_width = local_heads * value_width

    def across(value, distance):
        return lax.ppermute(value, "seq", [(s, s ^ distance) for s in range(places)])

    def sibling(value):
        return lax.ppermute(value, "head", [(0, 1), (1, 0)])

    def other_part(value):
        return lax.ppermute(value, "parts", [(p, p ^ 1) for p in range(parts)])

    same = [prepare(latents, q_gain, kv_gain, lengths, jnp.stack([place, core]).astype(jnp.int32))]
    other = [sibling(same[0])]
    for distance in range(1, half_places):
        low_bit = distance & -distance
        same.append(across(same[distance ^ low_bit], low_bit))
        other.append(sibling(same[distance]))
    groups = [place ^ distance for distance in range(half_places)]

    own_query = jnp.transpose(q_weight[0], (1, 2, 0))
    own_pair = jnp.transpose(kv_weight[0], (1, 0, 2))

    share = 2 if parts % 2 == 0 and local_heads % 2 == 0 else 1
    per_part = local_heads // share
    side = lax.rem(part, share)
    far = []
    for index in range(per_part):
        head = side * per_part + index
        first = across(lax.dynamic_index_in_dim(own_query, head, 0, keepdims=True), half_places)
        second = across(lax.dynamic_index_in_dim(own_pair, head, 0, keepdims=True), half_places)
        far.append((first, second, head))
        if share == 2:
            far.append((other_part(first), other_part(second), (1 - side) * per_part + index))

    positions = jnp.arange(tokens, dtype=jnp.int32)[:, None].astype(jnp.float32)
    lanes = jnp.arange(rope_width, dtype=jnp.int32)[None, :]
    angles = positions * frequencies(lanes, rope_width // 2)
    signs = jnp.where(lanes < rope_width // 2, -1.0, 1.0)
    table = jnp.concatenate([jnp.cos(angles), jnp.sin(angles) * signs], axis=1)

    pieces, offsets = [], []
    for distance in range(half_places):
        (mixed,) = attend(
            [same[distance]], [other[distance]], [groups[distance]], core, own_query, own_pair, table, lengths, rope_width
        )
        pieces.append(across(mixed, distance) if distance else mixed)
        offsets.append((place ^ distance) * block_width)
    for query_part, pair_part, head in far:
        mixed_all = attend(same, other, groups, core, query_part, pair_part, table, lengths, rope_width)
        for distance in range(half_places):
            pieces.append(across(mixed_all[distance], distance) if distance else mixed_all[0])
            offsets.append((place ^ distance ^ half_places) * block_width + head * value_width)
    return place_pieces(pieces, offsets, places * block_width)


def solution(mesh):
    return jax.shard_map(
        shards,
        mesh=mesh,
        in_specs=(
            P(("parts", "seq", "head"), None),
            P(),
            P(),
            P("head", None, "seq", None),
            P("head", None, "seq", None),
            P("parts", None),
        ),
        out_specs=P(("parts", "seq"), "head"),
        check_vma=False,
    )
```

time: 369 us -> 328 us (0.89)
  Pallas kernels: 0 us -> 196 us
  blocking collectives: 98.3 us -> 0 us
  matrix products: 96.7 us -> 0 us
  starting transfers between devices: 0.01 us -> 31.9 us
  waiting for transfers between devices: 103 us -> 78.5 us
  other arithmetic: 26.1 us -> 3.5 us
  local copies, waits for them, and re-layouts: 30.2 us -> 14.9 us
  between operations: 13.6 us -> 0.58 us
    pallas_call x0 -> x10, Pallas kernels: none -> 196 us  [the longest x1 129 us: place_pieces(): pl.pallas_call(partial(place_kernel, count), out_shape=jax.ShapeDtypeStru...]
    all_gather x1 -> x0, waiting for transfers between devices: 102 us -> none  [shards(): lax.all_gather(latents, ('seq', 'head'), axis=0, tiled=True)]
    all_to_all x1 -> x0, blocking collectives: 98.3 us -> none  [shards(): lax.all_to_all(mixed_all, 'seq', split_axis=0, concat_axis=1, tiled=True)]
    dot_general x25 -> x0, matrix products: 80.7 us -> none  [the longest x8 30.8 us: tile_scores(): jnp.einsum('qhd,khd->hqk', query_nope, key_nope, preferred_element_type=j...]
    ppermute x0 -> x30, waiting for transfers between devices: none -> 78.5 us  [the longest x22 78 us: across(): lax.ppermute(value, 'seq', [(s, s ^ distance) for s in range(places)])]
    ppermute x0 -> x30, starting transfers between devices: none -> 31.9 us  [the longest x22 26.3 us: across(): lax.ppermute(value, 'seq', [(s, s ^ distance) for s in range(places)])]
    unnamed x1 -> x0, matrix products: 16.1 us -> none
    all_to_all x2 -> x0, local copies, waits for them, and re-layouts: 13 us -> none  [shards(): lax.all_to_all(mixed_all, 'seq', split_axis=0, concat_axis=1, tiled=True)]
  transfers between devices with their start and end apart: 1 -> 30, of which waited for: 1 -> 7; matrix products, arithmetic and copies ran while one was open for 0% -> 3% of each run, Pallas kernels for 0% -> 20%
where the time goes in v1:
time: 328 us; the launch traced here: 325 us
  Pallas kernels  196 us (60%)
  waiting for transfers between devices  78.5 us (24%)
  starting transfers between devices  31.9 us (10%)
  local copies, waits for them, and re-layouts  14.9 us (5%)
  other arithmetic  3.5 us (1%)
    pallas_call x1, Pallas kernels, place_pieces(): pl.pallas_call(partial(place_kernel, count), out_shape=jax.ShapeDtypeStru...  129 us
    ppermute x22, waiting for transfers between devices, across(): lax.ppermute(value, 'seq', [(s, s ^ distance) for s in range(places)])  78 us
    pallas_call x8, Pallas kernels, attend(): pl.pallas_call(partial(attend_kernel, sizes), out_shape=[out_shape] * slo...  65.3 us
    ppermute x22, starting transfers between devices, across(): lax.ppermute(value, 'seq', [(s, s ^ distance) for s in range(places)])  26.3 us
    unnamed x53, local copies, waits for them, and re-layouts  9.2 us
  transfers between devices with their start and end apart: 30, of which 7 were waited for; matrix products, arithmetic and copies ran while one was open for 3% of the time, Pallas kernels for 20%

profile of v1, /device:TPU:0, one launch (start us, length us, event | category | flops | bytes accessed | tf_op | source)
XLA Modules:
  0.0 325.1 jit_solution(5107907017278001170)
XLA Ops:
  4.8 3.1 collective-permute-start.4
  9.4 23.0 %collective-permute-done.4.refs_0_.refs_2_ = bf16[256,2176]{1,0:T(8,128)(2,1)S(1)} collective-permute-done((bf16[256,2176]{1,0:T(8,128)(2,1)S(1)}, bf16[256,2176]{1,0:T(8,128)(2,1)S(1)}, u32[]{:S(2)}, u32[]{:S(2)}) %collective-permute-start.4) | collective-permute-done | bytes 1114144 | tf_op jit(solution)/shard_map/ppermute | solution.py:216
  34.2 2.3 copy.17
  36.5 1.9 dynamic-slice_bitcast_fusion.2
  38.4 2.6 collective-permute-start.21
  41.3 2.4 dynamic-slice_bitcast_fusion
  43.8 16.2 %collective-permute-done.21.kv_weight_ref = bf16[1,512,256]{2,1,0:T(8,128)(2,1)} collective-permute-done((bf16[1,512,256]{2,1,0:T(8,128)(2,1)}, bf16[1,512,256]{2,1,0:T(8,128)(2,1)}, u32[]{:S(2)}, u32[]{:S(2)}) %collective-permute-start.21) | collective-permute-done | bytes 262176 | tf_op jit(solution)/shard_map/ppermute | solution.py:216
  60.0 18.2 %collective-permute-done.11.kv_weight_ref = bf16[1,512,256]{2,1,0:T(8,128)(2,1)} collective-permute-done((bf16[1,512,256]{2,1,0:T(8,128)(2,1)}, bf16[1,512,256]{2,1,0:T(8,128)(2,1)}, u32[]{:S(2)}, u32[]{:S(2)}) %collective-permute-start.11) | collective-permute-done | bytes 262176 | tf_op jit(solution)/shard_map/ppermute | solution.py:216
  78.8 2.0 multiply_cosine_fusion
  80.8 9.7 %collective-permute-done.20.q_weight_ref = bf16[1,192,1536]{2,1,0:T(8,128)(2,1)} collective-permute-done((bf16[1,192,1536]{2,1,0:T(8,128)(2,1)}, bf16[1,192,1536]{2,1,0:T(8,128)(2,1)}, u32[]{:S(2)}, u32[]{:S(2)}) %collective-permute-start.20) | collective-permute-done | bytes 589856 | tf_op jit(solution)/shard_map/ppermute | solution.py:216
  95.8 7.5 %attend.10 = bf16[512,512]{1,0:T(8,128)(2,1)S(1)} custom-call(s32[2]{0:T(128)S(1)} %pad_add_fusion.3.place_ref, s32[8,8]{1,0:T(8,128)S(1)} %copy-done.9, f32[512,128]{1,0:T(8,128)S(1)} %pad_maximum_fusion.table_ref, bf16[4,192,1536]{2,1,0:T(8,128)(2,1)} %bitcast.52, bf16[4,512,256]{2,1,0:T(8,128)(2,1)S(1)} %bitcast.46, ...), custom_call_target="tpu_custom_call" | custom-call | flops 2415919104 | bytes 5505024 | tf_op jit(solution)/shard_map/attend/pallas_call | solution.py:149
  103.3 7.5 %attend.9 = bf16[512,512]{1,0:T(8,128)(2,1)S(1)} custom-call(s32[2]{0:T(128)S(1)} %pad_add_fusion.2.place_ref, s32[8,8]{1,0:T(8,128)S(1)} %copy-done.9, f32[512,128]{1,0:T(8,128)S(1)} %pad_maximum_fusion.table_ref, bf16[4,192,1536]{2,1,0:T(8,128)(2,1)} %bitcast.53, bf16[4,512,256]{2,1,0:T(8,128)(2,1)S(1)} %bitcast.47, ...), custom_call_target="tpu_custom_call" | custom-call | flops 2415919104 | bytes 5505024 | tf_op jit(solution)/shard_map/attend/pallas_call | solution.py:149
  112.7 6.5 %collective-permute-done.10.q_weight_ref = bf16[1,192,1536]{2,1,0:T(8,128)(2,1)} collective-permute-done((bf16[1,192,1536]{2,1,0:T(8,128)(2,1)}, bf16[1,192,1536]{2,1,0:T(8,128)(2,1)}, u32[]{:S(2)}, u32[]{:S(2)}) %collective-permute-start.10) | collective-permute-done | bytes 589856 | tf_op jit(solution)/shard_map/ppermute | solution.py:216
  121.4 8.7 %attend.15 = (bf16[512,128]{1,0:T(8,128)(2,1)S(1)}, bf16[512,128]{1,0:T(8,128)(2,1)S(1)}, bf16[512,128]{1,0:T(8,128)(2,1)S(1)}, bf16[512,128]{1,0:T(8,128)(2,1)S(1)}) custom-call(s32[5]{0:T(128)S(1)} %stack.155.place_ref, s32[8,8]{1,0:T(8,128)S(1)} %copy-done.9, f32[512,128]{1,0:T(8,128)S(1)} %pad_maximum_fusion.table_ref, ...), custom_call_target="tpu_custom_call" | custom-call | flops 2415919104 | bytes 9240576 | tf_op jit(solution)/shard_map/attend/pallas_call | solution.py:149
  132.3 8.6 %attend.14 = (bf16[512,128]{1,0:T(8,128)(2,1)S(1)}, bf16[512,128]{1,0:T(8,128)(2,1)S(1)}, bf16[512,128]{1,0:T(8,128)(2,1)S(1)}, bf16[512,128]{1,0:T(8,128)(2,1)S(1)}) custom-call(s32[5]{0:T(128)S(1)} %stack.155.place_ref, s32[8,8]{1,0:T(8,128)S(1)} %copy-done.9, f32[512,128]{1,0:T(8,128)S(1)} %pad_maximum_fusion.table_ref, ...), custom_call_target="tpu_custom_call" | custom-call | flops 2415919104 | bytes 9240576 | tf_op jit(solution)/shard_map/attend/pallas_call | solution.py:149
  141.5 8.2 %attend.11 = bf16[512,512]{1,0:T(8,128)(2,1)S(1)} custom-call(s32[2]{0:T(128)S(1)} %pad_add_fusion.4.place_ref, s32[8,8]{1,0:T(8,128)S(1)} %copy-done.9, f32[512,128]{1,0:T(8,128)S(1)} %pad_maximum_fusion.table_ref, bf16[4,192,1536]{2,1,0:T(8,128)(2,1)} %bitcast.54, bf16[4,512,256]{2,1,0:T(8,128)(2,1)S(1)} %bitcast.48, ...), custom_call_target="tpu_custom_call" | custom-call | flops 2415919104 | bytes 5505024 | tf_op jit(solution)/shard_map/attend/pallas_call | solution.py:149
  149.8 2.0 collective-permute-start.28
  153.4 1.9 collective-permute-start.9
  155.3 8.4 %attend.13 = (bf16[512,128]{1,0:T(8,128)(2,1)S(1)}, bf16[512,128]{1,0:T(8,128)(2,1)S(1)}, bf16[512,128]{1,0:T(8,128)(2,1)S(1)}, bf16[512,128]{1,0:T(8,128)(2,1)S(1)}) custom-call(s32[5]{0:T(128)S(1)} %stack.155.place_ref, s32[8,8]{1,0:T(8,128)S(1)} %copy-done.9, f32[512,128]{1,0:T(8,128)S(1)} %pad_maximum_fusion.table_ref, ...), custom_call_target="tpu_custom_call" | custom-call | flops 2415919104 | bytes 9240576 | tf_op jit(solution)/shard_map/attend/pallas_call | solution.py:149
  164.1 2.7 collective-permute-start.24
  167.3 4.4 %collective-permute-done.22.refs_13_ = bf16[512,128]{1,0:T(8,128)(2,1)S(1)} collective-permute-done((bf16[512,128]{1,0:T(8,128)(2,1)S(1)}, bf16[512,128]{1,0:T(8,128)(2,1)S(1)}, u32[]{:S(2)}, u32[]{:S(2)}) %collective-permute-start.22) | collective-permute-done | bytes 131104 | tf_op jit(solution)/shard_map/ppermute | solution.py:216
  173.1 8.8 %attend.12 = (bf16[512,128]{1,0:T(8,128)(2,1)S(1)}, bf16[512,128]{1,0:T(8,128)(2,1)S(1)}, bf16[512,128]{1,0:T(8,128)(2,1)S(1)}, bf16[512,128]{1,0:T(8,128)(2,1)S(1)}) custom-call(s32[5]{0:T(128)S(1)} %stack.155.place_ref, s32[8,8]{1,0:T(8,128)S(1)} %copy-done.9, f32[512,128]{1,0:T(8,128)S(1)} %pad_maximum_fusion.table_ref, ...), custom_call_target="tpu_custom_call" | custom-call | flops 2415919104 | bytes 9240576 | tf_op jit(solution)/shard_map/attend/pallas_call | solution.py:149
  186.6 7.5 %attend.8.refs_0_ = bf16[512,512]{1,0:T(8,128)(2,1)S(1)} custom-call(s32[2]{0:T(128)S(1)} %pad_add_fusion.place_ref, s32[8,8]{1,0:T(8,128)S(1)} %copy-done.9, f32[512,128]{1,0:T(8,128)S(1)} %pad_maximum_fusion.table_ref, bf16[4,192,1536]{2,1,0:T(8,128)(2,1)} %bitcast.55, bf16[4,512,256]{2,1,0:T(8,128)(2,1)S(1)} %bitcast.49, ...), custom_call_target="tpu_custom_call" | custom-call | flops 2415919104 | bytes 5505024 | tf_op jit(solution)/shard_map/attend/pallas_call | solution.py:149
  195.9 129.0 %place_pieces.1 = bf16[512,4096]{1,0:T(8,128)(2,1)} custom-call(s32[20]{0:T(128)} %stack.144.offsets_ref, bf16[512,512]{1,0:T(8,128)(2,1)} %copy-done.3, bf16[512,512]{1,0:T(8,128)(2,1)} %copy-done.12, bf16[512,512]{1,0:T(8,128)(2,1)} %copy-done.11, bf16[512,512]{1,0:T(8,128)(2,1)} %copy-done.13, bf16[512,128]{1,0:T(8,128)(2,1)} %copy-done.7, ...), custom_call_target="tpu_custom_call" | custom-call | tf_op jit(solution)/shard_map/place_pieces/pallas_call | solution.py:191
  (113 shorter events, 31.4 us)
Async XLA Ops:
  4.8 27.7 %collective-permute-start.4 = (bf16[256,2176]{1,0:T(8,128)(2,1)S(1)}, bf16[256,2176]{1,0:T(8,128)(2,1)S(1)}, u32[]{:S(2)}, u32[]{:S(2)}) collective-permute-start(bf16[256,2176]{1,0:T(8,128)(2,1)S(1)} %prepare.1.refs_0_), channel_id=1, source_target_pairs={{0,4},{2,6},{4,0},{6,2},{8,12},{10,14},{12,8},{14,10},{1,5},{3,7},... | collective-permute-start | bytes 3342344 | tf_op jit(solution)/shard_map/ppermute | solution.py:216
  7.9 33.4 %collective-permute-start.1 = (bf16[256,2176]{1,0:T(8,128)(2,1)S(1)}, bf16[256,2176]{1,0:T(8,128)(2,1)S(1)}, u32[]{:S(2)}, u32[]{:S(2)}) collective-permute-start(bf16[256,2176]{1,0:T(8,128)(2,1)S(1)} %prepare.1.refs_0_), channel_id=1, source_target_pairs={{0,2},{2,0},{4,6},{6,4},{8,10},{10,8},{12,14},{14,12},{1,3},{3,1},... | collective-permute-start | bytes 3342344 | tf_op jit(solution)/shard_map/ppermute | solution.py:216
  32.5 45.7 %collective-permute-start.7 = (bf16[256,2176]{1,0:T(8,128)(2,1)S(1)}, bf16[256,2176]{1,0:T(8,128)(2,1)}, u32[]{:S(2)}, u32[]{:S(2)}) collective-permute-start(bf16[256,2176]{1,0:T(8,128)(2,1)S(1)} %collective-permute-done.4.refs_0_.refs_2_), channel_id=1, source_target_pairs={{0,2},{2,0},{4,6},{6,4},{8,10},{10,8},{12,14},{14,12},{1,3},{3,1},... | collective-permute-start | bytes 3342344 | tf_op jit(solution)/shard_map/ppermute | solution.py:216
  36.5 54.0 %collective-permute-start.5 = (bf16[256,2176]{1,0:T(8,128)(2,1)S(1)}, bf16[256,2176]{1,0:T(8,128)(2,1)}, u32[]{:S(2)}, u32[]{:S(2)}) collective-permute-start(bf16[256,2176]{1,0:T(8,128)(2,1)S(1)} %collective-permute-done.4.refs_0_.refs_2_), channel_id=1, source_target_pairs={{0,1},{1,0},{2,3},{3,2},{4,5},{5,4},{6,7},{7,6},{8,9},{9,8},{10,11... | collective-permute-start | bytes 3342344 | tf_op jit(solution)/shard_map/ppermute | solution.py:219
  38.4 21.6 %collective-permute-start.21 = (bf16[1,512,256]{2,1,0:T(8,128)(2,1)}, bf16[1,512,256]{2,1,0:T(8,128)(2,1)}, u32[]{:S(2)}, u32[]{:S(2)}) collective-permute-start(bf16[1,512,256]{2,1,0:T(8,128)(2,1)} %get-tuple-element.39), channel_id=1, source_target_pairs={{0,8},{2,10},{4,12},{6,14},{8,0},{10,2},{12,4},{14,6},{1,9},{3,11}... | collective-permute-start | bytes 786440 | tf_op jit(solution)/shard_map/ppermute | solution.py:216
  41.0 37.2 %collective-permute-start.11 = (bf16[1,512,256]{2,1,0:T(8,128)(2,1)}, bf16[1,512,256]{2,1,0:T(8,128)(2,1)}, u32[]{:S(2)}, u32[]{:S(2)}) collective-permute-start(bf16[1,512,256]{2,1,0:T(8,128)(2,1)} %get-tuple-element.40), channel_id=1, source_target_pairs={{0,8},{2,10},{4,12},{6,14},{8,0},{10,2},{12,4},{14,6},{1,9},{3,11}... | collective-permute-start | bytes 786440 | tf_op jit(solution)/shard_map/ppermute | solution.py:216
  41.3 52.6 %collective-permute-start.2 = (bf16[256,2176]{1,0:T(8,128)(2,1)S(1)}, bf16[256,2176]{1,0:T(8,128)(2,1)}, u32[]{:S(2)}, u32[]{:S(2)}) collective-permute-start(bf16[256,2176]{1,0:T(8,128)(2,1)S(1)} %collective-permute-done.1.refs_0_.refs_1_), channel_id=1, source_target_pairs={{0,1},{1,0},{2,3},{3,2},{4,5},{5,4},{6,7},{7,6},{8,9},{9,8},{10,11... | collective-permute-start | bytes 3342344 | tf_op jit(solution)/shard_map/ppermute | solution.py:219
  59.9 30.5 %collective-permute-start.20 = (bf16[1,192,1536]{2,1,0:T(8,128)(2,1)}, bf16[1,192,1536]{2,1,0:T(8,128)(2,1)}, u32[]{:S(2)}, u32[]{:S(2)}) collective-permute-start(bf16[1,192,1536]{2,1,0:T(8,128)(2,1)} %get-tuple-element.37), channel_id=1, source_target_pairs={{0,8},{2,10},{4,12},{6,14},{8,0},{10,2},{12,4},{14,6},{1,9},{3,11}... | collective-permute-start | bytes 1769480 | tf_op jit(solution)/shard_map/ppermute | solution.py:216
  78.2 42.6 %collective-permute-start = (bf16[256,2176]{1,0:T(8,128)(2,1)S(1)}, bf16[256,2176]{1,0:T(8,128)(2,1)}, u32[]{:S(2)}, u32[]{:S(2)}) collective-permute-start(bf16[256,2176]{1,0:T(8,128)(2,1)S(1)} %prepare.1.refs_0_), channel_id=1, source_target_pairs={{0,1},{1,0},{2,3},{3,2},{4,5},{5,4},{6,7},{7,6},{8,9},{9,8},{10,11... | collective-permute-start | bytes 3342344 | tf_op jit(solution)/shard_map/ppermute | solution.py:219
  78.2 43.1 %collective-permute-start.8 = (bf16[256,2176]{1,0:T(8,128)(2,1)}, bf16[256,2176]{1,0:T(8,128)(2,1)}, u32[]{:S(2)}, u32[]{:S(2)}) collective-permute-start(bf16[256,2176]{1,0:T(8,128)(2,1)} %collective-permute-done.7.refs_0_.refs_3_), channel_id=1, source_target_pairs={{0,1},{1,0},{2,3},{3,2},{4,5},{5,4},{6,7},{7,6},{8,9},{9,8},{10,11... | collective-permute-start | bytes 3342344 | tf_op jit(solution)/shard_map/ppermute | solution.py:219
  90.5 28.8 %collective-permute-start.10 = (bf16[1,192,1536]{2,1,0:T(8,128)(2,1)}, bf16[1,192,1536]{2,1,0:T(8,128)(2,1)}, u32[]{:S(2)}, u32[]{:S(2)}) collective-permute-start(bf16[1,192,1536]{2,1,0:T(8,128)(2,1)} %get-tuple-element.38), channel_id=1, source_target_pairs={{0,8},{2,10},{4,12},{6,14},{8,0},{10,2},{12,4},{14,6},{1,9},{3,11}... | collective-permute-start | bytes 1769480 | tf_op jit(solution)/shard_map/ppermute | solution.py:216
  90.5 30.3 %collective-permute-start.25 = (bf16[1,192,1536]{2,1,0:T(8,128)(2,1)}, bf16[1,192,1536]{2,1,0:T(8,128)(2,1)}, u32[]{:S(2)}, u32[]{:S(2)}) collective-permute-start(bf16[1,192,1536]{2,1,0:T(8,128)(2,1)} %collective-permute-done.20.q_weight_ref), channel_id=1, source_target_pairs={{0,16},{16,0},{1,17},{17,1},{2,18},{18,2},{3,19},{19,3},{4,20},{20... | collective-permute-start | bytes 1769480 | tf_op jit(solution)/shard_map/ppermute | solution.py:222
  94.0 17.3 %collective-permute-start.26 = (bf16[1,512,256]{2,1,0:T(8,128)(2,1)}, bf16[1,512,256]{2,1,0:T(8,128)(2,1)S(1)}, u32[]{:S(2)}, u32[]{:S(2)}) collective-permute-start(bf16[1,512,256]{2,1,0:T(8,128)(2,1)} %collective-permute-done.21.kv_weight_ref), channel_id=1, source_target_pairs={{0,16},{16,0},{1,17},{17,1},{2,18},{18,2},{3,19},{19,3},{4,20},{20... | collective-permute-start | bytes 786440 | tf_op jit(solution)/shard_map/ppermute | solution.py:222
  111.3 38.5 %collective-permute-start.16 = (bf16[1,512,256]{2,1,0:T(8,128)(2,1)}, bf16[1,512,256]{2,1,0:T(8,128)(2,1)S(1)}, u32[]{:S(2)}, u32[]{:S(2)}) collective-permute-start(bf16[1,512,256]{2,1,0:T(8,128)(2,1)} %collective-permute-done.11.kv_weight_ref), channel_id=1, source_target_pairs={{0,16},{16,0},{1,17},{17,1},{2,18},{18,2},{3,19},{19,3},{4,20},{20... | collective-permute-start | bytes 786440 | tf_op jit(solution)/shard_map/ppermute | solution.py:222
  119.3 32.6 %collective-permute-start.15 = (bf16[1,192,1536]{2,1,0:T(8,128)(2,1)}, bf16[1,192,1536]{2,1,0:T(8,128)(2,1)S(1)}, u32[]{:S(2)}, u32[]{:S(2)}) collective-permute-start(bf16[1,192,1536]{2,1,0:T(8,128)(2,1)} %collective-permute-done.10.q_weight_ref), channel_id=1, source_target_pairs={{0,16},{16,0},{1,17},{17,1},{2,18},{18,2},{3,19},{19,3},{4,20},{20... | collective-permute-start | bytes 1769480 | tf_op jit(solution)/shard_map/ppermute | solution.py:222
  120.8 31.1 %collective-permute-start.6 = (bf16[512,512]{1,0:T(8,128)(2,1)S(1)}, bf16[512,512]{1,0:T(8,128)(2,1)S(1)}, u32[]{:S(2)}, u32[]{:S(2)}) collective-permute-start(bf16[512,512]{1,0:T(8,128)(2,1)S(1)} %attend.10), channel_id=1, source_target_pairs={{0,4},{2,6},{4,0},{6,2},{8,12},{10,14},{12,8},{14,10},{1,5},{3,7},... | collective-permute-start | bytes 1572872 | tf_op jit(solution)/shard_map/ppermute | solution.py:216
  120.8 32.6 %collective-permute-start.3 = (bf16[512,512]{1,0:T(8,128)(2,1)S(1)}, bf16[512,512]{1,0:T(8,128)(2,1)S(1)}, u32[]{:S(2)}, u32[]{:S(2)}) collective-permute-start(bf16[512,512]{1,0:T(8,128)(2,1)S(1)} %attend.9), channel_id=1, source_target_pairs={{0,2},{2,0},{4,6},{6,4},{8,10},{10,8},{12,14},{14,12},{1,3},{3,1},... | collective-permute-start | bytes 1572872 | tf_op jit(solution)/shard_map/ppermute | solution.py:216
  130.8 32.9 %collective-permute-start.27 = (bf16[512,128]{1,0:T(8,128)(2,1)S(1)}, bf16[512,128]{1,0:T(8,128)(2,1)S(1)}, u32[]{:S(2)}, u32[]{:S(2)}) collective-permute-start(bf16[512,128]{1,0:T(8,128)(2,1)S(1)} %get-tuple-element.34), channel_id=1, source_target_pairs={{0,2},{2,0},{4,6},{6,4},{8,10},{10,8},{12,14},{14,12},{1,3},{3,1},... | collective-permute-start | bytes 393224 | tf_op jit(solution)/shard_map/ppermute | solution.py:216
  151.8 15.0 %collective-permute-start.29 = (bf16[512,128]{1,0:T(8,128)(2,1)S(1)}, bf16[512,128]{1,0:T(8,128)(2,1)S(1)}, u32[]{:S(2)}, u32[]{:S(2)}) collective-permute-start(bf16[512,128]{1,0:T(8,128)(2,1)S(1)} %get-tuple-element.36), channel_id=1, source_target_pairs={{0,6},{2,4},{4,2},{6,0},{8,14},{10,12},{12,10},{14,8},{1,7},{3,5},... | collective-permute-start | bytes 393224 | tf_op jit(solution)/shard_map/ppermute | solution.py:216
  151.9 19.8 %collective-permute-start.22 = (bf16[512,128]{1,0:T(8,128)(2,1)S(1)}, bf16[512,128]{1,0:T(8,128)(2,1)S(1)}, u32[]{:S(2)}, u32[]{:S(2)}) collective-permute-start(bf16[512,128]{1,0:T(8,128)(2,1)S(1)} %get-tuple-element.30), channel_id=1, source_target_pairs={{0,2},{2,0},{4,6},{6,4},{8,10},{10,8},{12,14},{14,12},{1,3},{3,1},... | collective-permute-start | bytes 393224 | tf_op jit(solution)/shard_map/ppermute | solution.py:216
  153.4 41.6 %collective-permute-start.9 = (bf16[512,512]{1,0:T(8,128)(2,1)S(1)}, bf16[512,512]{1,0:T(8,128)(2,1)S(1)}, u32[]{:S(2)}, u32[]{:S(2)}) collective-permute-start(bf16[512,512]{1,0:T(8,128)(2,1)S(1)} %attend.11), channel_id=1, source_target_pairs={{0,6},{2,4},{4,2},{6,0},{8,14},{10,12},{12,10},{14,8},{1,7},{3,5},... | collective-permute-start | bytes 1572872 | tf_op jit(solution)/shard_map/ppermute | solution.py:216
  163.7 18.2 %collective-permute-start.23 = (bf16[512,128]{1,0:T(8,128)(2,1)S(1)}, bf16[512,128]{1,0:T(8,128)(2,1)S(1)}, u32[]{:S(2)}, u32[]{:S(2)}) collective-permute-start(bf16[512,128]{1,0:T(8,128)(2,1)S(1)} %get-tuple-element.31), channel_id=1, source_target_pairs={{0,4},{2,6},{4,0},{6,2},{8,12},{10,14},{12,8},{14,10},{1,5},{3,7},... | collective-permute-start | bytes 393224 | tf_op jit(solution)/shard_map/ppermute | solution.py:216
  164.1 19.0 %collective-permute-start.24 = (bf16[512,128]{1,0:T(8,128)(2,1)S(1)}, bf16[512,128]{1,0:T(8,128)(2,1)S(1)}, u32[]{:S(2)}, u32[]{:S(2)}) collective-permute-start(bf16[512,128]{1,0:T(8,128)(2,1)S(1)} %get-tuple-element.32), channel_id=1, source_target_pairs={{0,6},{2,4},{4,2},{6,0},{8,14},{10,12},{12,10},{14,8},{1,7},{3,5},... | collective-permute-start | bytes 393224 | tf_op jit(solution)/shard_map/ppermute | solution.py:216
  166.8 17.3 %collective-permute-start.17 = (bf16[512,128]{1,0:T(8,128)(2,1)S(1)}, bf16[512,128]{1,0:T(8,128)(2,1)S(1)}, u32[]{:S(2)}, u32[]{:S(2)}) collective-permute-start(bf16[512,128]{1,0:T(8,128)(2,1)S(1)} %get-tuple-element.26), channel_id=1, source_target_pairs={{0,2},{2,0},{4,6},{6,4},{8,10},{10,8},{12,14},{14,12},{1,3},{3,1},... | collective-permute-start | bytes 393224 | tf_op jit(solution)/shard_map/ppermute | solution.py:216
  (32 other events, 301.1 us)

commit v2 on v1

v2 whole, which is shorter than its diff:
```python
from functools import partial
import math

import jax
import jax.numpy as jnp
from jax import lax
from jax.experimental import pallas as pl
from jax.experimental.pallas import tpu as pltpu
from jax.sharding import PartitionSpec as P

epsilon = 1e-06
VMEM_LIMIT = 32 * 1024 * 1024
LIGHT = pl.CostEstimate(flops=1024, bytes_accessed=1024, transcendentals=0)
NT = (((1,), (1,)), ((), ()))
NN = (((1,), (0,)), ((), ()))


def frequencies(lane, half_width):
    steps = lax.rem(lane, half_width).astype(jnp.float32)
    return jnp.exp(steps * (-math.log(10000.0) / half_width))


def begins_of(lengths_ref, group, token_ids):
    begin = jnp.zeros_like(token_ids)
    start = jnp.int32(0)
    for slot in range(lengths_ref.shape[1]):
        begin = jnp.where(token_ids >= start, start, begin)
        start = start + lengths_ref[group, slot]
    return begin


def prepare_kernel(q_width, kv_width, place_ref, lengths_ref, latents_ref, q_gain_ref, kv_gain_ref, out_ref):
    rows = latents_ref.shape[1]
    rope_width = latents_ref.shape[0] - q_width - kv_width
    half_width = rope_width // 2

    def normalized(low, width, gain_ref):
        part = latents_ref[low : low + width, :].astype(jnp.float32)
        scale = lax.rsqrt(jnp.mean(part * part, axis=0, keepdims=True) + epsilon)
        return (jnp.transpose(part * scale) * gain_ref[...]).astype(jnp.bfloat16)

    out_ref[:, :q_width] = normalized(0, q_width, q_gain_ref)
    out_ref[:, q_width : q_width + kv_width] = normalized(q_width, kv_width, kv_gain_ref)
    token_ids = lax.broadcasted_iota(jnp.int32, (1, rows), 1) + place_ref[1] * rows
    position = (token_ids - begins_of(lengths_ref, place_ref[0], token_ids)).astype(jnp.float32)
    angle = position * frequencies(lax.broadcasted_iota(jnp.int32, (half_width, rows), 0), half_width)
    cosine, sine = jnp.cos(angle), jnp.sin(angle)
    rope = latents_ref[q_width + kv_width :, :].astype(jnp.float32)
    first, second = rope[:half_width], rope[half_width:]
    turned = jnp.concatenate([first * cosine - second * sine, second * cosine + first * sine], axis=0)
    spare = out_ref.shape[1] - q_width - kv_width - rope_width
    if spare:
        turned = jnp.concatenate([turned, jnp.zeros((spare, rows), jnp.float32)], axis=0)
    out_ref[:, q_width + kv_width :] = jnp.transpose(turned).astype(jnp.bfloat16)


def prepare(latents, q_gain, kv_gain, lengths, place):
    rows = latents.shape[0]
    width = -(-latents.shape[1] // 128) * 128
    smem = pl.BlockSpec(memory_space=pltpu.SMEM)
    vmem = pl.BlockSpec(memory_space=pltpu.VMEM)
    return pl.pallas_call(
        partial(prepare_kernel, q_gain.shape[0], kv_gain.shape[0]),
        out_shape=jax.ShapeDtypeStruct((rows, width), jnp.bfloat16),
        in_specs=[smem, smem, vmem, vmem, vmem],
        out_specs=vmem,
        compiler_params=pltpu.CompilerParams(vmem_limit_bytes=VMEM_LIMIT),
        cost_estimate=LIGHT,
        name="prepare",
    )(place, lengths, jnp.transpose(latents), q_gain[None, :], kv_gain[None, :])


def pick_kernel(index_ref, source_ref, out_ref):
    out_ref[...] = source_ref[...].reshape(out_ref.shape)


def pick(source, index, block, axis):
    shape = list(source.shape)
    shape[axis] = block
    out_shape = [entry for entry in shape if entry != 1]
    position = lambda step, index_ref: tuple(index_ref[0] if at == axis else 0 for at in range(len(shape)))
    return pl.pallas_call(
        pick_kernel,
        grid_spec=pltpu.PrefetchScalarGridSpec(
            num_scalar_prefetch=1,
            grid=(1,),
            in_specs=[pl.BlockSpec(tuple(shape), position)],
            out_specs=pl.BlockSpec(tuple(out_shape), lambda step, index_ref: (0,) * len(out_shape)),
        ),
        out_shape=jax.ShapeDtypeStruct(tuple(out_shape), source.dtype),
        compiler_params=pltpu.CompilerParams(vmem_limit_bytes=VMEM_LIMIT),
        cost_estimate=LIGHT,
        name="pick",
    )(jnp.reshape(index, (1,)).astype(jnp.int32), source)


def project(tokens_ref, sizes, weight_refs, pair_at):
    heads, q_width, kv_width, nope_width, rope_width, value_width = sizes
    query_width, pair_width = nope_width + rope_width, nope_width + value_width

    def dot(tokens, weight, dims):
        return lax.dot_general(tokens, weight, dims, preferred_element_type=jnp.float32)

    latent = tokens_ref[:, q_width : q_width + kv_width]
    if pair_at is None:
        query_ref, pair_ref = weight_refs
        joint = dot(latent, pair_ref[...], NN)
        pair = [joint[:, head * pair_width : (head + 1) * pair_width] for head in range(heads)]
    else:
        pair = []
        for head in range(heads):
            low = pair_at[head] * pair_width
            pair.append(dot(latent, weight_refs[heads + head][:, low : low + pair_width], NN))

    def query(low, high, chosen):
        parts = [(query_ref.at[head] if pair_at is None else weight_refs[head])[low:high, :] for head in chosen]
        return dot(tokens_ref[:, :q_width], jnp.concatenate(parts, axis=0), NT)

    nope = []
    for head in range(0, heads, 2):
        nope.append(query(0, nope_width, range(head, min(head + 2, heads))))
    group = nope_width // rope_width
    chosen = list(range(heads))
    while len(chosen) % group:
        chosen.append(heads - 1)
    rope = query(nope_width, query_width, chosen)
    return nope, rope, pair


def attend_kernel(sizes, slots, pair_at, place_ref, lengths_ref, table_ref, *refs):
    heads, q_width, kv_width, nope_width, rope_width, value_width = sizes
    weight_count = 2 if pair_at is None else 2 * heads
    weight_refs, refs = refs[:weight_count], refs[weight_count:]
    same_refs, other_refs, out_refs = refs[:slots], refs[slots : 2 * slots], refs[2 * slots : 3 * slots]
    tokens_ref, nope_ref, rope_ref, key_ref, value_ref, shared_ref, turn_ref, bias_ref = refs[3 * slots : 3 * slots + 8]
    result_ref = refs[-1] if slots > 1 else out_refs[0]
    core = place_ref[0]
    rows = same_refs[0].shape[0]
    tokens = 2 * rows
    half_width = rope_width // 2
    group_heads = nope_width // rope_width
    score_scale = (nope_width + rope_width) ** -0.5 * math.log2(math.e)
    slot_count = lengths_ref.shape[1]
    block = tokens // slot_count
    for head in range(heads):
        value_ref[head, :, value_width:] = jnp.ones((tokens, value_width), jnp.bfloat16)
    def one_group(slot, carry):
        group = place_ref[1 + slot]
        for index in range(slots):

            @pl.when(slot == index)
            def _(index=index):
                tokens_ref[pl.ds(pl.multiple_of(core * rows, rows), rows), :] = same_refs[index][...]
                tokens_ref[pl.ds(pl.multiple_of((1 - core) * rows, rows), rows), :] = other_refs[index][...]

        starts, start = [], jnp.int32(0)
        for index in range(slot_count):
            starts.append(start)
            start = start + lengths_ref[group, index]
        for index in range(slot_count):
            begin = jnp.int32(0)
            for entry in starts:
                begin = jnp.where(entry <= index * block, entry, begin)
            position = pl.multiple_of(index * block - begin, block)
            turn_ref[index * block : (index + 1) * block, :] = table_ref[pl.ds(position, block), :]
        row_ids = lax.broadcasted_iota(jnp.int32, (tokens, 1), 0)
        begins = begins_of(lengths_ref, group, row_ids)
        col_ids = lax.broadcasted_iota(jnp.int32, (tokens, tokens), 1)
        bias_ref[...] = jnp.where((col_ids <= row_ids) & (col_ids >= begins), 0.0, -jnp.inf)

        nope, rope, pair = project(tokens_ref, sizes, weight_refs, pair_at)
        for index, part in enumerate(nope):
            low = index * 2 * nope_width
            nope_ref[:, low : low + part.shape[1]] = (part * score_scale).astype(jnp.bfloat16)
        lane = lax.broadcasted_iota(jnp.int32, (tokens, nope_width), 1)
        is_first = lax.rem(lane, rope_width) < half_width
        for low in range(0, rope.shape[1], nope_width):
            part = rope[:, low : low + nope_width]
            swapped = jnp.where(
                is_first, pltpu.roll(part, nope_width - half_width, 1), pltpu.roll(part, half_width, 1)
            )
            turned = part * turn_ref[:, :nope_width] + swapped * turn_ref[:, nope_width:]
            rope_ref[:, low : low + nope_width] = (turned * score_scale).astype(jnp.bfloat16)
        for head in range(heads):
            both = pair[head].astype(jnp.bfloat16)
            key_ref[:, head * nope_width : (head + 1) * nope_width] = both[:, :nope_width]
            value_ref[head, :, :value_width] = both[:, nope_width:]
        shared = tokens_ref[:, q_width + kv_width : q_width + kv_width + rope_width]
        blank = jnp.zeros((tokens, rope_width), jnp.bfloat16)
        for index in range(group_heads):
            shared_ref[index] = jnp.concatenate(
                [shared if index == entry else blank for entry in range(group_heads)], axis=1
            )

        for head in range(heads):
            nope_span = slice(head * nope_width, (head + 1) * nope_width)
            rope_low = head // group_heads * nope_width
            for half in range(2):
                low, high = half * rows, (half + 1) * rows
                queries = jnp.concatenate(
                    [nope_ref[low:high, nope_span], rope_ref[low:high, rope_low : rope_low + nope_width]], axis=1
                )
                keys = jnp.concatenate([key_ref[:high, nope_span], shared_ref[head % group_heads, :high, :]], axis=1)
                scores = lax.dot_general(queries, keys, NT, preferred_element_type=jnp.float32)
                scores = scores + bias_ref[low:high, :high]
                terms = jnp.exp2(scores - jnp.max(scores, axis=1, keepdims=True)).astype(jnp.bfloat16)
                mixed = lax.dot_general(terms, value_ref[head, :high, :], NN, preferred_element_type=jnp.float32)
                result_ref[low:high, head * value_width : (head + 1) * value_width] = (
                    mixed[:, :value_width] / mixed[:, value_width:]
                ).astype(jnp.bfloat16)
        for index in range(slots if slots > 1 else 0):

            @pl.when(slot == index)
            def _(index=index):
                out_refs[index][...] = result_ref[...]

        return carry

    if slots > 1:
        lax.fori_loop(0, slots, one_group, 0)
    else:
        one_group(0, 0)


def attend(same, other, groups, core, weights, sizes, table, lengths, pair_at=None):
    slots = len(same)
    rows, width = same[0].shape
    heads, q_width, kv_width, nope_width, rope_width, value_width = sizes
    smem = pl.BlockSpec(memory_space=pltpu.SMEM)
    vmem = pl.BlockSpec(memory_space=pltpu.VMEM)
    place = jnp.stack([core] + groups).astype(jnp.int32)
    tokens = 2 * rows
    group_heads = nope_width // rope_width
    rope_heads = -(-heads // group_heads) * group_heads
    return pl.pallas_call(
        partial(attend_kernel, sizes, slots, pair_at),
        out_shape=[jax.ShapeDtypeStruct((tokens, heads * value_width), jnp.bfloat16)] * slots,
        in_specs=[smem, smem] + [vmem] * (1 + len(weights) + 2 * slots),
        out_specs=[vmem] * slots,
        scratch_shapes=[
            pltpu.VMEM((tokens, width), jnp.bfloat16),
            pltpu.VMEM((tokens, heads * nope_width), jnp.bfloat16),
            pltpu.VMEM((tokens, rope_heads * rope_width), jnp.bfloat16),
            pltpu.VMEM((tokens, heads * nope_width), jnp.bfloat16),
            pltpu.VMEM((heads, tokens, 2 * value_width), jnp.bfloat16),
            pltpu.VMEM((group_heads, tokens, nope_width), jnp.bfloat16),
            pltpu.VMEM((tokens, 2 * nope_width), jnp.float32),
            pltpu.VMEM((tokens, tokens), jnp.float32),
        ]
        + ([pltpu.VMEM((tokens, heads * value_width), jnp.bfloat16)] if slots > 1 else []),
        compiler_params=pltpu.CompilerParams(vmem_limit_bytes=VMEM_LIMIT),
        cost_estimate=LIGHT,
        name="attend",
    )(place, lengths, table, *weights, *same, *other)


def place_kernel(width, count, offsets_ref, *refs):
    pieces, out_ref, sems = refs[:count], refs[-2], refs[-1]
    copies = []
    for piece in pieces:
        for low in range(0, piece.shape[1], width):
            index = len(copies)
            columns = pl.ds(pl.multiple_of(offsets_ref[index], 128), width)
            copies.append(pltpu.make_async_copy(piece.at[:, low : low + width], out_ref.at[:, columns], sems.at[index]))
            copies[-1].start()
    for copy in copies:
        copy.wait()


def place_pieces(pieces, offsets, width, out_width, held=None):
    count = len(pieces)
    any_space = pl.BlockSpec(memory_space=pl.ANY)
    operands = [jnp.stack(offsets).astype(jnp.int32), *pieces]
    specs = [pl.BlockSpec(memory_space=pltpu.SMEM)] + [pl.BlockSpec(memory_space=pltpu.VMEM)] * count
    aliases = {}
    if held is not None:
        aliases = {len(operands): 0}
        operands.append(held)
        specs.append(any_space)
    return pl.pallas_call(
        partial(place_kernel, width, count),
        out_shape=jax.ShapeDtypeStruct((pieces[0].shape[0], out_width), pieces[0].dtype),
        in_specs=specs,
        out_specs=any_space,
        scratch_shapes=[pltpu.SemaphoreType.DMA((len(offsets),))],
        input_output_aliases=aliases,
        compiler_params=pltpu.CompilerParams(vmem_limit_bytes=VMEM_LIMIT),
        cost_estimate=LIGHT,
        name="place_pieces",
    )(*operands)


def after(value, *earlier):
    return lax.optimization_barrier((value, *earlier))[0]


def shards(latents, q_gain, kv_gain, q_weight, kv_weight, lengths):
    q_width, kv_width = q_gain.shape[0], kv_gain.shape[0]
    rope_width = latents.shape[1] - q_width - kv_width
    places = lax.axis_size("seq")
    parts = lax.axis_size("parts")
    half_places = places // 2
    place = lax.axis_index("seq")
    core = lax.axis_index("head")
    part = lax.axis_index("parts")
    tokens = 2 * latents.shape[0]
    local_heads = q_weight.shape[2]
    pair_width = kv_weight.shape[3]
    nope_width = q_weight.shape[3] - rope_width
    value_width = pair_width - nope_width
    block_width = local_heads * value_width
    sizes = (q_width, kv_width, nope_width, rope_width, value_width)

    def across(value, distance):
        return lax.ppermute(value, "seq", [(s, s ^ distance) for s in range(places)])

    def sibling(value):
        return lax.ppermute(value, "head", [(0, 1), (1, 0)])

    def other_part(value):
        return lax.ppermute(value, "parts", [(p, p ^ 1) for p in range(parts)])

    own_query = jnp.transpose(q_weight[0], (1, 2, 0))
    own_pair = jnp.reshape(kv_weight[0], (kv_width, local_heads * pair_width))
    positions = jnp.arange(tokens, dtype=jnp.int32)[:, None].astype(jnp.float32)
    lanes = jnp.arange(nope_width, dtype=jnp.int32)[None, :]
    angles = positions * frequencies(lanes, rope_width // 2)
    signs = jnp.where(lax.rem(lanes, rope_width) < rope_width // 2, -1.0, 1.0)
    table = jnp.concatenate([jnp.cos(angles), jnp.sin(angles) * signs], axis=1)
    groups = [place ^ distance for distance in range(half_places)]

    share = 2 if parts % 2 == 0 and local_heads % 2 == 0 else 1
    per_part = local_heads // share
    side = lax.rem(part, share)

    latent = prepare(latents, q_gain, kv_gain, lengths, jnp.stack([place, core]).astype(jnp.int32))
    same, other = [latent], [sibling(latent)]
    for distance in range(1, half_places):
        same.append(across(latent, distance) if distance & (distance - 1) == 0 else None)
    sent = [pick(own_query, side * per_part + index, 1, 0) for index in range(per_part)]
    sent.insert(1, pick(own_pair, side, per_part * pair_width, 1))
    far = [across(sent[0], half_places)]

    def near(distance, *earlier):
        (mixed,) = attend(
            [after(same[distance], *earlier)],
            [other[distance]],
            [groups[distance]],
            core,
            [own_query, own_pair],
            (local_heads, *sizes),
            table,
            lengths,
        )
        return mixed

    mixed = near(0)
    arrived = [mixed]
    direct = [entry for entry in same[1:] if entry is not None]
    early = far[0]
    for index in range(1, len(sent)):
        far.append(across(after(sent[index], far[index - 1]), half_places))
    for distance in range(1, half_places):
        if same[distance] is None:
            low_bit = distance & -distance
            same[distance] = across(after(same[distance ^ low_bit], mixed), low_bit)
            other.append(None)
        else:
            other.append(sibling(after(same[distance], mixed, early, *direct)))
    crossed = [other_part(after(far[0], mixed))] if share == 2 else []
    for distance in range(1, half_places):
        if other[distance] is None:
            other[distance] = sibling(after(same[distance], mixed, far[1]))
        mixed = near(distance, mixed)
        arrived.append(across(mixed, distance))
    if share == 2:
        crossed.append(other_part(after(far[1], arrived[half_places // 2])))

    placed = []
    for distance in range(half_places):
        base = (place ^ distance) * block_width
        placed.append((arrived[distance], [base + head * value_width for head in range(local_heads)]))
    previous, waiting = arrived[1:-1], arrived[-1:]
    for index in range(per_part):
        at = 2 * index
        chosen = [(far[at], far[1], side * per_part + index)]
        if share == 2:
            if index:
                crossed.append(other_part(after(far[at], mixed)))
            chosen.append((crossed[at], crossed[1], (1 - side) * per_part + index))
        for entries in [[entry] for entry in chosen] if index + 1 == per_part else [chosen]:
            mixed_all = attend(
                [after(same[0], mixed, *previous)] + same[1:],
                other,
                groups,
                core,
                [entry[0] for entry in entries] + [entry[1] for entry in entries],
                (len(entries), *sizes),
                table,
                lengths,
                [index] * len(entries),
            )
            mixed = mixed_all[0]
            received = [across(mixed_all[distance], distance) for distance in range(1, half_places)]
            previous = waiting + received[:-1]
            waiting = received[-1:]
            for distance, piece in enumerate([mixed] + received):
                base = (place ^ distance ^ half_places) * block_width
                placed.append((piece, [base + head * value_width for first, second, head in entries]))
    held, out_width = None, places * block_width
    late = len(placed) - 2 * half_places
    for batch in (placed[:late], placed[late:]):
        offsets = [offset for piece, starts in batch for offset in starts]
        held = place_pieces([piece for piece, starts in batch], offsets, value_width, out_width, held)
    return held


def solution(mesh):
    return jax.shard_map(
        shards,
        mesh=mesh,
        in_specs=(
            P(("parts", "seq", "head"), None),
            P(),
            P(),
            P("head", None, "seq", None),
            P("head", None, "seq", None),
            P("parts", None),
        ),
        out_specs=P(("parts", "seq"), "head"),
        check_vma=False,
    )
```

time: 328 us -> 186 us (0.57)
  Pallas kernels: 196 us -> 77.5 us
  waiting for transfers between devices: 78.5 us -> 59.4 us
    pallas_call x9 -> x12, Pallas kernels: 194 us -> 75 us  [the longest x7 68.7 us: attend(): pl.pallas_call(partial(attend_kernel, sizes, slots, pair_at), out_shape=[...]
    ppermute x22 -> x18, waiting for transfers between devices: 78 us -> 56.3 us  [across(): lax.ppermute(value, 'seq', [(s, s ^ distance) for s in range(places)])]
    dynamic_slice x2 -> x0, local copies, waits for them, and re-layouts: 4.25 us -> none  [the longest x1 2.35 us: shards(): lax.dynamic_index_in_dim(own_query, head, 0, keepdims=True)]
    unnamed x53 -> x35, local copies, waits for them, and re-layouts: 9.2 us -> 12 us
    ppermute x22 -> x18, starting transfers between devices: 26.3 us -> 26.8 us  [across(): lax.ppermute(value, 'seq', [(s, s ^ distance) for s in range(places)])]
  transfers between devices with their start and end apart: 30 -> 25, of which waited for: 7 -> 11; matrix products, arithmetic and copies ran while one was open for 3% -> 1% of each run, Pallas kernels for 20% -> 40%
where the time goes in v2:
time: 186 us; the launch traced here: 185 us
  Pallas kernels  77.5 us (42%)
  waiting for transfers between devices  59.4 us (32%)
  starting transfers between devices  33.5 us (18%)
  local copies, waits for them, and re-layouts  13 us (7%)
    pallas_call x7, Pallas kernels, attend(): pl.pallas_call(partial(attend_kernel, sizes, slots, pair_at), out_shape=[...  68.7 us
    ppermute x18, waiting for transfers between devices, across(): lax.ppermute(value, 'seq', [(s, s ^ distance) for s in range(places)])  56.3 us
    ppermute x18, starting transfers between devices, across(): lax.ppermute(value, 'seq', [(s, s ^ distance) for s in range(places)])  26.8 us
    unnamed x35, local copies, waits for them, and re-layouts  12 us
    ppermute x3, starting transfers between devices, other_part(): return lax.ppermute(value, 'parts', [(p, p ^ 1) for p in range(parts)])  5.74 us
    pallas_call x2, Pallas kernels, place_pieces(): pl.pallas_call(partial(place_kernel, width, count), out_shape=jax.ShapeDt...  4.63 us
  transfers between devices with their start and end apart: 25, of which 11 were waited for; matrix products, arithmetic and copies ran while one was open for 1% of the time, Pallas kernels for 40%

profile of v2, /device:TPU:0, one launch (start us, length us, event | category | flops | bytes accessed | tf_op | source)
XLA Modules:
  0.0 185.1 jit_solution(9830115371870979903)
XLA Ops:
  3.4 2.4 %prepare.1.refs_2_.refs_4_ = bf16[256,2176]{1,0:T(8,128)(2,1)} custom-call(s32[2]{0:T(128)S(1)} %pad_add_fusion.place_ref, s32[8,8]{1,0:T(8,128)S(1)} %copy-done.13, bf16[2112,256]{1,0:T(8,128)(2,1)S(1)} %bitcast.59, f32[1,1536]{1,0:T(1,128)S(1)} %broadcast_in_dim.18.q_gain_ref, f32[1,512]{1,0:T(1,128)S(1)} %bitcast.60), custom_call_target="tpu_custom_call" | custom-call | flops 1024 | bytes 1024 | tf_op jit(solution)/shard_map/prepare/pallas_call | solution.py:62
  6.3 2.5 %collective-permute-start.6 = (bf16[256,2176]{1,0:T(8,128)(2,1)}, bf16[256,2176]{1,0:T(8,128)(2,1)}, u32[]{:S(2)}, u32[]{:S(2)}) collective-permute-start(bf16[256,2176]{1,0:T(8,128)(2,1)} %prepare.1.refs_2_.refs_4_), channel_id=1, source_target_pairs={{0,2},{2,0},{4,6},{6,4},{8,10},{10,8},{12,14},{14,12},{1,3},{3,1},... | collective-permute-start | bytes 3342344 | tf_op jit(solution)/shard_map/ppermute | solution.py:315
  12.1 2.7 %collective-permute-start = (bf16[192,1536]{1,0:T(8,128)(2,1)S(1)}, bf16[192,1536]{1,0:T(8,128)(2,1)}, u32[]{:S(2)}, u32[]{:S(2)}) collective-permute-start(bf16[192,1536]{1,0:T(8,128)(2,1)S(1)} %pick.5), channel_id=1, source_target_pairs={{0,8},{2,10},{4,12},{6,14},{8,0},{10,2},{12,4},{14,6},{1,9},{3,11}... | collective-permute-start | bytes 1769480 | tf_op jit(solution)/shard_map/ppermute | solution.py:315
  18.4 6.2 %attend.7.refs_0_ = bf16[512,512]{1,0:T(8,128)(2,1)S(1)} custom-call(s32[2]{0:T(128)S(1)} %pad_add_fusion.1.place_ref, s32[8,8]{1,0:T(8,128)S(1)} %copy-done.14, f32[512,256]{1,0:T(8,128)S(1)} %pad_maximum_fusion.table_ref, bf16[4,192,1536]{2,1,0:T(8,128)(2,1)S(1)} %bitcast.49, bf16[512,1024]{1,0:T(8,128)(2,1)S(1)} %bitcast.54, ...), custom_call_target="tpu_custom_call" | custom-call | flops 1024 | bytes 1024 | tf_op jit(solution)/shard_map/attend/pallas_call | solution.py:235
  25.5 21.9 %collective-permute-done.refs_0_ = bf16[192,1536]{1,0:T(8,128)(2,1)} collective-permute-done((bf16[192,1536]{1,0:T(8,128)(2,1)S(1)}, bf16[192,1536]{1,0:T(8,128)(2,1)}, u32[]{:S(2)}, u32[]{:S(2)}) %collective-permute-start) | collective-permute-done | bytes 589856 | tf_op jit(solution)/shard_map/ppermute | solution.py:315
  50.2 2.6 %collective-permute-start.1 = (bf16[512,512]{1,0:T(8,128)(2,1)}, bf16[512,512]{1,0:T(8,128)(2,1)}, u32[]{:S(2)}, u32[]{:S(2)}) collective-permute-start(bf16[512,512]{1,0:T(8,128)(2,1)} %pick.4), channel_id=1, source_target_pairs={{0,8},{2,10},{4,12},{6,14},{8,0},{10,2},{12,4},{14,6},{1,9},{3,11}... | collective-permute-start | bytes 1572872 | tf_op jit(solution)/shard_map/ppermute | solution.py:315
  54.0 7.2 %attend.8 = bf16[512,512]{1,0:T(8,128)(2,1)} custom-call(s32[2]{0:T(128)S(1)} %pad_add_fusion.3.place_ref, s32[8,8]{1,0:T(8,128)S(1)} %copy-done.14, f32[512,256]{1,0:T(8,128)S(1)} %copy-done.3, bf16[4,192,1536]{2,1,0:T(8,128)(2,1)S(1)} %bitcast.50, bf16[512,1024]{1,0:T(8,128)(2,1)S(1)} %bitcast.56, ...), custom_call_target="tpu_custom_call" | custom-call | flops 1024 | bytes 1024 | tf_op jit(solution)/shard_map/attend/pallas_call | solution.py:235
  61.2 7.4 %attend.9 = bf16[512,512]{1,0:T(8,128)(2,1)} custom-call(s32[2]{0:T(128)S(1)} %pad_add_fusion.2.place_ref, s32[8,8]{1,0:T(8,128)S(1)} %copy-done.14, f32[512,256]{1,0:T(8,128)S(1)} %copy-done.3, bf16[4,192,1536]{2,1,0:T(8,128)(2,1)S(1)} %bitcast.51, bf16[512,1024]{1,0:T(8,128)(2,1)S(1)} %bitcast.57, ...), custom_call_target="tpu_custom_call" | custom-call | flops 1024 | bytes 1024 | tf_op jit(solution)/shard_map/attend/pallas_call | solution.py:235
  68.6 7.6 %collective-permute-done.1.refs_2_.refs_1_ = bf16[512,512]{1,0:T(8,128)(2,1)} collective-permute-done((bf16[512,512]{1,0:T(8,128)(2,1)}, bf16[512,512]{1,0:T(8,128)(2,1)}, u32[]{:S(2)}, u32[]{:S(2)}) %collective-permute-start.1) | collective-permute-done | bytes 524320 | tf_op jit(solution)/shard_map/ppermute | solution.py:315
  76.2 2.2 %collective-permute-start.9 = (bf16[512,512]{1,0:T(8,128)(2,1)}, bf16[512,512]{1,0:T(8,128)(2,1)}, u32[]{:S(2)}, u32[]{:S(2)}) collective-permute-start(bf16[512,512]{1,0:T(8,128)(2,1)} %attend.9), channel_id=1, source_target_pairs={{0,4},{2,6},{4,0},{6,2},{8,12},{10,14},{12,8},{14,10},{1,5},{3,7},... | collective-permute-start | bytes 1572872 | tf_op jit(solution)/shard_map/ppermute | solution.py:315
  80.8 1.9 %collective-permute-start.2 = (bf16[192,1536]{1,0:T(8,128)(2,1)}, bf16[192,1536]{1,0:T(8,128)(2,1)}, u32[]{:S(2)}, u32[]{:S(2)}) collective-permute-start(bf16[192,1536]{1,0:T(8,128)(2,1)} %pick.3), channel_id=1, source_target_pairs={{0,8},{2,10},{4,12},{6,14},{8,0},{10,2},{12,4},{14,6},{1,9},{3,11}... | collective-permute-start | bytes 1769480 | tf_op jit(solution)/shard_map/ppermute | solution.py:315
  84.2 15.3 %collective-permute-done.9.refs_2_ = bf16[512,512]{1,0:T(8,128)(2,1)} collective-permute-done((bf16[512,512]{1,0:T(8,128)(2,1)}, bf16[512,512]{1,0:T(8,128)(2,1)}, u32[]{:S(2)}, u32[]{:S(2)}) %collective-permute-start.9) | collective-permute-done | bytes 524320 | tf_op jit(solution)/shard_map/ppermute | solution.py:315
  99.5 2.4 %collective-permute-start.10 = (bf16[512,512]{1,0:T(8,128)(2,1)}, bf16[512,512]{1,0:T(8,128)(2,1)}, u32[]{:S(2)}, u32[]{:S(2)}) collective-permute-start(bf16[512,512]{1,0:T(8,128)(2,1)} %collective-permute-done.1.refs_2_.refs_1_), channel_id=1, source_target_pairs={{0,16},{16,0},{1,17},{17,1},{2,18},{18,2},{3,19},{19,3},{4,20},{20... | collective-permute-start | bytes 1572872 | tf_op jit(solution)/shard_map/ppermute | solution.py:321
  103.1 7.2 %attend.10 = bf16[512,512]{1,0:T(8,128)(2,1)} custom-call(s32[2]{0:T(128)S(1)} %pad_add_fusion.4.place_ref, s32[8,8]{1,0:T(8,128)S(1)} %copy-done.14, f32[512,256]{1,0:T(8,128)S(1)} %copy-done.4, bf16[4,192,1536]{2,1,0:T(8,128)(2,1)S(1)} %bitcast.53, bf16[512,1024]{1,0:T(8,128)(2,1)S(1)} %bitcast.58, ...), custom_call_target="tpu_custom_call" | custom-call | flops 1024 | bytes 1024 | tf_op jit(solution)/shard_map/attend/pallas_call | solution.py:235
  111.3 3.0 %collective-permute-done.10.refs_3_.refs_1_ = bf16[512,512]{1,0:T(8,128)(2,1)} collective-permute-done((bf16[512,512]{1,0:T(8,128)(2,1)}, bf16[512,512]{1,0:T(8,128)(2,1)}, u32[]{:S(2)}, u32[]{:S(2)}) %collective-permute-start.10) | collective-permute-done | bytes 524320 | tf_op jit(solution)/shard_map/ppermute | solution.py:321
  116.6 15.0 %attend.11 = (bf16[512,256]{1,0:T(8,128)(2,1)S(1)}, bf16[512,256]{1,0:T(8,128)(2,1)S(1)}, bf16[512,256]{1,0:T(8,128)(2,1)S(1)}, bf16[512,256]{1,0:T(8,128)(2,1)S(1)}) custom-call(s32[5]{0:T(128)S(1)} %stack.171.place_ref, s32[8,8]{1,0:T(8,128)S(1)} %copy-done.14, f32[512,256]{1,0:T(8,128)S(1)} %copy-done.5, bf16[192,1536]{1,0:T(8,128)(2,1)} %collective-permute-done.refs_0_, ...), custom_call_target="tpu_custom_call" | custom-call | flops 1024 | bytes 1024 | tf_op jit(solution)/shard_map/attend/pallas_call | solution.py:235
  131.7 1.8 collective-permute-start.20
  136.9 4.8 %collective-permute-done.15.refs_5_ = bf16[512,256]{1,0:T(8,128)(2,1)S(1)} collective-permute-done((bf16[512,256]{1,0:T(8,128)(2,1)S(1)}, bf16[512,256]{1,0:T(8,128)(2,1)S(1)}, u32[]{:S(2)}, u32[]{:S(2)}) %collective-permute-start.15) | collective-permute-done | bytes 262176 | tf_op jit(solution)/shard_map/ppermute | solution.py:315
  141.8 2.6 %collective-permute-done.16.refs_6_ = bf16[512,256]{1,0:T(8,128)(2,1)S(1)} collective-permute-done((bf16[512,256]{1,0:T(8,128)(2,1)S(1)}, bf16[512,256]{1,0:T(8,128)(2,1)S(1)}, u32[]{:S(2)}, u32[]{:S(2)}) %collective-permute-start.16) | collective-permute-done | bytes 262176 | tf_op jit(solution)/shard_map/ppermute | solution.py:315
  144.4 12.5 %attend.12 = (bf16[512,128]{1,0:T(8,128)(2,1)S(1)}, bf16[512,128]{1,0:T(8,128)(2,1)S(1)}, bf16[512,128]{1,0:T(8,128)(2,1)S(1)}, bf16[512,128]{1,0:T(8,128)(2,1)S(1)}) custom-call(s32[5]{0:T(128)S(1)} %stack.171.place_ref, s32[8,8]{1,0:T(8,128)S(1)} %copy-done.14, f32[512,256]{1,0:T(8,128)S(1)} %copy-done.5, ...), custom_call_target="tpu_custom_call" | custom-call | flops 1024 | bytes 1024 | tf_op jit(solution)/shard_map/attend/pallas_call | solution.py:235
  157.3 3.1 %collective-permute-start.19 = (bf16[512,128]{1,0:T(8,128)(2,1)S(1)}, bf16[512,128]{1,0:T(8,128)(2,1)S(1)}, u32[]{:S(2)}, u32[]{:S(2)}) collective-permute-start(bf16[512,128]{1,0:T(8,128)(2,1)S(1)} %get-tuple-element.51), channel_id=1, source_target_pairs={{0,6},{2,4},{4,2},{6,0},{8,14},{10,12},{12,10},{14,8},{1,7},{3,5},... | collective-permute-start | bytes 393224 | tf_op jit(solution)/shard_map/ppermute | solution.py:315
  162.2 13.0 %attend.13 = (bf16[512,128]{1,0:T(8,128)(2,1)S(1)}, bf16[512,128]{1,0:T(8,128)(2,1)}, bf16[512,128]{1,0:T(8,128)(2,1)}, bf16[512,128]{1,0:T(8,128)(2,1)S(1)}) custom-call(s32[5]{0:T(128)S(1)} %stack.171.place_ref, s32[8,8]{1,0:T(8,128)S(1)} %copy-done.14, f32[512,256]{1,0:T(8,128)S(1)} %copy-done.5, bf16[192,1536]{1,0:T(8,128)(2,1)S(1)} %collective-permute-done.20.refs_0_, ...), custom_call_target="tpu_custom_call" | custom-call | flops 1024 | bytes 1024 | tf_op jit(solution)/shard_map/attend/pallas_call | solution.py:235
  177.0 1.8 collective-permute-start.24
  179.0 3.1 %place_pieces.2.refs_8_ = bf16[512,4096]{1,0:T(8,128)(2,1)} custom-call(s32[24]{0:T(128)S(1)} %stack.201.offsets_ref, bf16[512,512]{1,0:T(8,128)(2,1)S(1)} %copy-done.11, bf16[512,512]{1,0:T(8,128)(2,1)} %collective-permute-done.13.refs_1_, bf16[512,512]{1,0:T(8,128)(2,1)} %collective-permute-done.9.refs_2_, ...), custom_call_target="tpu_custom_call" | custom-call | flops 1024 | bytes 1024 | tf_op jit(solution)/shard_map/place_pieces/pallas_call | solution.py:280
  (87 shorter events, 34.2 us)
Async XLA Ops:
  5.8 10.3 %collective-permute-start.3 = (bf16[256,2176]{1,0:T(8,128)(2,1)}, bf16[256,2176]{1,0:T(8,128)(2,1)S(1)}, u32[]{:S(2)}, u32[]{:S(2)}) collective-permute-start(bf16[256,2176]{1,0:T(8,128)(2,1)} %prepare.1.refs_2_.refs_4_), channel_id=1, source_target_pairs={{0,1},{1,0},{2,3},{3,2},{4,5},{5,4},{6,7},{7,6},{8,9},{9,8},{10,11... | collective-permute-start | bytes 3342344 | tf_op jit(solution)/shard_map/ppermute | solution.py:318
  6.3 41.2 %collective-permute-start.6 = (bf16[256,2176]{1,0:T(8,128)(2,1)}, bf16[256,2176]{1,0:T(8,128)(2,1)}, u32[]{:S(2)}, u32[]{:S(2)}) collective-permute-start(bf16[256,2176]{1,0:T(8,128)(2,1)} %prepare.1.refs_2_.refs_4_), channel_id=1, source_target_pairs={{0,2},{2,0},{4,6},{6,4},{8,10},{10,8},{12,14},{14,12},{1,3},{3,1},... | collective-permute-start | bytes 3342344 | tf_op jit(solution)/shard_map/ppermute | solution.py:315
  8.8 39.7 %collective-permute-start.5 = (bf16[256,2176]{1,0:T(8,128)(2,1)}, bf16[256,2176]{1,0:T(8,128)(2,1)}, u32[]{:S(2)}, u32[]{:S(2)}) collective-permute-start(bf16[256,2176]{1,0:T(8,128)(2,1)} %prepare.1.refs_2_.refs_4_), channel_id=1, source_target_pairs={{0,4},{2,6},{4,0},{6,2},{8,12},{10,14},{12,8},{14,10},{1,5},{3,7},... | collective-permute-start | bytes 3342344 | tf_op jit(solution)/shard_map/ppermute | solution.py:315
  12.1 35.4 %collective-permute-start = (bf16[192,1536]{1,0:T(8,128)(2,1)S(1)}, bf16[192,1536]{1,0:T(8,128)(2,1)}, u32[]{:S(2)}, u32[]{:S(2)}) collective-permute-start(bf16[192,1536]{1,0:T(8,128)(2,1)S(1)} %pick.5), channel_id=1, source_target_pairs={{0,8},{2,10},{4,12},{6,14},{8,0},{10,2},{12,4},{14,6},{1,9},{3,11}... | collective-permute-start | bytes 1769480 | tf_op jit(solution)/shard_map/ppermute | solution.py:315
  48.4 12.8 %collective-permute-start.8 = (bf16[256,2176]{1,0:T(8,128)(2,1)}, bf16[256,2176]{1,0:T(8,128)(2,1)}, u32[]{:S(2)}, u32[]{:S(2)}) collective-permute-start(bf16[256,2176]{1,0:T(8,128)(2,1)} %collective-permute-done.5.refs_2_.refs_6_.refs_4_), channel_id=1, source_target_pairs={{0,1},{1,0},{2,3},{3,2},{4,5},{5,4},{6,7},{7,6},{8,9},{9,8},{10,11... | collective-permute-start | bytes 3342344 | tf_op jit(solution)/shard_map/ppermute | solution.py:318
  49.0 27.3 %collective-permute-start.11 = (bf16[256,2176]{1,0:T(8,128)(2,1)}, bf16[256,2176]{1,0:T(8,128)(2,1)}, u32[]{:S(2)}, u32[]{:S(2)}) collective-permute-start(bf16[256,2176]{1,0:T(8,128)(2,1)} %collective-permute-done.5.refs_2_.refs_6_.refs_4_), channel_id=1, source_target_pairs={{0,2},{2,0},{4,6},{6,4},{8,10},{10,8},{12,14},{14,12},{1,3},{3,1},... | collective-permute-start | bytes 3342344 | tf_op jit(solution)/shard_map/ppermute | solution.py:315
  50.2 26.0 %collective-permute-start.1 = (bf16[512,512]{1,0:T(8,128)(2,1)}, bf16[512,512]{1,0:T(8,128)(2,1)}, u32[]{:S(2)}, u32[]{:S(2)}) collective-permute-start(bf16[512,512]{1,0:T(8,128)(2,1)} %pick.4), channel_id=1, source_target_pairs={{0,8},{2,10},{4,12},{6,14},{8,0},{10,2},{12,4},{14,6},{1,9},{3,11}... | collective-permute-start | bytes 1572872 | tf_op jit(solution)/shard_map/ppermute | solution.py:315
  76.2 25.8 %collective-permute-start.12 = (bf16[256,2176]{1,0:T(8,128)(2,1)}, bf16[256,2176]{1,0:T(8,128)(2,1)}, u32[]{:S(2)}, u32[]{:S(2)}) collective-permute-start(bf16[256,2176]{1,0:T(8,128)(2,1)} %collective-permute-done.11.refs_2_.refs_7_.refs_5_), channel_id=1, source_target_pairs={{0,1},{1,0},{2,3},{3,2},{4,5},{5,4},{6,7},{7,6},{8,9},{9,8},{10,11... | collective-permute-start | bytes 3342344 | tf_op jit(solution)/shard_map/ppermute | solution.py:318
  76.2 23.3 %collective-permute-start.9 = (bf16[512,512]{1,0:T(8,128)(2,1)}, bf16[512,512]{1,0:T(8,128)(2,1)}, u32[]{:S(2)}, u32[]{:S(2)}) collective-permute-start(bf16[512,512]{1,0:T(8,128)(2,1)} %attend.9), channel_id=1, source_target_pairs={{0,4},{2,6},{4,0},{6,2},{8,12},{10,14},{12,8},{14,10},{1,5},{3,7},... | collective-permute-start | bytes 1572872 | tf_op jit(solution)/shard_map/ppermute | solution.py:315
  79.3 32.0 %collective-permute-start.4 = (bf16[192,1536]{1,0:T(8,128)(2,1)}, bf16[192,1536]{1,0:T(8,128)(2,1)}, u32[]{:S(2)}, u32[]{:S(2)}) collective-permute-start(bf16[192,1536]{1,0:T(8,128)(2,1)} %collective-permute-done.refs_0_), channel_id=1, source_target_pairs={{0,16},{16,0},{1,17},{17,1},{2,18},{18,2},{3,19},{19,3},{4,20},{20... | collective-permute-start | bytes 1769480 | tf_op jit(solution)/shard_map/ppermute | solution.py:321
  80.8 50.9 %collective-permute-start.2 = (bf16[192,1536]{1,0:T(8,128)(2,1)}, bf16[192,1536]{1,0:T(8,128)(2,1)}, u32[]{:S(2)}, u32[]{:S(2)}) collective-permute-start(bf16[192,1536]{1,0:T(8,128)(2,1)} %pick.3), channel_id=1, source_target_pairs={{0,8},{2,10},{4,12},{6,14},{8,0},{10,2},{12,4},{14,6},{1,9},{3,11}... | collective-permute-start | bytes 1769480 | tf_op jit(solution)/shard_map/ppermute | solution.py:315
  82.7 28.6 %collective-permute-start.13 = (bf16[512,512]{1,0:T(8,128)(2,1)}, bf16[512,512]{1,0:T(8,128)(2,1)}, u32[]{:S(2)}, u32[]{:S(2)}) collective-permute-start(bf16[512,512]{1,0:T(8,128)(2,1)} %attend.8), channel_id=1, source_target_pairs={{0,2},{2,0},{4,6},{6,4},{8,10},{10,8},{12,14},{14,12},{1,3},{3,1},... | collective-permute-start | bytes 1572872 | tf_op jit(solution)/shard_map/ppermute | solution.py:315
  99.5 14.8 %collective-permute-start.10 = (bf16[512,512]{1,0:T(8,128)(2,1)}, bf16[512,512]{1,0:T(8,128)(2,1)}, u32[]{:S(2)}, u32[]{:S(2)}) collective-permute-start(bf16[512,512]{1,0:T(8,128)(2,1)} %collective-permute-done.1.refs_2_.refs_1_), channel_id=1, source_target_pairs={{0,16},{16,0},{1,17},{17,1},{2,18},{18,2},{3,19},{19,3},{4,20},{20... | collective-permute-start | bytes 1572872 | tf_op jit(solution)/shard_map/ppermute | solution.py:321
  110.3 34.1 %collective-permute-start.14 = (bf16[512,512]{1,0:T(8,128)(2,1)}, bf16[512,512]{1,0:T(8,128)(2,1)S(1)}, u32[]{:S(2)}, u32[]{:S(2)}) collective-permute-start(bf16[512,512]{1,0:T(8,128)(2,1)} %attend.10), channel_id=1, source_target_pairs={{0,6},{2,4},{4,2},{6,0},{8,14},{10,12},{12,10},{14,8},{1,7},{3,5},... | collective-permute-start | bytes 1572872 | tf_op jit(solution)/shard_map/ppermute | solution.py:315
  131.7 30.6 %collective-permute-start.20 = (bf16[192,1536]{1,0:T(8,128)(2,1)}, bf16[192,1536]{1,0:T(8,128)(2,1)S(1)}, u32[]{:S(2)}, u32[]{:S(2)}) collective-permute-start(bf16[192,1536]{1,0:T(8,128)(2,1)} %collective-permute-done.2.refs_0_), channel_id=1, source_target_pairs={{0,16},{16,0},{1,17},{17,1},{2,18},{18,2},{3,19},{19,3},{4,20},{20... | collective-permute-start | bytes 1769480 | tf_op jit(solution)/shard_map/ppermute | solution.py:321
  133.5 8.3 %collective-permute-start.15 = (bf16[512,256]{1,0:T(8,128)(2,1)S(1)}, bf16[512,256]{1,0:T(8,128)(2,1)S(1)}, u32[]{:S(2)}, u32[]{:S(2)}) collective-permute-start(bf16[512,256]{1,0:T(8,128)(2,1)S(1)} %get-tuple-element.45), channel_id=1, source_target_pairs={{0,2},{2,0},{4,6},{6,4},{8,10},{10,8},{12,14},{14,12},{1,3},{3,1},... | collective-permute-start | bytes 786440 | tf_op jit(solution)/shard_map/ppermute | solution.py:315
  135.1 9.2 %collective-permute-start.16 = (bf16[512,256]{1,0:T(8,128)(2,1)S(1)}, bf16[512,256]{1,0:T(8,128)(2,1)S(1)}, u32[]{:S(2)}, u32[]{:S(2)}) collective-permute-start(bf16[512,256]{1,0:T(8,128)(2,1)S(1)} %get-tuple-element.46), channel_id=1, source_target_pairs={{0,4},{2,6},{4,0},{6,2},{8,12},{10,14},{12,8},{14,10},{1,5},{3,7},... | collective-permute-start | bytes 786440 | tf_op jit(solution)/shard_map/ppermute | solution.py:315
  135.1 25.3 %collective-permute-start.21 = (bf16[512,256]{1,0:T(8,128)(2,1)S(1)}, bf16[512,256]{1,0:T(8,128)(2,1)S(1)}, u32[]{:S(2)}, u32[]{:S(2)}) collective-permute-start(bf16[512,256]{1,0:T(8,128)(2,1)S(1)} %get-tuple-element.53), channel_id=1, source_target_pairs={{0,6},{2,4},{4,2},{6,0},{8,14},{10,12},{12,10},{14,8},{1,7},{3,5},... | collective-permute-start | bytes 786440 | tf_op jit(solution)/shard_map/ppermute | solution.py:315
  156.9 5.0 %collective-permute-start.17 = (bf16[512,128]{1,0:T(8,128)(2,1)S(1)}, bf16[512,128]{1,0:T(8,128)(2,1)S(1)}, u32[]{:S(2)}, u32[]{:S(2)}) collective-permute-start(bf16[512,128]{1,0:T(8,128)(2,1)S(1)} %get-tuple-element.49), channel_id=1, source_target_pairs={{0,2},{2,0},{4,6},{6,4},{8,10},{10,8},{12,14},{14,12},{1,3},{3,1},... | collective-permute-start | bytes 393224 | tf_op jit(solution)/shard_map/ppermute | solution.py:315
  157.3 5.0 %collective-permute-start.18 = (bf16[512,128]{1,0:T(8,128)(2,1)S(1)}, bf16[512,128]{1,0:T(8,128)(2,1)S(1)}, u32[]{:S(2)}, u32[]{:S(2)}) collective-permute-start(bf16[512,128]{1,0:T(8,128)(2,1)S(1)} %get-tuple-element.50), channel_id=1, source_target_pairs={{0,4},{2,6},{4,0},{6,2},{8,12},{10,14},{12,8},{14,10},{1,5},{3,7},... | collective-permute-start | bytes 393224 | tf_op jit(solution)/shard_map/ppermute | solution.py:315
  157.3 24.8 %collective-permute-start.19 = (bf16[512,128]{1,0:T(8,128)(2,1)S(1)}, bf16[512,128]{1,0:T(8,128)(2,1)S(1)}, u32[]{:S(2)}, u32[]{:S(2)}) collective-permute-start(bf16[512,128]{1,0:T(8,128)(2,1)S(1)} %get-tuple-element.51), channel_id=1, source_target_pairs={{0,6},{2,4},{4,2},{6,0},{8,14},{10,12},{12,10},{14,8},{1,7},{3,5},... | collective-permute-start | bytes 393224 | tf_op jit(solution)/shard_map/ppermute | solution.py:315
  175.3 6.8 %collective-permute-start.22 = (bf16[512,128]{1,0:T(8,128)(2,1)}, bf16[512,128]{1,0:T(8,128)(2,1)S(1)}, u32[]{:S(2)}, u32[]{:S(2)}) collective-permute-start(bf16[512,128]{1,0:T(8,128)(2,1)} %get-tuple-element.56), channel_id=1, source_target_pairs={{0,2},{2,0},{4,6},{6,4},{8,10},{10,8},{12,14},{14,12},{1,3},{3,1},... | collective-permute-start | bytes 393224 | tf_op jit(solution)/shard_map/ppermute | solution.py:315
  177.0 5.2 %collective-permute-start.23 = (bf16[512,128]{1,0:T(8,128)(2,1)}, bf16[512,128]{1,0:T(8,128)(2,1)S(1)}, u32[]{:S(2)}, u32[]{:S(2)}) collective-permute-start(bf16[512,128]{1,0:T(8,128)(2,1)} %get-tuple-element.57), channel_id=1, source_target_pairs={{0,4},{2,6},{4,0},{6,2},{8,12},{10,14},{12,8},{14,10},{1,5},{3,7},... | collective-permute-start | bytes 393224 | tf_op jit(solution)/shard_map/ppermute | solution.py:315
  177.0 6.4 %collective-permute-start.24 = (bf16[512,128]{1,0:T(8,128)(2,1)S(1)}, bf16[512,128]{1,0:T(8,128)(2,1)S(1)}, u32[]{:S(2)}, u32[]{:S(2)}) collective-permute-start(bf16[512,128]{1,0:T(8,128)(2,1)S(1)} %get-tuple-element.58), channel_id=1, source_target_pairs={{0,6},{2,4},{4,2},{6,0},{8,14},{10,12},{12,10},{14,8},{1,7},{3,5},... | collective-permute-start | bytes 393224 | tf_op jit(solution)/shard_map/ppermute | solution.py:315
  (18 other events, 108.8 us)

commit v3 on v2

v3 whole, which is shorter than its diff:
```python
from functools import partial
import math

import jax
import jax.numpy as jnp
from jax import lax
from jax.experimental import pallas as pl
from jax.experimental.pallas import tpu as pltpu
from jax.sharding import PartitionSpec as P

epsilon = 1e-06
VMEM_LIMIT = 32 * 1024 * 1024
LIGHT = pl.CostEstimate(flops=1024, bytes_accessed=1024, transcendentals=0)
FAR = -(2.0**100)
NT = (((1,), (1,)), ((), ()))
NN = (((1,), (0,)), ((), ()))


def frequencies(lane, half_width):
    steps = lax.rem(lane, half_width).astype(jnp.float32)
    return jnp.exp(steps * (-math.log(10000.0) / half_width))


def prepare_kernel(q_width, kv_width, slot_count, place_ref, latents_ref, gain_ref, out_ref):
    rows = latents_ref.shape[1]
    rope_width = latents_ref.shape[0] - q_width - kv_width
    half_width = rope_width // 2

    def normalized(low, width):
        part = latents_ref[low : low + width, :].astype(jnp.float32)
        scale = lax.rsqrt(jnp.mean(part * part, axis=0, keepdims=True) + epsilon)
        return (jnp.transpose(part * scale) * gain_ref[:, low : low + width]).astype(jnp.bfloat16)

    out_ref[:, :q_width] = normalized(0, q_width)
    out_ref[:, q_width : q_width + kv_width] = normalized(q_width, kv_width)
    spare = out_ref.shape[1] - q_width - kv_width - rope_width
    token_ids = lax.broadcasted_iota(jnp.int32, (1, rows), 1) + place_ref[1] * rows
    slot_ids = lax.broadcasted_iota(jnp.int32, (spare, rows), 0)
    begin, start, inside = jnp.zeros_like(token_ids), jnp.int32(0), jnp.zeros((spare, rows), jnp.float32)
    for slot in range(slot_count):
        stop = start + place_ref[2 + place_ref[0] * slot_count + slot]
        begin = jnp.where(token_ids >= start, start, begin)
        member = jnp.where((token_ids >= start) & (token_ids < stop), 1.0, 0.0)
        inside = jnp.where(slot_ids == slot, member, inside)
        start = stop
    position = (token_ids - begin).astype(jnp.float32)
    angle = position * frequencies(lax.broadcasted_iota(jnp.int32, (half_width, rows), 0), half_width)
    cosine, sine = jnp.cos(angle), jnp.sin(angle)
    rope = latents_ref[q_width + kv_width :, :].astype(jnp.float32)
    first, second = rope[:half_width], rope[half_width:]
    turned = jnp.concatenate([first * cosine - second * sine, second * cosine + first * sine, inside], axis=0)
    out_ref[:, q_width + kv_width :] = jnp.transpose(turned).astype(jnp.bfloat16)


def prepare(latents, gains, q_width, kv_width, slot_count, place):
    rows = latents.shape[0]
    rope_width = latents.shape[1] - q_width - kv_width
    width = q_width + kv_width + -(-(rope_width + slot_count) // 128) * 128
    vmem = pl.BlockSpec(memory_space=pltpu.VMEM)
    return pl.pallas_call(
        partial(prepare_kernel, q_width, kv_width, slot_count),
        out_shape=jax.ShapeDtypeStruct((rows, width), jnp.bfloat16),
        in_specs=[pl.BlockSpec(memory_space=pltpu.SMEM), vmem, vmem],
        out_specs=vmem,
        compiler_params=pltpu.CompilerParams(vmem_limit_bytes=VMEM_LIMIT),
        cost_estimate=LIGHT,
        name="prepare",
    )(place, jnp.transpose(latents), gains[None, :])


def pick_kernel(index_ref, source_ref, out_ref):
    out_ref[...] = source_ref[...]


def pick(source, index, block, axis):
    shape = list(source.shape)
    shape[axis] = block
    out_shape = shape
    position = lambda step, index_ref: tuple(index_ref[0] if at == axis else 0 for at in range(len(shape)))
    return pl.pallas_call(
        pick_kernel,
        grid_spec=pltpu.PrefetchScalarGridSpec(
            num_scalar_prefetch=1,
            grid=(1,),
            in_specs=[pl.BlockSpec(tuple(shape), position)],
            out_specs=pl.BlockSpec(tuple(out_shape), lambda step, index_ref: (0,) * len(out_shape)),
        ),
        out_shape=jax.ShapeDtypeStruct(tuple(out_shape), source.dtype),
        compiler_params=pltpu.CompilerParams(vmem_limit_bytes=VMEM_LIMIT),
        cost_estimate=LIGHT,
        name="pick",
    )(jnp.reshape(index, (1,)).astype(jnp.int32), source)


def project(tokens_ref, sizes, weight_refs, chosen):
    heads, q_width, kv_width, nope_width, rope_width, value_width = sizes
    query_width, pair_width = nope_width + rope_width, nope_width + value_width

    def dot(tokens, weight, dims):
        return lax.dot_general(tokens, weight, dims, preferred_element_type=jnp.float32)

    latent = tokens_ref[:, q_width : q_width + kv_width]
    query_ref, pair_ref = weight_refs
    columns = [slice(number * pair_width, (number + 1) * pair_width) for number in chosen]
    every = dot(latent, pair_ref[:, columns[0].start : columns[-1].stop], NN)
    pair = [every[:, head * pair_width : (head + 1) * pair_width] for head in range(heads)]

    def query(low, high, picked):
        parts = [query_ref[number if query_ref.shape[0] > 1 else 0, low:high, :] for number in picked]
        return dot(tokens_ref[:, :q_width], jnp.concatenate(parts, axis=0), NT)

    nope = [query(0, nope_width, chosen[head : head + 2]) for head in range(0, heads, 2)]
    picked = list(chosen)
    while len(picked) * rope_width % nope_width:
        picked.append(picked[-1])
    return nope, query(nope_width, query_width, picked), pair


def attend_group(sizes, chosen, tokens_ref, weight_refs, scratch, out_ref):
    heads, q_width, kv_width, nope_width, rope_width, value_width = sizes
    query_ref, key_ref, value_ref, turn_ref, bias_ref = scratch
    tokens = tokens_ref.shape[0]
    rows = bias_ref.shape[0]
    half_width = rope_width // 2
    score_scale = (nope_width + rope_width) ** -0.5 * math.log2(math.e)
    nope, rope, pair = project(tokens_ref, sizes, weight_refs, chosen)
    lane = lax.broadcasted_iota(jnp.int32, (tokens, nope_width), 1)
    is_first = lax.rem(lane, rope_width) < half_width
    is_rope = lane < rope_width
    shared = tokens_ref[:, q_width + kv_width :]
    apart = jnp.where(is_rope, 0.0, (1.0 - shared.astype(jnp.float32)) * FAR)
    for head in range(heads):
        low = head % 2 * nope_width
        part = nope[head // 2][:, low : low + nope_width]
        query_ref[:, 2 * head * nope_width : (2 * head + 1) * nope_width] = (part * score_scale).astype(jnp.bfloat16)
        both = pair[head].astype(jnp.bfloat16)
        key_ref[:, head * nope_width : (head + 1) * nope_width] = both[:, :nope_width]
        value_ref[head, :, :value_width] = both[:, nope_width:]
    group_heads = nope_width // rope_width
    for low in range(0, rope.shape[1], nope_width):
        part = rope[:, low : low + nope_width]
        swapped = jnp.where(is_first, pltpu.roll(part, nope_width - half_width, 1), pltpu.roll(part, half_width, 1))
        turned = (part * turn_ref[:, :nope_width] + swapped * turn_ref[:, nope_width:]) * score_scale
        for index in range(group_heads):
            head = low // rope_width + index
            if head < heads:
                moved = pltpu.roll(turned, nope_width - index * rope_width, 1) if index else turned
                query_ref[:, (2 * head + 1) * nope_width : (2 * head + 2) * nope_width] = jnp.where(
                    is_rope, moved, apart
                ).astype(jnp.bfloat16)
    for head in range(heads):
        for half in range(2):
            low, high = half * rows, (half + 1) * rows
            queries = query_ref[low:high, 2 * head * nope_width : (2 * head + 2) * nope_width]
            keys = jnp.concatenate(
                [key_ref[:high, head * nope_width : (head + 1) * nope_width], tokens_ref[:high, q_width + kv_width :]], axis=1
            )
            scores = lax.dot_general(queries, keys, NT, preferred_element_type=jnp.float32)
            last = scores[:, low:] + bias_ref[...]
            scores = jnp.concatenate([scores[:, :low], last], axis=1) if half else last
            terms = jnp.exp2(scores - jnp.max(scores, axis=1, keepdims=True)).astype(jnp.bfloat16)
            mixed = lax.dot_general(terms, value_ref[head, :high, :], NN, preferred_element_type=jnp.float32)
            out_ref[low:high, head * value_width : (head + 1) * value_width] = (
                mixed[:, :value_width] / mixed[:, value_width:]
            ).astype(jnp.bfloat16)


def set_up(scratch):
    value_ref, bias_ref = scratch[2], scratch[4]
    rows = bias_ref.shape[0]
    heads, tokens, width = value_ref.shape
    row_ids = lax.broadcasted_iota(jnp.int32, (rows, rows), 0)
    col_ids = lax.broadcasted_iota(jnp.int32, (rows, rows), 1)
    bias_ref[...] = jnp.where(col_ids <= row_ids, 0.0, -jnp.inf)
    for head in range(heads):
        value_ref[head, :, width // 2 :] = jnp.ones((tokens, width // 2), jnp.bfloat16)


def set_turn(group, slot_count, place_ref, table_ref, turn_ref):
    block = turn_ref.shape[0] // slot_count
    starts, start = [], jnp.int32(0)
    for index in range(slot_count):
        starts.append(start)
        start = start + place_ref[2 + group * slot_count + index]
    for index in range(slot_count):
        begin = jnp.int32(0)
        for entry in starts:
            begin = jnp.where(entry <= index * block, entry, begin)
        position = pl.multiple_of(index * block - begin, block)
        turn_ref[index * block : (index + 1) * block, :] = table_ref[pl.ds(position, block), :]


def near_kernel(sizes, slot_count, distance, place_ref, table_ref, query_weight_ref, pair_weight_ref, same_ref, other_ref, out_ref, tokens_ref, *scratch):
    core, group = place_ref[1], place_ref[0] ^ distance
    rows = same_ref.shape[0]
    tokens_ref[pl.ds(pl.multiple_of(core * rows, rows), rows), :] = same_ref[...]
    tokens_ref[pl.ds(pl.multiple_of((1 - core) * rows, rows), rows), :] = other_ref[...]
    set_up(scratch)
    set_turn(group, slot_count, place_ref, table_ref, scratch[3])
    attend_group(sizes, list(range(sizes[0])), tokens_ref, (query_weight_ref, pair_weight_ref), scratch, out_ref)


def far_kernel(sizes, slot_count, slots, chosen, place_ref, table_ref, *refs):
    weight_refs, refs = refs[:2], refs[2:]
    token_refs, out_refs, refs = refs[:slots], refs[slots : 2 * slots], refs[2 * slots :]
    held_ref, result_ref, sems = refs[0], refs[1], refs[2]
    scratch = refs[3:]
    set_up(scratch)

    def fetch(slot):
        for index in range(slots):

            @pl.when(slot == index)
            def _(index=index):
                pltpu.make_async_copy(token_refs[index], held_ref.at[index % 2], sems.at[index % 2]).start()

    fetch(0)

    def one_group(slot, carry):
        turn = lax.rem(slot, 2)
        fetch(slot + 1)
        set_turn(place_ref[0] ^ slot, slot_count, place_ref, table_ref, scratch[3])
        pltpu.make_async_copy(token_refs[0], held_ref.at[turn], sems.at[turn]).wait()
        attend_group(sizes, chosen, held_ref.at[turn], weight_refs, scratch, result_ref)
        for index in range(slots):

            @pl.when(slot == index)
            def _(index=index):
                out_refs[index][...] = result_ref[...]

        return carry

    lax.fori_loop(0, slots, one_group, 0)


def scratch_for(sizes, tokens):
    heads, q_width, kv_width, nope_width, rope_width, value_width = sizes
    return [
        pltpu.VMEM((tokens, 2 * heads * nope_width), jnp.bfloat16),
        pltpu.VMEM((tokens, heads * nope_width), jnp.bfloat16),
        pltpu.VMEM((heads, tokens, 2 * value_width), jnp.bfloat16),
        pltpu.VMEM((tokens, 2 * nope_width), jnp.float32),
        pltpu.VMEM((tokens // 2, tokens // 2), jnp.float32),
    ]


def attend_near(sizes, slot_count, distance, place, table, query_weight, pair_weight, same, other):
    rows, width = same.shape
    heads, value_width = sizes[0], sizes[-1]
    vmem = pl.BlockSpec(memory_space=pltpu.VMEM)
    return pl.pallas_call(
        partial(near_kernel, sizes, slot_count, distance),
        out_shape=[
            jax.ShapeDtypeStruct((2 * rows, heads * value_width), jnp.bfloat16),
            jax.ShapeDtypeStruct((2 * rows, width), jnp.bfloat16),
        ],
        in_specs=[pl.BlockSpec(memory_space=pltpu.SMEM)] + [vmem] * 5,
        out_specs=[vmem, vmem],
        scratch_shapes=scratch_for(sizes, 2 * rows),
        compiler_params=pltpu.CompilerParams(vmem_limit_bytes=VMEM_LIMIT),
        cost_estimate=LIGHT,
        name="attend_near",
    )(place, table, query_weight, pair_weight, same, other)


def attend_far(sizes, slot_count, place, table, query_weight, pair_weight, chosen, groups):
    tokens, width = groups[0].shape
    slots, heads, value_width = len(groups), sizes[0], sizes[-1]
    vmem = pl.BlockSpec(memory_space=pltpu.VMEM)
    return pl.pallas_call(
        partial(far_kernel, sizes, slot_count, slots, chosen),
        out_shape=[jax.ShapeDtypeStruct((tokens, heads * value_width), jnp.bfloat16)] * slots,
        in_specs=[pl.BlockSpec(memory_space=pltpu.SMEM)]
        + [vmem] * 3
        + [pl.BlockSpec(memory_space=pl.ANY)] * slots,
        out_specs=[vmem] * slots,
        scratch_shapes=[
            pltpu.VMEM((2, tokens, width), jnp.bfloat16),
            pltpu.VMEM((tokens, heads * value_width), jnp.bfloat16),
            pltpu.SemaphoreType.DMA((2,)),
        ]
        + scratch_for(sizes, tokens),
        compiler_params=pltpu.CompilerParams(vmem_limit_bytes=VMEM_LIMIT),
        cost_estimate=LIGHT,
        name="attend_far",
    )(place, table, query_weight, pair_weight, *groups)


def place_kernel(width, count, offsets_ref, *refs):
    pieces, out_ref, sems = refs[:count], refs[-2], refs[-1]
    copies = []
    for piece in pieces:
        for low in range(0, piece.shape[1], width):
            index = len(copies)
            columns = pl.ds(pl.multiple_of(offsets_ref[index], 128), width)
            copies.append(pltpu.make_async_copy(piece.at[:, low : low + width], out_ref.at[:, columns], sems.at[index]))
            copies[-1].start()
    for copy in copies:
        copy.wait()


def place_pieces(pieces, offsets, width, out_width, held=None):
    count = len(pieces)
    any_space = pl.BlockSpec(memory_space=pl.ANY)
    operands = [jnp.stack(offsets).astype(jnp.int32), *pieces]
    specs = [pl.BlockSpec(memory_space=pltpu.SMEM)] + [pl.BlockSpec(memory_space=pltpu.VMEM)] * count
    aliases = {}
    if held is not None:
        aliases = {len(operands): 0}
        operands.append(held)
        specs.append(any_space)
    return pl.pallas_call(
        partial(place_kernel, width, count),
        out_shape=jax.ShapeDtypeStruct((pieces[0].shape[0], out_width), pieces[0].dtype),
        in_specs=specs,
        out_specs=any_space,
        scratch_shapes=[pltpu.SemaphoreType.DMA((len(offsets),))],
        input_output_aliases=aliases,
        compiler_params=pltpu.CompilerParams(vmem_limit_bytes=VMEM_LIMIT),
        cost_estimate=LIGHT,
        name="place_pieces",
    )(*operands)


def after(value, *earlier):
    return lax.optimization_barrier((value, *earlier))[0]


def shards(latents, q_gain, kv_gain, q_weight, kv_weight, lengths):
    q_width, kv_width = q_gain.shape[0], kv_gain.shape[0]
    rope_width = latents.shape[1] - q_width - kv_width
    places = lax.axis_size("seq")
    parts = lax.axis_size("parts")
    half_places = places // 2
    place = lax.axis_index("seq")
    core = lax.axis_index("head")
    part = lax.axis_index("parts")
    tokens = 2 * latents.shape[0]
    local_heads = q_weight.shape[2]
    pair_width = kv_weight.shape[3]
    nope_width = q_weight.shape[3] - rope_width
    value_width = pair_width - nope_width
    block_width = local_heads * value_width
    sizes = (q_width, kv_width, nope_width, rope_width, value_width)

    def across(value, distance):
        return lax.ppermute(value, "seq", [(s, s ^ distance) for s in range(places)])

    def sibling(value):
        return lax.ppermute(value, "head", [(0, 1), (1, 0)])

    def other_part(value):
        return lax.ppermute(value, "parts", [(p, p ^ 1) for p in range(parts)])

    slot_count = lengths.shape[1]
    gains = jnp.concatenate([q_gain, kv_gain])
    spot = jnp.concatenate([jnp.stack([place, core]).astype(jnp.int32), jnp.reshape(lengths, -1)])
    own_query = jnp.transpose(q_weight[0], (1, 2, 0))
    own_pair = jnp.reshape(kv_weight[0], (kv_width, local_heads * pair_width))
    positions = jnp.arange(tokens, dtype=jnp.int32)[:, None].astype(jnp.float32)
    lanes = jnp.arange(nope_width, dtype=jnp.int32)[None, :]
    angles = positions * frequencies(lanes, rope_width // 2)
    signs = jnp.where(lax.rem(lanes, rope_width) < rope_width // 2, -1.0, 1.0)
    table = jnp.concatenate([jnp.cos(angles), jnp.sin(angles) * signs], axis=1)
    share = 2 if parts % 2 == 0 and local_heads % 2 == 0 else 1
    per_part = local_heads // share
    side = lax.rem(part, share)

    sent_pair = pick(own_pair, side, per_part * pair_width, 1)
    sent_query = pick(own_query, side, per_part, 0)
    latent = prepare(latents, gains, q_width, kv_width, slot_count, spot)
    same, other = [latent], [sibling(latent)]
    for distance in range(1, half_places):
        same.append(across(latent, distance) if distance & (distance - 1) == 0 else None)
    far_pair = across(sent_pair, half_places)
    far_query = across(sent_query, half_places)

    joined = []

    def near(distance, *earlier):
        mixed, tokens_joined = attend_near(
            (local_heads, *sizes),
            slot_count,
            distance,
            spot,
            table,
            own_query,
            own_pair,
            after(same[distance], *earlier),
            other[distance],
        )
        joined.append(tokens_joined)
        return mixed

    mixed = near(0)
    arrived = [mixed]
    direct = [entry for entry in same[1:] if entry is not None]
    for distance in range(1, half_places):
        if same[distance] is None:
            low_bit = distance & -distance
            same[distance] = across(after(same[distance ^ low_bit], mixed), low_bit)
            other.append(None)
        else:
            other.append(sibling(after(same[distance], mixed, far_pair, *direct)))
    crossed_pair = other_part(after(far_pair, mixed)) if share == 2 else None
    for distance in range(1, half_places):
        if other[distance] is None:
            other[distance] = sibling(after(same[distance], mixed, far_query))
        mixed = near(distance, mixed)
        arrived.append(across(mixed, distance))
    placed = []
    for distance in range(half_places):
        base = (place ^ distance) * block_width
        placed.append((arrived[distance], [base + head * value_width for head in range(local_heads)]))

    rounds = [(far_query, far_pair, list(range(per_part)), side * per_part)]
    crossed = []
    if share == 2:
        for index in range(per_part):
            crossed.append(other_part(after(far_query[index : index + 1], *crossed)))
            rounds.append((crossed[index], crossed_pair, [index], (1 - side) * per_part))
    previous, waiting = arrived[1:-1], arrived[-1:]
    for queries, pairs, chosen, first in rounds:
        mixed_all = attend_far(
            (len(chosen), *sizes), slot_count, after(spot, mixed, *previous), table, queries, pairs, chosen, joined
        )
        mixed = mixed_all[0]
        received = [across(mixed_all[distance], distance) for distance in range(1, half_places)]
        previous, waiting = waiting + received[:-1], received[-1:]
        for distance, piece in enumerate([mixed] + received):
            base = (place ^ distance ^ half_places) * block_width
            placed.append((piece, [base + (first + number) * value_width for number in chosen]))
    held, out_width = None, places * block_width
    late = len(placed) - half_places
    for batch in (placed[:late], placed[late:]):
        offsets = [offset for piece, starts in batch for offset in starts]
        held = place_pieces([piece for piece, starts in batch], offsets, value_width, out_width, held)
    return held


def solution(mesh):
    return jax.shard_map(
        shards,
        mesh=mesh,
        in_specs=(
            P(("parts", "seq", "head"), None),
            P(),
            P(),
            P("head", None, "seq", None),
            P("head", None, "seq", None),
            P("parts", None),
        ),
        out_specs=P(("parts", "seq"), "head"),
        check_vma=False,
    )
```

time: 186 us -> 165 us (0.89)
  Pallas kernels: 77.5 us -> 63.2 us
  waiting for transfers between devices: 59.4 us -> 68.9 us
  starting transfers between devices: 33.5 us -> 25.3 us
  local copies, waits for them, and re-layouts: 13 us -> 5.21 us
    pallas_call x8, Pallas kernels: 71.1 us -> 58.2 us  [the longest x3 34.4 us: attend_far(): pl.pallas_call(partial(far_kernel, sizes, slot_count, slots, chosen), out...]
    unnamed x35 -> x13, local copies, waits for them, and re-layouts: 12 us -> 4.27 us
    ppermute x18 -> x17, waiting for transfers between devices: 56.3 us -> 63.1 us  [across(): lax.ppermute(value, 'seq', [(s, s ^ distance) for s in range(places)])]
    ppermute x18 -> x17, starting transfers between devices: 26.8 us -> 20.7 us  [across(): lax.ppermute(value, 'seq', [(s, s ^ distance) for s in range(places)])]
    ppermute x3, waiting for transfers between devices: 3.01 us -> 5.17 us  [other_part(): return lax.ppermute(value, 'parts', [(p, p ^ 1) for p in range(parts)])]
    ppermute x3, starting transfers between devices: 5.74 us -> 3.58 us  [other_part(): return lax.ppermute(value, 'parts', [(p, p ^ 1) for p in range(parts)])]
  transfers between devices with their start and end apart: 25 -> 24, of which waited for: 11 -> 10; matrix products, arithmetic and copies ran while one was open for 1% -> 2% of each run, Pallas kernels for 40% -> 36%
where the time goes in v3:
time: 165 us
  waiting for transfers between devices  68.9 us (42%)
  Pallas kernels  63.2 us (38%)
  starting transfers between devices  25.3 us (15%)
  local copies, waits for them, and re-layouts  5.21 us (3%)
  other arithmetic  1.92 us (1%)
    ppermute x17, waiting for transfers between devices, across(): lax.ppermute(value, 'seq', [(s, s ^ distance) for s in range(places)])  63.1 us
    pallas_call x3, Pallas kernels, attend_far(): pl.pallas_call(partial(far_kernel, sizes, slot_count, slots, chosen), out...  34.4 us
    pallas_call x4, Pallas kernels, attend_near(): pl.pallas_call(partial(near_kernel, sizes, slot_count, distance), out_sha...  22.4 us
    ppermute x17, starting transfers between devices, across(): lax.ppermute(value, 'seq', [(s, s ^ distance) for s in range(places)])  20.7 us
    ppermute x3, waiting for transfers between devices, other_part(): return lax.ppermute(value, 'parts', [(p, p ^ 1) for p in range(parts)])  5.17 us
    pallas_call x2, Pallas kernels, place_pieces(): pl.pallas_call(partial(place_kernel, width, count), out_shape=jax.ShapeDt...  4.87 us
    unnamed x13, local copies, waits for them, and re-layouts  4.27 us
    ppermute x3, starting transfers between devices, other_part(): return lax.ppermute(value, 'parts', [(p, p ^ 1) for p in range(parts)])  3.58 us
  transfers between devices with their start and end apart: 24, of which 10 were waited for; matrix products, arithmetic and copies ran while one was open for 2% of the time, Pallas kernels for 36%

profile of v3, /device:TPU:0, one launch (start us, length us, event | category | flops | bytes accessed | tf_op | source)
XLA Modules:
  0.0 164.9 jit_solution(1440536720775286454)
XLA Ops:
  4.7 2.7 %collective-permute-start = (bf16[256,2176]{1,0:T(8,128)(2,1)S(1)}, bf16[256,2176]{1,0:T(8,128)(2,1)S(1)}, u32[]{:S(2)}, u32[]{:S(2)}) collective-permute-start(bf16[256,2176]{1,0:T(8,128)(2,1)S(1)} %prepare.1.same_ref), channel_id=1, source_target_pairs={{0,4},{2,6},{4,0},{6,2},{8,12},{10,14},{12,8},{14,10},{1,5},{3,7},... | collective-permute-start | bytes 3342344 | tf_op jit(solution)/shard_map/ppermute | solution.py:347
  8.9 1.6 copy.8
  10.5 2.7 %collective-permute-start.4 = (bf16[512,512]{1,0:T(8,128)(2,1)S(1)}, bf16[512,512]{1,0:T(8,128)(2,1)S(1)}, u32[]{:S(2)}, u32[]{:S(2)}) collective-permute-start(bf16[512,512]{1,0:T(8,128)(2,1)S(1)} %pick.2), channel_id=1, source_target_pairs={{0,8},{2,10},{4,12},{6,14},{8,0},{10,2},{12,4},{14,6},{1,9},{3,11}... | collective-permute-start | bytes 1572872 | tf_op jit(solution)/shard_map/ppermute | solution.py:347
  14.7 6.1 %attend_near.4 = (bf16[512,512]{1,0:T(8,128)(2,1)S(1)}, bf16[512,2176]{1,0:T(8,128)(2,1)S(1)}) custom-call(s32[66]{0:T(128)S(1)} %pad_add_fusion.1.place_ref, f32[512,256]{1,0:T(8,128)S(1)} %pad_maximum_fusion.table_ref, bf16[4,192,1536]{2,1,0:T(8,128)(2,1)S(1)} %bitcast.44, bf16[512,1024]{1,0:T(8,128)(2,1)S(1)} %bitcast.49, ...), custom_call_target="tpu_custom_call" | custom-call | flops 1024 | bytes 1024 | tf_op jit(solution)/shard_map/attend_near/pallas_call | solution.py:251
  21.6 21.9 %collective-permute-done.4.refs_1_ = bf16[512,512]{1,0:T(8,128)(2,1)S(1)} collective-permute-done((bf16[512,512]{1,0:T(8,128)(2,1)S(1)}, bf16[512,512]{1,0:T(8,128)(2,1)S(1)}, u32[]{:S(2)}, u32[]{:S(2)}) %collective-permute-start.4) | collective-permute-done | bytes 524320 | tf_op jit(solution)/shard_map/ppermute | solution.py:347
  43.5 9.8 %collective-permute-done.same_ref = bf16[256,2176]{1,0:T(8,128)(2,1)S(1)} collective-permute-done((bf16[256,2176]{1,0:T(8,128)(2,1)S(1)}, bf16[256,2176]{1,0:T(8,128)(2,1)S(1)}, u32[]{:S(2)}, u32[]{:S(2)}) %collective-permute-start) | collective-permute-done | bytes 1114144 | tf_op jit(solution)/shard_map/ppermute | solution.py:347
  53.8 2.7 %collective-permute-start.2 = (bf16[256,2176]{1,0:T(8,128)(2,1)S(1)}, bf16[256,2176]{1,0:T(8,128)(2,1)S(1)}, u32[]{:S(2)}, u32[]{:S(2)}) collective-permute-start(bf16[256,2176]{1,0:T(8,128)(2,1)S(1)} %collective-permute-done.same_ref), channel_id=1, source_target_pairs={{0,2},{2,0},{4,6},{6,4},{8,10},{10,8},{12,14},{14,12},{1,3},{3,1},... | collective-permute-start | bytes 3342344 | tf_op jit(solution)/shard_map/ppermute | solution.py:347
  56.6 5.4 %attend_near.5 = (bf16[512,512]{1,0:T(8,128)(2,1)S(1)}, bf16[512,2176]{1,0:T(8,128)(2,1)S(1)}) custom-call(s32[66]{0:T(128)S(1)} %pad_add_fusion.1.place_ref, f32[512,256]{1,0:T(8,128)S(1)} %pad_maximum_fusion.table_ref, bf16[4,192,1536]{2,1,0:T(8,128)(2,1)S(1)} %bitcast.45, bf16[512,1024]{1,0:T(8,128)(2,1)S(1)} %bitcast.50, ...), custom_call_target="tpu_custom_call" | custom-call | flops 1024 | bytes 1024 | tf_op jit(solution)/shard_map/attend_near/pallas_call | solution.py:251
  62.0 5.5 %attend_near.6 = (bf16[512,512]{1,0:T(8,128)(2,1)S(1)}, bf16[512,2176]{1,0:T(8,128)(2,1)S(1)}) custom-call(s32[66]{0:T(128)S(1)} %pad_add_fusion.1.place_ref, f32[512,256]{1,0:T(8,128)S(1)} %pad_maximum_fusion.table_ref, bf16[4,192,1536]{2,1,0:T(8,128)(2,1)S(1)} %bitcast.46, bf16[512,1024]{1,0:T(8,128)(2,1)S(1)} %bitcast.51, ...), custom_call_target="tpu_custom_call" | custom-call | flops 1024 | bytes 1024 | tf_op jit(solution)/shard_map/attend_near/pallas_call | solution.py:251
  67.5 19.5 %collective-permute-done.7.refs_0_ = bf16[2,192,1536]{2,1,0:T(8,128)(2,1)S(1)} collective-permute-done((bf16[2,192,1536]{2,1,0:T(8,128)(2,1)S(1)}, bf16[2,192,1536]{2,1,0:T(8,128)(2,1)S(1)}, u32[]{:S(2)}, u32[]{:S(2)}) %collective-permute-start.7) | collective-permute-done | bytes 1179680 | tf_op jit(solution)/shard_map/ppermute | solution.py:347
  87.1 1.6 collective-permute-start.14
  89.8 5.4 %attend_near.7 = (bf16[512,512]{1,0:T(8,128)(2,1)S(1)}, bf16[512,2176]{1,0:T(8,128)(2,1)S(1)}) custom-call(s32[66]{0:T(128)S(1)} %pad_add_fusion.1.place_ref, f32[512,256]{1,0:T(8,128)S(1)} %pad_maximum_fusion.table_ref, bf16[4,192,1536]{2,1,0:T(8,128)(2,1)S(1)} %bitcast.47, bf16[512,1024]{1,0:T(8,128)(2,1)S(1)} %bitcast.52, ...), custom_call_target="tpu_custom_call" | custom-call | flops 1024 | bytes 1024 | tf_op jit(solution)/shard_map/attend_near/pallas_call | solution.py:251
  95.2 2.4 %collective-permute-start.11 = (bf16[512,512]{1,0:T(8,128)(2,1)S(1)}, bf16[512,512]{1,0:T(8,128)(2,1)S(1)}, u32[]{:S(2)}, u32[]{:S(2)}) collective-permute-start(bf16[512,512]{1,0:T(8,128)(2,1)S(1)} %get-tuple-element.47), channel_id=1, source_target_pairs={{0,6},{2,4},{4,2},{6,0},{8,14},{10,12},{12,10},{14,8},{1,7},{3,5},... | collective-permute-start | bytes 1572872 | tf_op jit(solution)/shard_map/ppermute | solution.py:347
  98.2 5.2 %collective-permute-done.14.refs_0_ = bf16[1,192,1536]{2,1,0:T(8,128)(2,1)S(1)} collective-permute-done((bf16[1,192,1536]{2,1,0:T(8,128)(2,1)S(1)}, bf16[1,192,1536]{2,1,0:T(8,128)(2,1)S(1)}, u32[]{:S(2)}, u32[]{:S(2)}) %collective-permute-start.14) | collective-permute-done | bytes 589856 | tf_op jit(solution)/shard_map/ppermute | solution.py:353
  104.8 12.5 %attend_far.3 = (bf16[512,256]{1,0:T(8,128)(2,1)S(1)}, bf16[512,256]{1,0:T(8,128)(2,1)S(1)}, bf16[512,256]{1,0:T(8,128)(2,1)S(1)}, bf16[512,256]{1,0:T(8,128)(2,1)S(1)}) custom-call(s32[66]{0:T(128)S(1)} %pad_add_fusion.1.place_ref, f32[512,256]{1,0:T(8,128)S(1)} %pad_maximum_fusion.table_ref, bf16[2,192,1536]{2,1,0:T(8,128)(2,1)S(1)} %collective-permute-done.7.refs_0_, ...), custom_call_target="tpu_custom_call" | custom-call | flops 1024 | bytes 1024 | tf_op jit(solution)/shard_map/attend_far/pallas_call | solution.py:270
  118.1 6.6 %collective-permute-done.12.refs_5_ = bf16[512,256]{1,0:T(8,128)(2,1)S(1)} collective-permute-done((bf16[512,256]{1,0:T(8,128)(2,1)S(1)}, bf16[512,256]{1,0:T(8,128)(2,1)S(1)}, u32[]{:S(2)}, u32[]{:S(2)}) %collective-permute-start.12) | collective-permute-done | bytes 262176 | tf_op jit(solution)/shard_map/ppermute | solution.py:347
  124.9 10.9 %attend_far.4 = (bf16[512,128]{1,0:T(8,128)(2,1)S(1)}, bf16[512,128]{1,0:T(8,128)(2,1)S(1)}, bf16[512,128]{1,0:T(8,128)(2,1)S(1)}, bf16[512,128]{1,0:T(8,128)(2,1)}) custom-call(s32[66]{0:T(128)S(1)} %pad_add_fusion.1.place_ref, f32[512,256]{1,0:T(8,128)S(1)} %pad_maximum_fusion.table_ref, bf16[1,192,1536]{2,1,0:T(8,128)(2,1)S(1)} %collective-permute-done.14.refs_0_, ...), custom_call_target="tpu_custom_call" | custom-call | flops 1024 | bytes 1024 | tf_op jit(solution)/shard_map/attend_far/pallas_call | solution.py:270
  135.8 1.6 collective-permute-start.17
  137.4 1.7 %collective-permute-start.18 = (bf16[512,128]{1,0:T(8,128)(2,1)S(1)}, bf16[512,128]{1,0:T(8,128)(2,1)S(1)}, u32[]{:S(2)}, u32[]{:S(2)}) collective-permute-start(bf16[512,128]{1,0:T(8,128)(2,1)S(1)} %get-tuple-element.61), channel_id=1, source_target_pairs={{0,4},{2,6},{4,0},{6,2},{8,12},{10,14},{12,8},{14,10},{1,5},{3,7},... | collective-permute-start | bytes 393224 | tf_op jit(solution)/shard_map/ppermute | solution.py:347
  139.4 2.9 %collective-permute-done.17.refs_9_ = bf16[512,128]{1,0:T(8,128)(2,1)S(1)} collective-permute-done((bf16[512,128]{1,0:T(8,128)(2,1)S(1)}, bf16[512,128]{1,0:T(8,128)(2,1)S(1)}, u32[]{:S(2)}, u32[]{:S(2)}) %collective-permute-start.17) | collective-permute-done | bytes 131104 | tf_op jit(solution)/shard_map/ppermute | solution.py:347
  142.4 11.0 %attend_far.5 = (bf16[512,128]{1,0:T(8,128)(2,1)S(1)}, bf16[512,128]{1,0:T(8,128)(2,1)}, bf16[512,128]{1,0:T(8,128)(2,1)}, bf16[512,128]{1,0:T(8,128)(2,1)}) custom-call(s32[66]{0:T(128)S(1)} %pad_add_fusion.1.place_ref, f32[512,256]{1,0:T(8,128)S(1)} %pad_maximum_fusion.table_ref, bf16[1,192,1536]{2,1,0:T(8,128)(2,1)S(1)} %collective-permute-done.19.refs_0_, ...), custom_call_target="tpu_custom_call" | custom-call | flops 1024 | bytes 1024 | tf_op jit(solution)/shard_map/attend_far/pallas_call | solution.py:270
  157.7 3.0 %place_pieces.2.refs_4_ = bf16[512,4096]{1,0:T(8,128)(2,1)} custom-call(s32[28]{0:T(128)S(1)} %stack.143.offsets_ref, bf16[512,512]{1,0:T(8,128)(2,1)S(1)} %copy-done.3, bf16[512,512]{1,0:T(8,128)(2,1)S(1)} %collective-permute-done.9.refs_1_, bf16[512,512]{1,0:T(8,128)(2,1)S(1)} %collective-permute-done.10.refs_2_, ...), custom_call_target="tpu_custom_call" | custom-call | flops 1024 | bytes 1024 | tf_op jit(solution)/shard_map/place_pieces/pallas_call | solution.py:312
  160.8 2.1 %collective-permute-done.22.refs_3_ = bf16[512,128]{1,0:T(8,128)(2,1)} collective-permute-done((bf16[512,128]{1,0:T(8,128)(2,1)}, bf16[512,128]{1,0:T(8,128)(2,1)}, u32[]{:S(2)}, u32[]{:S(2)}) %collective-permute-start.22) | collective-permute-done | bytes 131104 | tf_op jit(solution)/shard_map/ppermute | solution.py:347
  162.9 1.9 %place_pieces.3 = bf16[512,4096]{1,0:T(8,128)(2,1)} custom-call(s32[4]{0:T(128)S(1)} %pad_add_fusion.offsets_ref, bf16[512,128]{1,0:T(8,128)(2,1)S(1)} %copy-done.5, bf16[512,128]{1,0:T(8,128)(2,1)} %collective-permute-done.20.refs_1_, bf16[512,128]{1,0:T(8,128)(2,1)} %collective-permute-done.21.refs_2_, ...), custom_call_target="tpu_custom_call", output_to_operand_aliasing={{}: (5, {})} | custom-call | flops 1024 | bytes 1024 | tf_op jit(solution)/shard_map/place_pieces/pallas_call | solution.py:312
  (59 shorter events, 18.0 us)
Async XLA Ops:
  4.2 10.5 %collective-permute-start.1 = (bf16[256,2176]{1,0:T(8,128)(2,1)S(1)}, bf16[256,2176]{1,0:T(8,128)(2,1)}, u32[]{:S(2)}, u32[]{:S(2)}) collective-permute-start(bf16[256,2176]{1,0:T(8,128)(2,1)S(1)} %prepare.1.same_ref), channel_id=1, source_target_pairs={{0,1},{1,0},{2,3},{3,2},{4,5},{5,4},{6,7},{7,6},{8,9},{9,8},{10,11... | collective-permute-start | bytes 3342344 | tf_op jit(solution)/shard_map/ppermute | solution.py:350
  4.7 48.6 %collective-permute-start = (bf16[256,2176]{1,0:T(8,128)(2,1)S(1)}, bf16[256,2176]{1,0:T(8,128)(2,1)S(1)}, u32[]{:S(2)}, u32[]{:S(2)}) collective-permute-start(bf16[256,2176]{1,0:T(8,128)(2,1)S(1)} %prepare.1.same_ref), channel_id=1, source_target_pairs={{0,4},{2,6},{4,0},{6,2},{8,12},{10,14},{12,8},{14,10},{1,5},{3,7},... | collective-permute-start | bytes 3342344 | tf_op jit(solution)/shard_map/ppermute | solution.py:347
  7.4 46.0 %collective-permute-start.3 = (bf16[256,2176]{1,0:T(8,128)(2,1)S(1)}, bf16[256,2176]{1,0:T(8,128)(2,1)S(1)}, u32[]{:S(2)}, u32[]{:S(2)}) collective-permute-start(bf16[256,2176]{1,0:T(8,128)(2,1)S(1)} %prepare.1.same_ref), channel_id=1, source_target_pairs={{0,2},{2,0},{4,6},{6,4},{8,10},{10,8},{12,14},{14,12},{1,3},{3,1},... | collective-permute-start | bytes 3342344 | tf_op jit(solution)/shard_map/ppermute | solution.py:347
  10.5 33.0 %collective-permute-start.4 = (bf16[512,512]{1,0:T(8,128)(2,1)S(1)}, bf16[512,512]{1,0:T(8,128)(2,1)S(1)}, u32[]{:S(2)}, u32[]{:S(2)}) collective-permute-start(bf16[512,512]{1,0:T(8,128)(2,1)S(1)} %pick.2), channel_id=1, source_target_pairs={{0,8},{2,10},{4,12},{6,14},{8,0},{10,2},{12,4},{14,6},{1,9},{3,11}... | collective-permute-start | bytes 1572872 | tf_op jit(solution)/shard_map/ppermute | solution.py:347
  13.3 73.8 %collective-permute-start.7 = (bf16[2,192,1536]{2,1,0:T(8,128)(2,1)S(1)}, bf16[2,192,1536]{2,1,0:T(8,128)(2,1)S(1)}, u32[]{:S(2)}, u32[]{:S(2)}) collective-permute-start(bf16[2,192,1536]{2,1,0:T(8,128)(2,1)S(1)} %pick.3), channel_id=1, source_target_pairs={{0,8},{2,10},{4,12},{6,14},{8,0},{10,2},{12,4},{14,6},{1,9},{3,11}... | collective-permute-start | bytes 3538952 | tf_op jit(solution)/shard_map/ppermute | solution.py:347
  53.3 3.2 %collective-permute-start.5 = (bf16[256,2176]{1,0:T(8,128)(2,1)S(1)}, bf16[256,2176]{1,0:T(8,128)(2,1)S(1)}, u32[]{:S(2)}, u32[]{:S(2)}) collective-permute-start(bf16[256,2176]{1,0:T(8,128)(2,1)S(1)} %collective-permute-done.3.same_ref), channel_id=1, source_target_pairs={{0,1},{1,0},{2,3},{3,2},{4,5},{5,4},{6,7},{7,6},{8,9},{9,8},{10,11... | collective-permute-start | bytes 3342344 | tf_op jit(solution)/shard_map/ppermute | solution.py:350
  53.3 8.6 %collective-permute-start.6 = (bf16[256,2176]{1,0:T(8,128)(2,1)S(1)}, bf16[256,2176]{1,0:T(8,128)(2,1)S(1)}, u32[]{:S(2)}, u32[]{:S(2)}) collective-permute-start(bf16[256,2176]{1,0:T(8,128)(2,1)S(1)} %collective-permute-done.same_ref), channel_id=1, source_target_pairs={{0,1},{1,0},{2,3},{3,2},{4,5},{5,4},{6,7},{7,6},{8,9},{9,8},{10,11... | collective-permute-start | bytes 3342344 | tf_op jit(solution)/shard_map/ppermute | solution.py:350
  53.8 33.2 %collective-permute-start.2 = (bf16[256,2176]{1,0:T(8,128)(2,1)S(1)}, bf16[256,2176]{1,0:T(8,128)(2,1)S(1)}, u32[]{:S(2)}, u32[]{:S(2)}) collective-permute-start(bf16[256,2176]{1,0:T(8,128)(2,1)S(1)} %collective-permute-done.same_ref), channel_id=1, source_target_pairs={{0,2},{2,0},{4,6},{6,4},{8,10},{10,8},{12,14},{14,12},{1,3},{3,1},... | collective-permute-start | bytes 3342344 | tf_op jit(solution)/shard_map/ppermute | solution.py:347
  87.0 2.8 %collective-permute-start.8 = (bf16[256,2176]{1,0:T(8,128)(2,1)S(1)}, bf16[256,2176]{1,0:T(8,128)(2,1)S(1)}, u32[]{:S(2)}, u32[]{:S(2)}) collective-permute-start(bf16[256,2176]{1,0:T(8,128)(2,1)S(1)} %collective-permute-done.2.same_ref), channel_id=1, source_target_pairs={{0,1},{1,0},{2,3},{3,2},{4,5},{5,4},{6,7},{7,6},{8,9},{9,8},{10,11... | collective-permute-start | bytes 3342344 | tf_op jit(solution)/shard_map/ppermute | solution.py:350
  87.1 16.2 %collective-permute-start.14 = (bf16[1,192,1536]{2,1,0:T(8,128)(2,1)S(1)}, bf16[1,192,1536]{2,1,0:T(8,128)(2,1)S(1)}, u32[]{:S(2)}, u32[]{:S(2)}) collective-permute-start(bf16[1,192,1536]{2,1,0:T(8,128)(2,1)S(1)} %get-tuple-element.70), channel_id=1, source_target_pairs={{0,16},{16,0},{1,17},{17,1},{2,18},{18,2},{3,19},{19,3},{4,20},{20... | collective-permute-start | bytes 1769480 | tf_op jit(solution)/shard_map/ppermute | solution.py:353
  88.7 16.1 %collective-permute-start.9 = (bf16[512,512]{1,0:T(8,128)(2,1)S(1)}, bf16[512,512]{1,0:T(8,128)(2,1)S(1)}, u32[]{:S(2)}, u32[]{:S(2)}) collective-permute-start(bf16[512,512]{1,0:T(8,128)(2,1)S(1)} %get-tuple-element.41), channel_id=1, source_target_pairs={{0,2},{2,0},{4,6},{6,4},{8,10},{10,8},{12,14},{14,12},{1,3},{3,1},... | collective-permute-start | bytes 1572872 | tf_op jit(solution)/shard_map/ppermute | solution.py:347
  89.2 15.6 %collective-permute-start.10 = (bf16[512,512]{1,0:T(8,128)(2,1)S(1)}, bf16[512,512]{1,0:T(8,128)(2,1)S(1)}, u32[]{:S(2)}, u32[]{:S(2)}) collective-permute-start(bf16[512,512]{1,0:T(8,128)(2,1)S(1)} %get-tuple-element.44), channel_id=1, source_target_pairs={{0,4},{2,6},{4,0},{6,2},{8,12},{10,14},{12,8},{14,10},{1,5},{3,7},... | collective-permute-start | bytes 1572872 | tf_op jit(solution)/shard_map/ppermute | solution.py:347
  95.2 29.7 %collective-permute-start.11 = (bf16[512,512]{1,0:T(8,128)(2,1)S(1)}, bf16[512,512]{1,0:T(8,128)(2,1)S(1)}, u32[]{:S(2)}, u32[]{:S(2)}) collective-permute-start(bf16[512,512]{1,0:T(8,128)(2,1)S(1)} %get-tuple-element.47), channel_id=1, source_target_pairs={{0,6},{2,4},{4,2},{6,0},{8,14},{10,12},{12,10},{14,8},{1,7},{3,5},... | collective-permute-start | bytes 1572872 | tf_op jit(solution)/shard_map/ppermute | solution.py:347
  97.6 27.3 %collective-permute-start.15 = (bf16[512,512]{1,0:T(8,128)(2,1)S(1)}, bf16[512,512]{1,0:T(8,128)(2,1)S(1)}, u32[]{:S(2)}, u32[]{:S(2)}) collective-permute-start(bf16[512,512]{1,0:T(8,128)(2,1)S(1)} %collective-permute-done.4.refs_1_), channel_id=1, source_target_pairs={{0,16},{16,0},{1,17},{17,1},{2,18},{18,2},{3,19},{19,3},{4,20},{20... | collective-permute-start | bytes 1572872 | tf_op jit(solution)/shard_map/ppermute | solution.py:353
  103.3 39.0 %collective-permute-start.19 = (bf16[1,192,1536]{2,1,0:T(8,128)(2,1)S(1)}, bf16[1,192,1536]{2,1,0:T(8,128)(2,1)S(1)}, u32[]{:S(2)}, u32[]{:S(2)}) collective-permute-start(bf16[1,192,1536]{2,1,0:T(8,128)(2,1)S(1)} %get-tuple-element.63), channel_id=1, source_target_pairs={{0,16},{16,0},{1,17},{17,1},{2,18},{18,2},{3,19},{19,3},{4,20},{20... | collective-permute-start | bytes 1769480 | tf_op jit(solution)/shard_map/ppermute | solution.py:353
  117.3 7.3 %collective-permute-start.12 = (bf16[512,256]{1,0:T(8,128)(2,1)S(1)}, bf16[512,256]{1,0:T(8,128)(2,1)S(1)}, u32[]{:S(2)}, u32[]{:S(2)}) collective-permute-start(bf16[512,256]{1,0:T(8,128)(2,1)S(1)} %get-tuple-element.54), channel_id=1, source_target_pairs={{0,2},{2,0},{4,6},{6,4},{8,10},{10,8},{12,14},{14,12},{1,3},{3,1},... | collective-permute-start | bytes 786440 | tf_op jit(solution)/shard_map/ppermute | solution.py:347
  118.1 6.8 %collective-permute-start.13 = (bf16[512,256]{1,0:T(8,128)(2,1)S(1)}, bf16[512,256]{1,0:T(8,128)(2,1)S(1)}, u32[]{:S(2)}, u32[]{:S(2)}) collective-permute-start(bf16[512,256]{1,0:T(8,128)(2,1)S(1)} %get-tuple-element.55), channel_id=1, source_target_pairs={{0,4},{2,6},{4,0},{6,2},{8,12},{10,14},{12,8},{14,10},{1,5},{3,7},... | collective-permute-start | bytes 786440 | tf_op jit(solution)/shard_map/ppermute | solution.py:347
  124.6 14.7 %collective-permute-start.16 = (bf16[512,256]{1,0:T(8,128)(2,1)S(1)}, bf16[512,256]{1,0:T(8,128)(2,1)S(1)}, u32[]{:S(2)}, u32[]{:S(2)}) collective-permute-start(bf16[512,256]{1,0:T(8,128)(2,1)S(1)} %get-tuple-element.59), channel_id=1, source_target_pairs={{0,6},{2,4},{4,2},{6,0},{8,14},{10,12},{12,10},{14,8},{1,7},{3,5},... | collective-permute-start | bytes 786440 | tf_op jit(solution)/shard_map/ppermute | solution.py:347
  135.8 6.4 %collective-permute-start.17 = (bf16[512,128]{1,0:T(8,128)(2,1)S(1)}, bf16[512,128]{1,0:T(8,128)(2,1)S(1)}, u32[]{:S(2)}, u32[]{:S(2)}) collective-permute-start(bf16[512,128]{1,0:T(8,128)(2,1)S(1)} %get-tuple-element.60), channel_id=1, source_target_pairs={{0,2},{2,0},{4,6},{6,4},{8,10},{10,8},{12,14},{14,12},{1,3},{3,1},... | collective-permute-start | bytes 393224 | tf_op jit(solution)/shard_map/ppermute | solution.py:347
  137.4 5.0 %collective-permute-start.18 = (bf16[512,128]{1,0:T(8,128)(2,1)S(1)}, bf16[512,128]{1,0:T(8,128)(2,1)S(1)}, u32[]{:S(2)}, u32[]{:S(2)}) collective-permute-start(bf16[512,128]{1,0:T(8,128)(2,1)S(1)} %get-tuple-element.61), channel_id=1, source_target_pairs={{0,4},{2,6},{4,0},{6,2},{8,12},{10,14},{12,8},{14,10},{1,5},{3,7},... | collective-permute-start | bytes 393224 | tf_op jit(solution)/shard_map/ppermute | solution.py:347
  139.1 18.6 %collective-permute-start.23 = (bf16[512,128]{1,0:T(8,128)(2,1)}, bf16[512,128]{1,0:T(8,128)(2,1)}, u32[]{:S(2)}, u32[]{:S(2)}) collective-permute-start(bf16[512,128]{1,0:T(8,128)(2,1)} %get-tuple-element.68), channel_id=1, source_target_pairs={{0,6},{2,4},{4,2},{6,0},{8,14},{10,12},{12,10},{14,8},{1,7},{3,5},... | collective-permute-start | bytes 393224 | tf_op jit(solution)/shard_map/ppermute | solution.py:347
  154.0 6.7 %collective-permute-start.20 = (bf16[512,128]{1,0:T(8,128)(2,1)}, bf16[512,128]{1,0:T(8,128)(2,1)}, u32[]{:S(2)}, u32[]{:S(2)}) collective-permute-start(bf16[512,128]{1,0:T(8,128)(2,1)} %get-tuple-element.65), channel_id=1, source_target_pairs={{0,2},{2,0},{4,6},{6,4},{8,10},{10,8},{12,14},{14,12},{1,3},{3,1},... | collective-permute-start | bytes 393224 | tf_op jit(solution)/shard_map/ppermute | solution.py:347
  155.2 5.6 %collective-permute-start.21 = (bf16[512,128]{1,0:T(8,128)(2,1)}, bf16[512,128]{1,0:T(8,128)(2,1)}, u32[]{:S(2)}, u32[]{:S(2)}) collective-permute-start(bf16[512,128]{1,0:T(8,128)(2,1)} %get-tuple-element.66), channel_id=1, source_target_pairs={{0,4},{2,6},{4,0},{6,2},{8,12},{10,14},{12,8},{14,10},{1,5},{3,7},... | collective-permute-start | bytes 393224 | tf_op jit(solution)/shard_map/ppermute | solution.py:347
  156.7 6.2 %collective-permute-start.22 = (bf16[512,128]{1,0:T(8,128)(2,1)}, bf16[512,128]{1,0:T(8,128)(2,1)}, u32[]{:S(2)}, u32[]{:S(2)}) collective-permute-start(bf16[512,128]{1,0:T(8,128)(2,1)} %get-tuple-element.67), channel_id=1, source_target_pairs={{0,6},{2,4},{4,2},{6,0},{8,14},{10,12},{12,10},{14,8},{1,7},{3,5},... | collective-permute-start | bytes 393224 | tf_op jit(solution)/shard_map/ppermute | solution.py:347
  (6 other events, 27.5 us)

commit v4 on v3

--- a/solution.py
+++ b/solution.py
@@ -92,86 +92,113 @@
     )(jnp.reshape(index, (1,)).astype(jnp.int32), source)
 
 
-def project(tokens_ref, sizes, weight_refs, chosen):
+def attend_group(sizes, chosen, tokens_ref, weight_refs, scratch, out_ref):
     heads, q_width, kv_width, nope_width, rope_width, value_width = sizes
     query_width, pair_width = nope_width + rope_width, nope_width + value_width
-
-    def dot(tokens, weight, dims):
-        return lax.dot_general(tokens, weight, dims, preferred_element_type=jnp.float32)
-
-    latent = tokens_ref[:, q_width : q_width + kv_width]
-    query_ref, pair_ref = weight_refs
-    columns = [slice(number * pair_width, (number + 1) * pair_width) for number in chosen]
-    every = dot(latent, pair_ref[:, columns[0].start : columns[-1].stop], NN)
-    pair = [every[:, head * pair_width : (head + 1) * pair_width] for head in range(heads)]
-
-    def query(low, high, picked):
-        parts = [query_ref[number if query_ref.shape[0] > 1 else 0, low:high, :] for number in picked]
-        return dot(tokens_ref[:, :q_width], jnp.concatenate(parts, axis=0), NT)
-
-    nope = [query(0, nope_width, chosen[head : head + 2]) for head in range(0, heads, 2)]
-    picked = list(chosen)
-    while len(picked) * rope_width % nope_width:
-        picked.append(picked[-1])
-    return nope, query(nope_width, query_width, picked), pair
-
-
-def attend_group(sizes, chosen, tokens_ref, weight_refs, scratch, out_ref):
-    heads, q_width, kv_width, nope_width, rope_width, value_width = sizes
     query_ref, key_ref, value_ref, turn_ref, bias_ref = scratch
+    query_weight_ref, pair_weight_ref = weight_refs
     tokens = tokens_ref.shape[0]
     rows = bias_ref.shape[0]
     half_width = rope_width // 2
-    score_scale = (nope_width + rope_width) ** -0.5 * math.log2(math.e)
-    nope, rope, pair = project(tokens_ref, sizes, weight_refs, chosen)
+    group_heads = nope_width // rope_width
+    score_scale = query_width**-0.5 * math.log2(math.e)
     lane = lax.broadcasted_iota(jnp.int32, (tokens, nope_width), 1)
     is_first = lax.rem(lane, rope_width) < half_width
     is_rope = lane < rope_width
-    shared = tokens_ref[:, q_width + kv_width :]
-    apart = jnp.where(is_rope, 0.0, (1.0 - shared.astype(jnp.float32)) * FAR)
-    for head in range(heads):
-        low = head % 2 * nope_width
-        part = nope[head // 2][:, low : low + nope_width]
-        query_ref[:, 2 * head * nope_width : (2 * head + 1) * nope_width] = (part * score_scale).astype(jnp.bfloat16)
-        both = pair[head].astype(jnp.bfloat16)
-        key_ref[:, head * nope_width : (head + 1) * nope_width] = both[:, :nope_width]
-        value_ref[head, :, :value_width] = both[:, nope_width:]
-    group_heads = nope_width // rope_width
-    for low in range(0, rope.shape[1], nope_width):
-        part = rope[:, low : low + nope_width]
-        swapped = jnp.where(is_first, pltpu.roll(part, nope_width - half_width, 1), pltpu.roll(part, half_width, 1))
-        turned = (part * turn_ref[:, :nope_width] + swapped * turn_ref[:, nope_width:]) * score_scale
-        for index in range(group_heads):
-            head = low // rope_width + index
-            if head < heads:
-                moved = pltpu.roll(turned, nope_width - index * rope_width, 1) if index else turned
-                query_ref[:, (2 * head + 1) * nope_width : (2 * head + 2) * nope_width] = jnp.where(
-                    is_rope, moved, apart
-                ).astype(jnp.bfloat16)
-    for head in range(heads):
-        for half in range(2):
-            low, high = half * rows, (half + 1) * rows
-            queries = query_ref[low:high, 2 * head * nope_width : (2 * head + 2) * nope_width]
-            keys = jnp.concatenate(
-                [key_ref[:high, head * nope_width : (head + 1) * nope_width], tokens_ref[:high, q_width + kv_width :]], axis=1
-            )
-            scores = lax.dot_general(queries, keys, NT, preferred_element_type=jnp.float32)
-            last = scores[:, low:] + bias_ref[...]
-            scores = jnp.concatenate([scores[:, :low], last], axis=1) if half else last
-            terms = jnp.exp2(scores - jnp.max(scores, axis=1, keepdims=True)).astype(jnp.bfloat16)
-            mixed = lax.dot_general(terms, value_ref[head, :high, :], NN, preferred_element_type=jnp.float32)
-            out_ref[low:high, head * value_width : (head + 1) * value_width] = (
-                mixed[:, :value_width] / mixed[:, value_width:]
-            ).astype(jnp.bfloat16)
-
-
-def set_up(scratch):
+    rope_low = q_width + kv_width
+    apart = jnp.where(is_rope, 0.0, (1.0 - tokens_ref[:, rope_low:].astype(jnp.float32)) * FAR)
+
+    def dot(left, right, dims):
+        return lax.dot_general(left, right, dims, preferred_element_type=jnp.float32)
+
+    def project(some):
+        numbers = [chosen[head] for head in some]
+        while len(numbers) < group_heads:
+            numbers.append(numbers[-1])
+
+        def query(low, high, picked):
+            parts = [query_weight_ref[number, low:high, :] for number in picked]
+            return dot(tokens_ref[:, :q_width], jnp.concatenate(parts, axis=0), NT)
+
+        rope = query(nope_width, query_width, numbers)
+        nope = query(0, nope_width, numbers[: len(some)])
+        first, last = numbers[0] * pair_width, (numbers[len(some) - 1] + 1) * pair_width
+        pair = dot(tokens_ref[:, q_width:rope_low], pair_weight_ref[:, first:last], NN)
+        swapped = jnp.where(is_first, pltpu.roll(rope, nope_width - half_width, 1), pltpu.roll(rope, half_width, 1))
+        turned = (rope * turn_ref[:, :nope_width] + swapped * turn_ref[:, nope_width:]) * score_scale
+        for index, head in enumerate(some):
+            low = 2 * head * nope_width
+            part = nope[:, index * nope_width : (index + 1) * nope_width]
+            query_ref[:, low : low + nope_width] = (part * score_scale).astype(jnp.bfloat16)
+            moved = pltpu.roll(turned, nope_width - index * rope_width, 1) if index else turned
+            query_ref[:, low + nope_width : low + 2 * nope_width] = jnp.where(is_rope, moved, apart).astype(jnp.bfloat16)
+            both = pair[:, index * pair_width : (index + 1) * pair_width].astype(jnp.bfloat16)
+            key_ref[:, head * nope_width : (head + 1) * nope_width] = both[:, :nope_width]
+            value_ref[head, :, :value_width] = both[:, nope_width:]
+
+    def score(head, half):
+        low, high = half * rows, (half + 1) * rows
+        queries = query_ref[low:high, 2 * head * nope_width : (2 * head + 2) * nope_width]
+        shared = tokens_ref[:high, rope_low:]
+        keys = jnp.concatenate([key_ref[:high, head * nope_width : (head + 1) * nope_width], shared], axis=1)
+        return dot(queries, keys, NT)
+
+    def soften(half, scores):
+        low = half * rows
+        last = scores[:, low:] + bias_ref[...]
+        scores = jnp.concatenate([scores[:, :low], last], axis=1) if half else last
+        return jnp.exp2(scores - jnp.max(scores, axis=1, keepdims=True)).astype(jnp.bfloat16)
+
+    def mix(head, half, terms):
+        low, high = half * rows, (half + 1) * rows
+        mixed = dot(terms, value_ref[head, :high, :], NN)
+        out_ref[low:high, head * value_width : (head + 1) * value_width] = (
+            mixed[:, :value_width] / mixed[:, value_width:]
+        ).astype(jnp.bfloat16)
+
+    batches = [list(range(heads))[low : low + group_heads] for low in range(0, heads, group_heads)]
+    project(batches[0])
+    yield
+    terms = None
+    for number, batch in enumerate(batches):
+        scores = score(batch[0], 0)
+        if number + 1 < len(batches):
+            project(batches[number + 1])
+        else:
+            yield
+        for head in batch:
+            for half in range(2):
+                ahead = (head, 1) if half == 0 else (head + 1, 0)
+                following = score(*ahead) if ahead[0] in batch else None
+                held = soften(half, scores)
+                if terms is not None:
+                    mix(*terms)
+                terms = (head, half, held)
+                scores = following
+    yield
+    mix(*terms)
+
+
+def attend_groups(works):
+    works = list(works)
+    for index, work in enumerate(works):
+        if index == 0:
+            next(work)
+        next(work)
+        if index + 1 < len(works):
+            next(works[index + 1])
+        for rest in work:
+            pass
+
+
+def set_up(scratch, first=True):
     value_ref, bias_ref = scratch[2], scratch[4]
     rows = bias_ref.shape[0]
     heads, tokens, width = value_ref.shape
-    row_ids = lax.broadcasted_iota(jnp.int32, (rows, rows), 0)
-    col_ids = lax.broadcasted_iota(jnp.int32, (rows, rows), 1)
-    bias_ref[...] = jnp.where(col_ids <= row_ids, 0.0, -jnp.inf)
+    if first:
+        row_ids = lax.broadcasted_iota(jnp.int32, (rows, rows), 0)
+        col_ids = lax.broadcasted_iota(jnp.int32, (rows, rows), 1)
+        bias_ref[...] = jnp.where(col_ids <= row_ids, 0.0, -jnp.inf)
     for head in range(heads):
         value_ref[head, :, width // 2 :] = jnp.ones((tokens, width // 2), jnp.bfloat16)
 
@@ -197,40 +224,22 @@
     tokens_ref[pl.ds(pl.multiple_of((1 - core) * rows, rows), rows), :] = other_ref[...]
     set_up(scratch)
     set_turn(group, slot_count, place_ref, table_ref, scratch[3])
-    attend_group(sizes, list(range(sizes[0])), tokens_ref, (query_weight_ref, pair_weight_ref), scratch, out_ref)
-
-
-def far_kernel(sizes, slot_count, slots, chosen, place_ref, table_ref, *refs):
+    heads = list(range(sizes[0]))
+    attend_groups([attend_group(sizes, heads, tokens_ref, (query_weight_ref, pair_weight_ref), scratch, out_ref)])
+
+
+def far_kernel(sizes, slot_count, distances, chosen, place_ref, table_ref, *refs):
+    slots = len(distances)
     weight_refs, refs = refs[:2], refs[2:]
     token_refs, out_refs, refs = refs[:slots], refs[slots : 2 * slots], refs[2 * slots :]
-    held_ref, result_ref, sems = refs[0], refs[1], refs[2]
-    scratch = refs[3:]
-    set_up(scratch)
-
-    def fetch(slot):
-        for index in range(slots):
-
-            @pl.when(slot == index)
-            def _(index=index):
-                pltpu.make_async_copy(token_refs[index], held_ref.at[index % 2], sems.at[index % 2]).start()
-
-    fetch(0)
-
-    def one_group(slot, carry):
-        turn = lax.rem(slot, 2)
-        fetch(slot + 1)
-        set_turn(place_ref[0] ^ slot, slot_count, place_ref, table_ref, scratch[3])
-        pltpu.make_async_copy(token_refs[0], held_ref.at[turn], sems.at[turn]).wait()
-        attend_group(sizes, chosen, held_ref.at[turn], weight_refs, scratch, result_ref)
-        for index in range(slots):
-
-            @pl.when(slot == index)
-            def _(index=index):
-                out_refs[index][...] = result_ref[...]
-
-        return carry
-
-    lax.fori_loop(0, slots, one_group, 0)
+    bias_ref, refs = refs[0], refs[1:]
+    works = []
+    for slot in range(slots):
+        scratch = [*refs[4 * slot : 4 * slot + 4], bias_ref]
+        set_up(scratch, slot == 0)
+        set_turn(place_ref[0] ^ distances[slot], slot_count, place_ref, table_ref, scratch[3])
+        works.append(attend_group(sizes, chosen, token_refs[slot], weight_refs, scratch, out_refs[slot]))
+    attend_groups(works)
 
 
 def scratch_for(sizes, tokens):
@@ -263,23 +272,17 @@
     )(place, table, query_weight, pair_weight, same, other)
 
 
-def attend_far(sizes, slot_count, place, table, query_weight, pair_weight, chosen, groups):
-    tokens, width = groups[0].shape
+def attend_far(sizes, slot_count, distances, place, table, query_weight, pair_weight, chosen, groups):
+    tokens = groups[0].shape[0]
     slots, heads, value_width = len(groups), sizes[0], sizes[-1]
     vmem = pl.BlockSpec(memory_space=pltpu.VMEM)
+    own = scratch_for(sizes, tokens)
     return pl.pallas_call(
-        partial(far_kernel, sizes, slot_count, slots, chosen),
+        partial(far_kernel, sizes, slot_count, distances, chosen),
         out_shape=[jax.ShapeDtypeStruct((tokens, heads * value_width), jnp.bfloat16)] * slots,
-        in_specs=[pl.BlockSpec(memory_space=pltpu.SMEM)]
-        + [vmem] * 3
-        + [pl.BlockSpec(memory_space=pl.ANY)] * slots,
+        in_specs=[pl.BlockSpec(memory_space=pltpu.SMEM)] + [vmem] * (3 + slots),
         out_specs=[vmem] * slots,
-        scratch_shapes=[
-            pltpu.VMEM((2, tokens, width), jnp.bfloat16),
-            pltpu.VMEM((tokens, heads * value_width), jnp.bfloat16),
-            pltpu.SemaphoreType.DMA((2,)),
-        ]
-        + scratch_for(sizes, tokens),
+        scratch_shapes=own[4:] + own[:4] * slots,
         compiler_params=pltpu.CompilerParams(vmem_limit_bytes=VMEM_LIMIT),
         cost_estimate=LIGHT,
         name="attend_far",
@@ -402,10 +405,10 @@
             other.append(None)
         else:
             other.append(sibling(after(same[distance], mixed, far_pair, *direct)))
-    crossed_pair = other_part(after(far_pair, mixed)) if share == 2 else None
+    crossed_pair = [other_part(after(far_pair, mixed))] if share == 2 else []
     for distance in range(1, half_places):
         if other[distance] is None:
-            other[distance] = sibling(after(same[distance], mixed, far_query))
+            other[distance] = sibling(after(same[distance], mixed, far_query, *crossed_pair))
         mixed = near(distance, mixed)
         arrived.append(across(mixed, distance))
     placed = []
@@ -413,28 +416,43 @@
         base = (place ^ distance) * block_width
         placed.append((arrived[distance], [base + head * value_width for head in range(local_heads)]))
 
-    rounds = [(far_query, far_pair, list(range(per_part)), side * per_part)]
-    crossed = []
+    out_width = places * block_width
+
+    def flush(held):
+        offsets = [offset for piece, starts in placed for offset in starts]
+        held = place_pieces([piece for piece, starts in placed], offsets, value_width, out_width, held)
+        placed.clear()
+        return held
+
+    heads = list(range(per_part))
+    rounds = [(far_query, far_pair, side * per_part)]
     if share == 2:
-        for index in range(per_part):
-            crossed.append(other_part(after(far_query[index : index + 1], *crossed)))
-            rounds.append((crossed[index], crossed_pair, [index], (1 - side) * per_part))
-    previous, waiting = arrived[1:-1], arrived[-1:]
-    for queries, pairs, chosen, first in rounds:
-        mixed_all = attend_far(
-            (len(chosen), *sizes), slot_count, after(spot, mixed, *previous), table, queries, pairs, chosen, joined
-        )
-        mixed = mixed_all[0]
-        received = [across(mixed_all[distance], distance) for distance in range(1, half_places)]
-        previous, waiting = waiting + received[:-1], received[-1:]
-        for distance, piece in enumerate([mixed] + received):
-            base = (place ^ distance ^ half_places) * block_width
-            placed.append((piece, [base + (first + number) * value_width for number in chosen]))
-    held, out_width = None, places * block_width
-    late = len(placed) - half_places
-    for batch in (placed[:late], placed[late:]):
-        offsets = [offset for piece, starts in batch for offset in starts]
-        held = place_pieces([piece for piece, starts in batch], offsets, value_width, out_width, held)
+        rounds.append((other_part(far_query), crossed_pair[0], (1 - side) * per_part))
+    gates, first_sent, late = [], [], []
+    later = [arrived[1:-1], arrived[-1:], first_sent, []]
+    for number, (queries, pairs, first) in enumerate(rounds):
+        for distances in (list(range(1, half_places)), [0]):
+            mixed_some = attend_far(
+                (per_part, *sizes),
+                slot_count,
+                distances,
+                after(spot, mixed, *gates),
+                table,
+                queries,
+                pairs,
+                heads,
+                [joined[distance] for distance in distances],
+            )
+            mixed, gates = mixed_some[0], later.pop(0)
+            for distance, piece in zip(distances, mixed_some):
+                base = (place ^ distance ^ half_places) * block_width
+                received = across(piece, distance) if distance else piece
+                if number == 0 and distance:
+                    first_sent.append(received)
+                (late if number else placed).append((received, [base + (first + head) * value_width for head in heads]))
+    held = flush(None)
+    placed.extend(late)
+    held = flush(held)
     return held
 
 

time: 165 us -> 140 us (0.85)
  Pallas kernels: 63.2 us -> 47.7 us
  waiting for transfers between devices: 68.9 us -> 57.3 us
  local copies, waits for them, and re-layouts: 5.21 us -> 7.45 us
    pallas_call x3 -> x4, Pallas kernels: 34.4 us -> 19.7 us  [attend_far(): pl.pallas_call(partial(far_kernel, sizes, slot_count, distances, chosen),...]
    ppermute x17 -> x14, waiting for transfers between devices: 63.1 us -> 56.6 us  [across(): lax.ppermute(value, 'seq', [(s, s ^ distance) for s in range(places)])]
    ppermute x3 -> x2, waiting for transfers between devices: 5.17 us -> 0.01 us  [other_part(): return lax.ppermute(value, 'parts', [(p, p ^ 1) for p in range(parts)])]
    unnamed x13 -> x35, local copies, waits for them, and re-layouts: 4.27 us -> 6.5 us
    pallas_call x4, Pallas kernels: 22.4 us -> 20.5 us  [attend_near(): pl.pallas_call(partial(near_kernel, sizes, slot_count, distance), out_sha...]
    ppermute x3 -> x2, starting transfers between devices: 3.58 us -> 3.05 us  [other_part(): return lax.ppermute(value, 'parts', [(p, p ^ 1) for p in range(parts)])]
    ppermute x17 -> x14, starting transfers between devices: 20.7 us -> 20.8 us  [across(): lax.ppermute(value, 'seq', [(s, s ^ distance) for s in range(places)])]
  transfers between devices with their start and end apart: 24 -> 20, of which waited for: 10 -> 6; matrix products, arithmetic and copies ran while one was open for 2% -> 1% of each run, Pallas kernels for 36% -> 31%
where the time goes in v4:
time: 140 us
  waiting for transfers between devices  57.3 us (41%)
  Pallas kernels  47.7 us (34%)
  starting transfers between devices  24.8 us (18%)
  local copies, waits for them, and re-layouts  7.45 us (5%)
  other arithmetic  1.84 us (1%)
    ppermute x14, waiting for transfers between devices, across(): lax.ppermute(value, 'seq', [(s, s ^ distance) for s in range(places)])  56.6 us
    ppermute x14, starting transfers between devices, across(): lax.ppermute(value, 'seq', [(s, s ^ distance) for s in range(places)])  20.8 us
    pallas_call x4, Pallas kernels, attend_near(): pl.pallas_call(partial(near_kernel, sizes, slot_count, distance), out_sha...  20.5 us
    pallas_call x4, Pallas kernels, attend_far(): pl.pallas_call(partial(far_kernel, sizes, slot_count, distances, chosen),...  19.7 us
    unnamed x35, local copies, waits for them, and re-layouts  6.5 us
    pallas_call x2, Pallas kernels, place_pieces(): pl.pallas_call(partial(place_kernel, width, count), out_shape=jax.ShapeDt...  5.04 us
    ppermute x2, starting transfers between devices, other_part(): return lax.ppermute(value, 'parts', [(p, p ^ 1) for p in range(parts)])  3.05 us
  transfers between devices with their start and end apart: 20, of which 6 were waited for; matrix products, arithmetic and copies ran while one was open for 1% of the time, Pallas kernels for 31%

profile of v4, /device:TPU:0, one launch (start us, length us, event | category | flops | bytes accessed | tf_op | source)
XLA Modules:
  0.0 139.5 jit_solution(5248544109549355906)
XLA Ops:
  2.8 2.4 %prepare.1.same_ref = bf16[256,2176]{1,0:T(8,128)(2,1)} custom-call(s32[66]{0:T(128)S(1)} %pad_add_fusion.place_ref, bf16[2112,256]{1,0:T(8,128)(2,1)S(1)} %bitcast.53, f32[1,2048]{1,0:T(1,128)S(1)} %bitcast.54), custom_call_target="tpu_custom_call" | custom-call | flops 1024 | bytes 1024 | tf_op jit(solution)/shard_map/prepare/pallas_call | solution.py:60
  5.6 2.6 %collective-permute-start = (bf16[256,2176]{1,0:T(8,128)(2,1)}, bf16[256,2176]{1,0:T(8,128)(2,1)}, u32[]{:S(2)}, u32[]{:S(2)}) collective-permute-start(bf16[256,2176]{1,0:T(8,128)(2,1)} %prepare.1.same_ref), channel_id=1, source_target_pairs={{0,4},{2,6},{4,0},{6,2},{8,12},{10,14},{12,8},{14,10},{1,5},{3,7},... | collective-permute-start | bytes 3342344 | tf_op jit(solution)/shard_map/ppermute | solution.py:350
  8.2 1.5 %collective-permute-start.3 = (bf16[256,2176]{1,0:T(8,128)(2,1)}, bf16[256,2176]{1,0:T(8,128)(2,1)}, u32[]{:S(2)}, u32[]{:S(2)}) collective-permute-start(bf16[256,2176]{1,0:T(8,128)(2,1)} %prepare.1.same_ref), channel_id=1, source_target_pairs={{0,2},{2,0},{4,6},{6,4},{8,10},{10,8},{12,14},{14,12},{1,3},{3,1},... | collective-permute-start | bytes 3342344 | tf_op jit(solution)/shard_map/ppermute | solution.py:350
  10.0 2.7 %collective-permute-start.4 = (bf16[512,512]{1,0:T(8,128)(2,1)S(1)}, bf16[512,512]{1,0:T(8,128)(2,1)S(1)}, u32[]{:S(2)}, u32[]{:S(2)}) collective-permute-start(bf16[512,512]{1,0:T(8,128)(2,1)S(1)} %pick.2), channel_id=1, source_target_pairs={{0,8},{2,10},{4,12},{6,14},{8,0},{10,2},{12,4},{14,6},{1,9},{3,11}... | collective-permute-start | bytes 1572872 | tf_op jit(solution)/shard_map/ppermute | solution.py:350
  17.5 5.2 %attend_near.4 = (bf16[512,512]{1,0:T(8,128)(2,1)S(1)}, bf16[512,2176]{1,0:T(8,128)(2,1)S(1)}) custom-call(s32[66]{0:T(128)S(1)} %pad_add_fusion.place_ref, f32[512,256]{1,0:T(8,128)S(1)} %pad_maximum_fusion.table_ref, bf16[4,192,1536]{2,1,0:T(8,128)(2,1)S(1)} %bitcast.44, bf16[512,1024]{1,0:T(8,128)(2,1)S(1)} %bitcast.49, ...), custom_call_target="tpu_custom_call" | custom-call | flops 1024 | bytes 1024 | tf_op jit(solution)/shard_map/attend_near/pallas_call | solution.py:260
  23.5 21.1 %collective-permute-done.4.refs_1_ = bf16[512,512]{1,0:T(8,128)(2,1)S(1)} collective-permute-done((bf16[512,512]{1,0:T(8,128)(2,1)S(1)}, bf16[512,512]{1,0:T(8,128)(2,1)S(1)}, u32[]{:S(2)}, u32[]{:S(2)}) %collective-permute-start.4) | collective-permute-done | bytes 524320 | tf_op jit(solution)/shard_map/ppermute | solution.py:350
  44.6 11.6 %collective-permute-done.same_ref = bf16[256,2176]{1,0:T(8,128)(2,1)} collective-permute-done((bf16[256,2176]{1,0:T(8,128)(2,1)}, bf16[256,2176]{1,0:T(8,128)(2,1)}, u32[]{:S(2)}, u32[]{:S(2)}) %collective-permute-start) | collective-permute-done | bytes 1114144 | tf_op jit(solution)/shard_map/ppermute | solution.py:350
  56.7 2.7 %collective-permute-start.2 = (bf16[256,2176]{1,0:T(8,128)(2,1)}, bf16[256,2176]{1,0:T(8,128)(2,1)S(1)}, u32[]{:S(2)}, u32[]{:S(2)}) collective-permute-start(bf16[256,2176]{1,0:T(8,128)(2,1)} %collective-permute-done.same_ref), channel_id=1, source_target_pairs={{0,2},{2,0},{4,6},{6,4},{8,10},{10,8},{12,14},{14,12},{1,3},{3,1},... | collective-permute-start | bytes 3342344 | tf_op jit(solution)/shard_map/ppermute | solution.py:350
  60.9 5.3 %attend_near.5 = (bf16[512,512]{1,0:T(8,128)(2,1)S(1)}, bf16[512,2176]{1,0:T(8,128)(2,1)S(1)}) custom-call(s32[66]{0:T(128)S(1)} %pad_add_fusion.place_ref, f32[512,256]{1,0:T(8,128)S(1)} %pad_maximum_fusion.table_ref, bf16[4,192,1536]{2,1,0:T(8,128)(2,1)S(1)} %bitcast.45, bf16[512,1024]{1,0:T(8,128)(2,1)S(1)} %bitcast.50, ...), custom_call_target="tpu_custom_call" | custom-call | flops 1024 | bytes 1024 | tf_op jit(solution)/shard_map/attend_near/pallas_call | solution.py:260
  66.1 5.5 %attend_near.6 = (bf16[512,512]{1,0:T(8,128)(2,1)S(1)}, bf16[512,2176]{1,0:T(8,128)(2,1)S(1)}) custom-call(s32[66]{0:T(128)S(1)} %pad_add_fusion.place_ref, f32[512,256]{1,0:T(8,128)S(1)} %pad_maximum_fusion.table_ref, bf16[4,192,1536]{2,1,0:T(8,128)(2,1)S(1)} %bitcast.46, bf16[512,1024]{1,0:T(8,128)(2,1)S(1)} %bitcast.51, ...), custom_call_target="tpu_custom_call" | custom-call | flops 1024 | bytes 1024 | tf_op jit(solution)/shard_map/attend_near/pallas_call | solution.py:260
  71.6 15.0 %collective-permute-done.7.refs_0_ = bf16[2,192,1536]{2,1,0:T(8,128)(2,1)S(1)} collective-permute-done((bf16[2,192,1536]{2,1,0:T(8,128)(2,1)S(1)}, bf16[2,192,1536]{2,1,0:T(8,128)(2,1)S(1)}, u32[]{:S(2)}, u32[]{:S(2)}) %collective-permute-start.7) | collective-permute-done | bytes 1179680 | tf_op jit(solution)/shard_map/ppermute | solution.py:350
  86.6 1.6 %collective-permute-start.13 = (bf16[2,192,1536]{2,1,0:T(8,128)(2,1)S(1)}, bf16[2,192,1536]{2,1,0:T(8,128)(2,1)S(1)}, u32[]{:S(2)}, u32[]{:S(2)}) collective-permute-start(bf16[2,192,1536]{2,1,0:T(8,128)(2,1)S(1)} %collective-permute-done.7.refs_0_), channel_id=1, source_target_pairs={{0,16},{16,0},{1,17},{17,1},{2,18},{18,2},{3,19},{19,3},{4,20},{20... | collective-permute-start | bytes 3538952 | tf_op jit(solution)/shard_map/ppermute | solution.py:356
  89.4 4.5 %attend_near.7 = (bf16[512,512]{1,0:T(8,128)(2,1)S(1)}, bf16[512,2176]{1,0:T(8,128)(2,1)S(1)}) custom-call(s32[66]{0:T(128)S(1)} %pad_add_fusion.place_ref, f32[512,256]{1,0:T(8,128)S(1)} %pad_maximum_fusion.table_ref, bf16[4,192,1536]{2,1,0:T(8,128)(2,1)S(1)} %bitcast.47, bf16[512,1024]{1,0:T(8,128)(2,1)S(1)} %bitcast.52, ...), custom_call_target="tpu_custom_call" | custom-call | flops 1024 | bytes 1024 | tf_op jit(solution)/shard_map/attend_near/pallas_call | solution.py:260
  93.9 2.4 %collective-permute-start.12 = (bf16[512,512]{1,0:T(8,128)(2,1)S(1)}, bf16[512,512]{1,0:T(8,128)(2,1)S(1)}, u32[]{:S(2)}, u32[]{:S(2)}) collective-permute-start(bf16[512,512]{1,0:T(8,128)(2,1)S(1)} %get-tuple-element.42), channel_id=1, source_target_pairs={{0,6},{2,4},{4,2},{6,0},{8,14},{10,12},{12,10},{14,8},{1,7},{3,5},... | collective-permute-start | bytes 1572872 | tf_op jit(solution)/shard_map/ppermute | solution.py:350
  96.3 7.0 %attend_far.4 = (bf16[512,256]{1,0:T(8,128)(2,1)S(1)}, bf16[512,256]{1,0:T(8,128)(2,1)}, bf16[512,256]{1,0:T(8,128)(2,1)}) custom-call(s32[66]{0:T(128)S(1)} %pad_add_fusion.place_ref, f32[512,256]{1,0:T(8,128)S(1)} %pad_maximum_fusion.table_ref, bf16[2,192,1536]{2,1,0:T(8,128)(2,1)S(1)} %collective-permute-done.7.refs_0_, ...), custom_call_target="tpu_custom_call" | custom-call | flops 1024 | bytes 1024 | tf_op jit(solution)/shard_map/attend_far/pallas_call | solution.py:280
  104.5 2.3 %collective-permute-start.19 = (bf16[512,256]{1,0:T(8,128)(2,1)}, bf16[512,256]{1,0:T(8,128)(2,1)}, u32[]{:S(2)}, u32[]{:S(2)}) collective-permute-start(bf16[512,256]{1,0:T(8,128)(2,1)} %get-tuple-element.55), channel_id=1, source_target_pairs={{0,6},{2,4},{4,2},{6,0},{8,14},{10,12},{12,10},{14,8},{1,7},{3,5},... | collective-permute-start | bytes 786440 | tf_op jit(solution)/shard_map/ppermute | solution.py:350
  106.9 2.9 %attend_far.5.refs_7_ = bf16[512,256]{1,0:T(8,128)(2,1)S(1)} custom-call(s32[66]{0:T(128)S(1)} %pad_add_fusion.place_ref, f32[512,256]{1,0:T(8,128)S(1)} %pad_maximum_fusion.table_ref, bf16[2,192,1536]{2,1,0:T(8,128)(2,1)S(1)} %collective-permute-done.7.refs_0_, bf16[512,512]{1,0:T(8,128)(2,1)S(1)} %collective-permute-done.4.refs_1_, ...), custom_call_target="tpu_custom_call" | custom-call | flops 1024 | bytes 1024 | tf_op jit(solution)/shard_map/attend_far/pallas_call | solution.py:280
  109.8 5.9 %collective-permute-done.12.refs_3_ = bf16[512,512]{1,0:T(8,128)(2,1)S(1)} collective-permute-done((bf16[512,512]{1,0:T(8,128)(2,1)S(1)}, bf16[512,512]{1,0:T(8,128)(2,1)S(1)}, u32[]{:S(2)}, u32[]{:S(2)}) %collective-permute-start.12) | collective-permute-done | bytes 524320 | tf_op jit(solution)/shard_map/ppermute | solution.py:350
  115.7 7.0 %attend_far.6 = (bf16[512,256]{1,0:T(8,128)(2,1)}, bf16[512,256]{1,0:T(8,128)(2,1)}, bf16[512,256]{1,0:T(8,128)(2,1)}) custom-call(s32[66]{0:T(128)S(1)} %pad_add_fusion.place_ref, f32[512,256]{1,0:T(8,128)S(1)} %pad_maximum_fusion.table_ref, bf16[2,192,1536]{2,1,0:T(8,128)(2,1)S(1)} %collective-permute-done.13.refs_0_, ...), custom_call_target="tpu_custom_call" | custom-call | flops 1024 | bytes 1024 | tf_op jit(solution)/shard_map/attend_far/pallas_call | solution.py:280
  124.0 3.0 %collective-permute-start.16 = (bf16[512,256]{1,0:T(8,128)(2,1)}, bf16[512,256]{1,0:T(8,128)(2,1)}, u32[]{:S(2)}, u32[]{:S(2)}) collective-permute-start(bf16[512,256]{1,0:T(8,128)(2,1)} %get-tuple-element.53), channel_id=1, source_target_pairs={{0,6},{2,4},{4,2},{6,0},{8,14},{10,12},{12,10},{14,8},{1,7},{3,5},... | collective-permute-start | bytes 786440 | tf_op jit(solution)/shard_map/ppermute | solution.py:350
  128.5 2.7 %attend_far.7.refs_3_ = bf16[512,256]{1,0:T(8,128)(2,1)S(1)} custom-call(s32[66]{0:T(128)S(1)} %pad_add_fusion.place_ref, f32[512,256]{1,0:T(8,128)S(1)} %pad_maximum_fusion.table_ref, bf16[2,192,1536]{2,1,0:T(8,128)(2,1)S(1)} %copy-done.2, bf16[512,512]{1,0:T(8,128)(2,1)S(1)} %collective-permute-done.8.refs_1_, bf16[512,2176]{1,0:T(8,128)(2,1)S(1)} %get-tuple-element.49.refs_2_), custom_call_target="tpu_custom_call" | custom-call | flops 1024 | bytes 1024 | tf_op jit(solution)/shard_map/attend_far/pallas_call | solution.py:280
  131.2 2.9 %place_pieces.2.refs_4_ = bf16[512,4096]{1,0:T(8,128)(2,1)} custom-call(s32[24]{0:T(128)S(1)} %stack.143.offsets_ref, bf16[512,512]{1,0:T(8,128)(2,1)S(1)} %copy-done.7, bf16[512,512]{1,0:T(8,128)(2,1)S(1)} %copy-done.9, bf16[512,512]{1,0:T(8,128)(2,1)S(1)} %copy-done.11, bf16[512,512]{1,0:T(8,128)(2,1)S(1)} %copy-done.13, bf16[512,256]{1,0:T(8,128)(2,1)S(1)} %copy-done.15, ...), custom_call_target="tpu_custom_call" | custom-call | flops 1024 | bytes 1024 | tf_op jit(solution)/shard_map/place_pieces/pallas_call | solution.py:315
  134.2 3.0 %collective-permute-done.16.refs_2_ = bf16[512,256]{1,0:T(8,128)(2,1)} collective-permute-done((bf16[512,256]{1,0:T(8,128)(2,1)}, bf16[512,256]{1,0:T(8,128)(2,1)}, u32[]{:S(2)}, u32[]{:S(2)}) %collective-permute-start.16) | collective-permute-done | bytes 262176 | tf_op jit(solution)/shard_map/ppermute | solution.py:350
  137.2 2.1 %place_pieces.3 = bf16[512,4096]{1,0:T(8,128)(2,1)} custom-call(s32[8]{0:T(128)S(1)} %stack.116.offsets_ref, bf16[512,256]{1,0:T(8,128)(2,1)} %collective-permute-done.14.refs_0_, bf16[512,256]{1,0:T(8,128)(2,1)} %collective-permute-done.15.refs_1_, bf16[512,256]{1,0:T(8,128)(2,1)} %collective-permute-done.16.refs_2_, ...), custom_call_target="tpu_custom_call", output_to_operand_aliasing={{}: (5, {})} | custom-call | flops 1024 | bytes 1024 | tf_op jit(solution)/shard_map/place_pieces/pallas_call | solution.py:315
  (73 shorter events, 16.2 us)
Async XLA Ops:
  2.8 6.9 %copy-start.16 = (bf16[1,512,4,256]{3,2,1,0:T(4,128)(2,1)S(1)}, bf16[1,512,4,256]{3,2,1,0:T(4,128)(2,1)}, u32[]{:S(2)}) copy-start(bf16[1,512,4,256]{3,2,1,0:T(4,128)(2,1)} %param.10) | copy-start | bytes 3145732
  5.2 10.0 %collective-permute-start.1 = (bf16[256,2176]{1,0:T(8,128)(2,1)}, bf16[256,2176]{1,0:T(8,128)(2,1)S(1)}, u32[]{:S(2)}, u32[]{:S(2)}) collective-permute-start(bf16[256,2176]{1,0:T(8,128)(2,1)} %prepare.1.same_ref), channel_id=1, source_target_pairs={{0,1},{1,0},{2,3},{3,2},{4,5},{5,4},{6,7},{7,6},{8,9},{9,8},{10,11... | collective-permute-start | bytes 3342344 | tf_op jit(solution)/shard_map/ppermute | solution.py:353
  5.6 50.5 %collective-permute-start = (bf16[256,2176]{1,0:T(8,128)(2,1)}, bf16[256,2176]{1,0:T(8,128)(2,1)}, u32[]{:S(2)}, u32[]{:S(2)}) collective-permute-start(bf16[256,2176]{1,0:T(8,128)(2,1)} %prepare.1.same_ref), channel_id=1, source_target_pairs={{0,4},{2,6},{4,0},{6,2},{8,12},{10,14},{12,8},{14,10},{1,5},{3,7},... | collective-permute-start | bytes 3342344 | tf_op jit(solution)/shard_map/ppermute | solution.py:350
  8.2 47.9 %collective-permute-start.3 = (bf16[256,2176]{1,0:T(8,128)(2,1)}, bf16[256,2176]{1,0:T(8,128)(2,1)}, u32[]{:S(2)}, u32[]{:S(2)}) collective-permute-start(bf16[256,2176]{1,0:T(8,128)(2,1)} %prepare.1.same_ref), channel_id=1, source_target_pairs={{0,2},{2,0},{4,6},{6,4},{8,10},{10,8},{12,14},{14,12},{1,3},{3,1},... | collective-permute-start | bytes 3342344 | tf_op jit(solution)/shard_map/ppermute | solution.py:350
  10.0 34.6 %collective-permute-start.4 = (bf16[512,512]{1,0:T(8,128)(2,1)S(1)}, bf16[512,512]{1,0:T(8,128)(2,1)S(1)}, u32[]{:S(2)}, u32[]{:S(2)}) collective-permute-start(bf16[512,512]{1,0:T(8,128)(2,1)S(1)} %pick.2), channel_id=1, source_target_pairs={{0,8},{2,10},{4,12},{6,14},{8,0},{10,2},{12,4},{14,6},{1,9},{3,11}... | collective-permute-start | bytes 1572872 | tf_op jit(solution)/shard_map/ppermute | solution.py:350
  12.7 73.8 %collective-permute-start.7 = (bf16[2,192,1536]{2,1,0:T(8,128)(2,1)S(1)}, bf16[2,192,1536]{2,1,0:T(8,128)(2,1)S(1)}, u32[]{:S(2)}, u32[]{:S(2)}) collective-permute-start(bf16[2,192,1536]{2,1,0:T(8,128)(2,1)S(1)} %pick.3), channel_id=1, source_target_pairs={{0,8},{2,10},{4,12},{6,14},{8,0},{10,2},{12,4},{14,6},{1,9},{3,11}... | collective-permute-start | bytes 3538952 | tf_op jit(solution)/shard_map/ppermute | solution.py:350
  56.2 4.7 %collective-permute-start.5 = (bf16[256,2176]{1,0:T(8,128)(2,1)}, bf16[256,2176]{1,0:T(8,128)(2,1)S(1)}, u32[]{:S(2)}, u32[]{:S(2)}) collective-permute-start(bf16[256,2176]{1,0:T(8,128)(2,1)} %collective-permute-done.3.same_ref), channel_id=1, source_target_pairs={{0,1},{1,0},{2,3},{3,2},{4,5},{5,4},{6,7},{7,6},{8,9},{9,8},{10,11... | collective-permute-start | bytes 3342344 | tf_op jit(solution)/shard_map/ppermute | solution.py:353
  56.2 10.0 %collective-permute-start.6 = (bf16[256,2176]{1,0:T(8,128)(2,1)}, bf16[256,2176]{1,0:T(8,128)(2,1)S(1)}, u32[]{:S(2)}, u32[]{:S(2)}) collective-permute-start(bf16[256,2176]{1,0:T(8,128)(2,1)} %collective-permute-done.same_ref), channel_id=1, source_target_pairs={{0,1},{1,0},{2,3},{3,2},{4,5},{5,4},{6,7},{7,6},{8,9},{9,8},{10,11... | collective-permute-start | bytes 3342344 | tf_op jit(solution)/shard_map/ppermute | solution.py:353
  56.7 29.9 %collective-permute-start.2 = (bf16[256,2176]{1,0:T(8,128)(2,1)}, bf16[256,2176]{1,0:T(8,128)(2,1)S(1)}, u32[]{:S(2)}, u32[]{:S(2)}) collective-permute-start(bf16[256,2176]{1,0:T(8,128)(2,1)} %collective-permute-done.same_ref), channel_id=1, source_target_pairs={{0,2},{2,0},{4,6},{6,4},{8,10},{10,8},{12,14},{14,12},{1,3},{3,1},... | collective-permute-start | bytes 3342344 | tf_op jit(solution)/shard_map/ppermute | solution.py:350
  59.4 27.2 %collective-permute-start.8 = (bf16[512,512]{1,0:T(8,128)(2,1)S(1)}, bf16[512,512]{1,0:T(8,128)(2,1)S(1)}, u32[]{:S(2)}, u32[]{:S(2)}) collective-permute-start(bf16[512,512]{1,0:T(8,128)(2,1)S(1)} %collective-permute-done.4.refs_1_), channel_id=1, source_target_pairs={{0,16},{16,0},{1,17},{17,1},{2,18},{18,2},{3,19},{19,3},{4,20},{20... | collective-permute-start | bytes 1572872 | tf_op jit(solution)/shard_map/ppermute | solution.py:356
  86.6 2.8 %collective-permute-start.9 = (bf16[256,2176]{1,0:T(8,128)(2,1)S(1)}, bf16[256,2176]{1,0:T(8,128)(2,1)S(1)}, u32[]{:S(2)}, u32[]{:S(2)}) collective-permute-start(bf16[256,2176]{1,0:T(8,128)(2,1)S(1)} %collective-permute-done.2.same_ref), channel_id=1, source_target_pairs={{0,1},{1,0},{2,3},{3,2},{4,5},{5,4},{6,7},{7,6},{8,9},{9,8},{10,11... | collective-permute-start | bytes 3342344 | tf_op jit(solution)/shard_map/ppermute | solution.py:353
  86.6 29.1 %collective-permute-start.13 = (bf16[2,192,1536]{2,1,0:T(8,128)(2,1)S(1)}, bf16[2,192,1536]{2,1,0:T(8,128)(2,1)S(1)}, u32[]{:S(2)}, u32[]{:S(2)}) collective-permute-start(bf16[2,192,1536]{2,1,0:T(8,128)(2,1)S(1)} %collective-permute-done.7.refs_0_), channel_id=1, source_target_pairs={{0,16},{16,0},{1,17},{17,1},{2,18},{18,2},{3,19},{19,3},{4,20},{20... | collective-permute-start | bytes 3538952 | tf_op jit(solution)/shard_map/ppermute | solution.py:356
  88.2 15.6 %collective-permute-start.10 = (bf16[512,512]{1,0:T(8,128)(2,1)S(1)}, bf16[512,512]{1,0:T(8,128)(2,1)S(1)}, u32[]{:S(2)}, u32[]{:S(2)}) collective-permute-start(bf16[512,512]{1,0:T(8,128)(2,1)S(1)} %get-tuple-element.35), channel_id=1, source_target_pairs={{0,2},{2,0},{4,6},{6,4},{8,10},{10,8},{12,14},{14,12},{1,3},{3,1},... | collective-permute-start | bytes 1572872 | tf_op jit(solution)/shard_map/ppermute | solution.py:350
  88.7 15.1 %collective-permute-start.11 = (bf16[512,512]{1,0:T(8,128)(2,1)S(1)}, bf16[512,512]{1,0:T(8,128)(2,1)S(1)}, u32[]{:S(2)}, u32[]{:S(2)}) collective-permute-start(bf16[512,512]{1,0:T(8,128)(2,1)S(1)} %get-tuple-element.38), channel_id=1, source_target_pairs={{0,4},{2,6},{4,0},{6,2},{8,12},{10,14},{12,8},{14,10},{1,5},{3,7},... | collective-permute-start | bytes 1572872 | tf_op jit(solution)/shard_map/ppermute | solution.py:350
  93.9 21.8 %collective-permute-start.12 = (bf16[512,512]{1,0:T(8,128)(2,1)S(1)}, bf16[512,512]{1,0:T(8,128)(2,1)S(1)}, u32[]{:S(2)}, u32[]{:S(2)}) collective-permute-start(bf16[512,512]{1,0:T(8,128)(2,1)S(1)} %get-tuple-element.42), channel_id=1, source_target_pairs={{0,6},{2,4},{4,2},{6,0},{8,14},{10,12},{12,10},{14,8},{1,7},{3,5},... | collective-permute-start | bytes 1572872 | tf_op jit(solution)/shard_map/ppermute | solution.py:350
  103.3 20.0 %collective-permute-start.17 = (bf16[512,256]{1,0:T(8,128)(2,1)S(1)}, bf16[512,256]{1,0:T(8,128)(2,1)S(1)}, u32[]{:S(2)}, u32[]{:S(2)}) collective-permute-start(bf16[512,256]{1,0:T(8,128)(2,1)S(1)} %get-tuple-element.47), channel_id=1, source_target_pairs={{0,2},{2,0},{4,6},{6,4},{8,10},{10,8},{12,14},{14,12},{1,3},{3,1},... | collective-permute-start | bytes 786440 | tf_op jit(solution)/shard_map/ppermute | solution.py:350
  103.8 6.0 %copy-start.10 = (bf16[512,512]{1,0:T(8,128)(2,1)}, bf16[512,512]{1,0:T(8,128)(2,1)S(1)}, u32[]{:S(2)}) copy-start(bf16[512,512]{1,0:T(8,128)(2,1)S(1)} %collective-permute-done.11.refs_2_) | copy-start | bytes 1572868
  103.8 23.3 %collective-permute-start.18 = (bf16[512,256]{1,0:T(8,128)(2,1)}, bf16[512,256]{1,0:T(8,128)(2,1)}, u32[]{:S(2)}, u32[]{:S(2)}) collective-permute-start(bf16[512,256]{1,0:T(8,128)(2,1)} %get-tuple-element.54), channel_id=1, source_target_pairs={{0,4},{2,6},{4,0},{6,2},{8,12},{10,14},{12,8},{14,10},{1,5},{3,7},... | collective-permute-start | bytes 786440 | tf_op jit(solution)/shard_map/ppermute | solution.py:350
  104.5 22.6 %collective-permute-start.19 = (bf16[512,256]{1,0:T(8,128)(2,1)}, bf16[512,256]{1,0:T(8,128)(2,1)}, u32[]{:S(2)}, u32[]{:S(2)}) collective-permute-start(bf16[512,256]{1,0:T(8,128)(2,1)} %get-tuple-element.55), channel_id=1, source_target_pairs={{0,6},{2,4},{4,2},{6,0},{8,14},{10,12},{12,10},{14,8},{1,7},{3,5},... | collective-permute-start | bytes 786440 | tf_op jit(solution)/shard_map/ppermute | solution.py:350
  115.7 7.0 %copy-start.12 = (bf16[512,512]{1,0:T(8,128)(2,1)}, bf16[512,512]{1,0:T(8,128)(2,1)S(1)}, u32[]{:S(2)}) copy-start(bf16[512,512]{1,0:T(8,128)(2,1)S(1)} %collective-permute-done.12.refs_3_) | copy-start | bytes 1572868
  115.7 7.0 %copy-start.1 = (bf16[2,192,1536]{2,1,0:T(8,128)(2,1)}, bf16[2,192,1536]{2,1,0:T(8,128)(2,1)S(1)}, u32[]{:S(2)}) copy-start(bf16[2,192,1536]{2,1,0:T(8,128)(2,1)S(1)} %collective-permute-done.13.refs_0_) | copy-start | bytes 3538948
  122.8 11.4 %collective-permute-start.14 = (bf16[512,256]{1,0:T(8,128)(2,1)}, bf16[512,256]{1,0:T(8,128)(2,1)}, u32[]{:S(2)}, u32[]{:S(2)}) collective-permute-start(bf16[512,256]{1,0:T(8,128)(2,1)} %get-tuple-element.51), channel_id=1, source_target_pairs={{0,2},{2,0},{4,6},{6,4},{8,10},{10,8},{12,14},{14,12},{1,3},{3,1},... | collective-permute-start | bytes 786440 | tf_op jit(solution)/shard_map/ppermute | solution.py:350
  123.3 10.9 %collective-permute-start.15 = (bf16[512,256]{1,0:T(8,128)(2,1)}, bf16[512,256]{1,0:T(8,128)(2,1)}, u32[]{:S(2)}, u32[]{:S(2)}) collective-permute-start(bf16[512,256]{1,0:T(8,128)(2,1)} %get-tuple-element.52), channel_id=1, source_target_pairs={{0,4},{2,6},{4,0},{6,2},{8,12},{10,14},{12,8},{14,10},{1,5},{3,7},... | collective-permute-start | bytes 786440 | tf_op jit(solution)/shard_map/ppermute | solution.py:350
  124.0 13.2 %collective-permute-start.16 = (bf16[512,256]{1,0:T(8,128)(2,1)}, bf16[512,256]{1,0:T(8,128)(2,1)}, u32[]{:S(2)}, u32[]{:S(2)}) collective-permute-start(bf16[512,256]{1,0:T(8,128)(2,1)} %get-tuple-element.53), channel_id=1, source_target_pairs={{0,6},{2,4},{4,2},{6,0},{8,14},{10,12},{12,10},{14,8},{1,7},{3,5},... | collective-permute-start | bytes 786440 | tf_op jit(solution)/shard_map/ppermute | solution.py:350
  (13 other events, 29.0 us)

commit v5 on v4

--- a/solution.py
+++ b/solution.py
@@ -10,8 +10,10 @@
 
 epsilon = 1e-06
 VMEM_LIMIT = 32 * 1024 * 1024
+VMEM_MOST = 60 * 1024 * 1024
 LIGHT = pl.CostEstimate(flops=1024, bytes_accessed=1024, transcendentals=0)
 FAR = -(2.0**100)
+SCRATCH = 5
 NT = (((1,), (1,)), ((), ()))
 NN = (((1,), (0,)), ((), ()))
 
@@ -21,24 +23,38 @@
     return jnp.exp(steps * (-math.log(10000.0) / half_width))
 
 
-def prepare_kernel(q_width, kv_width, slot_count, place_ref, latents_ref, gain_ref, out_ref):
+def prepare_kernel(q_width, kv_width, place_ref, *refs):
+    sources, out_ref, held, sems = refs[:4], refs[4], refs[5:9], refs[9]
+    latents_ref, q_gain_ref, kv_gain_ref, lengths_ref = held
+    copies = [pltpu.make_async_copy(*pair, sems.at[index]) for index, pair in enumerate(zip(sources, held))]
+    for copy in copies:
+        copy.start()
+    for copy in copies:
+        copy.wait()
+    slot_count = lengths_ref.shape[1]
     rows = latents_ref.shape[1]
     rope_width = latents_ref.shape[0] - q_width - kv_width
     half_width = rope_width // 2
 
-    def normalized(low, width):
+    def normalize(low, width, gain_ref):
         part = latents_ref[low : low + width, :].astype(jnp.float32)
         scale = lax.rsqrt(jnp.mean(part * part, axis=0, keepdims=True) + epsilon)
-        return (jnp.transpose(part * scale) * gain_ref[:, low : low + width]).astype(jnp.bfloat16)
-
-    out_ref[:, :q_width] = normalized(0, q_width)
-    out_ref[:, q_width : q_width + kv_width] = normalized(q_width, kv_width)
+        normed = jnp.transpose(part * scale)
+        lanes = gain_ref.shape[1]
+        for index in range(gain_ref.shape[0]):
+            span = slice(index * lanes, (index + 1) * lanes)
+            out_ref[:, low + span.start : low + span.stop] = (normed[:, span] * gain_ref[index : index + 1, :]).astype(
+                jnp.bfloat16
+            )
+
+    normalize(0, q_width, q_gain_ref)
+    normalize(q_width, kv_width, kv_gain_ref)
     spare = out_ref.shape[1] - q_width - kv_width - rope_width
     token_ids = lax.broadcasted_iota(jnp.int32, (1, rows), 1) + place_ref[1] * rows
     slot_ids = lax.broadcasted_iota(jnp.int32, (spare, rows), 0)
     begin, start, inside = jnp.zeros_like(token_ids), jnp.int32(0), jnp.zeros((spare, rows), jnp.float32)
     for slot in range(slot_count):
-        stop = start + place_ref[2 + place_ref[0] * slot_count + slot]
+        stop = start + lengths_ref[place_ref[0], slot]
         begin = jnp.where(token_ids >= start, start, begin)
         member = jnp.where((token_ids >= start) & (token_ids < stop), 1.0, 0.0)
         inside = jnp.where(slot_ids == slot, member, inside)
@@ -52,20 +68,23 @@
     out_ref[:, q_width + kv_width :] = jnp.transpose(turned).astype(jnp.bfloat16)
 
 
-def prepare(latents, gains, q_width, kv_width, slot_count, place):
+def prepare(latents, q_gain, kv_gain, lengths, place):
     rows = latents.shape[0]
+    q_width, kv_width = q_gain.shape[0], kv_gain.shape[0]
     rope_width = latents.shape[1] - q_width - kv_width
-    width = q_width + kv_width + -(-(rope_width + slot_count) // 128) * 128
-    vmem = pl.BlockSpec(memory_space=pltpu.VMEM)
+    width = q_width + kv_width + -(-(rope_width + lengths.shape[1]) // 128) * 128
+    sources = [jnp.transpose(latents), jnp.reshape(q_gain, (-1, 128)), jnp.reshape(kv_gain, (-1, 128)), lengths]
+    held = [pltpu.VMEM(source.shape, source.dtype) for source in sources[:3]] + [pltpu.SMEM(lengths.shape, lengths.dtype)]
     return pl.pallas_call(
-        partial(prepare_kernel, q_width, kv_width, slot_count),
+        partial(prepare_kernel, q_width, kv_width),
         out_shape=jax.ShapeDtypeStruct((rows, width), jnp.bfloat16),
-        in_specs=[pl.BlockSpec(memory_space=pltpu.SMEM), vmem, vmem],
-        out_specs=vmem,
-        compiler_params=pltpu.CompilerParams(vmem_limit_bytes=VMEM_LIMIT),
+        in_specs=[pl.BlockSpec(memory_space=pltpu.SMEM)] + [pl.BlockSpec(memory_space=pl.ANY)] * len(sources),
+        out_specs=pl.BlockSpec(memory_space=pltpu.VMEM),
+        scratch_shapes=held + [pltpu.SemaphoreType.DMA((len(sources),))],
+        compiler_params=pltpu.CompilerParams(vmem_limit_bytes=VMEM_MOST),
         cost_estimate=LIGHT,
         name="prepare",
-    )(place, jnp.transpose(latents), gains[None, :])
+    )(place, *sources)
 
 
 def pick_kernel(index_ref, source_ref, out_ref):
@@ -117,7 +136,7 @@
             numbers.append(numbers[-1])
 
         def query(low, high, picked):
-            parts = [query_weight_ref[number, low:high, :] for number in picked]
+            parts = [query_weight_ref[number if query_weight_ref.shape[0] > 1 else 0, low:high, :] for number in picked]
             return dot(tokens_ref[:, :q_width], jnp.concatenate(parts, axis=0), NT)
 
         rope = query(nope_width, query_width, numbers)
@@ -217,11 +236,17 @@
         turn_ref[index * block : (index + 1) * block, :] = table_ref[pl.ds(position, block), :]
 
 
-def near_kernel(sizes, slot_count, distance, place_ref, table_ref, query_weight_ref, pair_weight_ref, same_ref, other_ref, out_ref, tokens_ref, *scratch):
+def near_kernel(sizes, slot_count, distance, own, place_ref, table_ref, query_weight_ref, pair_weight_ref, *refs):
+    count = len(refs) - 2 - SCRATCH
+    piece_refs, out_ref, tokens_ref, scratch = refs[:count], refs[count], refs[count + 1], refs[count + 2 :]
     core, group = place_ref[1], place_ref[0] ^ distance
-    rows = same_ref.shape[0]
-    tokens_ref[pl.ds(pl.multiple_of(core * rows, rows), rows), :] = same_ref[...]
-    tokens_ref[pl.ds(pl.multiple_of((1 - core) * rows, rows), rows), :] = other_ref[...]
+    half = tokens_ref.shape[0] // 2
+    for owner, some in ((core, piece_refs[:own]), (1 - core, piece_refs[own:])):
+        done = 0
+        for piece_ref in some:
+            rows = piece_ref.shape[0]
+            tokens_ref[pl.ds(pl.multiple_of(owner * half + done, rows), rows), :] = piece_ref[...]
+            done += rows
     set_up(scratch)
     set_turn(group, slot_count, place_ref, table_ref, scratch[3])
     heads = list(range(sizes[0]))
@@ -254,22 +279,23 @@
 
 
 def attend_near(sizes, slot_count, distance, place, table, query_weight, pair_weight, same, other):
-    rows, width = same.shape
+    pieces = [*same, *other]
+    tokens, width = sum(piece.shape[0] for piece in pieces), pieces[0].shape[1]
     heads, value_width = sizes[0], sizes[-1]
     vmem = pl.BlockSpec(memory_space=pltpu.VMEM)
     return pl.pallas_call(
-        partial(near_kernel, sizes, slot_count, distance),
+        partial(near_kernel, sizes, slot_count, distance, len(same)),
         out_shape=[
-            jax.ShapeDtypeStruct((2 * rows, heads * value_width), jnp.bfloat16),
-            jax.ShapeDtypeStruct((2 * rows, width), jnp.bfloat16),
+            jax.ShapeDtypeStruct((tokens, heads * value_width), jnp.bfloat16),
+            jax.ShapeDtypeStruct((tokens, width), jnp.bfloat16),
         ],
-        in_specs=[pl.BlockSpec(memory_space=pltpu.SMEM)] + [vmem] * 5,
+        in_specs=[pl.BlockSpec(memory_space=pltpu.SMEM)] + [vmem] * (3 + len(pieces)),
         out_specs=[vmem, vmem],
-        scratch_shapes=scratch_for(sizes, 2 * rows),
+        scratch_shapes=scratch_for(sizes, tokens),
         compiler_params=pltpu.CompilerParams(vmem_limit_bytes=VMEM_LIMIT),
         cost_estimate=LIGHT,
         name="attend_near",
-    )(place, table, query_weight, pair_weight, same, other)
+    )(place, table, query_weight, pair_weight, *pieces)
 
 
 def attend_far(sizes, slot_count, distances, place, table, query_weight, pair_weight, chosen, groups):
@@ -356,7 +382,6 @@
         return lax.ppermute(value, "parts", [(p, p ^ 1) for p in range(parts)])
 
     slot_count = lengths.shape[1]
-    gains = jnp.concatenate([q_gain, kv_gain])
     spot = jnp.concatenate([jnp.stack([place, core]).astype(jnp.int32), jnp.reshape(lengths, -1)])
     own_query = jnp.transpose(q_weight[0], (1, 2, 0))
     own_pair = jnp.reshape(kv_weight[0], (kv_width, local_heads * pair_width))
@@ -371,8 +396,8 @@
 
     sent_pair = pick(own_pair, side, per_part * pair_width, 1)
     sent_query = pick(own_query, side, per_part, 0)
-    latent = prepare(latents, gains, q_width, kv_width, slot_count, spot)
-    same, other = [latent], [sibling(latent)]
+    latent = prepare(latents, q_gain, kv_gain, lengths, jnp.stack([place, core]).astype(jnp.int32))
+    same, other = [latent], [[sibling(latent)]]
     for distance in range(1, half_places):
         same.append(across(latent, distance) if distance & (distance - 1) == 0 else None)
     far_pair = across(sent_pair, half_places)
@@ -385,11 +410,11 @@
             (local_heads, *sizes),
             slot_count,
             distance,
-            spot,
+            after(spot, *earlier),
             table,
             own_query,
             own_pair,
-            after(same[distance], *earlier),
+            [same[distance]],
             other[distance],
         )
         joined.append(tokens_joined)
@@ -404,11 +429,14 @@
             same[distance] = across(after(same[distance ^ low_bit], mixed), low_bit)
             other.append(None)
         else:
-            other.append(sibling(after(same[distance], mixed, far_pair, *direct)))
+            half_rows = same[distance].shape[0] // 2
+            piece = after(same[distance], mixed, far_pair, *direct)
+            parted = [piece[:half_rows], piece[half_rows:]] if distance == half_places // 2 else [piece]
+            other.append([sibling(piece) for piece in parted])
     crossed_pair = [other_part(after(far_pair, mixed))] if share == 2 else []
     for distance in range(1, half_places):
         if other[distance] is None:
-            other[distance] = sibling(after(same[distance], mixed, far_query, *crossed_pair))
+            other[distance] = [sibling(after(same[distance], mixed, far_query, *crossed_pair, *arrived[half_places // 2 :]))]
         mixed = near(distance, mixed)
         arrived.append(across(mixed, distance))
     placed = []
@@ -424,32 +452,39 @@
         placed.clear()
         return held
 
-    heads = list(range(per_part))
-    rounds = [(far_query, far_pair, side * per_part)]
+    rounds = [(far_query, far_pair, list(range(per_part)), side * per_part)]
     if share == 2:
-        rounds.append((other_part(far_query), crossed_pair[0], (1 - side) * per_part))
-    gates, first_sent, late = [], [], []
-    later = [arrived[1:-1], arrived[-1:], first_sent, []]
-    for number, (queries, pairs, first) in enumerate(rounds):
+        crossed = other_part(far_query[:1])
+        for index in range(per_part):
+            rounds.append((crossed, crossed_pair[0], [index], (1 - side) * per_part))
+    later = [[], arrived[1:-1], arrived[-1:]]
+    late = []
+    for number, (queries, pairs, heads, first) in enumerate(rounds):
+        sent = []
         for distances in (list(range(1, half_places)), [0]):
             mixed_some = attend_far(
-                (per_part, *sizes),
+                (len(heads), *sizes),
                 slot_count,
                 distances,
-                after(spot, mixed, *gates),
+                after(spot, mixed, *later.pop(0)),
                 table,
                 queries,
                 pairs,
                 heads,
                 [joined[distance] for distance in distances],
             )
-            mixed, gates = mixed_some[0], later.pop(0)
+            mixed = mixed_some[0]
             for distance, piece in zip(distances, mixed_some):
                 base = (place ^ distance ^ half_places) * block_width
-                received = across(piece, distance) if distance else piece
-                if number == 0 and distance:
-                    first_sent.append(received)
-                (late if number else placed).append((received, [base + (first + head) * value_width for head in heads]))
+                if distance:
+                    piece = across(piece, distance)
+                    sent.append(piece)
+                spans = [base + (first + head) * value_width for head in heads]
+                (late if number + 1 == len(rounds) else placed).append((piece, spans))
+            if distances[0] and number + 1 < len(rounds) - 1:
+                ahead = other_part(after(far_query[number + 1 : number + 2], rounds[number + 1][0], mixed))
+                rounds[number + 2] = (ahead, *rounds[number + 2][1:])
+        later += [sent, []]
     held = flush(None)
     placed.extend(late)
     held = flush(held)

time: 140 us -> 163 us (1.16)
  waiting for transfers between devices: 57.3 us -> 71.4 us
  Pallas kernels: 47.7 us -> 57.9 us
  starting transfers between devices: 24.8 us -> 21.9 us
  local copies, waits for them, and re-layouts: 7.45 us -> 9.16 us
    ppermute x14 -> x17, waiting for transfers between devices: 56.6 us -> 69 us  [across(): lax.ppermute(value, 'seq', [(s, s ^ distance) for s in range(places)])]
    pallas_call x4 -> x6, Pallas kernels: 19.7 us -> 26.7 us  [attend_far(): pl.pallas_call(partial(far_kernel, sizes, slot_count, distances, chosen),...]
    ppermute x14 -> x17, starting transfers between devices: 20.8 us -> 17.4 us  [across(): lax.ppermute(value, 'seq', [(s, s ^ distance) for s in range(places)])]
    slice x0 -> x2, local copies, waits for them, and re-layouts: none -> 2.81 us  [the longest x1 1.51 us: shards(): far_query[number + 1:number + 2]]
    pallas_call x2, Pallas kernels: 0.12 us -> 2.04 us  [pick(): pl.pallas_call(pick_kernel, grid_spec=pltpu.PrefetchScalarGridSpec(num_sc...]
    ppermute x2 -> x3, waiting for transfers between devices: 0.01 us -> 1.73 us  [other_part(): return lax.ppermute(value, 'parts', [(p, p ^ 1) for p in range(parts)])]
    unnamed x35 -> x55, local copies, waits for them, and re-layouts: 6.5 us -> 6.17 us
    ppermute x2 -> x3, starting transfers between devices: 3.05 us -> 3.38 us  [other_part(): return lax.ppermute(value, 'parts', [(p, p ^ 1) for p in range(parts)])]
  transfers between devices with their start and end apart: 20 -> 25, of which waited for: 6 -> 7; matrix products, arithmetic and copies ran while one was open for 1% -> 4% of each run, Pallas kernels for 31% -> 32%
where the time goes in v5:
time: 163 us
  waiting for transfers between devices  71.4 us (44%)
  Pallas kernels  57.9 us (36%)
  starting transfers between devices  21.9 us (13%)
  local copies, waits for them, and re-layouts  9.16 us (6%)
  other arithmetic  1.79 us (1%)
    ppermute x17, waiting for transfers between devices, across(): lax.ppermute(value, 'seq', [(s, s ^ distance) for s in range(places)])  69 us
    pallas_call x6, Pallas kernels, attend_far(): pl.pallas_call(partial(far_kernel, sizes, slot_count, distances, chosen),...  26.7 us
    pallas_call x4, Pallas kernels, attend_near(): pl.pallas_call(partial(near_kernel, sizes, slot_count, distance, len(same...  20.5 us
    ppermute x17, starting transfers between devices, across(): lax.ppermute(value, 'seq', [(s, s ^ distance) for s in range(places)])  17.4 us
    unnamed x55, local copies, waits for them, and re-layouts  6.17 us
    pallas_call x2, Pallas kernels, place_pieces(): pl.pallas_call(partial(place_kernel, width, count), out_shape=jax.ShapeDt...  4.91 us
    pallas_call x1, Pallas kernels, prepare(): pl.pallas_call(partial(prepare_kernel, q_width, kv_width), out_shape=jax....  3.81 us
    ppermute x3, starting transfers between devices, other_part(): return lax.ppermute(value, 'parts', [(p, p ^ 1) for p in range(parts)])  3.38 us
  transfers between devices with their start and end apart: 25, of which 7 were waited for; matrix products, arithmetic and copies ran while one was open for 4% of the time, Pallas kernels for 32%

profile of v5, /device:TPU:0, one launch (start us, length us, event | category | flops | bytes accessed | tf_op | source)
XLA Modules:
  0.0 162.8 jit_solution(9031512072809133170)
XLA Ops:
  0.6 3.8 %prepare.1.refs_0_ = bf16[256,2176]{1,0:T(8,128)(2,1)} custom-call(s32[2]{0:T(128)} %pad_add_fusion.2.place_ref, bf16[2112,256]{1,0:T(8,128)(2,1)} %bitcast.54, f32[12,128]{1,0:T(8,128)} %bitcast.56, f32[4,128]{1,0:T(4,128)} %bitcast.57, s32[8,8]{1,0:T(8,128)} %refs_3_.1), custom_call_target="tpu_custom_call" | custom-call | flops 1024 | bytes 1024 | tf_op jit(solution)/shard_map/prepare/pallas_call | solution.py:78
  4.9 2.6 %collective-permute-start.1 = (bf16[256,2176]{1,0:T(8,128)(2,1)}, bf16[256,2176]{1,0:T(8,128)(2,1)}, u32[]{:S(2)}, u32[]{:S(2)}) collective-permute-start(bf16[256,2176]{1,0:T(8,128)(2,1)} %prepare.1.refs_0_), channel_id=1, source_target_pairs={{0,2},{2,0},{4,6},{6,4},{8,10},{10,8},{12,14},{14,12},{1,3},{3,1},... | collective-permute-start | bytes 3342344 | tf_op jit(solution)/shard_map/ppermute | solution.py:376
  9.1 1.6 copy.8
  11.6 2.6 %collective-permute-start.2 = (bf16[512,512]{1,0:T(8,128)(2,1)}, bf16[512,512]{1,0:T(8,128)(2,1)}, u32[]{:S(2)}, u32[]{:S(2)}) collective-permute-start(bf16[512,512]{1,0:T(8,128)(2,1)} %pick.2), channel_id=1, source_target_pairs={{0,8},{2,10},{4,12},{6,14},{8,0},{10,2},{12,4},{14,6},{1,9},{3,11}... | collective-permute-start | bytes 1572872 | tf_op jit(solution)/shard_map/ppermute | solution.py:376
  18.2 5.2 %attend_near.4 = (bf16[512,512]{1,0:T(8,128)(2,1)S(1)}, bf16[512,2176]{1,0:T(8,128)(2,1)S(1)}) custom-call(s32[66]{0:T(128)S(1)} %pad_add_fusion.1.place_ref, f32[512,256]{1,0:T(8,128)S(1)} %pad_maximum_fusion.table_ref, bf16[4,192,1536]{2,1,0:T(8,128)(2,1)S(1)} %bitcast.45, bf16[512,1024]{1,0:T(8,128)(2,1)S(1)} %bitcast.50, ...), custom_call_target="tpu_custom_call" | custom-call | flops 1024 | bytes 1024 | tf_op jit(solution)/shard_map/attend_near/pallas_call | solution.py:286
  24.3 21.3 %collective-permute-done.2.refs_1_ = bf16[512,512]{1,0:T(8,128)(2,1)} collective-permute-done((bf16[512,512]{1,0:T(8,128)(2,1)}, bf16[512,512]{1,0:T(8,128)(2,1)}, u32[]{:S(2)}, u32[]{:S(2)}) %collective-permute-start.2) | collective-permute-done | bytes 524320 | tf_op jit(solution)/shard_map/ppermute | solution.py:376
  45.6 10.1 %collective-permute-done.3.refs_0_ = bf16[256,2176]{1,0:T(8,128)(2,1)} collective-permute-done((bf16[256,2176]{1,0:T(8,128)(2,1)}, bf16[256,2176]{1,0:T(8,128)(2,1)}, u32[]{:S(2)}, u32[]{:S(2)}) %collective-permute-start.3) | collective-permute-done | bytes 1114144 | tf_op jit(solution)/shard_map/ppermute | solution.py:376
  60.1 5.2 %attend_near.5 = (bf16[512,512]{1,0:T(8,128)(2,1)S(1)}, bf16[512,2176]{1,0:T(8,128)(2,1)S(1)}) custom-call(s32[66]{0:T(128)S(1)} %pad_add_fusion.1.place_ref, f32[512,256]{1,0:T(8,128)S(1)} %pad_maximum_fusion.table_ref, bf16[4,192,1536]{2,1,0:T(8,128)(2,1)S(1)} %bitcast.46, bf16[512,1024]{1,0:T(8,128)(2,1)S(1)} %bitcast.51, ...), custom_call_target="tpu_custom_call" | custom-call | flops 1024 | bytes 1024 | tf_op jit(solution)/shard_map/attend_near/pallas_call | solution.py:286
  65.4 5.5 %attend_near.6 = (bf16[512,512]{1,0:T(8,128)(2,1)S(1)}, bf16[512,2176]{1,0:T(8,128)(2,1)S(1)}) custom-call(s32[66]{0:T(128)S(1)} %pad_add_fusion.1.place_ref, f32[512,256]{1,0:T(8,128)S(1)} %pad_maximum_fusion.table_ref, bf16[4,192,1536]{2,1,0:T(8,128)(2,1)S(1)} %bitcast.47, bf16[512,1024]{1,0:T(8,128)(2,1)S(1)} %bitcast.52, ...), custom_call_target="tpu_custom_call" | custom-call | flops 1024 | bytes 1024 | tf_op jit(solution)/shard_map/attend_near/pallas_call | solution.py:286
  70.9 17.6 %collective-permute-done.8.refs_0_ = bf16[2,192,1536]{2,1,0:T(8,128)(2,1)} collective-permute-done((bf16[2,192,1536]{2,1,0:T(8,128)(2,1)}, bf16[2,192,1536]{2,1,0:T(8,128)(2,1)}, u32[]{:S(2)}, u32[]{:S(2)}) %collective-permute-start.8) | collective-permute-done | bytes 1179680 | tf_op jit(solution)/shard_map/ppermute | solution.py:376
  88.5 11.0 %collective-permute-done.10.refs_2_ = bf16[512,512]{1,0:T(8,128)(2,1)S(1)} collective-permute-done((bf16[512,512]{1,0:T(8,128)(2,1)S(1)}, bf16[512,512]{1,0:T(8,128)(2,1)S(1)}, u32[]{:S(2)}, u32[]{:S(2)}) %collective-permute-start.10) | collective-permute-done | bytes 524320 | tf_op jit(solution)/shard_map/ppermute | solution.py:376
  103.1 4.5 %attend_near.7 = (bf16[512,512]{1,0:T(8,128)(2,1)S(1)}, bf16[512,2176]{1,0:T(8,128)(2,1)S(1)}) custom-call(s32[66]{0:T(128)S(1)} %pad_add_fusion.1.place_ref, f32[512,256]{1,0:T(8,128)S(1)} %pad_maximum_fusion.table_ref, bf16[4,192,1536]{2,1,0:T(8,128)(2,1)S(1)} %bitcast.48, bf16[512,1024]{1,0:T(8,128)(2,1)S(1)} %bitcast.53, ...), custom_call_target="tpu_custom_call" | custom-call | flops 1024 | bytes 1024 | tf_op jit(solution)/shard_map/attend_near/pallas_call | solution.py:286
  107.7 7.2 %attend_far.6 = (bf16[512,256]{1,0:T(8,128)(2,1)S(1)}, bf16[512,256]{1,0:T(8,128)(2,1)S(1)}, bf16[512,256]{1,0:T(8,128)(2,1)S(1)}) custom-call(s32[66]{0:T(128)S(1)} %pad_add_fusion.1.place_ref, f32[512,256]{1,0:T(8,128)S(1)} %pad_maximum_fusion.table_ref, bf16[2,192,1536]{2,1,0:T(8,128)(2,1)} %collective-permute-done.8.refs_0_, ...), custom_call_target="tpu_custom_call" | custom-call | flops 1024 | bytes 1024 | tf_op jit(solution)/shard_map/attend_far/pallas_call | solution.py:306
  115.0 1.7 %collective-permute-done.14.refs_0_ = bf16[1,192,1536]{2,1,0:T(8,128)(2,1)S(1)} collective-permute-done((bf16[1,192,1536]{2,1,0:T(8,128)(2,1)S(1)}, bf16[1,192,1536]{2,1,0:T(8,128)(2,1)S(1)}, u32[]{:S(2)}, u32[]{:S(2)}) %collective-permute-start.14) | collective-permute-done | bytes 589856 | tf_op jit(solution)/shard_map/ppermute | solution.py:382
  119.1 9.0 %collective-permute-done.12.refs_1_ = bf16[512,512]{1,0:T(8,128)(2,1)S(1)} collective-permute-done((bf16[512,512]{1,0:T(8,128)(2,1)S(1)}, bf16[512,512]{1,0:T(8,128)(2,1)S(1)}, u32[]{:S(2)}, u32[]{:S(2)}) %collective-permute-start.12) | collective-permute-done | bytes 524320 | tf_op jit(solution)/shard_map/ppermute | solution.py:376
  128.1 4.0 %attend_far.7.refs_7_ = bf16[512,256]{1,0:T(8,128)(2,1)S(1)} custom-call(s32[66]{0:T(128)S(1)} %pad_add_fusion.1.place_ref, f32[512,256]{1,0:T(8,128)S(1)} %pad_maximum_fusion.table_ref, bf16[2,192,1536]{2,1,0:T(8,128)(2,1)} %collective-permute-done.8.refs_0_, bf16[512,512]{1,0:T(8,128)(2,1)} %collective-permute-done.2.refs_1_, ...), custom_call_target="tpu_custom_call" | custom-call | flops 1024 | bytes 1024 | tf_op jit(solution)/shard_map/attend_far/pallas_call | solution.py:306
  132.1 5.5 %attend_far.8 = (bf16[512,128]{1,0:T(8,128)(2,1)S(1)}, bf16[512,128]{1,0:T(8,128)(2,1)}, bf16[512,128]{1,0:T(8,128)(2,1)}) custom-call(s32[66]{0:T(128)S(1)} %pad_add_fusion.1.place_ref, f32[512,256]{1,0:T(8,128)S(1)} %pad_maximum_fusion.table_ref, bf16[1,192,1536]{2,1,0:T(8,128)(2,1)S(1)} %collective-permute-done.14.refs_0_, ...), custom_call_target="tpu_custom_call" | custom-call | flops 1024 | bytes 1024 | tf_op jit(solution)/shard_map/attend_far/pallas_call | solution.py:306
  138.7 2.2 %attend_far.9.refs_11_ = bf16[512,128]{1,0:T(8,128)(2,1)S(1)} custom-call(s32[66]{0:T(128)S(1)} %pad_add_fusion.1.place_ref, f32[512,256]{1,0:T(8,128)S(1)} %pad_maximum_fusion.table_ref, bf16[1,192,1536]{2,1,0:T(8,128)(2,1)S(1)} %collective-permute-done.14.refs_0_, bf16[512,512]{1,0:T(8,128)(2,1)S(1)} %collective-permute-done.9.refs_1_, ...), custom_call_target="tpu_custom_call" | custom-call | flops 1024 | bytes 1024 | tf_op jit(solution)/shard_map/attend_far/pallas_call | solution.py:306
  141.6 2.2 %collective-permute-start.23 = (bf16[512,128]{1,0:T(8,128)(2,1)}, bf16[512,128]{1,0:T(8,128)(2,1)}, u32[]{:S(2)}, u32[]{:S(2)}) collective-permute-start(bf16[512,128]{1,0:T(8,128)(2,1)} %get-tuple-element.66), channel_id=1, source_target_pairs={{0,4},{2,6},{4,0},{6,2},{8,12},{10,14},{12,8},{14,10},{1,5},{3,7},... | collective-permute-start | bytes 393224 | tf_op jit(solution)/shard_map/ppermute | solution.py:376
  144.4 5.5 %attend_far.10 = (bf16[512,128]{1,0:T(8,128)(2,1)}, bf16[512,128]{1,0:T(8,128)(2,1)}, bf16[512,128]{1,0:T(8,128)(2,1)}) custom-call(s32[66]{0:T(128)S(1)} %pad_add_fusion.1.place_ref, f32[512,256]{1,0:T(8,128)S(1)} %pad_maximum_fusion.table_ref, bf16[1,192,1536]{2,1,0:T(8,128)(2,1)S(1)} %collective-permute-done.18.refs_0_, ...), custom_call_target="tpu_custom_call" | custom-call | flops 1024 | bytes 1024 | tf_op jit(solution)/shard_map/attend_far/pallas_call | solution.py:306
  150.8 2.0 %collective-permute-start.20 = (bf16[512,128]{1,0:T(8,128)(2,1)}, bf16[512,128]{1,0:T(8,128)(2,1)}, u32[]{:S(2)}, u32[]{:S(2)}) collective-permute-start(bf16[512,128]{1,0:T(8,128)(2,1)} %get-tuple-element.64), channel_id=1, source_target_pairs={{0,4},{2,6},{4,0},{6,2},{8,12},{10,14},{12,8},{14,10},{1,5},{3,7},... | collective-permute-start | bytes 393224 | tf_op jit(solution)/shard_map/ppermute | solution.py:376
  155.3 2.2 %attend_far.11.refs_3_ = bf16[512,128]{1,0:T(8,128)(2,1)S(1)} custom-call(s32[66]{0:T(128)S(1)} %pad_add_fusion.1.place_ref, f32[512,256]{1,0:T(8,128)S(1)} %pad_maximum_fusion.table_ref, bf16[1,192,1536]{2,1,0:T(8,128)(2,1)S(1)} %copy-done.7, bf16[512,512]{1,0:T(8,128)(2,1)S(1)} %collective-permute-done.9.refs_1_, bf16[512,2176]{1,0:T(8,128)(2,1)S(1)} %copy-done.4), custom_call_target="tpu_custom_call" | custom-call | flops 1024 | bytes 1024 | tf_op jit(solution)/shard_map/attend_far/pallas_call | solution.py:306
  157.7 3.0 %place_pieces.2.refs_4_ = bf16[512,4096]{1,0:T(8,128)(2,1)} custom-call(s32[28]{0:T(128)S(1)} %stack.149.offsets_ref, bf16[512,512]{1,0:T(8,128)(2,1)S(1)} %copy-done.11, bf16[512,512]{1,0:T(8,128)(2,1)S(1)} %copy-done.15, bf16[512,512]{1,0:T(8,128)(2,1)S(1)} %copy-done.13, bf16[512,512]{1,0:T(8,128)(2,1)S(1)} %copy-done.17, ...), custom_call_target="tpu_custom_call" | custom-call | flops 1024 | bytes 1024 | tf_op jit(solution)/shard_map/place_pieces/pallas_call | solution.py:341
  160.8 1.9 %place_pieces.3 = bf16[512,4096]{1,0:T(8,128)(2,1)} custom-call(s32[4]{0:T(128)S(1)} %pad_add_fusion.offsets_ref, bf16[512,128]{1,0:T(8,128)(2,1)} %collective-permute-done.19.refs_0_, bf16[512,128]{1,0:T(8,128)(2,1)} %collective-permute-done.20.refs_1_, bf16[512,128]{1,0:T(8,128)(2,1)} %collective-permute-done.21.refs_2_, ...), custom_call_target="tpu_custom_call", output_to_operand_aliasing={{}: (5, {})} | custom-call | flops 1024 | bytes 1024 | tf_op jit(solution)/shard_map/place_pieces/pallas_call | solution.py:341
  (107 shorter events, 24.6 us)
Async XLA Ops:
  4.4 12.5 %collective-permute-start = (bf16[256,2176]{1,0:T(8,128)(2,1)}, bf16[256,2176]{1,0:T(8,128)(2,1)}, u32[]{:S(2)}, u32[]{:S(2)}) collective-permute-start(bf16[256,2176]{1,0:T(8,128)(2,1)} %prepare.1.refs_0_), channel_id=1, source_target_pairs={{0,1},{1,0},{2,3},{3,2},{4,5},{5,4},{6,7},{7,6},{8,9},{9,8},{10,11... | collective-permute-start | bytes 3342344 | tf_op jit(solution)/shard_map/ppermute | solution.py:379
  4.9 40.7 %collective-permute-start.1 = (bf16[256,2176]{1,0:T(8,128)(2,1)}, bf16[256,2176]{1,0:T(8,128)(2,1)}, u32[]{:S(2)}, u32[]{:S(2)}) collective-permute-start(bf16[256,2176]{1,0:T(8,128)(2,1)} %prepare.1.refs_0_), channel_id=1, source_target_pairs={{0,2},{2,0},{4,6},{6,4},{8,10},{10,8},{12,14},{14,12},{1,3},{3,1},... | collective-permute-start | bytes 3342344 | tf_op jit(solution)/shard_map/ppermute | solution.py:376
  7.5 48.2 %collective-permute-start.3 = (bf16[256,2176]{1,0:T(8,128)(2,1)}, bf16[256,2176]{1,0:T(8,128)(2,1)}, u32[]{:S(2)}, u32[]{:S(2)}) collective-permute-start(bf16[256,2176]{1,0:T(8,128)(2,1)} %prepare.1.refs_0_), channel_id=1, source_target_pairs={{0,4},{2,6},{4,0},{6,2},{8,12},{10,14},{12,8},{14,10},{1,5},{3,7},... | collective-permute-start | bytes 3342344 | tf_op jit(solution)/shard_map/ppermute | solution.py:376
  11.6 34.0 %collective-permute-start.2 = (bf16[512,512]{1,0:T(8,128)(2,1)}, bf16[512,512]{1,0:T(8,128)(2,1)}, u32[]{:S(2)}, u32[]{:S(2)}) collective-permute-start(bf16[512,512]{1,0:T(8,128)(2,1)} %pick.2), channel_id=1, source_target_pairs={{0,8},{2,10},{4,12},{6,14},{8,0},{10,2},{12,4},{14,6},{1,9},{3,11}... | collective-permute-start | bytes 1572872 | tf_op jit(solution)/shard_map/ppermute | solution.py:376
  15.3 73.2 %collective-permute-start.8 = (bf16[2,192,1536]{2,1,0:T(8,128)(2,1)}, bf16[2,192,1536]{2,1,0:T(8,128)(2,1)}, u32[]{:S(2)}, u32[]{:S(2)}) collective-permute-start(bf16[2,192,1536]{2,1,0:T(8,128)(2,1)} %pick.3), channel_id=1, source_target_pairs={{0,8},{2,10},{4,12},{6,14},{8,0},{10,2},{12,4},{14,6},{1,9},{3,11}... | collective-permute-start | bytes 3538952 | tf_op jit(solution)/shard_map/ppermute | solution.py:376
  55.7 32.8 %collective-permute-start.7 = (bf16[256,2176]{1,0:T(8,128)(2,1)}, bf16[256,2176]{1,0:T(8,128)(2,1)S(1)}, u32[]{:S(2)}, u32[]{:S(2)}) collective-permute-start(bf16[256,2176]{1,0:T(8,128)(2,1)} %collective-permute-done.3.refs_0_), channel_id=1, source_target_pairs={{0,2},{2,0},{4,6},{6,4},{8,10},{10,8},{12,14},{14,12},{1,3},{3,1},... | collective-permute-start | bytes 3342344 | tf_op jit(solution)/shard_map/ppermute | solution.py:376
  57.4 8.0 %collective-permute-start.5 = (bf16[128,2176]{1,0:T(8,128)(2,1)S(1)}, bf16[128,2176]{1,0:T(8,128)(2,1)S(1)}, u32[]{:S(2)}, u32[]{:S(2)}) collective-permute-start(bf16[128,2176]{1,0:T(8,128)(2,1)S(1)} %get-tuple-element.72), channel_id=1, source_target_pairs={{0,1},{1,0},{2,3},{3,2},{4,5},{5,4},{6,7},{7,6},{8,9},{9,8},{10,11... | collective-permute-start | bytes 1671176 | tf_op jit(solution)/shard_map/ppermute | solution.py:379
  57.7 7.8 %collective-permute-start.6 = (bf16[128,2176]{1,0:T(8,128)(2,1)S(1)}, bf16[128,2176]{1,0:T(8,128)(2,1)S(1)}, u32[]{:S(2)}, u32[]{:S(2)}) collective-permute-start(bf16[128,2176]{1,0:T(8,128)(2,1)S(1)} %get-tuple-element.71), channel_id=1, source_target_pairs={{0,1},{1,0},{2,3},{3,2},{4,5},{5,4},{6,7},{7,6},{8,9},{9,8},{10,11... | collective-permute-start | bytes 1671176 | tf_op jit(solution)/shard_map/ppermute | solution.py:379
  58.6 29.9 %collective-permute-start.9 = (bf16[512,512]{1,0:T(8,128)(2,1)}, bf16[512,512]{1,0:T(8,128)(2,1)S(1)}, u32[]{:S(2)}, u32[]{:S(2)}) collective-permute-start(bf16[512,512]{1,0:T(8,128)(2,1)} %collective-permute-done.2.refs_1_), channel_id=1, source_target_pairs={{0,16},{16,0},{1,17},{17,1},{2,18},{18,2},{3,19},{19,3},{4,20},{20... | collective-permute-start | bytes 1572872 | tf_op jit(solution)/shard_map/ppermute | solution.py:382
  70.9 28.7 %collective-permute-start.10 = (bf16[512,512]{1,0:T(8,128)(2,1)S(1)}, bf16[512,512]{1,0:T(8,128)(2,1)S(1)}, u32[]{:S(2)}, u32[]{:S(2)}) collective-permute-start(bf16[512,512]{1,0:T(8,128)(2,1)S(1)} %get-tuple-element.43), channel_id=1, source_target_pairs={{0,4},{2,6},{4,0},{6,2},{8,12},{10,14},{12,8},{14,10},{1,5},{3,7},... | collective-permute-start | bytes 1572872 | tf_op jit(solution)/shard_map/ppermute | solution.py:376
  99.6 3.5 %collective-permute-start.11 = (bf16[256,2176]{1,0:T(8,128)(2,1)S(1)}, bf16[256,2176]{1,0:T(8,128)(2,1)S(1)}, u32[]{:S(2)}, u32[]{:S(2)}) collective-permute-start(bf16[256,2176]{1,0:T(8,128)(2,1)S(1)} %collective-permute-done.7.refs_0_), channel_id=1, source_target_pairs={{0,1},{1,0},{2,3},{3,2},{4,5},{5,4},{6,7},{7,6},{8,9},{9,8},{10,11... | collective-permute-start | bytes 3342344 | tf_op jit(solution)/shard_map/ppermute | solution.py:379
  101.1 15.6 %collective-permute-start.14 = (bf16[1,192,1536]{2,1,0:T(8,128)(2,1)S(1)}, bf16[1,192,1536]{2,1,0:T(8,128)(2,1)S(1)}, u32[]{:S(2)}, u32[]{:S(2)}) collective-permute-start(bf16[1,192,1536]{2,1,0:T(8,128)(2,1)S(1)} %get-tuple-element.70), channel_id=1, source_target_pairs={{0,16},{16,0},{1,17},{17,1},{2,18},{18,2},{3,19},{19,3},{4,20},{20... | collective-permute-start | bytes 1769480 | tf_op jit(solution)/shard_map/ppermute | solution.py:382
  102.1 26.0 %collective-permute-start.12 = (bf16[512,512]{1,0:T(8,128)(2,1)S(1)}, bf16[512,512]{1,0:T(8,128)(2,1)S(1)}, u32[]{:S(2)}, u32[]{:S(2)}) collective-permute-start(bf16[512,512]{1,0:T(8,128)(2,1)S(1)} %get-tuple-element.40), channel_id=1, source_target_pairs={{0,2},{2,0},{4,6},{6,4},{8,10},{10,8},{12,14},{14,12},{1,3},{3,1},... | collective-permute-start | bytes 1572872 | tf_op jit(solution)/shard_map/ppermute | solution.py:376
  107.6 24.5 %collective-permute-start.13 = (bf16[512,512]{1,0:T(8,128)(2,1)S(1)}, bf16[512,512]{1,0:T(8,128)(2,1)S(1)}, u32[]{:S(2)}, u32[]{:S(2)}) collective-permute-start(bf16[512,512]{1,0:T(8,128)(2,1)S(1)} %get-tuple-element.48), channel_id=1, source_target_pairs={{0,6},{2,4},{4,2},{6,0},{8,14},{10,12},{12,10},{14,8},{1,7},{3,5},... | collective-permute-start | bytes 1572872 | tf_op jit(solution)/shard_map/ppermute | solution.py:376
  116.7 27.7 %collective-permute-start.18 = (bf16[1,192,1536]{2,1,0:T(8,128)(2,1)S(1)}, bf16[1,192,1536]{2,1,0:T(8,128)(2,1)S(1)}, u32[]{:S(2)}, u32[]{:S(2)}) collective-permute-start(bf16[1,192,1536]{2,1,0:T(8,128)(2,1)S(1)} %get-tuple-element.62), channel_id=1, source_target_pairs={{0,16},{16,0},{1,17},{17,1},{2,18},{18,2},{3,19},{19,3},{4,20},{20... | collective-permute-start | bytes 1769480 | tf_op jit(solution)/shard_map/ppermute | solution.py:382
  117.6 21.0 %collective-permute-start.15 = (bf16[512,256]{1,0:T(8,128)(2,1)S(1)}, bf16[512,256]{1,0:T(8,128)(2,1)S(1)}, u32[]{:S(2)}, u32[]{:S(2)}) collective-permute-start(bf16[512,256]{1,0:T(8,128)(2,1)S(1)} %get-tuple-element.53), channel_id=1, source_target_pairs={{0,2},{2,0},{4,6},{6,4},{8,10},{10,8},{12,14},{14,12},{1,3},{3,1},... | collective-permute-start | bytes 786440 | tf_op jit(solution)/shard_map/ppermute | solution.py:376
  118.6 20.0 %collective-permute-start.16 = (bf16[512,256]{1,0:T(8,128)(2,1)S(1)}, bf16[512,256]{1,0:T(8,128)(2,1)S(1)}, u32[]{:S(2)}, u32[]{:S(2)}) collective-permute-start(bf16[512,256]{1,0:T(8,128)(2,1)S(1)} %get-tuple-element.58), channel_id=1, source_target_pairs={{0,4},{2,6},{4,0},{6,2},{8,12},{10,14},{12,8},{14,10},{1,5},{3,7},... | collective-permute-start | bytes 786440 | tf_op jit(solution)/shard_map/ppermute | solution.py:376
  128.1 10.6 %collective-permute-start.17 = (bf16[512,256]{1,0:T(8,128)(2,1)S(1)}, bf16[512,256]{1,0:T(8,128)(2,1)S(1)}, u32[]{:S(2)}, u32[]{:S(2)}) collective-permute-start(bf16[512,256]{1,0:T(8,128)(2,1)S(1)} %get-tuple-element.59), channel_id=1, source_target_pairs={{0,6},{2,4},{4,2},{6,0},{8,14},{10,12},{12,10},{14,8},{1,7},{3,5},... | collective-permute-start | bytes 786440 | tf_op jit(solution)/shard_map/ppermute | solution.py:376
  137.6 15.3 %collective-permute-start.22 = (bf16[512,128]{1,0:T(8,128)(2,1)S(1)}, bf16[512,128]{1,0:T(8,128)(2,1)S(1)}, u32[]{:S(2)}, u32[]{:S(2)}) collective-permute-start(bf16[512,128]{1,0:T(8,128)(2,1)S(1)} %get-tuple-element.57), channel_id=1, source_target_pairs={{0,2},{2,0},{4,6},{6,4},{8,10},{10,8},{12,14},{14,12},{1,3},{3,1},... | collective-permute-start | bytes 393224 | tf_op jit(solution)/shard_map/ppermute | solution.py:376
  141.6 12.6 %collective-permute-start.23 = (bf16[512,128]{1,0:T(8,128)(2,1)}, bf16[512,128]{1,0:T(8,128)(2,1)}, u32[]{:S(2)}, u32[]{:S(2)}) collective-permute-start(bf16[512,128]{1,0:T(8,128)(2,1)} %get-tuple-element.66), channel_id=1, source_target_pairs={{0,4},{2,6},{4,0},{6,2},{8,12},{10,14},{12,8},{14,10},{1,5},{3,7},... | collective-permute-start | bytes 393224 | tf_op jit(solution)/shard_map/ppermute | solution.py:376
  143.9 10.3 %collective-permute-start.24 = (bf16[512,128]{1,0:T(8,128)(2,1)}, bf16[512,128]{1,0:T(8,128)(2,1)}, u32[]{:S(2)}, u32[]{:S(2)}) collective-permute-start(bf16[512,128]{1,0:T(8,128)(2,1)} %get-tuple-element.67), channel_id=1, source_target_pairs={{0,6},{2,4},{4,2},{6,0},{8,14},{10,12},{12,10},{14,8},{1,7},{3,5},... | collective-permute-start | bytes 393224 | tf_op jit(solution)/shard_map/ppermute | solution.py:376
  149.8 10.9 %collective-permute-start.19 = (bf16[512,128]{1,0:T(8,128)(2,1)}, bf16[512,128]{1,0:T(8,128)(2,1)}, u32[]{:S(2)}, u32[]{:S(2)}) collective-permute-start(bf16[512,128]{1,0:T(8,128)(2,1)} %get-tuple-element.63), channel_id=1, source_target_pairs={{0,2},{2,0},{4,6},{6,4},{8,10},{10,8},{12,14},{14,12},{1,3},{3,1},... | collective-permute-start | bytes 393224 | tf_op jit(solution)/shard_map/ppermute | solution.py:376
  150.8 9.9 %collective-permute-start.20 = (bf16[512,128]{1,0:T(8,128)(2,1)}, bf16[512,128]{1,0:T(8,128)(2,1)}, u32[]{:S(2)}, u32[]{:S(2)}) collective-permute-start(bf16[512,128]{1,0:T(8,128)(2,1)} %get-tuple-element.64), channel_id=1, source_target_pairs={{0,4},{2,6},{4,0},{6,2},{8,12},{10,14},{12,8},{14,10},{1,5},{3,7},... | collective-permute-start | bytes 393224 | tf_op jit(solution)/shard_map/ppermute | solution.py:376
  153.5 7.2 %collective-permute-start.21 = (bf16[512,128]{1,0:T(8,128)(2,1)}, bf16[512,128]{1,0:T(8,128)(2,1)}, u32[]{:S(2)}, u32[]{:S(2)}) collective-permute-start(bf16[512,128]{1,0:T(8,128)(2,1)} %get-tuple-element.65), channel_id=1, source_target_pairs={{0,6},{2,4},{4,2},{6,0},{8,14},{10,12},{12,10},{14,8},{1,7},{3,5},... | collective-permute-start | bytes 393224 | tf_op jit(solution)/shard_map/ppermute | solution.py:376
  (28 other events, 188.6 us)

commit v6 on v4

--- a/solution.py
+++ b/solution.py
@@ -10,8 +10,10 @@
 
 epsilon = 1e-06
 VMEM_LIMIT = 32 * 1024 * 1024
+VMEM_NEAR = 44 * 1024 * 1024
 LIGHT = pl.CostEstimate(flops=1024, bytes_accessed=1024, transcendentals=0)
 FAR = -(2.0**100)
+FETCHES = 4
 NT = (((1,), (1,)), ((), ()))
 NN = (((1,), (0,)), ((), ()))
 
@@ -68,31 +70,59 @@
     )(place, jnp.transpose(latents), gains[None, :])
 
 
-def pick_kernel(index_ref, source_ref, out_ref):
-    out_ref[...] = source_ref[...]
-
-
-def pick(source, index, block, axis):
-    shape = list(source.shape)
-    shape[axis] = block
-    out_shape = shape
-    position = lambda step, index_ref: tuple(index_ref[0] if at == axis else 0 for at in range(len(shape)))
+def pack_kernel(head_ref, query_ref, pair_ref, *out_refs):
+    query_rows, q_width = query_ref.shape[1:]
+    kv_width, pair_width = pair_ref.shape
+    slabs = [(out_ref, low) for out_ref in out_refs for low in range(0, out_ref.shape[0] - query_rows + 1, query_rows)]
+    for slab in range(q_width // kv_width):
+        out_ref, low = slabs[slab]
+        out_ref[low : low + query_rows, :] = query_ref[0, :, slab * kv_width : (slab + 1) * kv_width]
+    for fold in range(kv_width // pair_width):
+        span = slice(fold * pair_width, (fold + 1) * pair_width)
+        out_refs[-1][out_refs[-1].shape[0] - pair_width :, span] = pair_ref[span, :]
+
+
+def pack(head, query_weight, pair_weight, pair_width, parted):
+    query_rows, q_width = query_weight.shape[1:]
+    kv_width = pair_weight.shape[0]
+    slabs = q_width // kv_width
+    rows = [query_rows * (slabs - 1), query_rows + pair_width] if parted else [query_rows * slabs + pair_width]
     return pl.pallas_call(
-        pick_kernel,
+        pack_kernel,
         grid_spec=pltpu.PrefetchScalarGridSpec(
             num_scalar_prefetch=1,
             grid=(1,),
-            in_specs=[pl.BlockSpec(tuple(shape), position)],
-            out_specs=pl.BlockSpec(tuple(out_shape), lambda step, index_ref: (0,) * len(out_shape)),
+            in_specs=[
+                pl.BlockSpec((1, query_rows, q_width), lambda step, head_ref: (head_ref[0], 0, 0)),
+                pl.BlockSpec((kv_width, pair_width), lambda step, head_ref: (0, head_ref[0])),
+            ],
+            out_specs=[pl.BlockSpec((count, kv_width), lambda step, head_ref: (0, 0)) for count in rows],
         ),
-        out_shape=jax.ShapeDtypeStruct(tuple(out_shape), source.dtype),
+        out_shape=[jax.ShapeDtypeStruct((count, kv_width), jnp.bfloat16) for count in rows],
         compiler_params=pltpu.CompilerParams(vmem_limit_bytes=VMEM_LIMIT),
         cost_estimate=LIGHT,
-        name="pick",
-    )(jnp.reshape(index, (1,)).astype(jnp.int32), source)
-
-
-def attend_group(sizes, chosen, tokens_ref, weight_refs, scratch, out_ref):
+        name="pack",
+    )(jnp.reshape(head, (1,)).astype(jnp.int32), query_weight, pair_weight)
+
+
+def unpack(packed_refs, query_ref, pair_ref):
+    query_rows, q_width = query_ref.shape[1:]
+    kv_width = pair_ref.shape[0]
+    heads = query_ref.shape[0]
+    pair_width = pair_ref.shape[1] // heads
+    each = len(packed_refs) // heads
+    for head in range(heads):
+        some = packed_refs[head * each : (head + 1) * each]
+        slabs = [(ref, low) for ref in some for low in range(0, ref.shape[0] - query_rows + 1, query_rows)]
+        for slab in range(q_width // kv_width):
+            ref, low = slabs[slab]
+            query_ref[head, :, slab * kv_width : (slab + 1) * kv_width] = ref[low : low + query_rows, :]
+        for fold in range(kv_width // pair_width):
+            span = slice(fold * pair_width, (fold + 1) * pair_width)
+            pair_ref[span, head * pair_width : (head + 1) * pair_width] = some[-1][some[-1].shape[0] - pair_width :, span]
+
+
+def attend_group(sizes, chosen, tokens_ref, weight_refs, scratch, out_ref, copies):
     heads, q_width, kv_width, nope_width, rope_width, value_width = sizes
     query_width, pair_width = nope_width + rope_width, nope_width + value_width
     query_ref, key_ref, value_ref, turn_ref, bias_ref = scratch
@@ -106,6 +136,8 @@
     is_first = lax.rem(lane, rope_width) < half_width
     is_rope = lane < rope_width
     rope_low = q_width + kv_width
+    for copy in copies:
+        copy.wait()
     apart = jnp.where(is_rope, 0.0, (1.0 - tokens_ref[:, rope_low:].astype(jnp.float32)) * FAR)
 
     def dot(left, right, dims):
@@ -217,28 +249,43 @@
         turn_ref[index * block : (index + 1) * block, :] = table_ref[pl.ds(position, block), :]
 
 
-def near_kernel(sizes, slot_count, distance, place_ref, table_ref, query_weight_ref, pair_weight_ref, same_ref, other_ref, out_ref, tokens_ref, *scratch):
-    core, group = place_ref[1], place_ref[0] ^ distance
-    rows = same_ref.shape[0]
-    tokens_ref[pl.ds(pl.multiple_of(core * rows, rows), rows), :] = same_ref[...]
-    tokens_ref[pl.ds(pl.multiple_of((1 - core) * rows, rows), rows), :] = other_ref[...]
-    set_up(scratch)
-    set_turn(group, slot_count, place_ref, table_ref, scratch[3])
+def near_kernel(sizes, slot_count, distances, place_ref, table_ref, query_weight_ref, pair_weight_ref, groups_ref, *refs):
+    slots = len(distances)
+    out_refs, token_refs, sems, bias_ref = refs[:slots], refs[slots : 2 * slots], refs[2 * slots], refs[2 * slots + 1]
+    refs = refs[2 * slots + 2 :]
+    copies = []
+    for slot, distance in enumerate(distances):
+        source = groups_ref.at[lax.rem(place_ref[0] ^ distance, groups_ref.shape[0])]
+        step = source.shape[0] // FETCHES
+        copies.append([])
+        for index in range(FETCHES):
+            rows = pl.ds(index * step, step)
+            copies[slot].append(pltpu.make_async_copy(source.at[rows], token_refs[slot].at[rows], sems.at[slot, index]))
+            copies[slot][index].start()
     heads = list(range(sizes[0]))
-    attend_groups([attend_group(sizes, heads, tokens_ref, (query_weight_ref, pair_weight_ref), scratch, out_ref)])
-
-
-def far_kernel(sizes, slot_count, distances, chosen, place_ref, table_ref, *refs):
-    slots = len(distances)
-    weight_refs, refs = refs[:2], refs[2:]
+    works = []
+    for slot, distance in enumerate(distances):
+        scratch = [*refs[4 * slot : 4 * slot + 4], bias_ref]
+        set_up(scratch, slot == 0)
+        set_turn(place_ref[0] ^ distance, slot_count, place_ref, table_ref, scratch[3])
+        weights = (query_weight_ref, pair_weight_ref)
+        works.append(attend_group(sizes, heads, token_refs[slot], weights, scratch, out_refs[slot], copies[slot]))
+    attend_groups(works)
+
+
+def far_kernel(sizes, slot_count, distances, count, place_ref, table_ref, *refs):
+    slots, heads = len(distances), sizes[0]
+    packed_refs, refs = refs[:count], refs[count:]
     token_refs, out_refs, refs = refs[:slots], refs[slots : 2 * slots], refs[2 * slots :]
-    bias_ref, refs = refs[0], refs[1:]
+    query_weight_ref, pair_weight_ref, bias_ref, refs = refs[0], refs[1], refs[2], refs[3:]
+    unpack(packed_refs, query_weight_ref, pair_weight_ref)
     works = []
     for slot in range(slots):
         scratch = [*refs[4 * slot : 4 * slot + 4], bias_ref]
         set_up(scratch, slot == 0)
         set_turn(place_ref[0] ^ distances[slot], slot_count, place_ref, table_ref, scratch[3])
-        works.append(attend_group(sizes, chosen, token_refs[slot], weight_refs, scratch, out_refs[slot]))
+        weights = (query_weight_ref, pair_weight_ref)
+        works.append(attend_group(sizes, list(range(heads)), token_refs[slot], weights, scratch, out_refs[slot], []))
     attend_groups(works)
 
 
@@ -253,40 +300,46 @@
     ]
 
 
-def attend_near(sizes, slot_count, distance, place, table, query_weight, pair_weight, same, other):
-    rows, width = same.shape
-    heads, value_width = sizes[0], sizes[-1]
+def attend_near(sizes, slot_count, distances, place, table, query_weight, pair_weight, groups):
+    tokens, width = groups.shape[1:]
+    slots, heads, value_width = len(distances), sizes[0], sizes[-1]
     vmem = pl.BlockSpec(memory_space=pltpu.VMEM)
-    return pl.pallas_call(
-        partial(near_kernel, sizes, slot_count, distance),
-        out_shape=[
-            jax.ShapeDtypeStruct((2 * rows, heads * value_width), jnp.bfloat16),
-            jax.ShapeDtypeStruct((2 * rows, width), jnp.bfloat16),
-        ],
-        in_specs=[pl.BlockSpec(memory_space=pltpu.SMEM)] + [vmem] * 5,
-        out_specs=[vmem, vmem],
-        scratch_shapes=scratch_for(sizes, 2 * rows),
-        compiler_params=pltpu.CompilerParams(vmem_limit_bytes=VMEM_LIMIT),
+    own = scratch_for(sizes, tokens)
+    results = pl.pallas_call(
+        partial(near_kernel, sizes, slot_count, distances),
+        out_shape=[jax.ShapeDtypeStruct((tokens, heads * value_width), jnp.bfloat16)] * slots
+        + [jax.ShapeDtypeStruct((tokens, width), jnp.bfloat16)] * slots,
+        in_specs=[pl.BlockSpec(memory_space=pltpu.SMEM)] + [vmem] * 3 + [pl.BlockSpec(memory_space=pltpu.HBM)],
+        out_specs=[vmem] * (2 * slots),
+        scratch_shapes=[pltpu.SemaphoreType.DMA((slots, FETCHES))] + own[4:] + own[:4] * slots,
+        compiler_params=pltpu.CompilerParams(vmem_limit_bytes=VMEM_NEAR),
         cost_estimate=LIGHT,
         name="attend_near",
-    )(place, table, query_weight, pair_weight, same, other)
-
-
-def attend_far(sizes, slot_count, distances, place, table, query_weight, pair_weight, chosen, groups):
+    )(place, table, query_weight, pair_weight, groups)
+    return results[:slots], results[slots:]
+
+
+def attend_far(sizes, slot_count, distances, place, table, packed, groups):
     tokens = groups[0].shape[0]
-    slots, heads, value_width = len(groups), sizes[0], sizes[-1]
+    slots = len(groups)
+    heads, q_width, kv_width, nope_width, rope_width, value_width = sizes
     vmem = pl.BlockSpec(memory_space=pltpu.VMEM)
     own = scratch_for(sizes, tokens)
     return pl.pallas_call(
-        partial(far_kernel, sizes, slot_count, distances, chosen),
+        partial(far_kernel, sizes, slot_count, distances, len(packed)),
         out_shape=[jax.ShapeDtypeStruct((tokens, heads * value_width), jnp.bfloat16)] * slots,
-        in_specs=[pl.BlockSpec(memory_space=pltpu.SMEM)] + [vmem] * (3 + slots),
+        in_specs=[pl.BlockSpec(memory_space=pltpu.SMEM)] + [vmem] * (1 + len(packed) + slots),
         out_specs=[vmem] * slots,
-        scratch_shapes=own[4:] + own[:4] * slots,
+        scratch_shapes=[
+            pltpu.VMEM((heads, nope_width + rope_width, q_width), jnp.bfloat16),
+            pltpu.VMEM((kv_width, heads * (nope_width + value_width)), jnp.bfloat16),
+        ]
+        + own[4:]
+        + own[:4] * slots,
         compiler_params=pltpu.CompilerParams(vmem_limit_bytes=VMEM_LIMIT),
         cost_estimate=LIGHT,
         name="attend_far",
-    )(place, table, query_weight, pair_weight, *groups)
+    )(place, table, *packed, *groups)
 
 
 def place_kernel(width, count, offsets_ref, *refs):
@@ -332,10 +385,10 @@
 def shards(latents, q_gain, kv_gain, q_weight, kv_weight, lengths):
     q_width, kv_width = q_gain.shape[0], kv_gain.shape[0]
     rope_width = latents.shape[1] - q_width - kv_width
-    places = lax.axis_size("seq")
+    half_places = lax.axis_size("quad")
+    places = 2 * half_places
     parts = lax.axis_size("parts")
-    half_places = places // 2
-    place = lax.axis_index("seq")
+    place = lax.axis_index("half") * half_places + lax.axis_index("quad")
     core = lax.axis_index("head")
     part = lax.axis_index("parts")
     tokens = 2 * latents.shape[0]
@@ -347,10 +400,10 @@
     sizes = (q_width, kv_width, nope_width, rope_width, value_width)
 
     def across(value, distance):
-        return lax.ppermute(value, "seq", [(s, s ^ distance) for s in range(places)])
-
-    def sibling(value):
-        return lax.ppermute(value, "head", [(0, 1), (1, 0)])
+        return lax.ppermute(value, "quad", [(s, s ^ distance) for s in range(half_places)])
+
+    def opposite(value):
+        return lax.ppermute(value, "half", [(0, 1), (1, 0)])
 
     def other_part(value):
         return lax.ppermute(value, "parts", [(p, p ^ 1) for p in range(parts)])
@@ -369,52 +422,31 @@
     per_part = local_heads // share
     side = lax.rem(part, share)
 
-    sent_pair = pick(own_pair, side, per_part * pair_width, 1)
-    sent_query = pick(own_query, side, per_part, 0)
     latent = prepare(latents, gains, q_width, kv_width, slot_count, spot)
-    same, other = [latent], [sibling(latent)]
-    for distance in range(1, half_places):
-        same.append(across(latent, distance) if distance & (distance - 1) == 0 else None)
-    far_pair = across(sent_pair, half_places)
-    far_query = across(sent_query, half_places)
-
-    joined = []
-
-    def near(distance, *earlier):
-        mixed, tokens_joined = attend_near(
+    sent = [pack(side * per_part + index, own_query, own_pair, pair_width, index > 0) for index in range(per_part)]
+    groups = lax.all_gather(latent, ("quad", "head"), axis=0, tiled=True).reshape(half_places, tokens, latent.shape[1])
+    far = [[opposite(piece) for piece in pieces] for pieces in sent]
+
+    placed, joined, arrived = [], {}, {}
+    orders = [[*range(half_places // 2, half_places), *range(1, half_places // 2)], [0]]
+    mixed = None
+    for distances in orders:
+        results, fetched = attend_near(
             (local_heads, *sizes),
             slot_count,
-            distance,
-            spot,
+            distances,
+            spot if mixed is None else after(spot, mixed),
             table,
             own_query,
             own_pair,
-            after(same[distance], *earlier),
-            other[distance],
+            groups,
         )
-        joined.append(tokens_joined)
-        return mixed
-
-    mixed = near(0)
-    arrived = [mixed]
-    direct = [entry for entry in same[1:] if entry is not None]
-    for distance in range(1, half_places):
-        if same[distance] is None:
-            low_bit = distance & -distance
-            same[distance] = across(after(same[distance ^ low_bit], mixed), low_bit)
-            other.append(None)
-        else:
-            other.append(sibling(after(same[distance], mixed, far_pair, *direct)))
-    crossed_pair = [other_part(after(far_pair, mixed))] if share == 2 else []
-    for distance in range(1, half_places):
-        if other[distance] is None:
-            other[distance] = sibling(after(same[distance], mixed, far_query, *crossed_pair))
-        mixed = near(distance, mixed)
-        arrived.append(across(mixed, distance))
-    placed = []
-    for distance in range(half_places):
-        base = (place ^ distance) * block_width
-        placed.append((arrived[distance], [base + head * value_width for head in range(local_heads)]))
+        mixed = results[0]
+        for distance, result, rows in zip(distances, results, fetched):
+            joined[distance] = rows
+            arrived[distance] = across(result, distance) if distance else result
+            base = (place ^ distance) * block_width
+            placed.append((arrived[distance], [base + head * value_width for head in range(local_heads)]))
 
     out_width = places * block_width
 
@@ -424,32 +456,41 @@
         placed.clear()
         return held
 
-    heads = list(range(per_part))
-    rounds = [(far_query, far_pair, side * per_part)]
-    if share == 2:
-        rounds.append((other_part(far_query), crossed_pair[0], (1 - side) * per_part))
-    gates, first_sent, late = [], [], []
-    later = [arrived[1:-1], arrived[-1:], first_sent, []]
-    for number, (queries, pairs, first) in enumerate(rounds):
+    crossed = []
+    for index, pieces in enumerate(far if share == 2 else []):
+        crossed.append([other_part(after(piece, mixed) if index else piece) for piece in pieces])
+    rounds = []
+    for index in range(per_part):
+        weights, numbers = [*far[index]], [side * per_part + index]
+        if share == 2:
+            weights.extend(crossed[index])
+            numbers.append((1 - side) * per_part + index)
+        rounds.append((weights, numbers))
+    late, sent_before = [], []
+    for number, (weights, numbers) in enumerate(rounds):
+        last = number + 1 == len(rounds)
+        sent_now = []
         for distances in (list(range(1, half_places)), [0]):
+            gates = [arrived[distance] for distance in range(1, half_places - 1)] if last else []
+            if distances == [0] and last:
+                gates = [arrived[half_places - 1], *sent_before]
             mixed_some = attend_far(
-                (per_part, *sizes),
+                (len(numbers), *sizes),
                 slot_count,
                 distances,
                 after(spot, mixed, *gates),
                 table,
-                queries,
-                pairs,
-                heads,
+                weights,
                 [joined[distance] for distance in distances],
             )
-            mixed, gates = mixed_some[0], later.pop(0)
+            mixed = mixed_some[0]
             for distance, piece in zip(distances, mixed_some):
                 base = (place ^ distance ^ half_places) * block_width
-                received = across(piece, distance) if distance else piece
-                if number == 0 and distance:
-                    first_sent.append(received)
-                (late if number else placed).append((received, [base + (first + head) * value_width for head in heads]))
+                if distance:
+                    piece = across(piece, distance)
+                    sent_now.append(piece)
+                (late if last else placed).append((piece, [base + head * value_width for head in numbers]))
+        sent_before = sent_now
     held = flush(None)
     placed.extend(late)
     held = flush(held)
@@ -457,17 +498,19 @@
 
 
 def solution(mesh):
+    parts, places, cores = (mesh.shape[name] for name in ("parts", "seq", "head"))
+    devices = mesh.devices.reshape(parts, 2, places // 2, cores)
     return jax.shard_map(
         shards,
-        mesh=mesh,
+        mesh=jax.sharding.Mesh(devices, ("parts", "half", "quad", "head")),
         in_specs=(
-            P(("parts", "seq", "head"), None),
+            P(("parts", "half", "quad", "head"), None),
             P(),
             P(),
-            P("head", None, "seq", None),
-            P("head", None, "seq", None),
+            P("head", None, ("half", "quad"), None),
+            P("head", None, ("half", "quad"), None),
             P("parts", None),
         ),
-        out_specs=P(("parts", "seq"), "head"),
+        out_specs=P(("parts", "half", "quad"), "head"),
         check_vma=False,
     )

time: 140 us -> 179 us (1.28)
  waiting for transfers between devices: 57.3 us -> 77.4 us
  between operations: 0.46 us -> 13.7 us
  Pallas kernels: 47.7 us -> 52.7 us
    all_gather x0 -> x1, waiting for transfers between devices: none -> 31.8 us  [shards(): lax.all_gather(latent, ('quad', 'head'), axis=0, tiled=True)]
    ppermute x18 -> x12, waiting for transfers between devices: 57.3 us -> 45.6 us  [the longest x3 41.5 us: opposite(): return lax.ppermute(value, 'half', [(0, 1), (1, 0)])]
    pallas_call x10 -> x8, Pallas kernels: 40.3 us -> 45.3 us  [the longest x4 22 us: attend_far(): pl.pallas_call(partial(far_kernel, sizes, slot_count, distances, len(pack...]
    ppermute x18 -> x12, starting transfers between devices: 21.7 us -> 20.5 us  [the longest x9 13.5 us: across(): lax.ppermute(value, 'quad', [(s, s ^ distance) for s in range(half_places)])]
    ppermute x2 -> x3, starting transfers between devices: 3.05 us -> 4.26 us  [other_part(): return lax.ppermute(value, 'parts', [(p, p ^ 1) for p in range(parts)])]
    unnamed x35 -> x31, local copies, waits for them, and re-layouts: 6.5 us -> 7.23 us
  transfers between devices with their start and end apart: 20 -> 16, of which waited for: 6 -> 3; matrix products, arithmetic and copies ran while one was open for 1% -> 1% of each run, Pallas kernels for 31% -> 27%
where the time goes in v6:
time: 179 us
  waiting for transfers between devices  77.4 us (43%)
  Pallas kernels  52.7 us (29%)
  starting transfers between devices  24.7 us (14%)
  between operations  13.7 us (8%)
  local copies, waits for them, and re-layouts  8.18 us (5%)
  other arithmetic  1.83 us (1%)
    ppermute x3, waiting for transfers between devices, opposite(): return lax.ppermute(value, 'half', [(0, 1), (1, 0)])  41.5 us
    all_gather x1, waiting for transfers between devices, shards(): lax.all_gather(latent, ('quad', 'head'), axis=0, tiled=True)  31.8 us
    pallas_call x4, Pallas kernels, attend_far(): pl.pallas_call(partial(far_kernel, sizes, slot_count, distances, len(pack...  22 us
    pallas_call x2, Pallas kernels, attend_near(): pl.pallas_call(partial(near_kernel, sizes, slot_count, distances), out_sh...  21.4 us
    ppermute x9, starting transfers between devices, across(): lax.ppermute(value, 'quad', [(s, s ^ distance) for s in range(half_places)])  13.5 us
    unnamed x31, local copies, waits for them, and re-layouts  7.23 us
    ppermute x3, starting transfers between devices, opposite(): return lax.ppermute(value, 'half', [(0, 1), (1, 0)])  6.96 us
    pallas_call x2, Pallas kernels, place_pieces(): pl.pallas_call(partial(place_kernel, width, count), out_shape=jax.ShapeDt...  5.04 us
  transfers between devices with their start and end apart: 16, of which 3 were waited for; matrix products, arithmetic and copies ran while one was open for 1% of the time, Pallas kernels for 27%

profile of v6, /device:TPU:0, one launch (start us, length us, event | category | flops | bytes accessed | tf_op | source)
XLA Modules:
  0.0 178.6 jit_solution(10624823010011185212)
XLA Ops:
  8.1 1.2 copy-done.4
  9.3 2.4 %prepare.1 = bf16[256,2176]{1,0:T(8,128)(2,1)} custom-call(s32[66]{0:T(128)S(1)} %pad_add_fusion.place_ref, bf16[2112,256]{1,0:T(8,128)(2,1)S(1)} %bitcast.53, f32[1,2048]{1,0:T(1,128)S(1)} %bitcast.54), custom_call_target="tpu_custom_call" | custom-call | flops 1024 | bytes 1024 | tf_op jit(solution)/shard_map/prepare/pallas_call | solution.py:62
  11.7 1.4 copy.8
  14.2 4.0 %collective-permute-start = (bf16[832,512]{1,0:T(8,128)(2,1)}, bf16[832,512]{1,0:T(8,128)(2,1)}, u32[]{:S(2)}, u32[]{:S(2)}) collective-permute-start(bf16[832,512]{1,0:T(8,128)(2,1)} %pack.2), channel_id=1, source_target_pairs={{0,8},{8,0},{1,9},{9,1},{2,10},{10,2},{3,11},{11,3},{4,12},{12,4},... | collective-permute-start | bytes 2555912 | tf_op jit(solution)/shard_map/ppermute | solution.py:406
  19.2 2.9 %collective-permute-start.4 = (bf16[384,512]{1,0:T(8,128)(2,1)}, bf16[384,512]{1,0:T(8,128)(2,1)}, u32[]{:S(2)}, u32[]{:S(2)}) collective-permute-start(bf16[384,512]{1,0:T(8,128)(2,1)} %get-tuple-element.40), channel_id=1, source_target_pairs={{0,8},{8,0},{1,9},{9,1},{2,10},{10,2},{3,11},{11,3},{4,12},{12,4},... | collective-permute-start | bytes 1179656 | tf_op jit(solution)/shard_map/ppermute | solution.py:406
  22.1 41.5 %collective-permute-done.refs_0_ = bf16[832,512]{1,0:T(8,128)(2,1)} collective-permute-done((bf16[832,512]{1,0:T(8,128)(2,1)}, bf16[832,512]{1,0:T(8,128)(2,1)}, u32[]{:S(2)}, u32[]{:S(2)}) %collective-permute-start) | collective-permute-done | bytes 852000 | tf_op jit(solution)/shard_map/ppermute | solution.py:406
  63.7 2.2 %collective-permute-start.1 = (bf16[832,512]{1,0:T(8,128)(2,1)}, bf16[832,512]{1,0:T(8,128)(2,1)S(1)}, u32[]{:S(2)}, u32[]{:S(2)}) collective-permute-start(bf16[832,512]{1,0:T(8,128)(2,1)} %collective-permute-done.refs_0_), channel_id=1, source_target_pairs={{0,16},{16,0},{1,17},{17,1},{2,18},{18,2},{3,19},{19,3},{4,20},{20... | collective-permute-start | bytes 2555912 | tf_op jit(solution)/shard_map/ppermute | solution.py:409
  66.9 31.8 %all-gather.2.cloned.1.call-done = bf16[2048,2176]{1,0:T(8,128)(2,1)} async-done(((bf16[256,2176]{1,0:T(8,128)(2,1)}), bf16[2048,2176]{1,0:T(8,128)(2,1)}) %all-gather.2.cloned.1.call-update) | async-done | bytes 8912912 | tf_op jit(solution)/shard_map/all_gather | solution.py:427
  98.7 15.5 %attend_near.2 = (bf16[512,512]{1,0:T(8,128)(2,1)S(1)}, bf16[512,512]{1,0:T(8,128)(2,1)}, bf16[512,512]{1,0:T(8,128)(2,1)S(1)}, bf16[512,2176]{1,0:T(8,128)(2,1)...) custom-call(s32[66]{0:T(128)S(1)} %pad_add_fusion.place_ref, ...), custom_call_target="tpu_custom_call" | custom-call | flops 1024 | bytes 1024 | tf_op jit(solution)/shard_map/attend_near/pallas_call | solution.py:308
  114.3 2.1 %collective-permute-start.2 = (bf16[512,512]{1,0:T(8,128)(2,1)S(1)}, bf16[512,512]{1,0:T(8,128)(2,1)S(1)}, u32[]{:S(2)}, u32[]{:S(2)}) collective-permute-start(bf16[512,512]{1,0:T(8,128)(2,1)S(1)} %get-tuple-element.38), channel_id=1, source_target_pairs={{0,2},{2,0},{4,6},{6,4},{1,3},{3,1},{5,7},{7,5},{8,10},{10,8},{12,... | collective-permute-start | bytes 1572872 | tf_op jit(solution)/shard_map/ppermute | solution.py:403
  116.3 5.9 %attend_near.3 = (bf16[512,512]{1,0:T(8,128)(2,1)S(1)}, bf16[512,2176]{1,0:T(8,128)(2,1)S(1)}) custom-call(s32[66]{0:T(128)S(1)} %pad_add_fusion.place_ref, f32[512,256]{1,0:T(8,128)S(1)} %pad_maximum_fusion.table_ref, bf16[4,192,1536]{2,1,0:T(8,128)(2,1)S(1)} %bitcast.48, bf16[512,1024]{1,0:T(8,128)(2,1)S(1)} %bitcast.52, bf16[4,512,2176]{2,1,0:T(8,128)(2,1)} %bitcast.56), custom_call_target="tpu_custom_call" | custom-call | flops 1024 | bytes 1024 | tf_op jit(solution)/shard_map/attend_near/pallas_call | solution.py:308
  122.3 1.5 collective-permute-start.7
  124.4 1.4 collective-permute-start.11
  125.8 7.7 %attend_far.4 = (bf16[512,256]{1,0:T(8,128)(2,1)S(1)}, bf16[512,256]{1,0:T(8,128)(2,1)S(1)}, bf16[512,256]{1,0:T(8,128)(2,1)}) custom-call(s32[66]{0:T(128)S(1)} %pad_add_fusion.place_ref, f32[512,256]{1,0:T(8,128)S(1)} %pad_maximum_fusion.table_ref, bf16[832,512]{1,0:T(8,128)(2,1)} %collective-permute-done.refs_0_, ...), custom_call_target="tpu_custom_call" | custom-call | flops 1024 | bytes 1024 | tf_op jit(solution)/shard_map/attend_far/pallas_call | solution.py:328
  133.5 2.1 %collective-permute-start.12 = (bf16[512,256]{1,0:T(8,128)(2,1)S(1)}, bf16[512,256]{1,0:T(8,128)(2,1)S(1)}, u32[]{:S(2)}, u32[]{:S(2)}) collective-permute-start(bf16[512,256]{1,0:T(8,128)(2,1)S(1)} %get-tuple-element.35), channel_id=1, source_target_pairs={{0,2},{2,0},{4,6},{6,4},{1,3},{3,1},{5,7},{7,5},{8,10},{10,8},{12,... | collective-permute-start | bytes 786440 | tf_op jit(solution)/shard_map/ppermute | solution.py:403
  135.6 4.0 %collective-permute-done.2.refs_2_ = bf16[512,512]{1,0:T(8,128)(2,1)S(1)} collective-permute-done((bf16[512,512]{1,0:T(8,128)(2,1)S(1)}, bf16[512,512]{1,0:T(8,128)(2,1)S(1)}, u32[]{:S(2)}, u32[]{:S(2)}) %collective-permute-start.2) | collective-permute-done | bytes 524320 | tf_op jit(solution)/shard_map/ppermute | solution.py:403
  139.6 2.2 %collective-permute-start.13 = (bf16[512,256]{1,0:T(8,128)(2,1)S(1)}, bf16[512,256]{1,0:T(8,128)(2,1)S(1)}, u32[]{:S(2)}, u32[]{:S(2)}) collective-permute-start(bf16[512,256]{1,0:T(8,128)(2,1)S(1)} %get-tuple-element.48), channel_id=1, source_target_pairs={{0,4},{2,6},{4,0},{6,2},{1,5},{3,7},{5,1},{7,3},{8,12},{10,14},{12... | collective-permute-start | bytes 786440 | tf_op jit(solution)/shard_map/ppermute | solution.py:403
  141.8 3.3 %attend_far.5.refs_7_ = bf16[512,256]{1,0:T(8,128)(2,1)S(1)} custom-call(s32[66]{0:T(128)S(1)} %pad_add_fusion.place_ref, f32[512,256]{1,0:T(8,128)S(1)} %pad_maximum_fusion.table_ref, bf16[832,512]{1,0:T(8,128)(2,1)} %collective-permute-done.refs_0_, bf16[832,512]{1,0:T(8,128)(2,1)S(1)} %collective-permute-done.1.refs_1_, ...), custom_call_target="tpu_custom_call" | custom-call | flops 1024 | bytes 1024 | tf_op jit(solution)/shard_map/attend_far/pallas_call | solution.py:328
  145.2 2.2 %collective-permute-start.14 = (bf16[512,256]{1,0:T(8,128)(2,1)}, bf16[512,256]{1,0:T(8,128)(2,1)}, u32[]{:S(2)}, u32[]{:S(2)}) collective-permute-start(bf16[512,256]{1,0:T(8,128)(2,1)} %get-tuple-element.49), channel_id=1, source_target_pairs={{0,6},{2,4},{4,2},{6,0},{1,7},{3,5},{5,3},{7,1},{8,14},{10,12},{12... | collective-permute-start | bytes 786440 | tf_op jit(solution)/shard_map/ppermute | solution.py:403
  147.4 7.8 %attend_far.6 = (bf16[512,256]{1,0:T(8,128)(2,1)}, bf16[512,256]{1,0:T(8,128)(2,1)}, bf16[512,256]{1,0:T(8,128)(2,1)}) custom-call(s32[66]{0:T(128)S(1)} %pad_add_fusion.place_ref, f32[512,256]{1,0:T(8,128)S(1)} %pad_maximum_fusion.table_ref, bf16[384,512]{1,0:T(8,128)(2,1)} %collective-permute-done.4.refs_0_, ...), custom_call_target="tpu_custom_call" | custom-call | flops 1024 | bytes 1024 | tf_op jit(solution)/shard_map/attend_far/pallas_call | solution.py:328
  156.7 2.5 %collective-permute-start.8 = (bf16[512,256]{1,0:T(8,128)(2,1)}, bf16[512,256]{1,0:T(8,128)(2,1)}, u32[]{:S(2)}, u32[]{:S(2)}) collective-permute-start(bf16[512,256]{1,0:T(8,128)(2,1)} %get-tuple-element.44), channel_id=1, source_target_pairs={{0,2},{2,0},{4,6},{6,4},{1,3},{3,1},{5,7},{7,5},{8,10},{10,8},{12,... | collective-permute-start | bytes 786440 | tf_op jit(solution)/shard_map/ppermute | solution.py:403
  163.4 3.0 %place_pieces.2.refs_4_ = bf16[512,4096]{1,0:T(8,128)(2,1)} custom-call(s32[24]{0:T(128)S(1)} %stack.143.offsets_ref, bf16[512,512]{1,0:T(8,128)(2,1)S(1)} %copy-done.6, bf16[512,512]{1,0:T(8,128)(2,1)} %collective-permute-done.11.refs_1_, bf16[512,512]{1,0:T(8,128)(2,1)S(1)} %copy-done.8, bf16[512,512]{1,0:T(8,128)(2,1)S(1)} %copy-done.10, ...), custom_call_target="tpu_custom_call" | custom-call | flops 1024 | bytes 1024 | tf_op jit(solution)/shard_map/place_pieces/pallas_call | solution.py:368
  166.4 3.2 %attend_far.7.refs_3_ = bf16[512,256]{1,0:T(8,128)(2,1)S(1)} custom-call(s32[66]{0:T(128)S(1)} %pad_add_fusion.place_ref, f32[512,256]{1,0:T(8,128)S(1)} %pad_maximum_fusion.table_ref, bf16[384,512]{1,0:T(8,128)(2,1)} %collective-permute-done.4.refs_0_, bf16[448,512]{1,0:T(8,128)(2,1)S(1)} %collective-permute-done.5.refs_1_, ...), custom_call_target="tpu_custom_call" | custom-call | flops 1024 | bytes 1024 | tf_op jit(solution)/shard_map/attend_far/pallas_call | solution.py:328
  169.6 2.1 %place_pieces.3 = bf16[512,4096]{1,0:T(8,128)(2,1)} custom-call(s32[8]{0:T(128)S(1)} %stack.116.offsets_ref, bf16[512,256]{1,0:T(8,128)(2,1)} %collective-permute-done.8.refs_0_, bf16[512,256]{1,0:T(8,128)(2,1)} %collective-permute-done.9.refs_1_, bf16[512,256]{1,0:T(8,128)(2,1)S(1)} %collective-permute-done.10.refs_2_, ...), custom_call_target="tpu_custom_call", output_to_operand_aliasing={{}: (5, {})} | custom-call | flops 1024 | bytes 1024 | tf_op jit(solution)/shard_map/place_pieces/pallas_call | solution.py:368
  (60 shorter events, 11.0 us)
Async XLA Ops:
  6.5 92.2 %all-gather.2.cloned.1.call-start = ((), (), s32[]{:S(2)}) async-start(), calls=%async_computation | async-start | bytes 10027008 | tf_op jit(solution)/shard_map/all_gather | solution.py:427
  14.2 49.5 %collective-permute-start = (bf16[832,512]{1,0:T(8,128)(2,1)}, bf16[832,512]{1,0:T(8,128)(2,1)}, u32[]{:S(2)}, u32[]{:S(2)}) collective-permute-start(bf16[832,512]{1,0:T(8,128)(2,1)} %pack.2), channel_id=1, source_target_pairs={{0,8},{8,0},{1,9},{9,1},{2,10},{10,2},{3,11},{11,3},{4,12},{12,4},... | collective-permute-start | bytes 2555912 | tf_op jit(solution)/shard_map/ppermute | solution.py:406
  19.2 103.1 %collective-permute-start.5 = (bf16[448,512]{1,0:T(8,128)(2,1)}, bf16[448,512]{1,0:T(8,128)(2,1)S(1)}, u32[]{:S(2)}, u32[]{:S(2)}) collective-permute-start(bf16[448,512]{1,0:T(8,128)(2,1)} %get-tuple-element.41), channel_id=1, source_target_pairs={{0,8},{8,0},{1,9},{9,1},{2,10},{10,2},{3,11},{11,3},{4,12},{12,4},... | collective-permute-start | bytes 1376264 | tf_op jit(solution)/shard_map/ppermute | solution.py:406
  19.2 104.6 %collective-permute-start.4 = (bf16[384,512]{1,0:T(8,128)(2,1)}, bf16[384,512]{1,0:T(8,128)(2,1)}, u32[]{:S(2)}, u32[]{:S(2)}) collective-permute-start(bf16[384,512]{1,0:T(8,128)(2,1)} %get-tuple-element.40), channel_id=1, source_target_pairs={{0,8},{8,0},{1,9},{9,1},{2,10},{10,2},{3,11},{11,3},{4,12},{12,4},... | collective-permute-start | bytes 1179656 | tf_op jit(solution)/shard_map/ppermute | solution.py:406
  63.7 60.7 %collective-permute-start.1 = (bf16[832,512]{1,0:T(8,128)(2,1)}, bf16[832,512]{1,0:T(8,128)(2,1)S(1)}, u32[]{:S(2)}, u32[]{:S(2)}) collective-permute-start(bf16[832,512]{1,0:T(8,128)(2,1)} %collective-permute-done.refs_0_), channel_id=1, source_target_pairs={{0,16},{16,0},{1,17},{17,1},{2,18},{18,2},{3,19},{19,3},{4,20},{20... | collective-permute-start | bytes 2555912 | tf_op jit(solution)/shard_map/ppermute | solution.py:409
  98.7 17.7 %copy-start.1 = (bf16[1,1536,4,192]{1,3,2,0:T(8,128)(2,1)S(1)}, bf16[1,1536,4,192]{1,3,2,0:T(8,128)(2,1)}, u32[]{:S(2)}) copy-start(bf16[1,1536,4,192]{1,3,2,0:T(8,128)(2,1)} %param.9) | copy-start | bytes 7077892
  114.2 19.3 %collective-permute-start.3 = (bf16[512,512]{1,0:T(8,128)(2,1)S(1)}, bf16[512,512]{1,0:T(8,128)(2,1)S(1)}, u32[]{:S(2)}, u32[]{:S(2)}) collective-permute-start(bf16[512,512]{1,0:T(8,128)(2,1)S(1)} %get-tuple-element.28), channel_id=1, source_target_pairs={{0,4},{2,6},{4,0},{6,2},{1,5},{3,7},{5,1},{7,3},{8,12},{10,14},{12... | collective-permute-start | bytes 1572872 | tf_op jit(solution)/shard_map/ppermute | solution.py:403
  114.3 25.3 %collective-permute-start.2 = (bf16[512,512]{1,0:T(8,128)(2,1)S(1)}, bf16[512,512]{1,0:T(8,128)(2,1)S(1)}, u32[]{:S(2)}, u32[]{:S(2)}) collective-permute-start(bf16[512,512]{1,0:T(8,128)(2,1)S(1)} %get-tuple-element.38), channel_id=1, source_target_pairs={{0,2},{2,0},{4,6},{6,4},{1,3},{3,1},{5,7},{7,5},{8,10},{10,8},{12,... | collective-permute-start | bytes 1572872 | tf_op jit(solution)/shard_map/ppermute | solution.py:403
  122.3 11.2 %copy-start.9 = (bf16[512,512]{1,0:T(8,128)(2,1)}, bf16[512,512]{1,0:T(8,128)(2,1)S(1)}, u32[]{:S(2)}) copy-start(bf16[512,512]{1,0:T(8,128)(2,1)S(1)} %get-tuple-element.30.refs_3_) | copy-start | bytes 1572868
  122.3 19.6 %copy-start.2 = (bf16[512,2176]{1,0:T(8,128)(2,1)}, bf16[512,2176]{1,0:T(8,128)(2,1)S(1)}, u32[]{:S(2)}) copy-start(bf16[512,2176]{1,0:T(8,128)(2,1)S(1)} %get-tuple-element.37.refs_2_.refs_4_) | copy-start | bytes 6684676
  122.3 25.1 %collective-permute-start.7 = (bf16[448,512]{1,0:T(8,128)(2,1)S(1)}, bf16[448,512]{1,0:T(8,128)(2,1)S(1)}, u32[]{:S(2)}, u32[]{:S(2)}) collective-permute-start(bf16[448,512]{1,0:T(8,128)(2,1)S(1)} %collective-permute-done.5.refs_1_), channel_id=1, source_target_pairs={{0,16},{16,0},{1,17},{17,1},{2,18},{18,2},{3,19},{19,3},{4,20},{20... | collective-permute-start | bytes 1376264 | tf_op jit(solution)/shard_map/ppermute | solution.py:409
  123.8 21.4 %collective-permute-start.6 = (bf16[384,512]{1,0:T(8,128)(2,1)}, bf16[384,512]{1,0:T(8,128)(2,1)S(1)}, u32[]{:S(2)}, u32[]{:S(2)}) collective-permute-start(bf16[384,512]{1,0:T(8,128)(2,1)} %collective-permute-done.4.refs_0_), channel_id=1, source_target_pairs={{0,16},{16,0},{1,17},{17,1},{2,18},{18,2},{3,19},{19,3},{4,20},{20... | collective-permute-start | bytes 1179656 | tf_op jit(solution)/shard_map/ppermute | solution.py:409
  124.4 35.9 %collective-permute-start.11 = (bf16[512,512]{1,0:T(8,128)(2,1)}, bf16[512,512]{1,0:T(8,128)(2,1)}, u32[]{:S(2)}, u32[]{:S(2)}) collective-permute-start(bf16[512,512]{1,0:T(8,128)(2,1)} %get-tuple-element.47), channel_id=1, source_target_pairs={{0,6},{2,4},{4,2},{6,0},{1,7},{3,5},{5,3},{7,1},{8,14},{10,12},{12... | collective-permute-start | bytes 1572872 | tf_op jit(solution)/shard_map/ppermute | solution.py:403
  133.5 11.7 %copy-start.5 = (bf16[512,512]{1,0:T(8,128)(2,1)}, bf16[512,512]{1,0:T(8,128)(2,1)S(1)}, u32[]{:S(2)}) copy-start(bf16[512,512]{1,0:T(8,128)(2,1)S(1)} %collective-permute-done.3.refs_0_) | copy-start | bytes 1572868
  133.5 22.5 %collective-permute-start.12 = (bf16[512,256]{1,0:T(8,128)(2,1)S(1)}, bf16[512,256]{1,0:T(8,128)(2,1)S(1)}, u32[]{:S(2)}, u32[]{:S(2)}) collective-permute-start(bf16[512,256]{1,0:T(8,128)(2,1)S(1)} %get-tuple-element.35), channel_id=1, source_target_pairs={{0,2},{2,0},{4,6},{6,4},{1,3},{3,1},{5,7},{7,5},{8,10},{10,8},{12,... | collective-permute-start | bytes 786440 | tf_op jit(solution)/shard_map/ppermute | solution.py:403
  139.6 5.6 %copy-start.7 = (bf16[512,512]{1,0:T(8,128)(2,1)}, bf16[512,512]{1,0:T(8,128)(2,1)S(1)}, u32[]{:S(2)}) copy-start(bf16[512,512]{1,0:T(8,128)(2,1)S(1)} %collective-permute-done.2.refs_2_) | copy-start | bytes 1572868
  139.6 19.6 %collective-permute-start.13 = (bf16[512,256]{1,0:T(8,128)(2,1)S(1)}, bf16[512,256]{1,0:T(8,128)(2,1)S(1)}, u32[]{:S(2)}, u32[]{:S(2)}) collective-permute-start(bf16[512,256]{1,0:T(8,128)(2,1)S(1)} %get-tuple-element.48), channel_id=1, source_target_pairs={{0,4},{2,6},{4,0},{6,2},{1,5},{3,7},{5,1},{7,3},{8,12},{10,14},{12... | collective-permute-start | bytes 786440 | tf_op jit(solution)/shard_map/ppermute | solution.py:403
  145.2 15.1 %copy-start.6 = (bf16[512,512]{1,0:T(8,128)(2,1)S(1)}, bf16[512,512]{1,0:T(8,128)(2,1)}, u32[]{:S(2)}) copy-start(bf16[512,512]{1,0:T(8,128)(2,1)} %copy-done.5) | copy-start | bytes 1572868
  145.2 15.1 %copy-start.8 = (bf16[512,512]{1,0:T(8,128)(2,1)S(1)}, bf16[512,512]{1,0:T(8,128)(2,1)}, u32[]{:S(2)}) copy-start(bf16[512,512]{1,0:T(8,128)(2,1)} %copy-done.7) | copy-start | bytes 1572868
  145.2 15.1 %collective-permute-start.14 = (bf16[512,256]{1,0:T(8,128)(2,1)}, bf16[512,256]{1,0:T(8,128)(2,1)}, u32[]{:S(2)}, u32[]{:S(2)}) collective-permute-start(bf16[512,256]{1,0:T(8,128)(2,1)} %get-tuple-element.49), channel_id=1, source_target_pairs={{0,6},{2,4},{4,2},{6,0},{1,7},{3,5},{5,3},{7,1},{8,14},{10,12},{12... | collective-permute-start | bytes 786440 | tf_op jit(solution)/shard_map/ppermute | solution.py:403
  155.2 14.4 %collective-permute-start.10 = (bf16[512,256]{1,0:T(8,128)(2,1)}, bf16[512,256]{1,0:T(8,128)(2,1)S(1)}, u32[]{:S(2)}, u32[]{:S(2)}) collective-permute-start(bf16[512,256]{1,0:T(8,128)(2,1)} %get-tuple-element.46), channel_id=1, source_target_pairs={{0,6},{2,4},{4,2},{6,0},{1,7},{3,5},{5,3},{7,1},{8,14},{10,12},{12... | collective-permute-start | bytes 786440 | tf_op jit(solution)/shard_map/ppermute | solution.py:403
  156.7 12.9 %collective-permute-start.8 = (bf16[512,256]{1,0:T(8,128)(2,1)}, bf16[512,256]{1,0:T(8,128)(2,1)}, u32[]{:S(2)}, u32[]{:S(2)}) collective-permute-start(bf16[512,256]{1,0:T(8,128)(2,1)} %get-tuple-element.44), channel_id=1, source_target_pairs={{0,2},{2,0},{4,6},{6,4},{1,3},{3,1},{5,7},{7,5},{8,10},{10,8},{12,... | collective-permute-start | bytes 786440 | tf_op jit(solution)/shard_map/ppermute | solution.py:403
  159.9 9.7 %collective-permute-start.9 = (bf16[512,256]{1,0:T(8,128)(2,1)}, bf16[512,256]{1,0:T(8,128)(2,1)}, u32[]{:S(2)}, u32[]{:S(2)}) collective-permute-start(bf16[512,256]{1,0:T(8,128)(2,1)} %get-tuple-element.45), channel_id=1, source_target_pairs={{0,4},{2,6},{4,0},{6,2},{1,5},{3,7},{5,1},{7,3},{8,12},{10,14},{12... | collective-permute-start | bytes 786440 | tf_op jit(solution)/shard_map/ppermute | solution.py:403
  160.3 6.1 %copy-start.3 = (bf16[512,2176]{1,0:T(8,128)(2,1)S(1)}, bf16[512,2176]{1,0:T(8,128)(2,1)}, u32[]{:S(2)}) copy-start(bf16[512,2176]{1,0:T(8,128)(2,1)} %copy-done.2) | copy-start | bytes 6684676
  (7 other events, 9.6 us)
Sparse Core Ops, SparseCore 0:
  11.9 86.7 all-gather.1

commit v7 on v4

--- a/solution.py
+++ b/solution.py
@@ -375,8 +375,8 @@
     same, other = [latent], [sibling(latent)]
     for distance in range(1, half_places):
         same.append(across(latent, distance) if distance & (distance - 1) == 0 else None)
-    far_pair = across(sent_pair, half_places)
     far_query = across(sent_query, half_places)
+    far_pair = across(after(sent_pair, far_query), half_places)
 
     joined = []
 
@@ -404,11 +404,11 @@
             same[distance] = across(after(same[distance ^ low_bit], mixed), low_bit)
             other.append(None)
         else:
-            other.append(sibling(after(same[distance], mixed, far_pair, *direct)))
-    crossed_pair = [other_part(after(far_pair, mixed))] if share == 2 else []
+            other.append(sibling(after(same[distance], mixed, far_query, *direct)))
+    crossed_query = [other_part(after(far_query, mixed))] if share == 2 else []
     for distance in range(1, half_places):
         if other[distance] is None:
-            other[distance] = sibling(after(same[distance], mixed, far_query, *crossed_pair))
+            other[distance] = sibling(after(same[distance], mixed, far_pair, *crossed_query))
         mixed = near(distance, mixed)
         arrived.append(across(mixed, distance))
     placed = []
@@ -427,7 +427,7 @@
     heads = list(range(per_part))
     rounds = [(far_query, far_pair, side * per_part)]
     if share == 2:
-        rounds.append((other_part(far_query), crossed_pair[0], (1 - side) * per_part))
+        rounds.append((crossed_query[0], other_part(far_pair), (1 - side) * per_part))
     gates, first_sent, late = [], [], []
     later = [arrived[1:-1], arrived[-1:], first_sent, []]
     for number, (queries, pairs, first) in enumerate(rounds):

time: 140 us -> 140 us (level)
  waiting for transfers between devices: 57.3 us -> 63.8 us
  starting transfers between devices: 24.8 us -> 21.1 us
    ppermute x14, waiting for transfers between devices: 56.6 us -> 61.7 us  [across(): lax.ppermute(value, 'seq', [(s, s ^ distance) for s in range(places)])]
    ppermute x14, starting transfers between devices: 20.8 us -> 17.9 us  [across(): lax.ppermute(value, 'seq', [(s, s ^ distance) for s in range(places)])]
    pallas_call x4, Pallas kernels: 20.5 us -> 18.4 us  [attend_near(): pl.pallas_call(partial(near_kernel, sizes, slot_count, distance), out_sha...]
    pallas_call x4, Pallas kernels: 19.7 us -> 21.2 us  [attend_far(): pl.pallas_call(partial(far_kernel, sizes, slot_count, distances, chosen),...]
    unnamed x35 -> x39, local copies, waits for them, and re-layouts: 6.5 us -> 5.86 us
where the time goes in v7:
time: 140 us
  waiting for transfers between devices  63.8 us (46%)
  Pallas kernels  47.1 us (34%)
  starting transfers between devices  21.1 us (15%)
  local copies, waits for them, and re-layouts  6.12 us (4%)
    ppermute x14, waiting for transfers between devices, across(): lax.ppermute(value, 'seq', [(s, s ^ distance) for s in range(places)])  61.7 us
    pallas_call x4, Pallas kernels, attend_far(): pl.pallas_call(partial(far_kernel, sizes, slot_count, distances, chosen),...  21.2 us
    pallas_call x4, Pallas kernels, attend_near(): pl.pallas_call(partial(near_kernel, sizes, slot_count, distance), out_sha...  18.4 us
    ppermute x14, starting transfers between devices, across(): lax.ppermute(value, 'seq', [(s, s ^ distance) for s in range(places)])  17.9 us
    unnamed x39, local copies, waits for them, and re-layouts  5.86 us
    pallas_call x2, Pallas kernels, place_pieces(): pl.pallas_call(partial(place_kernel, width, count), out_shape=jax.ShapeDt...  5.04 us
  transfers between devices with their start and end apart: 20, of which 6 were waited for; matrix products, arithmetic and copies ran while one was open for 1% of the time, Pallas kernels for 31%

profile of v7, /device:TPU:0, one launch (start us, length us, event | category | flops | bytes accessed | tf_op | source)
XLA Modules:
  0.0 139.7 jit_solution(11385329650818454177)
XLA Ops:
  0.0 1.7 %copy-done = bf16[1,1536,4,192]{1,3,2,0:T(8,128)(2,1)S(1)} copy-done((bf16[1,1536,4,192]{1,3,2,0:T(8,128)(2,1)S(1)}, bf16[1,1536,4,192]{1,3,2,0:T(8,128)(2,1)}, u32[]{:S(2)}) %copy-start) | copy-done | bytes 2359320
  2.8 4.0 %collective-permute-start.4 = (bf16[2,192,1536]{2,1,0:T(8,128)(2,1)}, bf16[2,192,1536]{2,1,0:T(8,128)(2,1)}, u32[]{:S(2)}, u32[]{:S(2)}) collective-permute-start(bf16[2,192,1536]{2,1,0:T(8,128)(2,1)} %pick.2), channel_id=1, source_target_pairs={{0,8},{2,10},{4,12},{6,14},{8,0},{10,2},{12,4},{14,6},{1,9},{3,11}... | collective-permute-start | bytes 3538952 | tf_op jit(solution)/shard_map/ppermute | solution.py:350
  7.0 1.4 prepare.1.same_ref
  8.5 1.6 %collective-permute-start = (bf16[256,2176]{1,0:T(8,128)(2,1)S(1)}, bf16[256,2176]{1,0:T(8,128)(2,1)S(1)}, u32[]{:S(2)}, u32[]{:S(2)}) collective-permute-start(bf16[256,2176]{1,0:T(8,128)(2,1)S(1)} %prepare.1.same_ref), channel_id=1, source_target_pairs={{0,4},{2,6},{4,0},{6,2},{8,12},{10,14},{12,8},{14,10},{1,5},{3,7},... | collective-permute-start | bytes 3342344 | tf_op jit(solution)/shard_map/ppermute | solution.py:350
  10.1 1.5 %collective-permute-start.3 = (bf16[256,2176]{1,0:T(8,128)(2,1)S(1)}, bf16[256,2176]{1,0:T(8,128)(2,1)S(1)}, u32[]{:S(2)}, u32[]{:S(2)}) collective-permute-start(bf16[256,2176]{1,0:T(8,128)(2,1)S(1)} %prepare.1.same_ref), channel_id=1, source_target_pairs={{0,2},{2,0},{4,6},{6,4},{8,10},{10,8},{12,14},{14,12},{1,3},{3,1},... | collective-permute-start | bytes 3342344 | tf_op jit(solution)/shard_map/ppermute | solution.py:350
  13.3 4.5 %attend_near.4 = (bf16[512,512]{1,0:T(8,128)(2,1)S(1)}, bf16[512,2176]{1,0:T(8,128)(2,1)S(1)}) custom-call(s32[66]{0:T(128)S(1)} %pad_add_fusion.place_ref, f32[512,256]{1,0:T(8,128)S(1)} %pad_maximum_fusion.table_ref, bf16[4,192,1536]{2,1,0:T(8,128)(2,1)S(1)} %bitcast.44, bf16[512,1024]{1,0:T(8,128)(2,1)S(1)} %bitcast.48, ...), custom_call_target="tpu_custom_call" | custom-call | flops 1024 | bytes 1024 | tf_op jit(solution)/shard_map/attend_near/pallas_call | solution.py:260
  17.8 40.6 %collective-permute-done.4.refs_0_ = bf16[2,192,1536]{2,1,0:T(8,128)(2,1)} collective-permute-done((bf16[2,192,1536]{2,1,0:T(8,128)(2,1)}, bf16[2,192,1536]{2,1,0:T(8,128)(2,1)}, u32[]{:S(2)}, u32[]{:S(2)}) %collective-permute-start.4) | collective-permute-done | bytes 1179680 | tf_op jit(solution)/shard_map/ppermute | solution.py:350
  58.5 1.5 %collective-permute-start.8 = (bf16[2,192,1536]{2,1,0:T(8,128)(2,1)}, bf16[2,192,1536]{2,1,0:T(8,128)(2,1)S(1)}, u32[]{:S(2)}, u32[]{:S(2)}) collective-permute-start(bf16[2,192,1536]{2,1,0:T(8,128)(2,1)} %collective-permute-done.4.refs_0_), channel_id=1, source_target_pairs={{0,16},{16,0},{1,17},{17,1},{2,18},{18,2},{3,19},{19,3},{4,20},{20... | collective-permute-start | bytes 3538952 | tf_op jit(solution)/shard_map/ppermute | solution.py:356
  60.5 1.5 %collective-permute-start.2 = (bf16[256,2176]{1,0:T(8,128)(2,1)S(1)}, bf16[256,2176]{1,0:T(8,128)(2,1)S(1)}, u32[]{:S(2)}, u32[]{:S(2)}) collective-permute-start(bf16[256,2176]{1,0:T(8,128)(2,1)S(1)} %collective-permute-done.same_ref), channel_id=1, source_target_pairs={{0,2},{2,0},{4,6},{6,4},{8,10},{10,8},{12,14},{14,12},{1,3},{3,1},... | collective-permute-start | bytes 3342344 | tf_op jit(solution)/shard_map/ppermute | solution.py:350
  62.8 4.5 %attend_near.5 = (bf16[512,512]{1,0:T(8,128)(2,1)S(1)}, bf16[512,2176]{1,0:T(8,128)(2,1)S(1)}) custom-call(s32[66]{0:T(128)S(1)} %pad_add_fusion.place_ref, f32[512,256]{1,0:T(8,128)S(1)} %pad_maximum_fusion.table_ref, bf16[4,192,1536]{2,1,0:T(8,128)(2,1)S(1)} %bitcast.45, bf16[512,1024]{1,0:T(8,128)(2,1)S(1)} %bitcast.50, ...), custom_call_target="tpu_custom_call" | custom-call | flops 1024 | bytes 1024 | tf_op jit(solution)/shard_map/attend_near/pallas_call | solution.py:260
  67.4 4.7 %attend_near.6 = (bf16[512,512]{1,0:T(8,128)(2,1)S(1)}, bf16[512,2176]{1,0:T(8,128)(2,1)S(1)}) custom-call(s32[66]{0:T(128)S(1)} %pad_add_fusion.place_ref, f32[512,256]{1,0:T(8,128)S(1)} %pad_maximum_fusion.table_ref, bf16[4,192,1536]{2,1,0:T(8,128)(2,1)S(1)} %bitcast.46, bf16[512,1024]{1,0:T(8,128)(2,1)S(1)} %bitcast.51, ...), custom_call_target="tpu_custom_call" | custom-call | flops 1024 | bytes 1024 | tf_op jit(solution)/shard_map/attend_near/pallas_call | solution.py:260
  72.1 15.8 %collective-permute-done.7.refs_1_ = bf16[512,512]{1,0:T(8,128)(2,1)S(1)} collective-permute-done((bf16[512,512]{1,0:T(8,128)(2,1)S(1)}, bf16[512,512]{1,0:T(8,128)(2,1)S(1)}, u32[]{:S(2)}, u32[]{:S(2)}) %collective-permute-start.7) | collective-permute-done | bytes 524320 | tf_op jit(solution)/shard_map/ppermute | solution.py:350
  89.3 1.5 %collective-permute-done.9.other_ref = bf16[256,2176]{1,0:T(8,128)(2,1)S(1)} collective-permute-done((bf16[256,2176]{1,0:T(8,128)(2,1)S(1)}, bf16[256,2176]{1,0:T(8,128)(2,1)S(1)}, u32[]{:S(2)}, u32[]{:S(2)}) %collective-permute-start.9) | collective-permute-done | bytes 1114144 | tf_op jit(solution)/shard_map/ppermute | solution.py:353
  90.8 4.5 %attend_near.7 = (bf16[512,512]{1,0:T(8,128)(2,1)S(1)}, bf16[512,2176]{1,0:T(8,128)(2,1)S(1)}) custom-call(s32[66]{0:T(128)S(1)} %pad_add_fusion.place_ref, f32[512,256]{1,0:T(8,128)S(1)} %pad_maximum_fusion.table_ref, bf16[4,192,1536]{2,1,0:T(8,128)(2,1)S(1)} %bitcast.47, bf16[512,1024]{1,0:T(8,128)(2,1)S(1)} %bitcast.52, ...), custom_call_target="tpu_custom_call" | custom-call | flops 1024 | bytes 1024 | tf_op jit(solution)/shard_map/attend_near/pallas_call | solution.py:260
  97.2 7.8 %attend_far.4 = (bf16[512,256]{1,0:T(8,128)(2,1)S(1)}, bf16[512,256]{1,0:T(8,128)(2,1)}, bf16[512,256]{1,0:T(8,128)(2,1)}) custom-call(s32[66]{0:T(128)S(1)} %pad_add_fusion.place_ref, f32[512,256]{1,0:T(8,128)S(1)} %pad_maximum_fusion.table_ref, bf16[2,192,1536]{2,1,0:T(8,128)(2,1)} %collective-permute-done.4.refs_0_, ...), custom_call_target="tpu_custom_call" | custom-call | flops 1024 | bytes 1024 | tf_op jit(solution)/shard_map/attend_far/pallas_call | solution.py:280
  107.2 2.1 %collective-permute-start.18 = (bf16[512,256]{1,0:T(8,128)(2,1)}, bf16[512,256]{1,0:T(8,128)(2,1)}, u32[]{:S(2)}, u32[]{:S(2)}) collective-permute-start(bf16[512,256]{1,0:T(8,128)(2,1)} %get-tuple-element.56), channel_id=1, source_target_pairs={{0,4},{2,6},{4,0},{6,2},{8,12},{10,14},{12,8},{14,10},{1,5},{3,7},... | collective-permute-start | bytes 786440 | tf_op jit(solution)/shard_map/ppermute | solution.py:350
  110.1 3.7 %attend_far.5.refs_7_ = bf16[512,256]{1,0:T(8,128)(2,1)S(1)} custom-call(s32[66]{0:T(128)S(1)} %pad_add_fusion.place_ref, f32[512,256]{1,0:T(8,128)S(1)} %pad_maximum_fusion.table_ref, bf16[2,192,1536]{2,1,0:T(8,128)(2,1)} %collective-permute-done.4.refs_0_, bf16[512,512]{1,0:T(8,128)(2,1)S(1)} %collective-permute-done.7.refs_1_, ...), custom_call_target="tpu_custom_call" | custom-call | flops 1024 | bytes 1024 | tf_op jit(solution)/shard_map/attend_far/pallas_call | solution.py:280
  113.7 1.9 %collective-permute-done.12.refs_3_ = bf16[512,512]{1,0:T(8,128)(2,1)S(1)} collective-permute-done((bf16[512,512]{1,0:T(8,128)(2,1)S(1)}, bf16[512,512]{1,0:T(8,128)(2,1)S(1)}, u32[]{:S(2)}, u32[]{:S(2)}) %collective-permute-start.12) | collective-permute-done | bytes 524320 | tf_op jit(solution)/shard_map/ppermute | solution.py:350
  115.6 7.0 %attend_far.6 = (bf16[512,256]{1,0:T(8,128)(2,1)}, bf16[512,256]{1,0:T(8,128)(2,1)}, bf16[512,256]{1,0:T(8,128)(2,1)}) custom-call(s32[66]{0:T(128)S(1)} %pad_add_fusion.place_ref, f32[512,256]{1,0:T(8,128)S(1)} %pad_maximum_fusion.table_ref, bf16[2,192,1536]{2,1,0:T(8,128)(2,1)S(1)} %collective-permute-done.8.refs_0_, ...), custom_call_target="tpu_custom_call" | custom-call | flops 1024 | bytes 1024 | tf_op jit(solution)/shard_map/attend_far/pallas_call | solution.py:280
  124.6 2.3 %collective-permute-start.16 = (bf16[512,256]{1,0:T(8,128)(2,1)}, bf16[512,256]{1,0:T(8,128)(2,1)}, u32[]{:S(2)}, u32[]{:S(2)}) collective-permute-start(bf16[512,256]{1,0:T(8,128)(2,1)} %get-tuple-element.55), channel_id=1, source_target_pairs={{0,6},{2,4},{4,2},{6,0},{8,14},{10,12},{12,10},{14,8},{1,7},{3,5},... | collective-permute-start | bytes 786440 | tf_op jit(solution)/shard_map/ppermute | solution.py:350
  128.3 2.7 %attend_far.7.refs_3_ = bf16[512,256]{1,0:T(8,128)(2,1)S(1)} custom-call(s32[66]{0:T(128)S(1)} %pad_add_fusion.place_ref, f32[512,256]{1,0:T(8,128)S(1)} %pad_maximum_fusion.table_ref, bf16[2,192,1536]{2,1,0:T(8,128)(2,1)S(1)} %copy-done.3, bf16[512,512]{1,0:T(8,128)(2,1)S(1)} %collective-permute-done.13.refs_1_, bf16[512,2176]{1,0:T(8,128)(2,1)S(1)} %get-tuple-element.51.refs_2_), custom_call_target="tpu_custom_call" | custom-call | flops 1024 | bytes 1024 | tf_op jit(solution)/shard_map/attend_far/pallas_call | solution.py:280
  131.1 2.9 %place_pieces.2.refs_4_ = bf16[512,4096]{1,0:T(8,128)(2,1)} custom-call(s32[24]{0:T(128)S(1)} %stack.143.offsets_ref, bf16[512,512]{1,0:T(8,128)(2,1)S(1)} %copy-done.6, bf16[512,512]{1,0:T(8,128)(2,1)S(1)} %copy-done.8, bf16[512,512]{1,0:T(8,128)(2,1)S(1)} %copy-done.10, bf16[512,512]{1,0:T(8,128)(2,1)S(1)} %copy-done.12, bf16[512,256]{1,0:T(8,128)(2,1)S(1)} %copy-done.14, ...), custom_call_target="tpu_custom_call" | custom-call | flops 1024 | bytes 1024 | tf_op jit(solution)/shard_map/place_pieces/pallas_call | solution.py:315
  134.0 3.4 %collective-permute-done.16.refs_2_ = bf16[512,256]{1,0:T(8,128)(2,1)} collective-permute-done((bf16[512,256]{1,0:T(8,128)(2,1)}, bf16[512,256]{1,0:T(8,128)(2,1)}, u32[]{:S(2)}, u32[]{:S(2)}) %collective-permute-start.16) | collective-permute-done | bytes 262176 | tf_op jit(solution)/shard_map/ppermute | solution.py:350
  137.4 2.1 %place_pieces.3 = bf16[512,4096]{1,0:T(8,128)(2,1)} custom-call(s32[8]{0:T(128)S(1)} %stack.116.offsets_ref, bf16[512,256]{1,0:T(8,128)(2,1)} %collective-permute-done.14.refs_0_, bf16[512,256]{1,0:T(8,128)(2,1)} %collective-permute-done.15.refs_1_, bf16[512,256]{1,0:T(8,128)(2,1)} %collective-permute-done.16.refs_2_, ...), custom_call_target="tpu_custom_call", output_to_operand_aliasing={{}: (5, {})} | custom-call | flops 1024 | bytes 1024 | tf_op jit(solution)/shard_map/place_pieces/pallas_call | solution.py:315
  (77 shorter events, 13.9 us)
Async XLA Ops:
  2.8 8.9 %copy-start.15 = (bf16[1,512,4,256]{3,2,1,0:T(4,128)(2,1)S(1)}, bf16[1,512,4,256]{3,2,1,0:T(4,128)(2,1)}, u32[]{:S(2)}) copy-start(bf16[1,512,4,256]{3,2,1,0:T(4,128)(2,1)} %param.10) | copy-start | bytes 3145732
  2.8 55.7 %collective-permute-start.4 = (bf16[2,192,1536]{2,1,0:T(8,128)(2,1)}, bf16[2,192,1536]{2,1,0:T(8,128)(2,1)}, u32[]{:S(2)}, u32[]{:S(2)}) collective-permute-start(bf16[2,192,1536]{2,1,0:T(8,128)(2,1)} %pick.2), channel_id=1, source_target_pairs={{0,8},{2,10},{4,12},{6,14},{8,0},{10,2},{12,4},{14,6},{1,9},{3,11}... | collective-permute-start | bytes 3538952 | tf_op jit(solution)/shard_map/ppermute | solution.py:350
  8.4 4.5 %collective-permute-start.1 = (bf16[256,2176]{1,0:T(8,128)(2,1)S(1)}, bf16[256,2176]{1,0:T(8,128)(2,1)S(1)}, u32[]{:S(2)}, u32[]{:S(2)}) collective-permute-start(bf16[256,2176]{1,0:T(8,128)(2,1)S(1)} %prepare.1.same_ref), channel_id=1, source_target_pairs={{0,1},{1,0},{2,3},{3,2},{4,5},{5,4},{6,7},{7,6},{8,9},{9,8},{10,11... | collective-permute-start | bytes 3342344 | tf_op jit(solution)/shard_map/ppermute | solution.py:353
  8.5 51.6 %collective-permute-start = (bf16[256,2176]{1,0:T(8,128)(2,1)S(1)}, bf16[256,2176]{1,0:T(8,128)(2,1)S(1)}, u32[]{:S(2)}, u32[]{:S(2)}) collective-permute-start(bf16[256,2176]{1,0:T(8,128)(2,1)S(1)} %prepare.1.same_ref), channel_id=1, source_target_pairs={{0,4},{2,6},{4,0},{6,2},{8,12},{10,14},{12,8},{14,10},{1,5},{3,7},... | collective-permute-start | bytes 3342344 | tf_op jit(solution)/shard_map/ppermute | solution.py:350
  10.1 49.9 %collective-permute-start.3 = (bf16[256,2176]{1,0:T(8,128)(2,1)S(1)}, bf16[256,2176]{1,0:T(8,128)(2,1)S(1)}, u32[]{:S(2)}, u32[]{:S(2)}) collective-permute-start(bf16[256,2176]{1,0:T(8,128)(2,1)S(1)} %prepare.1.same_ref), channel_id=1, source_target_pairs={{0,2},{2,0},{4,6},{6,4},{8,10},{10,8},{12,14},{14,12},{1,3},{3,1},... | collective-permute-start | bytes 3342344 | tf_op jit(solution)/shard_map/ppermute | solution.py:350
  17.8 49.5 %copy-start.5 = (bf16[512,512]{1,0:T(8,128)(2,1)}, bf16[512,512]{1,0:T(8,128)(2,1)S(1)}, u32[]{:S(2)}) copy-start(bf16[512,512]{1,0:T(8,128)(2,1)S(1)} %get-tuple-element.32.refs_0_) | copy-start | bytes 1572868
  58.5 29.4 %collective-permute-start.8 = (bf16[2,192,1536]{2,1,0:T(8,128)(2,1)}, bf16[2,192,1536]{2,1,0:T(8,128)(2,1)S(1)}, u32[]{:S(2)}, u32[]{:S(2)}) collective-permute-start(bf16[2,192,1536]{2,1,0:T(8,128)(2,1)} %collective-permute-done.4.refs_0_), channel_id=1, source_target_pairs={{0,16},{16,0},{1,17},{17,1},{2,18},{18,2},{3,19},{19,3},{4,20},{20... | collective-permute-start | bytes 3538952 | tf_op jit(solution)/shard_map/ppermute | solution.py:356
  60.0 2.8 %collective-permute-start.5 = (bf16[256,2176]{1,0:T(8,128)(2,1)S(1)}, bf16[256,2176]{1,0:T(8,128)(2,1)S(1)}, u32[]{:S(2)}, u32[]{:S(2)}) collective-permute-start(bf16[256,2176]{1,0:T(8,128)(2,1)S(1)} %collective-permute-done.3.same_ref), channel_id=1, source_target_pairs={{0,1},{1,0},{2,3},{3,2},{4,5},{5,4},{6,7},{7,6},{8,9},{9,8},{10,11... | collective-permute-start | bytes 3342344 | tf_op jit(solution)/shard_map/ppermute | solution.py:353
  60.0 7.3 %collective-permute-start.6 = (bf16[256,2176]{1,0:T(8,128)(2,1)S(1)}, bf16[256,2176]{1,0:T(8,128)(2,1)S(1)}, u32[]{:S(2)}, u32[]{:S(2)}) collective-permute-start(bf16[256,2176]{1,0:T(8,128)(2,1)S(1)} %collective-permute-done.same_ref), channel_id=1, source_target_pairs={{0,1},{1,0},{2,3},{3,2},{4,5},{5,4},{6,7},{7,6},{8,9},{9,8},{10,11... | collective-permute-start | bytes 3342344 | tf_op jit(solution)/shard_map/ppermute | solution.py:353
  60.5 27.4 %collective-permute-start.2 = (bf16[256,2176]{1,0:T(8,128)(2,1)S(1)}, bf16[256,2176]{1,0:T(8,128)(2,1)S(1)}, u32[]{:S(2)}, u32[]{:S(2)}) collective-permute-start(bf16[256,2176]{1,0:T(8,128)(2,1)S(1)} %collective-permute-done.same_ref), channel_id=1, source_target_pairs={{0,2},{2,0},{4,6},{6,4},{8,10},{10,8},{12,14},{14,12},{1,3},{3,1},... | collective-permute-start | bytes 3342344 | tf_op jit(solution)/shard_map/ppermute | solution.py:350
  62.1 25.8 %collective-permute-start.7 = (bf16[512,512]{1,0:T(8,128)(2,1)S(1)}, bf16[512,512]{1,0:T(8,128)(2,1)S(1)}, u32[]{:S(2)}, u32[]{:S(2)}) collective-permute-start(bf16[512,512]{1,0:T(8,128)(2,1)S(1)} %pick.3), channel_id=1, source_target_pairs={{0,8},{2,10},{4,12},{6,14},{8,0},{10,2},{12,4},{14,6},{1,9},{3,11}... | collective-permute-start | bytes 1572872 | tf_op jit(solution)/shard_map/ppermute | solution.py:350
  87.9 27.7 %copy-start.2 = (bf16[2,192,1536]{2,1,0:T(8,128)(2,1)}, bf16[2,192,1536]{2,1,0:T(8,128)(2,1)S(1)}, u32[]{:S(2)}) copy-start(bf16[2,192,1536]{2,1,0:T(8,128)(2,1)S(1)} %collective-permute-done.8.refs_0_) | copy-start | bytes 3538948
  87.9 2.8 %collective-permute-start.9 = (bf16[256,2176]{1,0:T(8,128)(2,1)S(1)}, bf16[256,2176]{1,0:T(8,128)(2,1)S(1)}, u32[]{:S(2)}, u32[]{:S(2)}) collective-permute-start(bf16[256,2176]{1,0:T(8,128)(2,1)S(1)} %collective-permute-done.2.same_ref), channel_id=1, source_target_pairs={{0,1},{1,0},{2,3},{3,2},{4,5},{5,4},{6,7},{7,6},{8,9},{9,8},{10,11... | collective-permute-start | bytes 3342344 | tf_op jit(solution)/shard_map/ppermute | solution.py:353
  88.0 17.6 %collective-permute-start.10 = (bf16[512,512]{1,0:T(8,128)(2,1)S(1)}, bf16[512,512]{1,0:T(8,128)(2,1)S(1)}, u32[]{:S(2)}, u32[]{:S(2)}) collective-permute-start(bf16[512,512]{1,0:T(8,128)(2,1)S(1)} %get-tuple-element.36), channel_id=1, source_target_pairs={{0,2},{2,0},{4,6},{6,4},{8,10},{10,8},{12,14},{14,12},{1,3},{3,1},... | collective-permute-start | bytes 1572872 | tf_op jit(solution)/shard_map/ppermute | solution.py:350
  88.7 17.7 %collective-permute-start.11 = (bf16[512,512]{1,0:T(8,128)(2,1)S(1)}, bf16[512,512]{1,0:T(8,128)(2,1)S(1)}, u32[]{:S(2)}, u32[]{:S(2)}) collective-permute-start(bf16[512,512]{1,0:T(8,128)(2,1)S(1)} %get-tuple-element.39), channel_id=1, source_target_pairs={{0,4},{2,6},{4,0},{6,2},{8,12},{10,14},{12,8},{14,10},{1,5},{3,7},... | collective-permute-start | bytes 1572872 | tf_op jit(solution)/shard_map/ppermute | solution.py:350
  95.3 20.3 %collective-permute-start.12 = (bf16[512,512]{1,0:T(8,128)(2,1)S(1)}, bf16[512,512]{1,0:T(8,128)(2,1)S(1)}, u32[]{:S(2)}, u32[]{:S(2)}) collective-permute-start(bf16[512,512]{1,0:T(8,128)(2,1)S(1)} %get-tuple-element.44), channel_id=1, source_target_pairs={{0,6},{2,4},{4,2},{6,0},{8,14},{10,12},{12,10},{14,8},{1,7},{3,5},... | collective-permute-start | bytes 1572872 | tf_op jit(solution)/shard_map/ppermute | solution.py:350
  96.2 19.4 %collective-permute-start.13 = (bf16[512,512]{1,0:T(8,128)(2,1)S(1)}, bf16[512,512]{1,0:T(8,128)(2,1)S(1)}, u32[]{:S(2)}, u32[]{:S(2)}) collective-permute-start(bf16[512,512]{1,0:T(8,128)(2,1)S(1)} %collective-permute-done.7.refs_1_), channel_id=1, source_target_pairs={{0,16},{16,0},{1,17},{17,1},{2,18},{18,2},{3,19},{19,3},{4,20},{20... | collective-permute-start | bytes 1572872 | tf_op jit(solution)/shard_map/ppermute | solution.py:356
  105.0 18.9 %collective-permute-start.17 = (bf16[512,256]{1,0:T(8,128)(2,1)S(1)}, bf16[512,256]{1,0:T(8,128)(2,1)S(1)}, u32[]{:S(2)}, u32[]{:S(2)}) collective-permute-start(bf16[512,256]{1,0:T(8,128)(2,1)S(1)} %get-tuple-element.49), channel_id=1, source_target_pairs={{0,2},{2,0},{4,6},{6,4},{8,10},{10,8},{12,14},{14,12},{1,3},{3,1},... | collective-permute-start | bytes 786440 | tf_op jit(solution)/shard_map/ppermute | solution.py:350
  107.2 19.9 %collective-permute-start.18 = (bf16[512,256]{1,0:T(8,128)(2,1)}, bf16[512,256]{1,0:T(8,128)(2,1)}, u32[]{:S(2)}, u32[]{:S(2)}) collective-permute-start(bf16[512,256]{1,0:T(8,128)(2,1)} %get-tuple-element.56), channel_id=1, source_target_pairs={{0,4},{2,6},{4,0},{6,2},{8,12},{10,14},{12,8},{14,10},{1,5},{3,7},... | collective-permute-start | bytes 786440 | tf_op jit(solution)/shard_map/ppermute | solution.py:350
  109.2 17.8 %collective-permute-start.19 = (bf16[512,256]{1,0:T(8,128)(2,1)}, bf16[512,256]{1,0:T(8,128)(2,1)}, u32[]{:S(2)}, u32[]{:S(2)}) collective-permute-start(bf16[512,256]{1,0:T(8,128)(2,1)} %get-tuple-element.57), channel_id=1, source_target_pairs={{0,6},{2,4},{4,2},{6,0},{8,14},{10,12},{12,10},{14,8},{1,7},{3,5},... | collective-permute-start | bytes 786440 | tf_op jit(solution)/shard_map/ppermute | solution.py:350
  115.6 7.0 %copy-start.11 = (bf16[512,512]{1,0:T(8,128)(2,1)}, bf16[512,512]{1,0:T(8,128)(2,1)S(1)}, u32[]{:S(2)}) copy-start(bf16[512,512]{1,0:T(8,128)(2,1)S(1)} %collective-permute-done.12.refs_3_) | copy-start | bytes 1572868
  122.6 11.4 %collective-permute-start.14 = (bf16[512,256]{1,0:T(8,128)(2,1)}, bf16[512,256]{1,0:T(8,128)(2,1)}, u32[]{:S(2)}, u32[]{:S(2)}) collective-permute-start(bf16[512,256]{1,0:T(8,128)(2,1)} %get-tuple-element.53), channel_id=1, source_target_pairs={{0,2},{2,0},{4,6},{6,4},{8,10},{10,8},{12,14},{14,12},{1,3},{3,1},... | collective-permute-start | bytes 786440 | tf_op jit(solution)/shard_map/ppermute | solution.py:350
  123.2 10.8 %collective-permute-start.15 = (bf16[512,256]{1,0:T(8,128)(2,1)}, bf16[512,256]{1,0:T(8,128)(2,1)}, u32[]{:S(2)}, u32[]{:S(2)}) collective-permute-start(bf16[512,256]{1,0:T(8,128)(2,1)} %get-tuple-element.54), channel_id=1, source_target_pairs={{0,4},{2,6},{4,0},{6,2},{8,12},{10,14},{12,8},{14,10},{1,5},{3,7},... | collective-permute-start | bytes 786440 | tf_op jit(solution)/shard_map/ppermute | solution.py:350
  124.6 12.8 %collective-permute-start.16 = (bf16[512,256]{1,0:T(8,128)(2,1)}, bf16[512,256]{1,0:T(8,128)(2,1)}, u32[]{:S(2)}, u32[]{:S(2)}) collective-permute-start(bf16[512,256]{1,0:T(8,128)(2,1)} %get-tuple-element.55), channel_id=1, source_target_pairs={{0,6},{2,4},{4,2},{6,0},{8,14},{10,12},{12,10},{14,8},{1,7},{3,5},... | collective-permute-start | bytes 786440 | tf_op jit(solution)/shard_map/ppermute | solution.py:350
  (15 other events, 41.6 us)

commit v8 on v7

--- a/solution.py
+++ b/solution.py
@@ -92,11 +92,11 @@
     )(jnp.reshape(index, (1,)).astype(jnp.int32), source)
 
 
-def attend_group(sizes, chosen, tokens_ref, weight_refs, scratch, out_ref):
+def attend_group(sizes, chosen, tokens_ref, scratch, out_refs):
     heads, q_width, kv_width, nope_width, rope_width, value_width = sizes
     query_width, pair_width = nope_width + rope_width, nope_width + value_width
     query_ref, key_ref, value_ref, turn_ref, bias_ref = scratch
-    query_weight_ref, pair_weight_ref = weight_refs
+    out_heads = heads // len(out_refs)
     tokens = tokens_ref.shape[0]
     rows = bias_ref.shape[0]
     half_width = rope_width // 2
@@ -112,18 +112,19 @@
         return lax.dot_general(left, right, dims, preferred_element_type=jnp.float32)
 
     def project(some):
-        numbers = [chosen[head] for head in some]
-        while len(numbers) < group_heads:
-            numbers.append(numbers[-1])
+        picked = [chosen[head] for head in some]
+        while len(picked) < group_heads:
+            picked.append(picked[-1])
 
         def query(low, high, picked):
-            parts = [query_weight_ref[number, low:high, :] for number in picked]
+            parts = [query_weight_ref[number, low:high, :] for query_weight_ref, _, number in picked]
             return dot(tokens_ref[:, :q_width], jnp.concatenate(parts, axis=0), NT)
 
-        rope = query(nope_width, query_width, numbers)
-        nope = query(0, nope_width, numbers[: len(some)])
-        first, last = numbers[0] * pair_width, (numbers[len(some) - 1] + 1) * pair_width
-        pair = dot(tokens_ref[:, q_width:rope_low], pair_weight_ref[:, first:last], NN)
+        rope = query(nope_width, query_width, picked)
+        nope = query(0, nope_width, picked[: len(some)])
+        latent = tokens_ref[:, q_width:rope_low]
+        pairs = [weight_ref[:, number * pair_width : (number + 1) * pair_width] for _, weight_ref, number in picked]
+        pair = dot(latent, jnp.concatenate(pairs[: len(some)], axis=1), NN)
         swapped = jnp.where(is_first, pltpu.roll(rope, nope_width - half_width, 1), pltpu.roll(rope, half_width, 1))
         turned = (rope * turn_ref[:, :nope_width] + swapped * turn_ref[:, nope_width:]) * score_scale
         for index, head in enumerate(some):
@@ -152,7 +153,8 @@
     def mix(head, half, terms):
         low, high = half * rows, (half + 1) * rows
         mixed = dot(terms, value_ref[head, :high, :], NN)
-        out_ref[low:high, head * value_width : (head + 1) * value_width] = (
+        column = head % out_heads * value_width
+        out_refs[head // out_heads][low:high, column : column + value_width] = (
             mixed[:, :value_width] / mixed[:, value_width:]
         ).astype(jnp.bfloat16)
 
@@ -224,21 +226,23 @@
     tokens_ref[pl.ds(pl.multiple_of((1 - core) * rows, rows), rows), :] = other_ref[...]
     set_up(scratch)
     set_turn(group, slot_count, place_ref, table_ref, scratch[3])
-    heads = list(range(sizes[0]))
-    attend_groups([attend_group(sizes, heads, tokens_ref, (query_weight_ref, pair_weight_ref), scratch, out_ref)])
-
-
-def far_kernel(sizes, slot_count, distances, chosen, place_ref, table_ref, *refs):
+    chosen = [(query_weight_ref, pair_weight_ref, head) for head in range(sizes[0])]
+    attend_groups([attend_group(sizes, chosen, tokens_ref, scratch, [out_ref])])
+
+
+def far_kernel(sizes, slot_count, distances, parts, arrays, place_ref, table_ref, *refs):
     slots = len(distances)
-    weight_refs, refs = refs[:2], refs[2:]
-    token_refs, out_refs, refs = refs[:slots], refs[slots : 2 * slots], refs[2 * slots :]
+    query_refs, pair_refs, refs = refs[:arrays], refs[arrays : 2 * arrays], refs[2 * arrays :]
+    token_refs, out_refs, refs = refs[:slots], refs[slots : slots + sum(parts)], refs[slots + sum(parts) :]
     bias_ref, refs = refs[0], refs[1:]
-    works = []
+    chosen = [(*both, number) for both in zip(query_refs, pair_refs) for number in range(both[0].shape[0])]
+    works, first = [], 0
     for slot in range(slots):
         scratch = [*refs[4 * slot : 4 * slot + 4], bias_ref]
         set_up(scratch, slot == 0)
         set_turn(place_ref[0] ^ distances[slot], slot_count, place_ref, table_ref, scratch[3])
-        works.append(attend_group(sizes, chosen, token_refs[slot], weight_refs, scratch, out_refs[slot]))
+        works.append(attend_group(sizes, chosen, token_refs[slot], scratch, out_refs[first : first + parts[slot]]))
+        first += parts[slot]
     attend_groups(works)
 
 
@@ -272,21 +276,23 @@
     )(place, table, query_weight, pair_weight, same, other)
 
 
-def attend_far(sizes, slot_count, distances, place, table, query_weight, pair_weight, chosen, groups):
+def attend_far(sizes, slot_count, distances, parts, place, table, queries, pairs, groups):
     tokens = groups[0].shape[0]
     slots, heads, value_width = len(groups), sizes[0], sizes[-1]
     vmem = pl.BlockSpec(memory_space=pltpu.VMEM)
     own = scratch_for(sizes, tokens)
-    return pl.pallas_call(
-        partial(far_kernel, sizes, slot_count, distances, chosen),
-        out_shape=[jax.ShapeDtypeStruct((tokens, heads * value_width), jnp.bfloat16)] * slots,
-        in_specs=[pl.BlockSpec(memory_space=pltpu.SMEM)] + [vmem] * (3 + slots),
-        out_specs=[vmem] * slots,
+    shapes = [jax.ShapeDtypeStruct((tokens, heads // part * value_width), jnp.bfloat16) for part in parts for _ in range(part)]
+    results = pl.pallas_call(
+        partial(far_kernel, sizes, slot_count, distances, parts, len(queries)),
+        out_shape=shapes,
+        in_specs=[pl.BlockSpec(memory_space=pltpu.SMEM)] + [vmem] * (1 + 2 * len(queries) + slots),
+        out_specs=[vmem] * len(shapes),
         scratch_shapes=own[4:] + own[:4] * slots,
         compiler_params=pltpu.CompilerParams(vmem_limit_bytes=VMEM_LIMIT),
         cost_estimate=LIGHT,
         name="attend_far",
-    )(place, table, query_weight, pair_weight, *groups)
+    )(place, table, *queries, *pairs, *groups)
+    return [results[sum(parts[:slot]) : sum(parts[: slot + 1])] for slot in range(slots)]
 
 
 def place_kernel(width, count, offsets_ref, *refs):
@@ -424,32 +430,33 @@
         placed.clear()
         return held
 
-    heads = list(range(per_part))
-    rounds = [(far_query, far_pair, side * per_part)]
+    queries, pairs = [far_query], [far_pair]
+    numbers = [side * per_part + index for index in range(per_part)]
     if share == 2:
-        rounds.append((crossed_query[0], other_part(far_pair), (1 - side) * per_part))
-    gates, first_sent, late = [], [], []
-    later = [arrived[1:-1], arrived[-1:], first_sent, []]
-    for number, (queries, pairs, first) in enumerate(rounds):
-        for distances in (list(range(1, half_places)), [0]):
-            mixed_some = attend_far(
-                (per_part, *sizes),
-                slot_count,
-                distances,
-                after(spot, mixed, *gates),
-                table,
-                queries,
-                pairs,
-                heads,
-                [joined[distance] for distance in distances],
-            )
-            mixed, gates = mixed_some[0], later.pop(0)
-            for distance, piece in zip(distances, mixed_some):
-                base = (place ^ distance ^ half_places) * block_width
-                received = across(piece, distance) if distance else piece
-                if number == 0 and distance:
-                    first_sent.append(received)
-                (late if number else placed).append((received, [base + (first + head) * value_width for head in heads]))
+        queries.append(crossed_query[0])
+        pairs.append(other_part(far_pair))
+        numbers += [(1 - side) * per_part + index for index in range(per_part)]
+    late, gates = [], []
+    for distances in (list(range(half_places // 2, half_places)), list(range(1, half_places // 2)) + [0]):
+        parts_of = [share if 0 < distance < half_places // 2 else 1 for distance in distances]
+        mixed_some = attend_far(
+            (len(numbers), *sizes),
+            slot_count,
+            distances,
+            parts_of,
+            after(spot, mixed, *gates),
+            table,
+            queries,
+            pairs,
+            [joined[distance] for distance in distances],
+        )
+        mixed, gates = mixed_some[0][0], arrived[1:]
+        for distance, pieces in zip(distances, mixed_some):
+            base = (place ^ distance ^ half_places) * block_width
+            each = len(numbers) // len(pieces)
+            for index, piece in enumerate(pieces):
+                spans = [base + number * value_width for number in numbers[index * each : (index + 1) * each]]
+                late.append((across(piece, distance) if distance else piece, spans))
     held = flush(None)
     placed.extend(late)
     held = flush(held)

time: 140 us -> 151 us (1.079)
  waiting for transfers between devices: 63.8 us -> 83.3 us
  Pallas kernels: 47.1 us -> 41.8 us
  local copies, waits for them, and re-layouts: 6.12 us -> 3.33 us
    ppermute x14 -> x12, waiting for transfers between devices: 61.7 us -> 77.8 us  [across(): lax.ppermute(value, 'seq', [(s, s ^ distance) for s in range(places)])]
    ppermute x2, waiting for transfers between devices: 0.01 us -> 4.84 us  [other_part(): return lax.ppermute(value, 'parts', [(p, p ^ 1) for p in range(parts)])]
    pallas_call x4 -> x2, Pallas kernels: 21.2 us -> 17.3 us  [attend_far(): pl.pallas_call(partial(far_kernel, sizes, slot_count, distances, parts, l...]
    unnamed x39 -> x19, local copies, waits for them, and re-layouts: 5.86 us -> 3.06 us
    ppermute x14 -> x12, starting transfers between devices: 17.9 us -> 16.9 us  [across(): lax.ppermute(value, 'seq', [(s, s ^ distance) for s in range(places)])]
  transfers between devices with their start and end apart: 20 -> 18, of which waited for: 6 -> 8; matrix products, arithmetic and copies ran while one was open for 1% -> 1% of each run, Pallas kernels for 31% -> 26%
where the time goes in v8:
time: 151 us; the launch traced here: 150 us
  waiting for transfers between devices  83.3 us (55%)
  Pallas kernels  41.8 us (28%)
  starting transfers between devices  20.4 us (14%)
  local copies, waits for them, and re-layouts  3.33 us (2%)
    ppermute x12, waiting for transfers between devices, across(): lax.ppermute(value, 'seq', [(s, s ^ distance) for s in range(places)])  77.8 us
    pallas_call x4, Pallas kernels, attend_near(): pl.pallas_call(partial(near_kernel, sizes, slot_count, distance), out_sha...  18.3 us
    pallas_call x2, Pallas kernels, attend_far(): pl.pallas_call(partial(far_kernel, sizes, slot_count, distances, parts, l...  17.3 us
    ppermute x12, starting transfers between devices, across(): lax.ppermute(value, 'seq', [(s, s ^ distance) for s in range(places)])  16.9 us
    ppermute x2, waiting for transfers between devices, other_part(): return lax.ppermute(value, 'parts', [(p, p ^ 1) for p in range(parts)])  4.84 us
    pallas_call x2, Pallas kernels, place_pieces(): pl.pallas_call(partial(place_kernel, width, count), out_shape=jax.ShapeDt...  4.63 us
    unnamed x19, local copies, waits for them, and re-layouts  3.06 us
  transfers between devices with their start and end apart: 18, of which 8 were waited for; matrix products, arithmetic and copies ran while one was open for 1% of the time, Pallas kernels for 26%

profile of v8, /device:TPU:0, one launch (start us, length us, event | category | flops | bytes accessed | tf_op | source)
XLA Modules:
  0.0 150.4 jit_solution(490580826892483854)
XLA Ops:
  0.0 1.7 %copy-done = bf16[1,1536,4,192]{1,3,2,0:T(8,128)(2,1)S(1)} copy-done((bf16[1,1536,4,192]{1,3,2,0:T(8,128)(2,1)S(1)}, bf16[1,1536,4,192]{1,3,2,0:T(8,128)(2,1)}, u32[]{:S(2)}) %copy-start) | copy-done | bytes 2359320
  1.8 4.1 %collective-permute-start.4 = (bf16[2,192,1536]{2,1,0:T(8,128)(2,1)S(1)}, bf16[2,192,1536]{2,1,0:T(8,128)(2,1)S(1)}, u32[]{:S(2)}, u32[]{:S(2)}) collective-permute-start(bf16[2,192,1536]{2,1,0:T(8,128)(2,1)S(1)} %pick.2), channel_id=1, source_target_pairs={{0,8},{2,10},{4,12},{6,14},{8,0},{10,2},{12,4},{14,6},{1,9},{3,11}... | collective-permute-start | bytes 3538952 | tf_op jit(solution)/shard_map/ppermute | solution.py:356
  7.5 1.6 %collective-permute-start = (bf16[256,2176]{1,0:T(8,128)(2,1)S(1)}, bf16[256,2176]{1,0:T(8,128)(2,1)S(1)}, u32[]{:S(2)}, u32[]{:S(2)}) collective-permute-start(bf16[256,2176]{1,0:T(8,128)(2,1)S(1)} %prepare.1.same_ref), channel_id=1, source_target_pairs={{0,4},{2,6},{4,0},{6,2},{8,12},{10,14},{12,8},{14,10},{1,5},{3,7},... | collective-permute-start | bytes 3342344 | tf_op jit(solution)/shard_map/ppermute | solution.py:356
  9.2 1.5 %collective-permute-start.3 = (bf16[256,2176]{1,0:T(8,128)(2,1)S(1)}, bf16[256,2176]{1,0:T(8,128)(2,1)S(1)}, u32[]{:S(2)}, u32[]{:S(2)}) collective-permute-start(bf16[256,2176]{1,0:T(8,128)(2,1)S(1)} %prepare.1.same_ref), channel_id=1, source_target_pairs={{0,2},{2,0},{4,6},{6,4},{8,10},{10,8},{12,14},{14,12},{1,3},{3,1},... | collective-permute-start | bytes 3342344 | tf_op jit(solution)/shard_map/ppermute | solution.py:356
  12.4 4.5 %attend_near.4 = (bf16[512,512]{1,0:T(8,128)(2,1)S(1)}, bf16[512,2176]{1,0:T(8,128)(2,1)S(1)}) custom-call(s32[66]{0:T(128)S(1)} %pad_add_fusion.place_ref, f32[512,256]{1,0:T(8,128)S(1)} %pad_maximum_fusion.table_ref, bf16[4,192,1536]{2,1,0:T(8,128)(2,1)S(1)} %bitcast.44, bf16[512,1024]{1,0:T(8,128)(2,1)S(1)} %bitcast.48, ...), custom_call_target="tpu_custom_call" | custom-call | flops 1024 | bytes 1024 | tf_op jit(solution)/shard_map/attend_near/pallas_call | solution.py:264
  16.9 40.3 %collective-permute-done.4.refs_0_ = bf16[2,192,1536]{2,1,0:T(8,128)(2,1)S(1)} collective-permute-done((bf16[2,192,1536]{2,1,0:T(8,128)(2,1)S(1)}, bf16[2,192,1536]{2,1,0:T(8,128)(2,1)S(1)}, u32[]{:S(2)}, u32[]{:S(2)}) %collective-permute-start.4) | collective-permute-done | bytes 1179680 | tf_op jit(solution)/shard_map/ppermute | solution.py:356
  57.2 1.5 %collective-permute-start.8 = (bf16[2,192,1536]{2,1,0:T(8,128)(2,1)S(1)}, bf16[2,192,1536]{2,1,0:T(8,128)(2,1)S(1)}, u32[]{:S(2)}, u32[]{:S(2)}) collective-permute-start(bf16[2,192,1536]{2,1,0:T(8,128)(2,1)S(1)} %collective-permute-done.4.refs_0_), channel_id=1, source_target_pairs={{0,16},{16,0},{1,17},{17,1},{2,18},{18,2},{3,19},{19,3},{4,20},{20... | collective-permute-start | bytes 3538952 | tf_op jit(solution)/shard_map/ppermute | solution.py:362
  59.3 1.5 %collective-permute-start.2 = (bf16[256,2176]{1,0:T(8,128)(2,1)S(1)}, bf16[256,2176]{1,0:T(8,128)(2,1)S(1)}, u32[]{:S(2)}, u32[]{:S(2)}) collective-permute-start(bf16[256,2176]{1,0:T(8,128)(2,1)S(1)} %collective-permute-done.same_ref), channel_id=1, source_target_pairs={{0,2},{2,0},{4,6},{6,4},{8,10},{10,8},{12,14},{14,12},{1,3},{3,1},... | collective-permute-start | bytes 3342344 | tf_op jit(solution)/shard_map/ppermute | solution.py:356
  61.9 4.5 %attend_near.5 = (bf16[512,512]{1,0:T(8,128)(2,1)S(1)}, bf16[512,2176]{1,0:T(8,128)(2,1)S(1)}) custom-call(s32[66]{0:T(128)S(1)} %pad_add_fusion.place_ref, f32[512,256]{1,0:T(8,128)S(1)} %pad_maximum_fusion.table_ref, bf16[4,192,1536]{2,1,0:T(8,128)(2,1)S(1)} %bitcast.45, bf16[512,1024]{1,0:T(8,128)(2,1)S(1)} %bitcast.50, ...), custom_call_target="tpu_custom_call" | custom-call | flops 1024 | bytes 1024 | tf_op jit(solution)/shard_map/attend_near/pallas_call | solution.py:264
  66.4 4.7 %attend_near.6 = (bf16[512,512]{1,0:T(8,128)(2,1)S(1)}, bf16[512,2176]{1,0:T(8,128)(2,1)S(1)}) custom-call(s32[66]{0:T(128)S(1)} %pad_add_fusion.place_ref, f32[512,256]{1,0:T(8,128)S(1)} %pad_maximum_fusion.table_ref, bf16[4,192,1536]{2,1,0:T(8,128)(2,1)S(1)} %bitcast.46, bf16[512,1024]{1,0:T(8,128)(2,1)S(1)} %bitcast.51, ...), custom_call_target="tpu_custom_call" | custom-call | flops 1024 | bytes 1024 | tf_op jit(solution)/shard_map/attend_near/pallas_call | solution.py:264
  71.2 15.5 %collective-permute-done.7.refs_2_ = bf16[512,512]{1,0:T(8,128)(2,1)S(1)} collective-permute-done((bf16[512,512]{1,0:T(8,128)(2,1)S(1)}, bf16[512,512]{1,0:T(8,128)(2,1)S(1)}, u32[]{:S(2)}, u32[]{:S(2)}) %collective-permute-start.7) | collective-permute-done | bytes 524320 | tf_op jit(solution)/shard_map/ppermute | solution.py:356
  89.4 4.5 %attend_near.7 = (bf16[512,512]{1,0:T(8,128)(2,1)S(1)}, bf16[512,2176]{1,0:T(8,128)(2,1)S(1)}) custom-call(s32[66]{0:T(128)S(1)} %pad_add_fusion.place_ref, f32[512,256]{1,0:T(8,128)S(1)} %pad_maximum_fusion.table_ref, bf16[4,192,1536]{2,1,0:T(8,128)(2,1)S(1)} %bitcast.47, bf16[512,1024]{1,0:T(8,128)(2,1)S(1)} %bitcast.52, ...), custom_call_target="tpu_custom_call" | custom-call | flops 1024 | bytes 1024 | tf_op jit(solution)/shard_map/attend_near/pallas_call | solution.py:264
  94.0 2.2 %collective-permute-start.15 = (bf16[512,512]{1,0:T(8,128)(2,1)S(1)}, bf16[512,512]{1,0:T(8,128)(2,1)S(1)}, u32[]{:S(2)}, u32[]{:S(2)}) collective-permute-start(bf16[512,512]{1,0:T(8,128)(2,1)S(1)} %get-tuple-element.41), channel_id=1, source_target_pairs={{0,6},{2,4},{4,2},{6,0},{8,14},{10,12},{12,10},{14,8},{1,7},{3,5},... | collective-permute-start | bytes 1572872 | tf_op jit(solution)/shard_map/ppermute | solution.py:356
  96.2 4.8 %collective-permute-done.10.refs_3_ = bf16[512,512]{1,0:T(8,128)(2,1)S(1)} collective-permute-done((bf16[512,512]{1,0:T(8,128)(2,1)S(1)}, bf16[512,512]{1,0:T(8,128)(2,1)S(1)}, u32[]{:S(2)}, u32[]{:S(2)}) %collective-permute-start.10) | collective-permute-done | bytes 524320 | tf_op jit(solution)/shard_map/ppermute | solution.py:362
  101.0 9.0 %attend_far.2 = (bf16[512,512]{1,0:T(8,128)(2,1)}, bf16[512,512]{1,0:T(8,128)(2,1)}) custom-call(s32[66]{0:T(128)S(1)} %pad_add_fusion.place_ref, f32[512,256]{1,0:T(8,128)S(1)} %pad_maximum_fusion.table_ref, bf16[2,192,1536]{2,1,0:T(8,128)(2,1)S(1)} %collective-permute-done.4.refs_0_, bf16[2,192,1536]{2,1,0:T(8,128)(2,1)S(1)} %collective-permute-done.8.refs_1_, ...), custom_call_target="tpu_custom_call" | custom-call | flops 1024 | bytes 1024 | tf_op jit(solution)/shard_map/attend_far/pallas_call | solution.py:285
  110.0 2.1 %collective-permute-start.12 = (bf16[512,512]{1,0:T(8,128)(2,1)}, bf16[512,512]{1,0:T(8,128)(2,1)}, u32[]{:S(2)}, u32[]{:S(2)}) collective-permute-start(bf16[512,512]{1,0:T(8,128)(2,1)} %get-tuple-element.46), channel_id=1, source_target_pairs={{0,6},{2,4},{4,2},{6,0},{8,14},{10,12},{12,10},{14,8},{1,7},{3,5},... | collective-permute-start | bytes 1572872 | tf_op jit(solution)/shard_map/ppermute | solution.py:356
  112.1 3.5 %collective-permute-done.15.refs_3_ = bf16[512,512]{1,0:T(8,128)(2,1)S(1)} collective-permute-done((bf16[512,512]{1,0:T(8,128)(2,1)S(1)}, bf16[512,512]{1,0:T(8,128)(2,1)S(1)}, u32[]{:S(2)}, u32[]{:S(2)}) %collective-permute-start.15) | collective-permute-done | bytes 524320 | tf_op jit(solution)/shard_map/ppermute | solution.py:356
  115.6 8.4 %attend_far.3 = (bf16[512,256]{1,0:T(8,128)(2,1)}, bf16[512,256]{1,0:T(8,128)(2,1)}, bf16[512,512]{1,0:T(8,128)(2,1)S(1)}) custom-call(s32[66]{0:T(128)S(1)} %pad_add_fusion.place_ref, f32[512,256]{1,0:T(8,128)S(1)} %pad_maximum_fusion.table_ref, bf16[2,192,1536]{2,1,0:T(8,128)(2,1)S(1)} %collective-permute-done.4.refs_0_, ...), custom_call_target="tpu_custom_call" | custom-call | flops 1024 | bytes 1024 | tf_op jit(solution)/shard_map/attend_far/pallas_call | solution.py:285
  125.4 1.4 collective-permute-start.17
  127.0 2.0 %place_pieces.2.refs_5_ = bf16[512,4096]{1,0:T(8,128)(2,1)} custom-call(s32[16]{0:T(128)S(1)} %stack.143.offsets_ref, bf16[512,512]{1,0:T(8,128)(2,1)S(1)} %get-tuple-element.29.refs_0_, bf16[512,512]{1,0:T(8,128)(2,1)S(1)} %collective-permute-done.13.refs_1_, bf16[512,512]{1,0:T(8,128)(2,1)S(1)} %collective-permute-done.14.refs_2_, ...), custom_call_target="tpu_custom_call" | custom-call | flops 1024 | bytes 1024 | tf_op jit(solution)/shard_map/place_pieces/pallas_call | solution.py:321
  129.0 8.1 %collective-permute-done.12.refs_1_ = bf16[512,512]{1,0:T(8,128)(2,1)} collective-permute-done((bf16[512,512]{1,0:T(8,128)(2,1)}, bf16[512,512]{1,0:T(8,128)(2,1)}, u32[]{:S(2)}, u32[]{:S(2)}) %collective-permute-start.12) | collective-permute-done | bytes 524320 | tf_op jit(solution)/shard_map/ppermute | solution.py:356
  137.2 5.6 %collective-permute-done.16.refs_2_ = bf16[512,256]{1,0:T(8,128)(2,1)S(1)} collective-permute-done((bf16[512,256]{1,0:T(8,128)(2,1)}, bf16[512,256]{1,0:T(8,128)(2,1)S(1)}, u32[]{:S(2)}, u32[]{:S(2)}) %collective-permute-start.16) | collective-permute-done | bytes 262176 | tf_op jit(solution)/shard_map/ppermute | solution.py:356
  142.7 4.8 %collective-permute-done.17.refs_3_ = bf16[512,256]{1,0:T(8,128)(2,1)S(1)} collective-permute-done((bf16[512,256]{1,0:T(8,128)(2,1)}, bf16[512,256]{1,0:T(8,128)(2,1)S(1)}, u32[]{:S(2)}, u32[]{:S(2)}) %collective-permute-start.17) | collective-permute-done | bytes 262176 | tf_op jit(solution)/shard_map/ppermute | solution.py:356
  147.5 2.6 %place_pieces.3 = bf16[512,4096]{1,0:T(8,128)(2,1)} custom-call(s32[16]{0:T(128)S(1)} %stack.124.offsets_ref, bf16[512,512]{1,0:T(8,128)(2,1)} %collective-permute-done.11.refs_0_, bf16[512,512]{1,0:T(8,128)(2,1)} %collective-permute-done.12.refs_1_, bf16[512,256]{1,0:T(8,128)(2,1)S(1)} %collective-permute-done.16.refs_2_, ...), custom_call_target="tpu_custom_call", output_to_operand_aliasing={{}: (6, {})} | custom-call | flops 1024 | bytes 1024 | tf_op jit(solution)/shard_map/place_pieces/pallas_call | solution.py:321
  (51 shorter events, 9.3 us)
Async XLA Ops:
  1.7 4.2 %copy-start.7 = (s32[8,8]{1,0:T(8,128)S(1)}, s32[8,8]{1,0:T(8,128)}, u32[]{:S(2)}) copy-start(s32[8,8]{1,0:T(8,128)} %param.11) | copy-start | bytes 772
  1.7 4.3 %copy-start.6 = (f32[1536]{0:T(1024)S(1)}, f32[1536]{0:T(1024)}, u32[]{:S(2)}) copy-start(f32[1536]{0:T(1024)} %param.7) | copy-start | bytes 18436
  1.7 4.3 %copy-start.8 = (f32[512]{0:T(512)S(1)}, f32[512]{0:T(512)}, u32[]{:S(2)}) copy-start(f32[512]{0:T(512)} %param.8) | copy-start | bytes 6148
  1.7 4.4 %copy-start.2 = (bf16[256,2112]{0,1:T(8,128)(2,1)S(1)}, bf16[256,2112]{0,1:T(8,128)(2,1)}, u32[]{:S(2)}) copy-start(bf16[256,2112]{0,1:T(8,128)(2,1)} %param.6) | copy-start | bytes 3244036
  1.8 55.5 %collective-permute-start.4 = (bf16[2,192,1536]{2,1,0:T(8,128)(2,1)S(1)}, bf16[2,192,1536]{2,1,0:T(8,128)(2,1)S(1)}, u32[]{:S(2)}, u32[]{:S(2)}) collective-permute-start(bf16[2,192,1536]{2,1,0:T(8,128)(2,1)S(1)} %pick.2), channel_id=1, source_target_pairs={{0,8},{2,10},{4,12},{6,14},{8,0},{10,2},{12,4},{14,6},{1,9},{3,11}... | collective-permute-start | bytes 3538952 | tf_op jit(solution)/shard_map/ppermute | solution.py:356
  6.0 4.7 %copy-start.5 = (bf16[1,512,4,256]{3,2,1,0:T(4,128)(2,1)S(1)}, bf16[1,512,4,256]{3,2,1,0:T(4,128)(2,1)}, u32[]{:S(2)}) copy-start(bf16[1,512,4,256]{3,2,1,0:T(4,128)(2,1)} %param.10) | copy-start | bytes 3145732
  7.5 4.5 %collective-permute-start.1 = (bf16[256,2176]{1,0:T(8,128)(2,1)S(1)}, bf16[256,2176]{1,0:T(8,128)(2,1)S(1)}, u32[]{:S(2)}, u32[]{:S(2)}) collective-permute-start(bf16[256,2176]{1,0:T(8,128)(2,1)S(1)} %prepare.1.same_ref), channel_id=1, source_target_pairs={{0,1},{1,0},{2,3},{3,2},{4,5},{5,4},{6,7},{7,6},{8,9},{9,8},{10,11... | collective-permute-start | bytes 3342344 | tf_op jit(solution)/shard_map/ppermute | solution.py:359
  7.5 51.2 %collective-permute-start = (bf16[256,2176]{1,0:T(8,128)(2,1)S(1)}, bf16[256,2176]{1,0:T(8,128)(2,1)S(1)}, u32[]{:S(2)}, u32[]{:S(2)}) collective-permute-start(bf16[256,2176]{1,0:T(8,128)(2,1)S(1)} %prepare.1.same_ref), channel_id=1, source_target_pairs={{0,4},{2,6},{4,0},{6,2},{8,12},{10,14},{12,8},{14,10},{1,5},{3,7},... | collective-permute-start | bytes 3342344 | tf_op jit(solution)/shard_map/ppermute | solution.py:356
  9.2 49.6 %collective-permute-start.3 = (bf16[256,2176]{1,0:T(8,128)(2,1)S(1)}, bf16[256,2176]{1,0:T(8,128)(2,1)S(1)}, u32[]{:S(2)}, u32[]{:S(2)}) collective-permute-start(bf16[256,2176]{1,0:T(8,128)(2,1)S(1)} %prepare.1.same_ref), channel_id=1, source_target_pairs={{0,2},{2,0},{4,6},{6,4},{8,10},{10,8},{12,14},{14,12},{1,3},{3,1},... | collective-permute-start | bytes 3342344 | tf_op jit(solution)/shard_map/ppermute | solution.py:356
  57.2 29.4 %collective-permute-start.8 = (bf16[2,192,1536]{2,1,0:T(8,128)(2,1)S(1)}, bf16[2,192,1536]{2,1,0:T(8,128)(2,1)S(1)}, u32[]{:S(2)}, u32[]{:S(2)}) collective-permute-start(bf16[2,192,1536]{2,1,0:T(8,128)(2,1)S(1)} %collective-permute-done.4.refs_0_), channel_id=1, source_target_pairs={{0,16},{16,0},{1,17},{17,1},{2,18},{18,2},{3,19},{19,3},{4,20},{20... | collective-permute-start | bytes 3538952 | tf_op jit(solution)/shard_map/ppermute | solution.py:362
  58.8 3.1 %collective-permute-start.5 = (bf16[256,2176]{1,0:T(8,128)(2,1)S(1)}, bf16[256,2176]{1,0:T(8,128)(2,1)S(1)}, u32[]{:S(2)}, u32[]{:S(2)}) collective-permute-start(bf16[256,2176]{1,0:T(8,128)(2,1)S(1)} %collective-permute-done.3.same_ref), channel_id=1, source_target_pairs={{0,1},{1,0},{2,3},{3,2},{4,5},{5,4},{6,7},{7,6},{8,9},{9,8},{10,11... | collective-permute-start | bytes 3342344 | tf_op jit(solution)/shard_map/ppermute | solution.py:359
  58.8 7.6 %collective-permute-start.6 = (bf16[256,2176]{1,0:T(8,128)(2,1)S(1)}, bf16[256,2176]{1,0:T(8,128)(2,1)S(1)}, u32[]{:S(2)}, u32[]{:S(2)}) collective-permute-start(bf16[256,2176]{1,0:T(8,128)(2,1)S(1)} %collective-permute-done.same_ref), channel_id=1, source_target_pairs={{0,1},{1,0},{2,3},{3,2},{4,5},{5,4},{6,7},{7,6},{8,9},{9,8},{10,11... | collective-permute-start | bytes 3342344 | tf_op jit(solution)/shard_map/ppermute | solution.py:359
  59.3 27.4 %collective-permute-start.2 = (bf16[256,2176]{1,0:T(8,128)(2,1)S(1)}, bf16[256,2176]{1,0:T(8,128)(2,1)S(1)}, u32[]{:S(2)}, u32[]{:S(2)}) collective-permute-start(bf16[256,2176]{1,0:T(8,128)(2,1)S(1)} %collective-permute-done.same_ref), channel_id=1, source_target_pairs={{0,2},{2,0},{4,6},{6,4},{8,10},{10,8},{12,14},{14,12},{1,3},{3,1},... | collective-permute-start | bytes 3342344 | tf_op jit(solution)/shard_map/ppermute | solution.py:356
  60.8 25.8 %collective-permute-start.7 = (bf16[512,512]{1,0:T(8,128)(2,1)S(1)}, bf16[512,512]{1,0:T(8,128)(2,1)S(1)}, u32[]{:S(2)}, u32[]{:S(2)}) collective-permute-start(bf16[512,512]{1,0:T(8,128)(2,1)S(1)} %pick.3), channel_id=1, source_target_pairs={{0,8},{2,10},{4,12},{6,14},{8,0},{10,2},{12,4},{14,6},{1,9},{3,11}... | collective-permute-start | bytes 1572872 | tf_op jit(solution)/shard_map/ppermute | solution.py:356
  86.7 2.8 %collective-permute-start.9 = (bf16[256,2176]{1,0:T(8,128)(2,1)S(1)}, bf16[256,2176]{1,0:T(8,128)(2,1)S(1)}, u32[]{:S(2)}, u32[]{:S(2)}) collective-permute-start(bf16[256,2176]{1,0:T(8,128)(2,1)S(1)} %collective-permute-done.2.same_ref), channel_id=1, source_target_pairs={{0,1},{1,0},{2,3},{3,2},{4,5},{5,4},{6,7},{7,6},{8,9},{9,8},{10,11... | collective-permute-start | bytes 3342344 | tf_op jit(solution)/shard_map/ppermute | solution.py:359
  86.7 14.3 %collective-permute-start.10 = (bf16[512,512]{1,0:T(8,128)(2,1)S(1)}, bf16[512,512]{1,0:T(8,128)(2,1)S(1)}, u32[]{:S(2)}, u32[]{:S(2)}) collective-permute-start(bf16[512,512]{1,0:T(8,128)(2,1)S(1)} %collective-permute-done.7.refs_2_), channel_id=1, source_target_pairs={{0,16},{16,0},{1,17},{17,1},{2,18},{18,2},{3,19},{19,3},{4,20},{20... | collective-permute-start | bytes 1572872 | tf_op jit(solution)/shard_map/ppermute | solution.py:362
  88.1 24.0 %collective-permute-start.13 = (bf16[512,512]{1,0:T(8,128)(2,1)S(1)}, bf16[512,512]{1,0:T(8,128)(2,1)S(1)}, u32[]{:S(2)}, u32[]{:S(2)}) collective-permute-start(bf16[512,512]{1,0:T(8,128)(2,1)S(1)} %get-tuple-element.33), channel_id=1, source_target_pairs={{0,2},{2,0},{4,6},{6,4},{8,10},{10,8},{12,14},{14,12},{1,3},{3,1},... | collective-permute-start | bytes 1572872 | tf_op jit(solution)/shard_map/ppermute | solution.py:356
  88.7 23.4 %collective-permute-start.14 = (bf16[512,512]{1,0:T(8,128)(2,1)S(1)}, bf16[512,512]{1,0:T(8,128)(2,1)S(1)}, u32[]{:S(2)}, u32[]{:S(2)}) collective-permute-start(bf16[512,512]{1,0:T(8,128)(2,1)S(1)} %get-tuple-element.36), channel_id=1, source_target_pairs={{0,4},{2,6},{4,0},{6,2},{8,12},{10,14},{12,8},{14,10},{1,5},{3,7},... | collective-permute-start | bytes 1572872 | tf_op jit(solution)/shard_map/ppermute | solution.py:356
  94.0 21.6 %collective-permute-start.15 = (bf16[512,512]{1,0:T(8,128)(2,1)S(1)}, bf16[512,512]{1,0:T(8,128)(2,1)S(1)}, u32[]{:S(2)}, u32[]{:S(2)}) collective-permute-start(bf16[512,512]{1,0:T(8,128)(2,1)S(1)} %get-tuple-element.41), channel_id=1, source_target_pairs={{0,6},{2,4},{4,2},{6,0},{8,14},{10,12},{12,10},{14,8},{1,7},{3,5},... | collective-permute-start | bytes 1572872 | tf_op jit(solution)/shard_map/ppermute | solution.py:356
  110.0 19.0 %collective-permute-start.11 = (bf16[512,512]{1,0:T(8,128)(2,1)}, bf16[512,512]{1,0:T(8,128)(2,1)}, u32[]{:S(2)}, u32[]{:S(2)}) collective-permute-start(bf16[512,512]{1,0:T(8,128)(2,1)} %get-tuple-element.45), channel_id=1, source_target_pairs={{0,4},{2,6},{4,0},{6,2},{8,12},{10,14},{12,8},{14,10},{1,5},{3,7},... | collective-permute-start | bytes 1572872 | tf_op jit(solution)/shard_map/ppermute | solution.py:356
  110.0 27.2 %collective-permute-start.12 = (bf16[512,512]{1,0:T(8,128)(2,1)}, bf16[512,512]{1,0:T(8,128)(2,1)}, u32[]{:S(2)}, u32[]{:S(2)}) collective-permute-start(bf16[512,512]{1,0:T(8,128)(2,1)} %get-tuple-element.46), channel_id=1, source_target_pairs={{0,6},{2,4},{4,2},{6,0},{8,14},{10,12},{12,10},{14,8},{1,7},{3,5},... | collective-permute-start | bytes 1572872 | tf_op jit(solution)/shard_map/ppermute | solution.py:356
  124.8 17.9 %collective-permute-start.16 = (bf16[512,256]{1,0:T(8,128)(2,1)}, bf16[512,256]{1,0:T(8,128)(2,1)S(1)}, u32[]{:S(2)}, u32[]{:S(2)}) collective-permute-start(bf16[512,256]{1,0:T(8,128)(2,1)} %get-tuple-element.50), channel_id=1, source_target_pairs={{0,2},{2,0},{4,6},{6,4},{8,10},{10,8},{12,14},{14,12},{1,3},{3,1},... | collective-permute-start | bytes 786440 | tf_op jit(solution)/shard_map/ppermute | solution.py:356
  125.4 22.1 %collective-permute-start.17 = (bf16[512,256]{1,0:T(8,128)(2,1)}, bf16[512,256]{1,0:T(8,128)(2,1)S(1)}, u32[]{:S(2)}, u32[]{:S(2)}) collective-permute-start(bf16[512,256]{1,0:T(8,128)(2,1)} %get-tuple-element.51), channel_id=1, source_target_pairs={{0,2},{2,0},{4,6},{6,4},{8,10},{10,8},{12,14},{14,12},{1,3},{3,1},... | collective-permute-start | bytes 786440 | tf_op jit(solution)/shard_map/ppermute | solution.py:356
  127.0 20.5 %copy-start.4 = (bf16[512,512]{1,0:T(8,128)(2,1)S(1)}, bf16[512,512]{1,0:T(8,128)(2,1)}, u32[]{:S(2)}) copy-start(bf16[512,512]{1,0:T(8,128)(2,1)} %copy-done.3) | copy-start | bytes 1572868
  (3 other events, 4.1 us)

commit v9 on v8

--- a/solution.py
+++ b/solution.py
@@ -19,6 +19,16 @@
 def frequencies(lane, half_width):
     steps = lax.rem(lane, half_width).astype(jnp.float32)
     return jnp.exp(steps * (-math.log(10000.0) / half_width))
+
+
+def swapped_bits(slot):
+    return (slot & ~3) | (slot & 1) << 1 | (slot & 2) >> 1
+
+
+def distance_of(slot, core, half_places):
+    if half_places < 4:
+        return slot
+    return jnp.where(core == 0, slot, swapped_bits(slot))
 
 
 def prepare_kernel(q_width, kv_width, slot_count, place_ref, latents_ref, gain_ref, out_ref):
@@ -219,8 +229,9 @@
         turn_ref[index * block : (index + 1) * block, :] = table_ref[pl.ds(position, block), :]
 
 
-def near_kernel(sizes, slot_count, distance, place_ref, table_ref, query_weight_ref, pair_weight_ref, same_ref, other_ref, out_ref, tokens_ref, *scratch):
-    core, group = place_ref[1], place_ref[0] ^ distance
+def near_kernel(sizes, slot_count, slot, half_places, place_ref, table_ref, query_weight_ref, pair_weight_ref, same_ref, other_ref, out_ref, tokens_ref, *scratch):
+    core = place_ref[1]
+    group = place_ref[0] ^ distance_of(slot, core, half_places)
     rows = same_ref.shape[0]
     tokens_ref[pl.ds(pl.multiple_of(core * rows, rows), rows), :] = same_ref[...]
     tokens_ref[pl.ds(pl.multiple_of((1 - core) * rows, rows), rows), :] = other_ref[...]
@@ -230,8 +241,8 @@
     attend_groups([attend_group(sizes, chosen, tokens_ref, scratch, [out_ref])])
 
 
-def far_kernel(sizes, slot_count, distances, parts, arrays, place_ref, table_ref, *refs):
-    slots = len(distances)
+def far_kernel(sizes, slot_count, numbers, half_places, parts, arrays, place_ref, table_ref, *refs):
+    slots = len(numbers)
     query_refs, pair_refs, refs = refs[:arrays], refs[arrays : 2 * arrays], refs[2 * arrays :]
     token_refs, out_refs, refs = refs[:slots], refs[slots : slots + sum(parts)], refs[slots + sum(parts) :]
     bias_ref, refs = refs[0], refs[1:]
@@ -240,7 +251,8 @@
     for slot in range(slots):
         scratch = [*refs[4 * slot : 4 * slot + 4], bias_ref]
         set_up(scratch, slot == 0)
-        set_turn(place_ref[0] ^ distances[slot], slot_count, place_ref, table_ref, scratch[3])
+        group = place_ref[0] ^ distance_of(numbers[slot], place_ref[1], half_places)
+        set_turn(group, slot_count, place_ref, table_ref, scratch[3])
         works.append(attend_group(sizes, chosen, token_refs[slot], scratch, out_refs[first : first + parts[slot]]))
         first += parts[slot]
     attend_groups(works)
@@ -257,12 +269,12 @@
     ]
 
 
-def attend_near(sizes, slot_count, distance, place, table, query_weight, pair_weight, same, other):
+def attend_near(sizes, slot_count, slot, half_places, place, table, query_weight, pair_weight, same, other):
     rows, width = same.shape
     heads, value_width = sizes[0], sizes[-1]
     vmem = pl.BlockSpec(memory_space=pltpu.VMEM)
     return pl.pallas_call(
-        partial(near_kernel, sizes, slot_count, distance),
+        partial(near_kernel, sizes, slot_count, slot, half_places),
         out_shape=[
             jax.ShapeDtypeStruct((2 * rows, heads * value_width), jnp.bfloat16),
             jax.ShapeDtypeStruct((2 * rows, width), jnp.bfloat16),
@@ -276,14 +288,14 @@
     )(place, table, query_weight, pair_weight, same, other)
 
 
-def attend_far(sizes, slot_count, distances, parts, place, table, queries, pairs, groups):
+def attend_far(sizes, slot_count, numbers, half_places, parts, place, table, queries, pairs, groups):
     tokens = groups[0].shape[0]
     slots, heads, value_width = len(groups), sizes[0], sizes[-1]
     vmem = pl.BlockSpec(memory_space=pltpu.VMEM)
     own = scratch_for(sizes, tokens)
     shapes = [jax.ShapeDtypeStruct((tokens, heads // part * value_width), jnp.bfloat16) for part in parts for _ in range(part)]
     results = pl.pallas_call(
-        partial(far_kernel, sizes, slot_count, distances, parts, len(queries)),
+        partial(far_kernel, sizes, slot_count, numbers, half_places, parts, len(queries)),
         out_shape=shapes,
         in_specs=[pl.BlockSpec(memory_space=pltpu.SMEM)] + [vmem] * (1 + 2 * len(queries) + slots),
         out_specs=[vmem] * len(shapes),
@@ -352,8 +364,16 @@
     block_width = local_heads * value_width
     sizes = (q_width, kv_width, nope_width, rope_width, value_width)
 
-    def across(value, distance):
-        return lax.ppermute(value, "seq", [(s, s ^ distance) for s in range(places)])
+    def away(slot):
+        return place ^ distance_of(slot, core, half_places)
+
+    def opposite(value):
+        return lax.ppermute(value, "seq", [(s, s ^ half_places) for s in range(places)])
+
+    def across(value, slot):
+        other_slot = slot if half_places < 4 else swapped_bits(slot)
+        pairs = [(2 * s + c, 2 * (s ^ distance) + c) for s in range(places) for c, distance in enumerate((slot, other_slot))]
+        return lax.ppermute(value, ("seq", "head"), pairs)
 
     def sibling(value):
         return lax.ppermute(value, "head", [(0, 1), (1, 0)])
@@ -381,8 +401,8 @@
     same, other = [latent], [sibling(latent)]
     for distance in range(1, half_places):
         same.append(across(latent, distance) if distance & (distance - 1) == 0 else None)
-    far_query = across(sent_query, half_places)
-    far_pair = across(after(sent_pair, far_query), half_places)
+    far_query = opposite(sent_query)
+    far_pair = opposite(after(sent_pair, far_query))
 
     joined = []
 
@@ -391,6 +411,7 @@
             (local_heads, *sizes),
             slot_count,
             distance,
+            half_places,
             spot,
             table,
             own_query,
@@ -404,22 +425,25 @@
     mixed = near(0)
     arrived = [mixed]
     direct = [entry for entry in same[1:] if entry is not None]
+    partner = [slot if half_places < 4 else swapped_bits(slot) for slot in range(half_places)]
     for distance in range(1, half_places):
         if same[distance] is None:
             low_bit = distance & -distance
             same[distance] = across(after(same[distance ^ low_bit], mixed), low_bit)
+    for distance in range(1, half_places):
+        if distance & (distance - 1) == 0:
+            other.append(sibling(after(same[partner[distance]], mixed, far_query, *direct)))
+        else:
             other.append(None)
-        else:
-            other.append(sibling(after(same[distance], mixed, far_query, *direct)))
     crossed_query = [other_part(after(far_query, mixed))] if share == 2 else []
     for distance in range(1, half_places):
         if other[distance] is None:
-            other[distance] = sibling(after(same[distance], mixed, far_pair, *crossed_query))
+            other[distance] = sibling(after(same[partner[distance]], mixed, far_pair, *crossed_query))
         mixed = near(distance, mixed)
         arrived.append(across(mixed, distance))
     placed = []
     for distance in range(half_places):
-        base = (place ^ distance) * block_width
+        base = away(distance) * block_width
         placed.append((arrived[distance], [base + head * value_width for head in range(local_heads)]))
 
     out_width = places * block_width
@@ -443,6 +467,7 @@
             (len(numbers), *sizes),
             slot_count,
             distances,
+            half_places,
             parts_of,
             after(spot, mixed, *gates),
             table,
@@ -452,7 +477,7 @@
         )
         mixed, gates = mixed_some[0][0], arrived[1:]
         for distance, pieces in zip(distances, mixed_some):
-            base = (place ^ distance ^ half_places) * block_width
+            base = (away(distance) ^ half_places) * block_width
             each = len(numbers) // len(pieces)
             for index, piece in enumerate(pieces):
                 spans = [base + number * value_width for number in numbers[index * each : (index + 1) * each]]

time: 151 us -> 138 us (0.914)
  waiting for transfers between devices: 83.3 us -> 67.6 us
  starting transfers between devices: 20.4 us -> 23.7 us
    ppermute x12, waiting for transfers between devices: 77.8 us -> 60.6 us  [the longest x2 50 us: opposite(): lax.ppermute(value, 'seq', [(s, s ^ half_places) for s in range(places)])]
    ppermute x12, starting transfers between devices: 16.9 us -> 19.3 us  [the longest x10 14.1 us: across(): return lax.ppermute(value, ('seq', 'head'), pairs)]
    ppermute x2, waiting for transfers between devices: 4.84 us -> 6.97 us  [other_part(): return lax.ppermute(value, 'parts', [(p, p ^ 1) for p in range(parts)])]
  transfers between devices with their start and end apart: 18 -> 18, of which waited for: 8 -> 9; matrix products, arithmetic and copies ran while one was open for 1% -> 1% of each run, Pallas kernels for 26% -> 28%
where the time goes in v9:
time: 138 us
  waiting for transfers between devices  67.6 us (49%)
  Pallas kernels  41.8 us (30%)
  starting transfers between devices  23.7 us (17%)
  local copies, waits for them, and re-layouts  3.33 us (2%)
    ppermute x2, waiting for transfers between devices, opposite(): lax.ppermute(value, 'seq', [(s, s ^ half_places) for s in range(places)])  50 us
    pallas_call x4, Pallas kernels, attend_near(): pl.pallas_call(partial(near_kernel, sizes, slot_count, slot, half_places)...  18.3 us
    pallas_call x2, Pallas kernels, attend_far(): pl.pallas_call(partial(far_kernel, sizes, slot_count, numbers, half_place...  17.4 us
    ppermute x10, starting transfers between devices, across(): return lax.ppermute(value, ('seq', 'head'), pairs)  14.1 us
    ppermute x10, waiting for transfers between devices, across(): return lax.ppermute(value, ('seq', 'head'), pairs)  10.6 us
    ppermute x2, waiting for transfers between devices, other_part(): return lax.ppermute(value, 'parts', [(p, p ^ 1) for p in range(parts)])  6.97 us
    ppermute x2, starting transfers between devices, opposite(): lax.ppermute(value, 'seq', [(s, s ^ half_places) for s in range(places)])  5.19 us
    pallas_call x2, Pallas kernels, place_pieces(): pl.pallas_call(partial(place_kernel, width, count), out_shape=jax.ShapeDt...  4.63 us
  transfers between devices with their start and end apart: 18, of which 9 were waited for; matrix products, arithmetic and copies ran while one was open for 1% of the time, Pallas kernels for 28%

profile of v9, /device:TPU:0, one launch (start us, length us, event | category | flops | bytes accessed | tf_op | source)
XLA Modules:
  0.0 138.0 jit_solution(15426098421363154558)
XLA Ops:
  0.0 1.7 %copy-done = bf16[1,1536,4,192]{1,3,2,0:T(8,128)(2,1)S(1)} copy-done((bf16[1,1536,4,192]{1,3,2,0:T(8,128)(2,1)S(1)}, bf16[1,1536,4,192]{1,3,2,0:T(8,128)(2,1)}, u32[]{:S(2)}) %copy-start) | copy-done | bytes 2359320
  1.8 4.1 %collective-permute-start.4 = (bf16[2,192,1536]{2,1,0:T(8,128)(2,1)S(1)}, bf16[2,192,1536]{2,1,0:T(8,128)(2,1)S(1)}, u32[]{:S(2)}, u32[]{:S(2)}) collective-permute-start(bf16[2,192,1536]{2,1,0:T(8,128)(2,1)S(1)} %pick.2), channel_id=1, source_target_pairs={{0,8},{2,10},{4,12},{6,14},{8,0},{10,2},{12,4},{14,6},{1,9},{3,11}... | collective-permute-start | bytes 3538952 | tf_op jit(solution)/shard_map/ppermute | solution.py:371
  7.5 1.6 %collective-permute-start = (bf16[256,2176]{1,0:T(8,128)(2,1)S(1)}, bf16[256,2176]{1,0:T(8,128)(2,1)S(1)}, u32[]{:S(2)}, u32[]{:S(2)}) collective-permute-start(bf16[256,2176]{1,0:T(8,128)(2,1)S(1)} %prepare.1.same_ref), channel_id=1, source_target_pairs={{0,4},{1,3},{2,6},{3,1},{4,0},{5,7},{6,2},{7,5},{8,12},{9,11},{10,... | collective-permute-start | bytes 3342344 | tf_op jit(solution)/shard_map/ppermute | solution.py:376
  9.2 1.5 %collective-permute-start.3 = (bf16[256,2176]{1,0:T(8,128)(2,1)S(1)}, bf16[256,2176]{1,0:T(8,128)(2,1)S(1)}, u32[]{:S(2)}, u32[]{:S(2)}) collective-permute-start(bf16[256,2176]{1,0:T(8,128)(2,1)S(1)} %prepare.1.same_ref), channel_id=1, source_target_pairs={{0,2},{1,5},{2,0},{3,7},{4,6},{5,1},{6,4},{7,3},{8,10},{9,13},{10,... | collective-permute-start | bytes 3342344 | tf_op jit(solution)/shard_map/ppermute | solution.py:376
  12.4 4.5 %attend_near.4 = (bf16[512,512]{1,0:T(8,128)(2,1)S(1)}, bf16[512,2176]{1,0:T(8,128)(2,1)S(1)}) custom-call(s32[66]{0:T(128)S(1)} %pad_add_fusion.place_ref, f32[512,256]{1,0:T(8,128)S(1)} %pad_maximum_fusion.table_ref, bf16[4,192,1536]{2,1,0:T(8,128)(2,1)S(1)} %bitcast.44, bf16[512,1024]{1,0:T(8,128)(2,1)S(1)} %bitcast.48, ...), custom_call_target="tpu_custom_call" | custom-call | flops 1024 | bytes 1024 | tf_op jit(solution)/shard_map/attend_near/pallas_call | solution.py:276
  16.9 40.3 %collective-permute-done.4.refs_0_ = bf16[2,192,1536]{2,1,0:T(8,128)(2,1)S(1)} collective-permute-done((bf16[2,192,1536]{2,1,0:T(8,128)(2,1)S(1)}, bf16[2,192,1536]{2,1,0:T(8,128)(2,1)S(1)}, u32[]{:S(2)}, u32[]{:S(2)}) %collective-permute-start.4) | collective-permute-done | bytes 1179680 | tf_op jit(solution)/shard_map/ppermute | solution.py:371
  57.2 1.5 %collective-permute-start.8 = (bf16[2,192,1536]{2,1,0:T(8,128)(2,1)S(1)}, bf16[2,192,1536]{2,1,0:T(8,128)(2,1)S(1)}, u32[]{:S(2)}, u32[]{:S(2)}) collective-permute-start(bf16[2,192,1536]{2,1,0:T(8,128)(2,1)S(1)} %collective-permute-done.4.refs_0_), channel_id=1, source_target_pairs={{0,16},{16,0},{1,17},{17,1},{2,18},{18,2},{3,19},{19,3},{4,20},{20... | collective-permute-start | bytes 3538952 | tf_op jit(solution)/shard_map/ppermute | solution.py:382
  59.3 1.6 %collective-permute-start.2 = (bf16[256,2176]{1,0:T(8,128)(2,1)S(1)}, bf16[256,2176]{1,0:T(8,128)(2,1)S(1)}, u32[]{:S(2)}, u32[]{:S(2)}) collective-permute-start(bf16[256,2176]{1,0:T(8,128)(2,1)S(1)} %collective-permute-done.same_ref), channel_id=1, source_target_pairs={{0,2},{1,5},{2,0},{3,7},{4,6},{5,1},{6,4},{7,3},{8,10},{9,13},{10,... | collective-permute-start | bytes 3342344 | tf_op jit(solution)/shard_map/ppermute | solution.py:376
  62.1 4.5 %attend_near.5 = (bf16[512,512]{1,0:T(8,128)(2,1)S(1)}, bf16[512,2176]{1,0:T(8,128)(2,1)S(1)}) custom-call(s32[66]{0:T(128)S(1)} %pad_add_fusion.place_ref, f32[512,256]{1,0:T(8,128)S(1)} %pad_maximum_fusion.table_ref, bf16[4,192,1536]{2,1,0:T(8,128)(2,1)S(1)} %bitcast.45, bf16[512,1024]{1,0:T(8,128)(2,1)S(1)} %bitcast.50, ...), custom_call_target="tpu_custom_call" | custom-call | flops 1024 | bytes 1024 | tf_op jit(solution)/shard_map/attend_near/pallas_call | solution.py:276
  66.6 4.7 %attend_near.6 = (bf16[512,512]{1,0:T(8,128)(2,1)S(1)}, bf16[512,2176]{1,0:T(8,128)(2,1)S(1)}) custom-call(s32[66]{0:T(128)S(1)} %pad_add_fusion.place_ref, f32[512,256]{1,0:T(8,128)S(1)} %pad_maximum_fusion.table_ref, bf16[4,192,1536]{2,1,0:T(8,128)(2,1)S(1)} %bitcast.46, bf16[512,1024]{1,0:T(8,128)(2,1)S(1)} %bitcast.51, ...), custom_call_target="tpu_custom_call" | custom-call | flops 1024 | bytes 1024 | tf_op jit(solution)/shard_map/attend_near/pallas_call | solution.py:276
  71.3 9.7 %collective-permute-done.7.refs_2_ = bf16[512,512]{1,0:T(8,128)(2,1)S(1)} collective-permute-done((bf16[512,512]{1,0:T(8,128)(2,1)S(1)}, bf16[512,512]{1,0:T(8,128)(2,1)S(1)}, u32[]{:S(2)}, u32[]{:S(2)}) %collective-permute-start.7) | collective-permute-done | bytes 524320 | tf_op jit(solution)/shard_map/ppermute | solution.py:371
  81.0 3.3 %collective-permute-done.8.refs_1_ = bf16[2,192,1536]{2,1,0:T(8,128)(2,1)S(1)} collective-permute-done((bf16[2,192,1536]{2,1,0:T(8,128)(2,1)S(1)}, bf16[2,192,1536]{2,1,0:T(8,128)(2,1)S(1)}, u32[]{:S(2)}, u32[]{:S(2)}) %collective-permute-start.8) | collective-permute-done | bytes 1179680 | tf_op jit(solution)/shard_map/ppermute | solution.py:382
  85.1 1.5 %collective-permute-start.10 = (bf16[512,512]{1,0:T(8,128)(2,1)S(1)}, bf16[512,512]{1,0:T(8,128)(2,1)S(1)}, u32[]{:S(2)}, u32[]{:S(2)}) collective-permute-start(bf16[512,512]{1,0:T(8,128)(2,1)S(1)} %collective-permute-done.7.refs_2_), channel_id=1, source_target_pairs={{0,16},{16,0},{1,17},{17,1},{2,18},{18,2},{3,19},{19,3},{4,20},{20... | collective-permute-start | bytes 1572872 | tf_op jit(solution)/shard_map/ppermute | solution.py:382
  88.0 1.8 %collective-permute-start.14 = (bf16[512,512]{1,0:T(8,128)(2,1)S(1)}, bf16[512,512]{1,0:T(8,128)(2,1)S(1)}, u32[]{:S(2)}, u32[]{:S(2)}) collective-permute-start(bf16[512,512]{1,0:T(8,128)(2,1)S(1)} %get-tuple-element.36), channel_id=1, source_target_pairs={{0,4},{1,3},{2,6},{3,1},{4,0},{5,7},{6,2},{7,5},{8,12},{9,11},{10,... | collective-permute-start | bytes 1572872 | tf_op jit(solution)/shard_map/ppermute | solution.py:376
  89.8 4.5 %attend_near.7 = (bf16[512,512]{1,0:T(8,128)(2,1)S(1)}, bf16[512,2176]{1,0:T(8,128)(2,1)S(1)}) custom-call(s32[66]{0:T(128)S(1)} %pad_add_fusion.place_ref, f32[512,256]{1,0:T(8,128)S(1)} %pad_maximum_fusion.table_ref, bf16[4,192,1536]{2,1,0:T(8,128)(2,1)S(1)} %bitcast.47, bf16[512,1024]{1,0:T(8,128)(2,1)S(1)} %bitcast.52, ...), custom_call_target="tpu_custom_call" | custom-call | flops 1024 | bytes 1024 | tf_op jit(solution)/shard_map/attend_near/pallas_call | solution.py:276
  95.2 3.7 %collective-permute-done.10.refs_3_ = bf16[512,512]{1,0:T(8,128)(2,1)S(1)} collective-permute-done((bf16[512,512]{1,0:T(8,128)(2,1)S(1)}, bf16[512,512]{1,0:T(8,128)(2,1)S(1)}, u32[]{:S(2)}, u32[]{:S(2)}) %collective-permute-start.10) | collective-permute-done | bytes 524320 | tf_op jit(solution)/shard_map/ppermute | solution.py:382
  98.9 9.0 %attend_far.2 = (bf16[512,512]{1,0:T(8,128)(2,1)}, bf16[512,512]{1,0:T(8,128)(2,1)}) custom-call(s32[66]{0:T(128)S(1)} %pad_add_fusion.place_ref, f32[512,256]{1,0:T(8,128)S(1)} %pad_maximum_fusion.table_ref, bf16[2,192,1536]{2,1,0:T(8,128)(2,1)S(1)} %collective-permute-done.4.refs_0_, bf16[2,192,1536]{2,1,0:T(8,128)(2,1)S(1)} %collective-permute-done.8.refs_1_, ...), custom_call_target="tpu_custom_call" | custom-call | flops 1024 | bytes 1024 | tf_op jit(solution)/shard_map/attend_far/pallas_call | solution.py:297
  107.9 2.3 %collective-permute-start.11 = (bf16[512,512]{1,0:T(8,128)(2,1)}, bf16[512,512]{1,0:T(8,128)(2,1)}, u32[]{:S(2)}, u32[]{:S(2)}) collective-permute-start(bf16[512,512]{1,0:T(8,128)(2,1)} %get-tuple-element.45), channel_id=1, source_target_pairs={{0,4},{1,3},{2,6},{3,1},{4,0},{5,7},{6,2},{7,5},{8,12},{9,11},{10,... | collective-permute-start | bytes 1572872 | tf_op jit(solution)/shard_map/ppermute | solution.py:376
  112.9 8.4 %attend_far.3 = (bf16[512,256]{1,0:T(8,128)(2,1)}, bf16[512,256]{1,0:T(8,128)(2,1)}, bf16[512,512]{1,0:T(8,128)(2,1)S(1)}) custom-call(s32[66]{0:T(128)S(1)} %pad_add_fusion.place_ref, f32[512,256]{1,0:T(8,128)S(1)} %pad_maximum_fusion.table_ref, bf16[2,192,1536]{2,1,0:T(8,128)(2,1)S(1)} %collective-permute-done.4.refs_0_, ...), custom_call_target="tpu_custom_call" | custom-call | flops 1024 | bytes 1024 | tf_op jit(solution)/shard_map/attend_far/pallas_call | solution.py:297
  122.1 1.7 %collective-permute-start.16 = (bf16[512,256]{1,0:T(8,128)(2,1)}, bf16[512,256]{1,0:T(8,128)(2,1)S(1)}, u32[]{:S(2)}, u32[]{:S(2)}) collective-permute-start(bf16[512,256]{1,0:T(8,128)(2,1)} %get-tuple-element.50), channel_id=1, source_target_pairs={{0,2},{1,5},{2,0},{3,7},{4,6},{5,1},{6,4},{7,3},{8,10},{9,13},{10,... | collective-permute-start | bytes 786440 | tf_op jit(solution)/shard_map/ppermute | solution.py:376
  124.3 2.0 %place_pieces.2.refs_5_ = bf16[512,4096]{1,0:T(8,128)(2,1)} custom-call(s32[16]{0:T(128)S(1)} %stack.143.offsets_ref, bf16[512,512]{1,0:T(8,128)(2,1)S(1)} %get-tuple-element.29.refs_0_, bf16[512,512]{1,0:T(8,128)(2,1)S(1)} %collective-permute-done.13.refs_1_, bf16[512,512]{1,0:T(8,128)(2,1)S(1)} %collective-permute-done.14.refs_2_, ...), custom_call_target="tpu_custom_call" | custom-call | flops 1024 | bytes 1024 | tf_op jit(solution)/shard_map/place_pieces/pallas_call | solution.py:333
  126.3 5.8 %collective-permute-done.12.refs_1_ = bf16[512,512]{1,0:T(8,128)(2,1)} collective-permute-done((bf16[512,512]{1,0:T(8,128)(2,1)}, bf16[512,512]{1,0:T(8,128)(2,1)}, u32[]{:S(2)}, u32[]{:S(2)}) %collective-permute-start.12) | collective-permute-done | bytes 524320 | tf_op jit(solution)/shard_map/ppermute | solution.py:376
  132.3 2.8 %collective-permute-done.17.refs_3_ = bf16[512,256]{1,0:T(8,128)(2,1)S(1)} collective-permute-done((bf16[512,256]{1,0:T(8,128)(2,1)}, bf16[512,256]{1,0:T(8,128)(2,1)S(1)}, u32[]{:S(2)}, u32[]{:S(2)}) %collective-permute-start.17) | collective-permute-done | bytes 262176 | tf_op jit(solution)/shard_map/ppermute | solution.py:376
  135.1 2.6 %place_pieces.3 = bf16[512,4096]{1,0:T(8,128)(2,1)} custom-call(s32[16]{0:T(128)S(1)} %stack.124.offsets_ref, bf16[512,512]{1,0:T(8,128)(2,1)} %collective-permute-done.11.refs_0_, bf16[512,512]{1,0:T(8,128)(2,1)} %collective-permute-done.12.refs_1_, bf16[512,256]{1,0:T(8,128)(2,1)S(1)} %collective-permute-done.16.refs_2_, ...), custom_call_target="tpu_custom_call", output_to_operand_aliasing={{}: (6, {})} | custom-call | flops 1024 | bytes 1024 | tf_op jit(solution)/shard_map/place_pieces/pallas_call | solution.py:333
  (51 shorter events, 12.3 us)
Async XLA Ops:
  1.7 4.2 %copy-start.7 = (s32[8,8]{1,0:T(8,128)S(1)}, s32[8,8]{1,0:T(8,128)}, u32[]{:S(2)}) copy-start(s32[8,8]{1,0:T(8,128)} %param.11) | copy-start | bytes 772
  1.7 4.3 %copy-start.6 = (f32[1536]{0:T(1024)S(1)}, f32[1536]{0:T(1024)}, u32[]{:S(2)}) copy-start(f32[1536]{0:T(1024)} %param.7) | copy-start | bytes 18436
  1.7 4.3 %copy-start.8 = (f32[512]{0:T(512)S(1)}, f32[512]{0:T(512)}, u32[]{:S(2)}) copy-start(f32[512]{0:T(512)} %param.8) | copy-start | bytes 6148
  1.7 4.4 %copy-start.2 = (bf16[256,2112]{0,1:T(8,128)(2,1)S(1)}, bf16[256,2112]{0,1:T(8,128)(2,1)}, u32[]{:S(2)}) copy-start(bf16[256,2112]{0,1:T(8,128)(2,1)} %param.6) | copy-start | bytes 3244036
  1.8 55.5 %collective-permute-start.4 = (bf16[2,192,1536]{2,1,0:T(8,128)(2,1)S(1)}, bf16[2,192,1536]{2,1,0:T(8,128)(2,1)S(1)}, u32[]{:S(2)}, u32[]{:S(2)}) collective-permute-start(bf16[2,192,1536]{2,1,0:T(8,128)(2,1)S(1)} %pick.2), channel_id=1, source_target_pairs={{0,8},{2,10},{4,12},{6,14},{8,0},{10,2},{12,4},{14,6},{1,9},{3,11}... | collective-permute-start | bytes 3538952 | tf_op jit(solution)/shard_map/ppermute | solution.py:371
  6.0 4.7 %copy-start.5 = (bf16[1,512,4,256]{3,2,1,0:T(4,128)(2,1)S(1)}, bf16[1,512,4,256]{3,2,1,0:T(4,128)(2,1)}, u32[]{:S(2)}) copy-start(bf16[1,512,4,256]{3,2,1,0:T(4,128)(2,1)} %param.10) | copy-start | bytes 3145732
  7.5 4.5 %collective-permute-start.1 = (bf16[256,2176]{1,0:T(8,128)(2,1)S(1)}, bf16[256,2176]{1,0:T(8,128)(2,1)S(1)}, u32[]{:S(2)}, u32[]{:S(2)}) collective-permute-start(bf16[256,2176]{1,0:T(8,128)(2,1)S(1)} %prepare.1.same_ref), channel_id=1, source_target_pairs={{0,1},{1,0},{2,3},{3,2},{4,5},{5,4},{6,7},{7,6},{8,9},{9,8},{10,11... | collective-permute-start | bytes 3342344 | tf_op jit(solution)/shard_map/ppermute | solution.py:379
  7.5 51.2 %collective-permute-start = (bf16[256,2176]{1,0:T(8,128)(2,1)S(1)}, bf16[256,2176]{1,0:T(8,128)(2,1)S(1)}, u32[]{:S(2)}, u32[]{:S(2)}) collective-permute-start(bf16[256,2176]{1,0:T(8,128)(2,1)S(1)} %prepare.1.same_ref), channel_id=1, source_target_pairs={{0,4},{1,3},{2,6},{3,1},{4,0},{5,7},{6,2},{7,5},{8,12},{9,11},{10,... | collective-permute-start | bytes 3342344 | tf_op jit(solution)/shard_map/ppermute | solution.py:376
  9.2 49.6 %collective-permute-start.3 = (bf16[256,2176]{1,0:T(8,128)(2,1)S(1)}, bf16[256,2176]{1,0:T(8,128)(2,1)S(1)}, u32[]{:S(2)}, u32[]{:S(2)}) collective-permute-start(bf16[256,2176]{1,0:T(8,128)(2,1)S(1)} %prepare.1.same_ref), channel_id=1, source_target_pairs={{0,2},{1,5},{2,0},{3,7},{4,6},{5,1},{6,4},{7,3},{8,10},{9,13},{10,... | collective-permute-start | bytes 3342344 | tf_op jit(solution)/shard_map/ppermute | solution.py:376
  57.2 27.1 %collective-permute-start.8 = (bf16[2,192,1536]{2,1,0:T(8,128)(2,1)S(1)}, bf16[2,192,1536]{2,1,0:T(8,128)(2,1)S(1)}, u32[]{:S(2)}, u32[]{:S(2)}) collective-permute-start(bf16[2,192,1536]{2,1,0:T(8,128)(2,1)S(1)} %collective-permute-done.4.refs_0_), channel_id=1, source_target_pairs={{0,16},{16,0},{1,17},{17,1},{2,18},{18,2},{3,19},{19,3},{4,20},{20... | collective-permute-start | bytes 3538952 | tf_op jit(solution)/shard_map/ppermute | solution.py:382
  58.8 3.3 %collective-permute-start.5 = (bf16[256,2176]{1,0:T(8,128)(2,1)S(1)}, bf16[256,2176]{1,0:T(8,128)(2,1)S(1)}, u32[]{:S(2)}, u32[]{:S(2)}) collective-permute-start(bf16[256,2176]{1,0:T(8,128)(2,1)S(1)} %collective-permute-done.same_ref), channel_id=1, source_target_pairs={{0,1},{1,0},{2,3},{3,2},{4,5},{5,4},{6,7},{7,6},{8,9},{9,8},{10,11... | collective-permute-start | bytes 3342344 | tf_op jit(solution)/shard_map/ppermute | solution.py:379
  59.0 7.6 %collective-permute-start.6 = (bf16[256,2176]{1,0:T(8,128)(2,1)S(1)}, bf16[256,2176]{1,0:T(8,128)(2,1)S(1)}, u32[]{:S(2)}, u32[]{:S(2)}) collective-permute-start(bf16[256,2176]{1,0:T(8,128)(2,1)S(1)} %collective-permute-done.3.same_ref), channel_id=1, source_target_pairs={{0,1},{1,0},{2,3},{3,2},{4,5},{5,4},{6,7},{7,6},{8,9},{9,8},{10,11... | collective-permute-start | bytes 3342344 | tf_op jit(solution)/shard_map/ppermute | solution.py:379
  59.3 21.8 %collective-permute-start.2 = (bf16[256,2176]{1,0:T(8,128)(2,1)S(1)}, bf16[256,2176]{1,0:T(8,128)(2,1)S(1)}, u32[]{:S(2)}, u32[]{:S(2)}) collective-permute-start(bf16[256,2176]{1,0:T(8,128)(2,1)S(1)} %collective-permute-done.same_ref), channel_id=1, source_target_pairs={{0,2},{1,5},{2,0},{3,7},{4,6},{5,1},{6,4},{7,3},{8,10},{9,13},{10,... | collective-permute-start | bytes 3342344 | tf_op jit(solution)/shard_map/ppermute | solution.py:376
  61.0 20.1 %collective-permute-start.7 = (bf16[512,512]{1,0:T(8,128)(2,1)S(1)}, bf16[512,512]{1,0:T(8,128)(2,1)S(1)}, u32[]{:S(2)}, u32[]{:S(2)}) collective-permute-start(bf16[512,512]{1,0:T(8,128)(2,1)S(1)} %pick.3), channel_id=1, source_target_pairs={{0,8},{2,10},{4,12},{6,14},{8,0},{10,2},{12,4},{14,6},{1,9},{3,11}... | collective-permute-start | bytes 1572872 | tf_op jit(solution)/shard_map/ppermute | solution.py:371
  84.3 5.5 %collective-permute-start.9 = (bf16[256,2176]{1,0:T(8,128)(2,1)S(1)}, bf16[256,2176]{1,0:T(8,128)(2,1)S(1)}, u32[]{:S(2)}, u32[]{:S(2)}) collective-permute-start(bf16[256,2176]{1,0:T(8,128)(2,1)S(1)} %collective-permute-done.2.same_ref), channel_id=1, source_target_pairs={{0,1},{1,0},{2,3},{3,2},{4,5},{5,4},{6,7},{7,6},{8,9},{9,8},{10,11... | collective-permute-start | bytes 3342344 | tf_op jit(solution)/shard_map/ppermute | solution.py:379
  85.1 13.8 %collective-permute-start.10 = (bf16[512,512]{1,0:T(8,128)(2,1)S(1)}, bf16[512,512]{1,0:T(8,128)(2,1)S(1)}, u32[]{:S(2)}, u32[]{:S(2)}) collective-permute-start(bf16[512,512]{1,0:T(8,128)(2,1)S(1)} %collective-permute-done.7.refs_2_), channel_id=1, source_target_pairs={{0,16},{16,0},{1,17},{17,1},{2,18},{18,2},{3,19},{19,3},{4,20},{20... | collective-permute-start | bytes 1572872 | tf_op jit(solution)/shard_map/ppermute | solution.py:382
  86.6 25.0 %collective-permute-start.13 = (bf16[512,512]{1,0:T(8,128)(2,1)S(1)}, bf16[512,512]{1,0:T(8,128)(2,1)S(1)}, u32[]{:S(2)}, u32[]{:S(2)}) collective-permute-start(bf16[512,512]{1,0:T(8,128)(2,1)S(1)} %get-tuple-element.33), channel_id=1, source_target_pairs={{0,2},{1,5},{2,0},{3,7},{4,6},{5,1},{6,4},{7,3},{8,10},{9,13},{10,... | collective-permute-start | bytes 1572872 | tf_op jit(solution)/shard_map/ppermute | solution.py:376
  88.0 23.6 %collective-permute-start.14 = (bf16[512,512]{1,0:T(8,128)(2,1)S(1)}, bf16[512,512]{1,0:T(8,128)(2,1)S(1)}, u32[]{:S(2)}, u32[]{:S(2)}) collective-permute-start(bf16[512,512]{1,0:T(8,128)(2,1)S(1)} %get-tuple-element.36), channel_id=1, source_target_pairs={{0,4},{1,3},{2,6},{3,1},{4,0},{5,7},{6,2},{7,5},{8,12},{9,11},{10,... | collective-permute-start | bytes 1572872 | tf_op jit(solution)/shard_map/ppermute | solution.py:376
  94.3 18.5 %collective-permute-start.15 = (bf16[512,512]{1,0:T(8,128)(2,1)S(1)}, bf16[512,512]{1,0:T(8,128)(2,1)S(1)}, u32[]{:S(2)}, u32[]{:S(2)}) collective-permute-start(bf16[512,512]{1,0:T(8,128)(2,1)S(1)} %get-tuple-element.41), channel_id=1, source_target_pairs={{0,6},{1,7},{2,4},{3,5},{4,2},{5,3},{6,0},{7,1},{8,14},{9,15},{10,... | collective-permute-start | bytes 1572872 | tf_op jit(solution)/shard_map/ppermute | solution.py:376
  107.9 18.4 %collective-permute-start.11 = (bf16[512,512]{1,0:T(8,128)(2,1)}, bf16[512,512]{1,0:T(8,128)(2,1)}, u32[]{:S(2)}, u32[]{:S(2)}) collective-permute-start(bf16[512,512]{1,0:T(8,128)(2,1)} %get-tuple-element.45), channel_id=1, source_target_pairs={{0,4},{1,3},{2,6},{3,1},{4,0},{5,7},{6,2},{7,5},{8,12},{9,11},{10,... | collective-permute-start | bytes 1572872 | tf_op jit(solution)/shard_map/ppermute | solution.py:376
  110.1 21.9 %collective-permute-start.12 = (bf16[512,512]{1,0:T(8,128)(2,1)}, bf16[512,512]{1,0:T(8,128)(2,1)}, u32[]{:S(2)}, u32[]{:S(2)}) collective-permute-start(bf16[512,512]{1,0:T(8,128)(2,1)} %get-tuple-element.46), channel_id=1, source_target_pairs={{0,6},{1,7},{2,4},{3,5},{4,2},{5,3},{6,0},{7,1},{8,14},{9,15},{10,... | collective-permute-start | bytes 1572872 | tf_op jit(solution)/shard_map/ppermute | solution.py:376
  122.1 10.3 %collective-permute-start.16 = (bf16[512,256]{1,0:T(8,128)(2,1)}, bf16[512,256]{1,0:T(8,128)(2,1)S(1)}, u32[]{:S(2)}, u32[]{:S(2)}) collective-permute-start(bf16[512,256]{1,0:T(8,128)(2,1)} %get-tuple-element.50), channel_id=1, source_target_pairs={{0,2},{1,5},{2,0},{3,7},{4,6},{5,1},{6,4},{7,3},{8,10},{9,13},{10,... | collective-permute-start | bytes 786440 | tf_op jit(solution)/shard_map/ppermute | solution.py:376
  123.8 11.3 %collective-permute-start.17 = (bf16[512,256]{1,0:T(8,128)(2,1)}, bf16[512,256]{1,0:T(8,128)(2,1)S(1)}, u32[]{:S(2)}, u32[]{:S(2)}) collective-permute-start(bf16[512,256]{1,0:T(8,128)(2,1)} %get-tuple-element.51), channel_id=1, source_target_pairs={{0,2},{1,5},{2,0},{3,7},{4,6},{5,1},{6,4},{7,3},{8,10},{9,13},{10,... | collective-permute-start | bytes 786440 | tf_op jit(solution)/shard_map/ppermute | solution.py:376
  124.3 10.8 %copy-start.4 = (bf16[512,512]{1,0:T(8,128)(2,1)S(1)}, bf16[512,512]{1,0:T(8,128)(2,1)}, u32[]{:S(2)}) copy-start(bf16[512,512]{1,0:T(8,128)(2,1)} %copy-done.3) | copy-start | bytes 1572868
  (3 other events, 4.1 us)

commit v10 on v9

--- a/solution.py
+++ b/solution.py
@@ -432,13 +432,12 @@
             same[distance] = across(after(same[distance ^ low_bit], mixed), low_bit)
     for distance in range(1, half_places):
         if distance & (distance - 1) == 0:
-            other.append(sibling(after(same[partner[distance]], mixed, far_query, *direct)))
+            other.append(sibling(after(same[partner[distance]], mixed, *direct)))
         else:
             other.append(None)
-    crossed_query = [other_part(after(far_query, mixed))] if share == 2 else []
     for distance in range(1, half_places):
         if other[distance] is None:
-            other[distance] = sibling(after(same[partner[distance]], mixed, far_pair, *crossed_query))
+            other[distance] = sibling(after(same[partner[distance]], mixed, far_query))
         mixed = near(distance, mixed)
         arrived.append(across(mixed, distance))
     placed = []
@@ -454,34 +453,43 @@
         placed.clear()
         return held
 
-    queries, pairs = [far_query], [far_pair]
-    numbers = [side * per_part + index for index in range(per_part)]
+    straight = (far_query, far_pair, [side * per_part + index for index in range(per_part)])
+    sets = [straight]
     if share == 2:
-        queries.append(crossed_query[0])
-        pairs.append(other_part(far_pair))
-        numbers += [(1 - side) * per_part + index for index in range(per_part)]
-    late, gates = [], []
-    for distances in (list(range(half_places // 2, half_places)), list(range(1, half_places // 2)) + [0]):
-        parts_of = [share if 0 < distance < half_places // 2 else 1 for distance in distances]
+        crossed_query, crossed_pair = other_part(far_query), other_part(after(far_pair, mixed))
+        sets.append((crossed_query, crossed_pair, [(1 - side) * per_part + index for index in range(per_part)]))
+    neighbours, middle = list(range(1, half_places)), half_places // 2
+    calls = [(sets[:1], neighbours, 1, arrived[1:])]
+    if share == 2:
+        calls.append((sets[1:], list(range(middle, half_places)), 1, []))
+        calls.append((sets[1:], list(range(1, middle)), per_part, []))
+    calls.append((sets, [0], 1, []))
+    late, sent = [], []
+    for chosen, slots, parts_of, gates in calls:
+        numbers = [number for _, _, some in chosen for number in some]
         mixed_some = attend_far(
             (len(numbers), *sizes),
             slot_count,
-            distances,
+            slots,
             half_places,
-            parts_of,
-            after(spot, mixed, *gates),
+            [parts_of] * len(slots),
+            after(spot, mixed, *gates, *(sent if slots == [0] else [])),
             table,
-            queries,
-            pairs,
-            [joined[distance] for distance in distances],
+            [query for query, _, _ in chosen],
+            [pair for _, pair, _ in chosen],
+            [joined[slot] for slot in slots],
         )
-        mixed, gates = mixed_some[0][0], arrived[1:]
-        for distance, pieces in zip(distances, mixed_some):
-            base = (away(distance) ^ half_places) * block_width
+        mixed = mixed_some[0][0]
+        for slot, pieces in zip(slots, mixed_some):
+            base = (away(slot) ^ half_places) * block_width
             each = len(numbers) // len(pieces)
             for index, piece in enumerate(pieces):
                 spans = [base + number * value_width for number in numbers[index * each : (index + 1) * each]]
-                late.append((across(piece, distance) if distance else piece, spans))
+                if slot:
+                    piece = across(piece, slot)
+                    if slots == neighbours:
+                        sent.append(piece)
+                (placed if slots == neighbours else late).append((piece, spans))
     held = flush(None)
     placed.extend(late)
     held = flush(held)

time: 138 us -> 158 us (1.14)
  local copies, waits for them, and re-layouts: 3.33 us -> 12.8 us
  starting transfers between devices: 23.7 us -> 29.8 us
  Pallas kernels: 41.8 us -> 47.4 us
  waiting for transfers between devices: 67.6 us -> 65.1 us
    ppermute x10 -> x13, waiting for transfers between devices: 10.6 us -> 49.6 us  [across(): return lax.ppermute(value, ('seq', 'head'), pairs)]
    ppermute x2, waiting for transfers between devices: 50 us -> 15.5 us  [opposite(): lax.ppermute(value, 'seq', [(s, s ^ half_places) for s in range(places)])]
    unnamed x19 -> x41, local copies, waits for them, and re-layouts: 3.06 us -> 11.8 us
    ppermute x2, waiting for transfers between devices: 6.97 us -> 0.01 us  [other_part(): return lax.ppermute(value, 'parts', [(p, p ^ 1) for p in range(parts)])]
    ppermute x10 -> x13, starting transfers between devices: 14.1 us -> 18.3 us  [across(): return lax.ppermute(value, ('seq', 'head'), pairs)]
    ppermute x4, starting transfers between devices: 1.34 us -> 4.42 us  [sibling(): return lax.ppermute(value, 'head', [(0, 1), (1, 0)])]
    pallas_call x2 -> x4, Pallas kernels: 17.4 us -> 20.3 us  [attend_far(): pl.pallas_call(partial(far_kernel, sizes, slot_count, numbers, half_place...]
    pallas_call x4, Pallas kernels: 18.3 us -> 20.5 us  [attend_near(): pl.pallas_call(partial(near_kernel, sizes, slot_count, slot, half_places)...]
  transfers between devices with their start and end apart: 18 -> 21, of which waited for: 9 -> 6; matrix products, arithmetic and copies ran while one was open for 1% -> 1% of each run, Pallas kernels for 28% -> 28%
where the time goes in v10:
time: 158 us; the launch traced here: 157 us
  waiting for transfers between devices  65.1 us (41%)
  Pallas kernels  47.4 us (30%)
  starting transfers between devices  29.8 us (19%)
  local copies, waits for them, and re-layouts  12.8 us (8%)
  other arithmetic  1.84 us (1%)
    ppermute x13, waiting for transfers between devices, across(): return lax.ppermute(value, ('seq', 'head'), pairs)  49.6 us
    pallas_call x4, Pallas kernels, attend_near(): pl.pallas_call(partial(near_kernel, sizes, slot_count, slot, half_places)...  20.5 us
    pallas_call x4, Pallas kernels, attend_far(): pl.pallas_call(partial(far_kernel, sizes, slot_count, numbers, half_place...  20.3 us
    ppermute x13, starting transfers between devices, across(): return lax.ppermute(value, ('seq', 'head'), pairs)  18.3 us
    ppermute x2, waiting for transfers between devices, opposite(): lax.ppermute(value, 'seq', [(s, s ^ half_places) for s in range(places)])  15.5 us
    unnamed x41, local copies, waits for them, and re-layouts  11.8 us
    pallas_call x2, Pallas kernels, place_pieces(): pl.pallas_call(partial(place_kernel, width, count), out_shape=jax.ShapeDt...  5.07 us
    ppermute x2, starting transfers between devices, opposite(): lax.ppermute(value, 'seq', [(s, s ^ half_places) for s in range(places)])  4.8 us
  transfers between devices with their start and end apart: 21, of which 6 were waited for; matrix products, arithmetic and copies ran while one was open for 1% of the time, Pallas kernels for 28%

profile of v10, /device:TPU:0, one launch (start us, length us, event | category | flops | bytes accessed | tf_op | source)
XLA Modules:
  0.0 157.3 jit_solution(11377784176896401675)
XLA Ops:
  4.7 2.7 %collective-permute-start = (bf16[256,2176]{1,0:T(8,128)(2,1)S(1)}, bf16[256,2176]{1,0:T(8,128)(2,1)}, u32[]{:S(2)}, u32[]{:S(2)}) collective-permute-start(bf16[256,2176]{1,0:T(8,128)(2,1)S(1)} %prepare.1.same_ref), channel_id=1, source_target_pairs={{0,4},{1,3},{2,6},{3,1},{4,0},{5,7},{6,2},{7,5},{8,12},{9,11},{10,... | collective-permute-start | bytes 3342344 | tf_op jit(solution)/shard_map/ppermute | solution.py:376
  8.9 1.7 %copy-done = bf16[1,1536,4,192]{1,3,2,0:T(8,128)(2,1)S(1)} copy-done((bf16[1,1536,4,192]{1,3,2,0:T(8,128)(2,1)S(1)}, bf16[1,1536,4,192]{1,3,2,0:T(8,128)(2,1)}, u32[]{:S(2)}) %copy-start) | copy-done | bytes 2359320
  10.6 2.7 %collective-permute-start.6 = (bf16[2,192,1536]{2,1,0:T(8,128)(2,1)S(1)}, bf16[2,192,1536]{2,1,0:T(8,128)(2,1)S(1)}, u32[]{:S(2)}, u32[]{:S(2)}) collective-permute-start(bf16[2,192,1536]{2,1,0:T(8,128)(2,1)S(1)} %pick.2), channel_id=1, source_target_pairs={{0,8},{2,10},{4,12},{6,14},{8,0},{10,2},{12,4},{14,6},{1,9},{3,11}... | collective-permute-start | bytes 3538952 | tf_op jit(solution)/shard_map/ppermute | solution.py:371
  15.0 5.3 %attend_near.4 = (bf16[512,512]{1,0:T(8,128)(2,1)S(1)}, bf16[512,2176]{1,0:T(8,128)(2,1)S(1)}) custom-call(s32[66]{0:T(128)S(1)} %pad_add_fusion.place_ref, f32[512,256]{1,0:T(8,128)S(1)} %pad_maximum_fusion.table_ref, bf16[4,192,1536]{2,1,0:T(8,128)(2,1)S(1)} %bitcast.44, bf16[512,1024]{1,0:T(8,128)(2,1)S(1)} %bitcast.48, ...), custom_call_target="tpu_custom_call" | custom-call | flops 1024 | bytes 1024 | tf_op jit(solution)/shard_map/attend_near/pallas_call | solution.py:276
  21.0 31.9 %collective-permute-done.same_ref = bf16[256,2176]{1,0:T(8,128)(2,1)} collective-permute-done((bf16[256,2176]{1,0:T(8,128)(2,1)S(1)}, bf16[256,2176]{1,0:T(8,128)(2,1)}, u32[]{:S(2)}, u32[]{:S(2)}) %collective-permute-start) | collective-permute-done | bytes 1114144 | tf_op jit(solution)/shard_map/ppermute | solution.py:376
  54.1 2.7 %collective-permute-start.2 = (bf16[256,2176]{1,0:T(8,128)(2,1)}, bf16[256,2176]{1,0:T(8,128)(2,1)S(1)}, u32[]{:S(2)}, u32[]{:S(2)}) collective-permute-start(bf16[256,2176]{1,0:T(8,128)(2,1)} %collective-permute-done.same_ref), channel_id=1, source_target_pairs={{0,2},{1,5},{2,0},{3,7},{4,6},{5,1},{6,4},{7,3},{8,10},{9,13},{10,... | collective-permute-start | bytes 3342344 | tf_op jit(solution)/shard_map/ppermute | solution.py:376
  56.8 5.3 %attend_near.5 = (bf16[512,512]{1,0:T(8,128)(2,1)S(1)}, bf16[512,2176]{1,0:T(8,128)(2,1)S(1)}) custom-call(s32[66]{0:T(128)S(1)} %pad_add_fusion.place_ref, f32[512,256]{1,0:T(8,128)S(1)} %pad_maximum_fusion.table_ref, bf16[4,192,1536]{2,1,0:T(8,128)(2,1)S(1)} %bitcast.45, bf16[512,1024]{1,0:T(8,128)(2,1)S(1)} %bitcast.49, ...), custom_call_target="tpu_custom_call" | custom-call | flops 1024 | bytes 1024 | tf_op jit(solution)/shard_map/attend_near/pallas_call | solution.py:276
  62.1 5.4 %attend_near.6 = (bf16[512,512]{1,0:T(8,128)(2,1)S(1)}, bf16[512,2176]{1,0:T(8,128)(2,1)S(1)}) custom-call(s32[66]{0:T(128)S(1)} %pad_add_fusion.place_ref, f32[512,256]{1,0:T(8,128)S(1)} %pad_maximum_fusion.table_ref, bf16[4,192,1536]{2,1,0:T(8,128)(2,1)S(1)} %bitcast.46, bf16[512,1024]{1,0:T(8,128)(2,1)S(1)} %bitcast.50, ...), custom_call_target="tpu_custom_call" | custom-call | flops 1024 | bytes 1024 | tf_op jit(solution)/shard_map/attend_near/pallas_call | solution.py:276
  67.6 2.9 %collective-permute-done.2.same_ref = bf16[256,2176]{1,0:T(8,128)(2,1)S(1)} collective-permute-done((bf16[256,2176]{1,0:T(8,128)(2,1)}, bf16[256,2176]{1,0:T(8,128)(2,1)S(1)}, u32[]{:S(2)}, u32[]{:S(2)}) %collective-permute-start.2) | collective-permute-done | bytes 1114144 | tf_op jit(solution)/shard_map/ppermute | solution.py:376
  70.5 2.7 %collective-permute-start.7 = (bf16[256,2176]{1,0:T(8,128)(2,1)S(1)}, bf16[256,2176]{1,0:T(8,128)(2,1)S(1)}, u32[]{:S(2)}, u32[]{:S(2)}) collective-permute-start(bf16[256,2176]{1,0:T(8,128)(2,1)S(1)} %collective-permute-done.2.same_ref), channel_id=1, source_target_pairs={{0,1},{1,0},{2,3},{3,2},{4,5},{5,4},{6,7},{7,6},{8,9},{9,8},{10,11... | collective-permute-start | bytes 3342344 | tf_op jit(solution)/shard_map/ppermute | solution.py:379
  73.2 1.9 %collective-permute-start.12 = (bf16[2,192,1536]{2,1,0:T(8,128)(2,1)S(1)}, bf16[2,192,1536]{2,1,0:T(8,128)(2,1)S(1)}, u32[]{:S(2)}, u32[]{:S(2)}) collective-permute-start(bf16[2,192,1536]{2,1,0:T(8,128)(2,1)S(1)} %collective-permute-done.6.refs_0_), channel_id=1, source_target_pairs={{0,16},{16,0},{1,17},{17,1},{2,18},{18,2},{3,19},{19,3},{4,20},{20... | collective-permute-start | bytes 3538952 | tf_op jit(solution)/shard_map/ppermute | solution.py:382
  75.2 2.2 %collective-permute-start.11 = (bf16[512,512]{1,0:T(8,128)(2,1)S(1)}, bf16[512,512]{1,0:T(8,128)(2,1)S(1)}, u32[]{:S(2)}, u32[]{:S(2)}) collective-permute-start(bf16[512,512]{1,0:T(8,128)(2,1)S(1)} %pick.3), channel_id=1, source_target_pairs={{0,8},{2,10},{4,12},{6,14},{8,0},{10,2},{12,4},{14,6},{1,9},{3,11}... | collective-permute-start | bytes 1572872 | tf_op jit(solution)/shard_map/ppermute | solution.py:371
  78.6 2.1 %collective-permute-start.9 = (bf16[512,512]{1,0:T(8,128)(2,1)S(1)}, bf16[512,512]{1,0:T(8,128)(2,1)S(1)}, u32[]{:S(2)}, u32[]{:S(2)}) collective-permute-start(bf16[512,512]{1,0:T(8,128)(2,1)S(1)} %get-tuple-element.40), channel_id=1, source_target_pairs={{0,4},{1,3},{2,6},{3,1},{4,0},{5,7},{6,2},{7,5},{8,12},{9,11},{10,... | collective-permute-start | bytes 1572872 | tf_op jit(solution)/shard_map/ppermute | solution.py:376
  80.7 4.5 %attend_near.7 = (bf16[512,512]{1,0:T(8,128)(2,1)S(1)}, bf16[512,2176]{1,0:T(8,128)(2,1)S(1)}) custom-call(s32[66]{0:T(128)S(1)} %pad_add_fusion.place_ref, f32[512,256]{1,0:T(8,128)S(1)} %pad_maximum_fusion.table_ref, bf16[4,192,1536]{2,1,0:T(8,128)(2,1)S(1)} %bitcast.47, bf16[512,1024]{1,0:T(8,128)(2,1)S(1)} %bitcast.52, ...), custom_call_target="tpu_custom_call" | custom-call | flops 1024 | bytes 1024 | tf_op jit(solution)/shard_map/attend_near/pallas_call | solution.py:276
  85.5 15.5 %collective-permute-done.11.refs_1_.refs_2_ = bf16[512,512]{1,0:T(8,128)(2,1)S(1)} collective-permute-done((bf16[512,512]{1,0:T(8,128)(2,1)S(1)}, bf16[512,512]{1,0:T(8,128)(2,1)S(1)}, u32[]{:S(2)}, u32[]{:S(2)}) %collective-permute-start.11) | collective-permute-done | bytes 524320 | tf_op jit(solution)/shard_map/ppermute | solution.py:371
  101.4 2.3 %collective-permute-done.9.refs_2_ = bf16[512,512]{1,0:T(8,128)(2,1)S(1)} collective-permute-done((bf16[512,512]{1,0:T(8,128)(2,1)S(1)}, bf16[512,512]{1,0:T(8,128)(2,1)S(1)}, u32[]{:S(2)}, u32[]{:S(2)}) %collective-permute-start.9) | collective-permute-done | bytes 524320 | tf_op jit(solution)/shard_map/ppermute | solution.py:376
  103.7 9.4 %collective-permute-done.10.refs_3_ = bf16[512,512]{1,0:T(8,128)(2,1)S(1)} collective-permute-done((bf16[512,512]{1,0:T(8,128)(2,1)S(1)}, bf16[512,512]{1,0:T(8,128)(2,1)S(1)}, u32[]{:S(2)}, u32[]{:S(2)}) %collective-permute-start.10) | collective-permute-done | bytes 524320 | tf_op jit(solution)/shard_map/ppermute | solution.py:376
  113.0 7.0 %attend_far.4 = (bf16[512,256]{1,0:T(8,128)(2,1)S(1)}, bf16[512,256]{1,0:T(8,128)(2,1)S(1)}, bf16[512,256]{1,0:T(8,128)(2,1)}) custom-call(s32[66]{0:T(128)S(1)} %pad_add_fusion.place_ref, f32[512,256]{1,0:T(8,128)S(1)} %pad_maximum_fusion.table_ref, bf16[2,192,1536]{2,1,0:T(8,128)(2,1)S(1)} %collective-permute-done.6.refs_0_, ...), custom_call_target="tpu_custom_call" | custom-call | flops 1024 | bytes 1024 | tf_op jit(solution)/shard_map/attend_far/pallas_call | solution.py:297
  123.6 5.4 %attend_far.5 = (bf16[512,256]{1,0:T(8,128)(2,1)}, bf16[512,256]{1,0:T(8,128)(2,1)}) custom-call(s32[66]{0:T(128)S(1)} %pad_add_fusion.place_ref, f32[512,256]{1,0:T(8,128)S(1)} %pad_maximum_fusion.table_ref, bf16[2,192,1536]{2,1,0:T(8,128)(2,1)S(1)} %collective-permute-done.12.refs_0_.refs_1_, bf16[512,512]{1,0:T(8,128)(2,1)S(1)} %collective-permute-done.13.refs_1_.refs_3_, ...), custom_call_target="tpu_custom_call" | custom-call | flops 1024 | bytes 1024 | tf_op jit(solution)/shard_map/attend_far/pallas_call | solution.py:297
  131.4 3.4 %attend_far.6 = (bf16[512,128]{1,0:T(8,128)(2,1)}, bf16[512,128]{1,0:T(8,128)(2,1)}) custom-call(s32[66]{0:T(128)S(1)} %pad_add_fusion.place_ref, f32[512,256]{1,0:T(8,128)S(1)} %pad_maximum_fusion.table_ref, bf16[2,192,1536]{2,1,0:T(8,128)(2,1)S(1)} %collective-permute-done.12.refs_0_.refs_1_, bf16[512,512]{1,0:T(8,128)(2,1)S(1)} %collective-permute-done.13.refs_1_.refs_3_, ...), custom_call_target="tpu_custom_call" | custom-call | flops 1024 | bytes 1024 | tf_op jit(solution)/shard_map/attend_far/pallas_call | solution.py:297
  134.8 3.0 %collective-permute-done.18.refs_4_ = bf16[512,256]{1,0:T(8,128)(2,1)S(1)} collective-permute-done((bf16[512,256]{1,0:T(8,128)(2,1)S(1)}, bf16[512,256]{1,0:T(8,128)(2,1)S(1)}, u32[]{:S(2)}, u32[]{:S(2)}) %collective-permute-start.18) | collective-permute-done | bytes 262176 | tf_op jit(solution)/shard_map/ppermute | solution.py:376
  147.6 2.9 %place_pieces.2.refs_5_ = bf16[512,4096]{1,0:T(8,128)(2,1)} custom-call(s32[22]{0:T(128)S(1)} %stack.143.offsets_ref, bf16[512,512]{1,0:T(8,128)(2,1)S(1)} %copy-done.8, bf16[512,512]{1,0:T(8,128)(2,1)S(1)} %copy-done.10, bf16[512,512]{1,0:T(8,128)(2,1)S(1)} %copy-done.12, bf16[512,512]{1,0:T(8,128)(2,1)S(1)} %copy-done.14, bf16[512,256]{1,0:T(8,128)(2,1)S(1)} %copy-done.16, ...), custom_call_target="tpu_custom_call" | custom-call | flops 1024 | bytes 1024 | tf_op jit(solution)/shard_map/place_pieces/pallas_call | solution.py:333
  150.5 4.4 %attend_far.7.refs_4_ = bf16[512,512]{1,0:T(8,128)(2,1)S(1)} custom-call(s32[66]{0:T(128)S(1)} %pad_add_fusion.place_ref, f32[512,256]{1,0:T(8,128)S(1)} %pad_maximum_fusion.table_ref, bf16[2,192,1536]{2,1,0:T(8,128)(2,1)S(1)} %collective-permute-done.6.refs_0_, bf16[2,192,1536]{2,1,0:T(8,128)(2,1)S(1)} %collective-permute-done.12.refs_0_.refs_1_, ...), custom_call_target="tpu_custom_call" | custom-call | flops 1024 | bytes 1024 | tf_op jit(solution)/shard_map/attend_far/pallas_call | solution.py:297
  155.0 2.2 %place_pieces.3 = bf16[512,4096]{1,0:T(8,128)(2,1)} custom-call(s32[10]{0:T(128)S(1)} %stack.118.offsets_ref, bf16[512,256]{1,0:T(8,128)(2,1)} %collective-permute-done.14.refs_0_, bf16[512,256]{1,0:T(8,128)(2,1)} %collective-permute-done.15.refs_1_, bf16[512,128]{1,0:T(8,128)(2,1)S(1)} %collective-permute-done.16.refs_2_, ...), custom_call_target="tpu_custom_call", output_to_operand_aliasing={{}: (6, {})} | custom-call | flops 1024 | bytes 1024 | tf_op jit(solution)/shard_map/place_pieces/pallas_call | solution.py:333
  (81 shorter events, 27.4 us)
Async XLA Ops:
  4.2 10.4 %collective-permute-start.1 = (bf16[256,2176]{1,0:T(8,128)(2,1)S(1)}, bf16[256,2176]{1,0:T(8,128)(2,1)}, u32[]{:S(2)}, u32[]{:S(2)}) collective-permute-start(bf16[256,2176]{1,0:T(8,128)(2,1)S(1)} %prepare.1.same_ref), channel_id=1, source_target_pairs={{0,1},{1,0},{2,3},{3,2},{4,5},{5,4},{6,7},{7,6},{8,9},{9,8},{10,11... | collective-permute-start | bytes 3342344 | tf_op jit(solution)/shard_map/ppermute | solution.py:379
  4.7 48.3 %collective-permute-start = (bf16[256,2176]{1,0:T(8,128)(2,1)S(1)}, bf16[256,2176]{1,0:T(8,128)(2,1)}, u32[]{:S(2)}, u32[]{:S(2)}) collective-permute-start(bf16[256,2176]{1,0:T(8,128)(2,1)S(1)} %prepare.1.same_ref), channel_id=1, source_target_pairs={{0,4},{1,3},{2,6},{3,1},{4,0},{5,7},{6,2},{7,5},{8,12},{9,11},{10,... | collective-permute-start | bytes 3342344 | tf_op jit(solution)/shard_map/ppermute | solution.py:376
  7.4 45.6 %collective-permute-start.3 = (bf16[256,2176]{1,0:T(8,128)(2,1)S(1)}, bf16[256,2176]{1,0:T(8,128)(2,1)}, u32[]{:S(2)}, u32[]{:S(2)}) collective-permute-start(bf16[256,2176]{1,0:T(8,128)(2,1)S(1)} %prepare.1.same_ref), channel_id=1, source_target_pairs={{0,2},{1,5},{2,0},{3,7},{4,6},{5,1},{6,4},{7,3},{8,10},{9,13},{10,... | collective-permute-start | bytes 3342344 | tf_op jit(solution)/shard_map/ppermute | solution.py:376
  10.6 56.9 %collective-permute-start.6 = (bf16[2,192,1536]{2,1,0:T(8,128)(2,1)S(1)}, bf16[2,192,1536]{2,1,0:T(8,128)(2,1)S(1)}, u32[]{:S(2)}, u32[]{:S(2)}) collective-permute-start(bf16[2,192,1536]{2,1,0:T(8,128)(2,1)S(1)} %pick.2), channel_id=1, source_target_pairs={{0,8},{2,10},{4,12},{6,14},{8,0},{10,2},{12,4},{14,6},{1,9},{3,11}... | collective-permute-start | bytes 3538952 | tf_op jit(solution)/shard_map/ppermute | solution.py:371
  21.0 41.1 %copy-start.2 = (bf16[512,2176]{1,0:T(8,128)(2,1)}, bf16[512,2176]{1,0:T(8,128)(2,1)S(1)}, u32[]{:S(2)}) copy-start(bf16[512,2176]{1,0:T(8,128)(2,1)S(1)} %get-tuple-element.60.refs_4_) | copy-start | bytes 6684676
  53.0 3.9 %collective-permute-start.4 = (bf16[256,2176]{1,0:T(8,128)(2,1)}, bf16[256,2176]{1,0:T(8,128)(2,1)S(1)}, u32[]{:S(2)}, u32[]{:S(2)}) collective-permute-start(bf16[256,2176]{1,0:T(8,128)(2,1)} %collective-permute-done.same_ref), channel_id=1, source_target_pairs={{0,1},{1,0},{2,3},{3,2},{4,5},{5,4},{6,7},{7,6},{8,9},{9,8},{10,11... | collective-permute-start | bytes 3342344 | tf_op jit(solution)/shard_map/ppermute | solution.py:379
  54.1 8.0 %collective-permute-start.5 = (bf16[256,2176]{1,0:T(8,128)(2,1)}, bf16[256,2176]{1,0:T(8,128)(2,1)S(1)}, u32[]{:S(2)}, u32[]{:S(2)}) collective-permute-start(bf16[256,2176]{1,0:T(8,128)(2,1)} %collective-permute-done.3.same_ref), channel_id=1, source_target_pairs={{0,1},{1,0},{2,3},{3,2},{4,5},{5,4},{6,7},{7,6},{8,9},{9,8},{10,11... | collective-permute-start | bytes 3342344 | tf_op jit(solution)/shard_map/ppermute | solution.py:379
  54.1 16.4 %collective-permute-start.2 = (bf16[256,2176]{1,0:T(8,128)(2,1)}, bf16[256,2176]{1,0:T(8,128)(2,1)S(1)}, u32[]{:S(2)}, u32[]{:S(2)}) collective-permute-start(bf16[256,2176]{1,0:T(8,128)(2,1)} %collective-permute-done.same_ref), channel_id=1, source_target_pairs={{0,2},{1,5},{2,0},{3,7},{4,6},{5,1},{6,4},{7,3},{8,10},{9,13},{10,... | collective-permute-start | bytes 3342344 | tf_op jit(solution)/shard_map/ppermute | solution.py:376
  70.5 10.1 %collective-permute-start.7 = (bf16[256,2176]{1,0:T(8,128)(2,1)S(1)}, bf16[256,2176]{1,0:T(8,128)(2,1)S(1)}, u32[]{:S(2)}, u32[]{:S(2)}) collective-permute-start(bf16[256,2176]{1,0:T(8,128)(2,1)S(1)} %collective-permute-done.2.same_ref), channel_id=1, source_target_pairs={{0,1},{1,0},{2,3},{3,2},{4,5},{5,4},{6,7},{7,6},{8,9},{9,8},{10,11... | collective-permute-start | bytes 3342344 | tf_op jit(solution)/shard_map/ppermute | solution.py:379
  73.2 50.4 %collective-permute-start.12 = (bf16[2,192,1536]{2,1,0:T(8,128)(2,1)S(1)}, bf16[2,192,1536]{2,1,0:T(8,128)(2,1)S(1)}, u32[]{:S(2)}, u32[]{:S(2)}) collective-permute-start(bf16[2,192,1536]{2,1,0:T(8,128)(2,1)S(1)} %collective-permute-done.6.refs_0_), channel_id=1, source_target_pairs={{0,16},{16,0},{1,17},{17,1},{2,18},{18,2},{3,19},{19,3},{4,20},{20... | collective-permute-start | bytes 3538952 | tf_op jit(solution)/shard_map/ppermute | solution.py:382
  75.2 25.9 %collective-permute-start.11 = (bf16[512,512]{1,0:T(8,128)(2,1)S(1)}, bf16[512,512]{1,0:T(8,128)(2,1)S(1)}, u32[]{:S(2)}, u32[]{:S(2)}) collective-permute-start(bf16[512,512]{1,0:T(8,128)(2,1)S(1)} %pick.3), channel_id=1, source_target_pairs={{0,8},{2,10},{4,12},{6,14},{8,0},{10,2},{12,4},{14,6},{1,9},{3,11}... | collective-permute-start | bytes 1572872 | tf_op jit(solution)/shard_map/ppermute | solution.py:371
  77.4 24.0 %collective-permute-start.8 = (bf16[512,512]{1,0:T(8,128)(2,1)S(1)}, bf16[512,512]{1,0:T(8,128)(2,1)S(1)}, u32[]{:S(2)}, u32[]{:S(2)}) collective-permute-start(bf16[512,512]{1,0:T(8,128)(2,1)S(1)} %get-tuple-element.37), channel_id=1, source_target_pairs={{0,2},{1,5},{2,0},{3,7},{4,6},{5,1},{6,4},{7,3},{8,10},{9,13},{10,... | collective-permute-start | bytes 1572872 | tf_op jit(solution)/shard_map/ppermute | solution.py:376
  78.6 25.1 %collective-permute-start.9 = (bf16[512,512]{1,0:T(8,128)(2,1)S(1)}, bf16[512,512]{1,0:T(8,128)(2,1)S(1)}, u32[]{:S(2)}, u32[]{:S(2)}) collective-permute-start(bf16[512,512]{1,0:T(8,128)(2,1)S(1)} %get-tuple-element.40), channel_id=1, source_target_pairs={{0,4},{1,3},{2,6},{3,1},{4,0},{5,7},{6,2},{7,5},{8,12},{9,11},{10,... | collective-permute-start | bytes 1572872 | tf_op jit(solution)/shard_map/ppermute | solution.py:376
  85.2 27.8 %collective-permute-start.10 = (bf16[512,512]{1,0:T(8,128)(2,1)S(1)}, bf16[512,512]{1,0:T(8,128)(2,1)S(1)}, u32[]{:S(2)}, u32[]{:S(2)}) collective-permute-start(bf16[512,512]{1,0:T(8,128)(2,1)S(1)} %get-tuple-element.43), channel_id=1, source_target_pairs={{0,6},{1,7},{2,4},{3,5},{4,2},{5,3},{6,0},{7,1},{8,14},{9,15},{10,... | collective-permute-start | bytes 1572872 | tf_op jit(solution)/shard_map/ppermute | solution.py:376
  101.1 19.0 %copy-start.4 = (bf16[512,512]{1,0:T(8,128)(2,1)}, bf16[512,512]{1,0:T(8,128)(2,1)S(1)}, u32[]{:S(2)}) copy-start(bf16[512,512]{1,0:T(8,128)(2,1)S(1)} %collective-permute-done.11.refs_1_.refs_2_) | copy-start | bytes 1572868
  101.1 22.6 %collective-permute-start.13 = (bf16[512,512]{1,0:T(8,128)(2,1)S(1)}, bf16[512,512]{1,0:T(8,128)(2,1)S(1)}, u32[]{:S(2)}, u32[]{:S(2)}) collective-permute-start(bf16[512,512]{1,0:T(8,128)(2,1)S(1)} %collective-permute-done.11.refs_1_.refs_2_), channel_id=1, source_target_pairs={{0,16},{16,0},{1,17},{17,1},{2,18},{18,2},{3,19},{19,3},{4,20},{20... | collective-permute-start | bytes 1572872 | tf_op jit(solution)/shard_map/ppermute | solution.py:382
  101.4 18.7 %copy-start.9 = (bf16[512,512]{1,0:T(8,128)(2,1)}, bf16[512,512]{1,0:T(8,128)(2,1)S(1)}, u32[]{:S(2)}) copy-start(bf16[512,512]{1,0:T(8,128)(2,1)S(1)} %collective-permute-done.8.refs_1_) | copy-start | bytes 1572868
  120.1 17.7 %collective-permute-start.18 = (bf16[512,256]{1,0:T(8,128)(2,1)S(1)}, bf16[512,256]{1,0:T(8,128)(2,1)S(1)}, u32[]{:S(2)}, u32[]{:S(2)}) collective-permute-start(bf16[512,256]{1,0:T(8,128)(2,1)S(1)} %get-tuple-element.49), channel_id=1, source_target_pairs={{0,2},{1,5},{2,0},{3,7},{4,6},{5,1},{6,4},{7,3},{8,10},{9,13},{10,... | collective-permute-start | bytes 786440 | tf_op jit(solution)/shard_map/ppermute | solution.py:376
  121.0 18.4 %collective-permute-start.19 = (bf16[512,256]{1,0:T(8,128)(2,1)S(1)}, bf16[512,256]{1,0:T(8,128)(2,1)S(1)}, u32[]{:S(2)}, u32[]{:S(2)}) collective-permute-start(bf16[512,256]{1,0:T(8,128)(2,1)S(1)} %get-tuple-element.57), channel_id=1, source_target_pairs={{0,4},{1,3},{2,6},{3,1},{4,0},{5,7},{6,2},{7,5},{8,12},{9,11},{10,... | collective-permute-start | bytes 786440 | tf_op jit(solution)/shard_map/ppermute | solution.py:376
  122.0 19.4 %collective-permute-start.20 = (bf16[512,256]{1,0:T(8,128)(2,1)}, bf16[512,256]{1,0:T(8,128)(2,1)}, u32[]{:S(2)}, u32[]{:S(2)}) collective-permute-start(bf16[512,256]{1,0:T(8,128)(2,1)} %get-tuple-element.58), channel_id=1, source_target_pairs={{0,6},{1,7},{2,4},{3,5},{4,2},{5,3},{6,0},{7,1},{8,14},{9,15},{10,... | collective-permute-start | bytes 786440 | tf_op jit(solution)/shard_map/ppermute | solution.py:376
  129.1 25.9 %collective-permute-start.14 = (bf16[512,256]{1,0:T(8,128)(2,1)}, bf16[512,256]{1,0:T(8,128)(2,1)}, u32[]{:S(2)}, u32[]{:S(2)}) collective-permute-start(bf16[512,256]{1,0:T(8,128)(2,1)} %get-tuple-element.52), channel_id=1, source_target_pairs={{0,4},{1,3},{2,6},{3,1},{4,0},{5,7},{6,2},{7,5},{8,12},{9,11},{10,... | collective-permute-start | bytes 786440 | tf_op jit(solution)/shard_map/ppermute | solution.py:376
  130.1 24.8 %collective-permute-start.15 = (bf16[512,256]{1,0:T(8,128)(2,1)}, bf16[512,256]{1,0:T(8,128)(2,1)}, u32[]{:S(2)}, u32[]{:S(2)}) collective-permute-start(bf16[512,256]{1,0:T(8,128)(2,1)} %get-tuple-element.53), channel_id=1, source_target_pairs={{0,6},{1,7},{2,4},{3,5},{4,2},{5,3},{6,0},{7,1},{8,14},{9,15},{10,... | collective-permute-start | bytes 786440 | tf_op jit(solution)/shard_map/ppermute | solution.py:376
  138.5 16.4 %collective-permute-start.16 = (bf16[512,128]{1,0:T(8,128)(2,1)}, bf16[512,128]{1,0:T(8,128)(2,1)S(1)}, u32[]{:S(2)}, u32[]{:S(2)}) collective-permute-start(bf16[512,128]{1,0:T(8,128)(2,1)} %get-tuple-element.55), channel_id=1, source_target_pairs={{0,2},{1,5},{2,0},{3,7},{4,6},{5,1},{6,4},{7,3},{8,10},{9,13},{10,... | collective-permute-start | bytes 393224 | tf_op jit(solution)/shard_map/ppermute | solution.py:376
  140.0 14.9 %collective-permute-start.17 = (bf16[512,128]{1,0:T(8,128)(2,1)}, bf16[512,128]{1,0:T(8,128)(2,1)}, u32[]{:S(2)}, u32[]{:S(2)}) collective-permute-start(bf16[512,128]{1,0:T(8,128)(2,1)} %get-tuple-element.56), channel_id=1, source_target_pairs={{0,2},{1,5},{2,0},{3,7},{4,6},{5,1},{6,4},{7,3},{8,10},{9,13},{10,... | collective-permute-start | bytes 393224 | tf_op jit(solution)/shard_map/ppermute | solution.py:376
  (17 other events, 51.0 us)

commit v11 on v10

--- a/solution.py
+++ b/solution.py
@@ -9,7 +9,7 @@
 from jax.sharding import PartitionSpec as P
 
 epsilon = 1e-06
-VMEM_LIMIT = 32 * 1024 * 1024
+VMEM_LIMIT = 20 * 1024 * 1024
 LIGHT = pl.CostEstimate(flops=1024, bytes_accessed=1024, transcendentals=0)
 FAR = -(2.0**100)
 NT = (((1,), (1,)), ((), ()))
@@ -432,12 +432,13 @@
             same[distance] = across(after(same[distance ^ low_bit], mixed), low_bit)
     for distance in range(1, half_places):
         if distance & (distance - 1) == 0:
-            other.append(sibling(after(same[partner[distance]], mixed, *direct)))
+            other.append(sibling(after(same[partner[distance]], mixed, far_query, *direct)))
         else:
             other.append(None)
+    crossed_query = [other_part(after(far_query, mixed))] if share == 2 else []
     for distance in range(1, half_places):
         if other[distance] is None:
-            other[distance] = sibling(after(same[partner[distance]], mixed, far_query))
+            other[distance] = sibling(after(same[partner[distance]], mixed, far_pair, *crossed_query))
         mixed = near(distance, mixed)
         arrived.append(across(mixed, distance))
     placed = []
@@ -456,14 +457,13 @@
     straight = (far_query, far_pair, [side * per_part + index for index in range(per_part)])
     sets = [straight]
     if share == 2:
-        crossed_query, crossed_pair = other_part(far_query), other_part(after(far_pair, mixed))
-        sets.append((crossed_query, crossed_pair, [(1 - side) * per_part + index for index in range(per_part)]))
+        sets.append((crossed_query[0], other_part(far_pair), [(1 - side) * per_part + index for index in range(per_part)]))
     neighbours, middle = list(range(1, half_places)), half_places // 2
-    calls = [(sets[:1], neighbours, 1, arrived[1:])]
+    calls = [(sets[:1], neighbours, 1, [])]
     if share == 2:
         calls.append((sets[1:], list(range(middle, half_places)), 1, []))
         calls.append((sets[1:], list(range(1, middle)), per_part, []))
-    calls.append((sets, [0], 1, []))
+    calls.append((sets, [0], 1, arrived[1:]))
     late, sent = [], []
     for chosen, slots, parts_of, gates in calls:
         numbers = [number for _, _, some in chosen for number in some]

time: 158 us -> 152 us (0.962)
  Pallas kernels: 47.4 us -> 45.4 us
  waiting for transfers between devices: 65.1 us -> 63.4 us
    ppermute x13, waiting for transfers between devices: 49.6 us -> 14 us  [across(): return lax.ppermute(value, ('seq', 'head'), pairs)]
    ppermute x2, waiting for transfers between devices: 15.5 us -> 46.6 us  [opposite(): lax.ppermute(value, 'seq', [(s, s ^ half_places) for s in range(places)])]
    ppermute x2, waiting for transfers between devices: 0.01 us -> 2.8 us  [other_part(): return lax.ppermute(value, 'parts', [(p, p ^ 1) for p in range(parts)])]
    ppermute x4, starting transfers between devices: 4.42 us -> 2.57 us  [sibling(): return lax.ppermute(value, 'head', [(0, 1), (1, 0)])]
    unnamed x41 -> x45, local copies, waits for them, and re-layouts: 11.8 us -> 12.7 us
  transfers between devices with their start and end apart: 21 -> 21, of which waited for: 6 -> 6; matrix products, arithmetic and copies ran while one was open for 1% -> 2% of each run, Pallas kernels for 28% -> 28%
where the time goes in v11:
time: 152 us
  waiting for transfers between devices  63.4 us (42%)
  Pallas kernels  45.4 us (30%)
  starting transfers between devices  28.7 us (19%)
  local copies, waits for them, and re-layouts  13 us (9%)
    ppermute x2, waiting for transfers between devices, opposite(): lax.ppermute(value, 'seq', [(s, s ^ half_places) for s in range(places)])  46.6 us
    pallas_call x4, Pallas kernels, attend_far(): pl.pallas_call(partial(far_kernel, sizes, slot_count, numbers, half_place...  19.6 us
    pallas_call x4, Pallas kernels, attend_near(): pl.pallas_call(partial(near_kernel, sizes, slot_count, slot, half_places)...  19.1 us
    ppermute x13, starting transfers between devices, across(): return lax.ppermute(value, ('seq', 'head'), pairs)  18.2 us
    ppermute x13, waiting for transfers between devices, across(): return lax.ppermute(value, ('seq', 'head'), pairs)  14 us
    unnamed x45, local copies, waits for them, and re-layouts  12.7 us
    pallas_call x2, Pallas kernels, place_pieces(): pl.pallas_call(partial(place_kernel, width, count), out_shape=jax.ShapeDt...  5.16 us
    ppermute x2, starting transfers between devices, opposite(): lax.ppermute(value, 'seq', [(s, s ^ half_places) for s in range(places)])  4.81 us
  transfers between devices with their start and end apart: 21, of which 6 were waited for; matrix products, arithmetic and copies ran while one was open for 2% of the time, Pallas kernels for 28%

profile of v11, /device:TPU:0, one launch (start us, length us, event | category | flops | bytes accessed | tf_op | source)
XLA Modules:
  0.0 152.1 jit_solution(3999272945142220501)
XLA Ops:
  0.0 1.7 %copy-done = bf16[1,1536,4,192]{1,3,2,0:T(8,128)(2,1)S(1)} copy-done((bf16[1,1536,4,192]{1,3,2,0:T(8,128)(2,1)S(1)}, bf16[1,1536,4,192]{1,3,2,0:T(8,128)(2,1)}, u32[]{:S(2)}) %copy-start) | copy-done | bytes 2359320
  1.8 4.1 %collective-permute-start.4 = (bf16[2,192,1536]{2,1,0:T(8,128)(2,1)S(1)}, bf16[2,192,1536]{2,1,0:T(8,128)(2,1)S(1)}, u32[]{:S(2)}, u32[]{:S(2)}) collective-permute-start(bf16[2,192,1536]{2,1,0:T(8,128)(2,1)S(1)} %pick.2), channel_id=1, source_target_pairs={{0,8},{2,10},{4,12},{6,14},{8,0},{10,2},{12,4},{14,6},{1,9},{3,11}... | collective-permute-start | bytes 3538952 | tf_op jit(solution)/shard_map/ppermute | solution.py:371
  8.7 1.6 %collective-permute-start = (bf16[256,2176]{1,0:T(8,128)(2,1)S(1)}, bf16[256,2176]{1,0:T(8,128)(2,1)S(1)}, u32[]{:S(2)}, u32[]{:S(2)}) collective-permute-start(bf16[256,2176]{1,0:T(8,128)(2,1)S(1)} %prepare.1.same_ref), channel_id=1, source_target_pairs={{0,4},{1,3},{2,6},{3,1},{4,0},{5,7},{6,2},{7,5},{8,12},{9,11},{10,... | collective-permute-start | bytes 3342344 | tf_op jit(solution)/shard_map/ppermute | solution.py:376
  11.9 1.6 %copy.8 = bf16[64,8,4,256]{3,1,2,0:T(8,128)(2,1)S(1)} copy(bf16[64,8,4,256]{3,2,1,0:T(4,128)(2,1)} %bitcast.55) | data formatting | bytes 2097152
  14.6 4.5 %attend_near.4 = (bf16[512,512]{1,0:T(8,128)(2,1)S(1)}, bf16[512,2176]{1,0:T(8,128)(2,1)S(1)}) custom-call(s32[66]{0:T(128)S(1)} %pad_add_fusion.place_ref, f32[512,256]{1,0:T(8,128)S(1)} %pad_maximum_fusion.table_ref, bf16[4,192,1536]{2,1,0:T(8,128)(2,1)S(1)} %bitcast.44, bf16[512,1024]{1,0:T(8,128)(2,1)S(1)} %bitcast.48, ...), custom_call_target="tpu_custom_call" | custom-call | flops 1024 | bytes 1024 | tf_op jit(solution)/shard_map/attend_near/pallas_call | solution.py:276
  19.9 37.3 %collective-permute-done.4.refs_0_ = bf16[2,192,1536]{2,1,0:T(8,128)(2,1)S(1)} collective-permute-done((bf16[2,192,1536]{2,1,0:T(8,128)(2,1)S(1)}, bf16[2,192,1536]{2,1,0:T(8,128)(2,1)S(1)}, u32[]{:S(2)}, u32[]{:S(2)}) %collective-permute-start.4) | collective-permute-done | bytes 1179680 | tf_op jit(solution)/shard_map/ppermute | solution.py:371
  60.2 1.9 %collective-permute-start.2 = (bf16[256,2176]{1,0:T(8,128)(2,1)S(1)}, bf16[256,2176]{1,0:T(8,128)(2,1)S(1)}, u32[]{:S(2)}, u32[]{:S(2)}) collective-permute-start(bf16[256,2176]{1,0:T(8,128)(2,1)S(1)} %collective-permute-done.same_ref), channel_id=1, source_target_pairs={{0,2},{1,5},{2,0},{3,7},{4,6},{5,1},{6,4},{7,3},{8,10},{9,13},{10,... | collective-permute-start | bytes 3342344 | tf_op jit(solution)/shard_map/ppermute | solution.py:376
  62.9 4.5 %attend_near.5 = (bf16[512,512]{1,0:T(8,128)(2,1)S(1)}, bf16[512,2176]{1,0:T(8,128)(2,1)S(1)}) custom-call(s32[66]{0:T(128)S(1)} %pad_add_fusion.place_ref, f32[512,256]{1,0:T(8,128)S(1)} %pad_maximum_fusion.table_ref, bf16[4,192,1536]{2,1,0:T(8,128)(2,1)S(1)} %bitcast.45, bf16[512,1024]{1,0:T(8,128)(2,1)S(1)} %bitcast.50, ...), custom_call_target="tpu_custom_call" | custom-call | flops 1024 | bytes 1024 | tf_op jit(solution)/shard_map/attend_near/pallas_call | solution.py:276
  67.4 4.7 %attend_near.6 = (bf16[512,512]{1,0:T(8,128)(2,1)S(1)}, bf16[512,2176]{1,0:T(8,128)(2,1)S(1)}) custom-call(s32[66]{0:T(128)S(1)} %pad_add_fusion.place_ref, f32[512,256]{1,0:T(8,128)S(1)} %pad_maximum_fusion.table_ref, bf16[4,192,1536]{2,1,0:T(8,128)(2,1)S(1)} %bitcast.46, bf16[512,1024]{1,0:T(8,128)(2,1)S(1)} %bitcast.51, ...), custom_call_target="tpu_custom_call" | custom-call | flops 1024 | bytes 1024 | tf_op jit(solution)/shard_map/attend_near/pallas_call | solution.py:276
  72.2 9.3 %collective-permute-done.7.refs_1_.refs_2_ = bf16[512,512]{1,0:T(8,128)(2,1)S(1)} collective-permute-done((bf16[512,512]{1,0:T(8,128)(2,1)S(1)}, bf16[512,512]{1,0:T(8,128)(2,1)S(1)}, u32[]{:S(2)}, u32[]{:S(2)}) %collective-permute-start.7) | collective-permute-done | bytes 524320 | tf_op jit(solution)/shard_map/ppermute | solution.py:371
  81.5 2.8 %collective-permute-done.8.refs_0_.refs_1_ = bf16[2,192,1536]{2,1,0:T(8,128)(2,1)S(1)} collective-permute-done((bf16[2,192,1536]{2,1,0:T(8,128)(2,1)S(1)}, bf16[2,192,1536]{2,1,0:T(8,128)(2,1)S(1)}, u32[]{:S(2)}, u32[]{:S(2)}) %collective-permute-start.8) | collective-permute-done | bytes 1179680 | tf_op jit(solution)/shard_map/ppermute | solution.py:382
  84.3 2.0 %collective-permute-start.9 = (bf16[256,2176]{1,0:T(8,128)(2,1)S(1)}, bf16[256,2176]{1,0:T(8,128)(2,1)S(1)}, u32[]{:S(2)}, u32[]{:S(2)}) collective-permute-start(bf16[256,2176]{1,0:T(8,128)(2,1)S(1)} %collective-permute-done.2.same_ref), channel_id=1, source_target_pairs={{0,1},{1,0},{2,3},{3,2},{4,5},{5,4},{6,7},{7,6},{8,9},{9,8},{10,11... | collective-permute-start | bytes 3342344 | tf_op jit(solution)/shard_map/ppermute | solution.py:379
  90.7 5.3 %attend_near.7 = (bf16[512,512]{1,0:T(8,128)(2,1)}, bf16[512,2176]{1,0:T(8,128)(2,1)S(1)}) custom-call(s32[66]{0:T(128)S(1)} %pad_add_fusion.place_ref, f32[512,256]{1,0:T(8,128)S(1)} %pad_maximum_fusion.table_ref, bf16[4,192,1536]{2,1,0:T(8,128)(2,1)S(1)} %bitcast.47, bf16[512,1024]{1,0:T(8,128)(2,1)S(1)} %bitcast.52, ...), custom_call_target="tpu_custom_call" | custom-call | flops 1024 | bytes 1024 | tf_op jit(solution)/shard_map/attend_near/pallas_call | solution.py:276
  96.6 6.4 %attend_far.4 = (bf16[512,256]{1,0:T(8,128)(2,1)S(1)}, bf16[512,256]{1,0:T(8,128)(2,1)S(1)}, bf16[512,256]{1,0:T(8,128)(2,1)S(1)}) custom-call(s32[66]{0:T(128)S(1)} %pad_add_fusion.place_ref, f32[512,256]{1,0:T(8,128)S(1)} %pad_maximum_fusion.table_ref, bf16[2,192,1536]{2,1,0:T(8,128)(2,1)S(1)} %collective-permute-done.4.refs_0_, ...), custom_call_target="tpu_custom_call" | custom-call | flops 1024 | bytes 1024 | tf_op jit(solution)/shard_map/attend_far/pallas_call | solution.py:297
  106.0 6.3 %collective-permute-done.15.refs_1_ = bf16[512,512]{1,0:T(8,128)(2,1)S(1)} collective-permute-done((bf16[512,512]{1,0:T(8,128)(2,1)S(1)}, bf16[512,512]{1,0:T(8,128)(2,1)S(1)}, u32[]{:S(2)}, u32[]{:S(2)}) %collective-permute-start.15) | collective-permute-done | bytes 524320 | tf_op jit(solution)/shard_map/ppermute | solution.py:376
  112.7 5.4 %attend_far.5 = (bf16[512,256]{1,0:T(8,128)(2,1)}, bf16[512,256]{1,0:T(8,128)(2,1)}) custom-call(s32[66]{0:T(128)S(1)} %pad_add_fusion.place_ref, f32[512,256]{1,0:T(8,128)S(1)} %pad_maximum_fusion.table_ref, bf16[2,192,1536]{2,1,0:T(8,128)(2,1)S(1)} %collective-permute-done.8.refs_0_.refs_1_, bf16[512,512]{1,0:T(8,128)(2,1)S(1)} %collective-permute-done.10.refs_1_.refs_3_, ...), custom_call_target="tpu_custom_call" | custom-call | flops 1024 | bytes 1024 | tf_op jit(solution)/shard_map/attend_far/pallas_call | solution.py:297
  118.1 2.5 %collective-permute-start.11 = (bf16[512,256]{1,0:T(8,128)(2,1)}, bf16[512,256]{1,0:T(8,128)(2,1)}, u32[]{:S(2)}, u32[]{:S(2)}) collective-permute-start(bf16[512,256]{1,0:T(8,128)(2,1)} %get-tuple-element.52), channel_id=1, source_target_pairs={{0,4},{1,3},{2,6},{3,1},{4,0},{5,7},{6,2},{7,5},{8,12},{9,11},{10,... | collective-permute-start | bytes 786440 | tf_op jit(solution)/shard_map/ppermute | solution.py:376
  120.6 6.7 %collective-permute-done.18.refs_4_ = bf16[512,256]{1,0:T(8,128)(2,1)S(1)} collective-permute-done((bf16[512,256]{1,0:T(8,128)(2,1)S(1)}, bf16[512,256]{1,0:T(8,128)(2,1)S(1)}, u32[]{:S(2)}, u32[]{:S(2)}) %collective-permute-start.18) | collective-permute-done | bytes 262176 | tf_op jit(solution)/shard_map/ppermute | solution.py:376
  127.4 1.8 %collective-permute-start.12 = (bf16[512,256]{1,0:T(8,128)(2,1)}, bf16[512,256]{1,0:T(8,128)(2,1)}, u32[]{:S(2)}, u32[]{:S(2)}) collective-permute-start(bf16[512,256]{1,0:T(8,128)(2,1)} %get-tuple-element.53), channel_id=1, source_target_pairs={{0,6},{1,7},{2,4},{3,5},{4,2},{5,3},{6,0},{7,1},{8,14},{9,15},{10,... | collective-permute-start | bytes 786440 | tf_op jit(solution)/shard_map/ppermute | solution.py:376
  129.1 3.4 %attend_far.6 = (bf16[512,128]{1,0:T(8,128)(2,1)}, bf16[512,128]{1,0:T(8,128)(2,1)}) custom-call(s32[66]{0:T(128)S(1)} %pad_add_fusion.place_ref, f32[512,256]{1,0:T(8,128)S(1)} %pad_maximum_fusion.table_ref, bf16[2,192,1536]{2,1,0:T(8,128)(2,1)S(1)} %collective-permute-done.8.refs_0_.refs_1_, bf16[512,512]{1,0:T(8,128)(2,1)S(1)} %collective-permute-done.10.refs_1_.refs_3_, ...), custom_call_target="tpu_custom_call" | custom-call | flops 1024 | bytes 1024 | tf_op jit(solution)/shard_map/attend_far/pallas_call | solution.py:297
  134.1 1.8 %collective-permute-start.14 = (bf16[512,128]{1,0:T(8,128)(2,1)}, bf16[512,128]{1,0:T(8,128)(2,1)}, u32[]{:S(2)}, u32[]{:S(2)}) collective-permute-start(bf16[512,128]{1,0:T(8,128)(2,1)} %get-tuple-element.56), channel_id=1, source_target_pairs={{0,2},{1,5},{2,0},{3,7},{4,6},{5,1},{6,4},{7,3},{8,10},{9,13},{10,... | collective-permute-start | bytes 393224 | tf_op jit(solution)/shard_map/ppermute | solution.py:376
  142.2 2.9 %place_pieces.2.refs_5_ = bf16[512,4096]{1,0:T(8,128)(2,1)} custom-call(s32[22]{0:T(128)S(1)} %stack.143.offsets_ref, bf16[512,512]{1,0:T(8,128)(2,1)S(1)} %copy-done.8, bf16[512,512]{1,0:T(8,128)(2,1)S(1)} %copy-done.10, bf16[512,512]{1,0:T(8,128)(2,1)S(1)} %copy-done.12, bf16[512,512]{1,0:T(8,128)(2,1)} %collective-permute-done.17.refs_3_, ...), custom_call_target="tpu_custom_call" | custom-call | flops 1024 | bytes 1024 | tf_op jit(solution)/shard_map/place_pieces/pallas_call | solution.py:333
  145.2 4.4 %attend_far.7.refs_4_ = bf16[512,512]{1,0:T(8,128)(2,1)S(1)} custom-call(s32[66]{0:T(128)S(1)} %pad_add_fusion.place_ref, f32[512,256]{1,0:T(8,128)S(1)} %pad_maximum_fusion.table_ref, bf16[2,192,1536]{2,1,0:T(8,128)(2,1)S(1)} %collective-permute-done.4.refs_0_, bf16[2,192,1536]{2,1,0:T(8,128)(2,1)S(1)} %collective-permute-done.8.refs_0_.refs_1_, ...), custom_call_target="tpu_custom_call" | custom-call | flops 1024 | bytes 1024 | tf_op jit(solution)/shard_map/attend_far/pallas_call | solution.py:297
  149.7 2.2 %place_pieces.3 = bf16[512,4096]{1,0:T(8,128)(2,1)} custom-call(s32[10]{0:T(128)S(1)} %stack.118.offsets_ref, bf16[512,256]{1,0:T(8,128)(2,1)} %collective-permute-done.11.refs_0_, bf16[512,256]{1,0:T(8,128)(2,1)} %collective-permute-done.12.refs_1_, bf16[512,128]{1,0:T(8,128)(2,1)S(1)} %collective-permute-done.13.refs_2_, ...), custom_call_target="tpu_custom_call", output_to_operand_aliasing={{}: (6, {})} | custom-call | flops 1024 | bytes 1024 | tf_op jit(solution)/shard_map/place_pieces/pallas_call | solution.py:333
  (85 shorter events, 26.2 us)
Async XLA Ops:
  1.8 55.5 %collective-permute-start.4 = (bf16[2,192,1536]{2,1,0:T(8,128)(2,1)S(1)}, bf16[2,192,1536]{2,1,0:T(8,128)(2,1)S(1)}, u32[]{:S(2)}, u32[]{:S(2)}) collective-permute-start(bf16[2,192,1536]{2,1,0:T(8,128)(2,1)S(1)} %pick.2), channel_id=1, source_target_pairs={{0,8},{2,10},{4,12},{6,14},{8,0},{10,2},{12,4},{14,6},{1,9},{3,11}... | collective-permute-start | bytes 3538952 | tf_op jit(solution)/shard_map/ppermute | solution.py:371
  8.7 5.9 %collective-permute-start.1 = (bf16[256,2176]{1,0:T(8,128)(2,1)S(1)}, bf16[256,2176]{1,0:T(8,128)(2,1)S(1)}, u32[]{:S(2)}, u32[]{:S(2)}) collective-permute-start(bf16[256,2176]{1,0:T(8,128)(2,1)S(1)} %prepare.1.same_ref), channel_id=1, source_target_pairs={{0,1},{1,0},{2,3},{3,2},{4,5},{5,4},{6,7},{7,6},{8,9},{9,8},{10,11... | collective-permute-start | bytes 3342344 | tf_op jit(solution)/shard_map/ppermute | solution.py:379
  8.7 51.0 %collective-permute-start = (bf16[256,2176]{1,0:T(8,128)(2,1)S(1)}, bf16[256,2176]{1,0:T(8,128)(2,1)S(1)}, u32[]{:S(2)}, u32[]{:S(2)}) collective-permute-start(bf16[256,2176]{1,0:T(8,128)(2,1)S(1)} %prepare.1.same_ref), channel_id=1, source_target_pairs={{0,4},{1,3},{2,6},{3,1},{4,0},{5,7},{6,2},{7,5},{8,12},{9,11},{10,... | collective-permute-start | bytes 3342344 | tf_op jit(solution)/shard_map/ppermute | solution.py:376
  10.4 49.3 %collective-permute-start.3 = (bf16[256,2176]{1,0:T(8,128)(2,1)S(1)}, bf16[256,2176]{1,0:T(8,128)(2,1)S(1)}, u32[]{:S(2)}, u32[]{:S(2)}) collective-permute-start(bf16[256,2176]{1,0:T(8,128)(2,1)S(1)} %prepare.1.same_ref), channel_id=1, source_target_pairs={{0,2},{1,5},{2,0},{3,7},{4,6},{5,1},{6,4},{7,3},{8,10},{9,13},{10,... | collective-permute-start | bytes 3342344 | tf_op jit(solution)/shard_map/ppermute | solution.py:376
  19.9 47.5 %copy-start.2 = (bf16[512,2176]{1,0:T(8,128)(2,1)}, bf16[512,2176]{1,0:T(8,128)(2,1)S(1)}, u32[]{:S(2)}) copy-start(bf16[512,2176]{1,0:T(8,128)(2,1)S(1)} %get-tuple-element.60.refs_4_) | copy-start | bytes 6684676
  57.2 27.1 %collective-permute-start.8 = (bf16[2,192,1536]{2,1,0:T(8,128)(2,1)S(1)}, bf16[2,192,1536]{2,1,0:T(8,128)(2,1)S(1)}, u32[]{:S(2)}, u32[]{:S(2)}) collective-permute-start(bf16[2,192,1536]{2,1,0:T(8,128)(2,1)S(1)} %collective-permute-done.4.refs_0_), channel_id=1, source_target_pairs={{0,16},{16,0},{1,17},{17,1},{2,18},{18,2},{3,19},{19,3},{4,20},{20... | collective-permute-start | bytes 3538952 | tf_op jit(solution)/shard_map/ppermute | solution.py:382
  59.7 3.2 %collective-permute-start.5 = (bf16[256,2176]{1,0:T(8,128)(2,1)S(1)}, bf16[256,2176]{1,0:T(8,128)(2,1)S(1)}, u32[]{:S(2)}, u32[]{:S(2)}) collective-permute-start(bf16[256,2176]{1,0:T(8,128)(2,1)S(1)} %collective-permute-done.same_ref), channel_id=1, source_target_pairs={{0,1},{1,0},{2,3},{3,2},{4,5},{5,4},{6,7},{7,6},{8,9},{9,8},{10,11... | collective-permute-start | bytes 3342344 | tf_op jit(solution)/shard_map/ppermute | solution.py:379
  60.2 7.2 %collective-permute-start.6 = (bf16[256,2176]{1,0:T(8,128)(2,1)S(1)}, bf16[256,2176]{1,0:T(8,128)(2,1)S(1)}, u32[]{:S(2)}, u32[]{:S(2)}) collective-permute-start(bf16[256,2176]{1,0:T(8,128)(2,1)S(1)} %collective-permute-done.3.same_ref), channel_id=1, source_target_pairs={{0,1},{1,0},{2,3},{3,2},{4,5},{5,4},{6,7},{7,6},{8,9},{9,8},{10,11... | collective-permute-start | bytes 3342344 | tf_op jit(solution)/shard_map/ppermute | solution.py:379
  60.2 21.3 %collective-permute-start.2 = (bf16[256,2176]{1,0:T(8,128)(2,1)S(1)}, bf16[256,2176]{1,0:T(8,128)(2,1)S(1)}, u32[]{:S(2)}, u32[]{:S(2)}) collective-permute-start(bf16[256,2176]{1,0:T(8,128)(2,1)S(1)} %collective-permute-done.same_ref), channel_id=1, source_target_pairs={{0,2},{1,5},{2,0},{3,7},{4,6},{5,1},{6,4},{7,3},{8,10},{9,13},{10,... | collective-permute-start | bytes 3342344 | tf_op jit(solution)/shard_map/ppermute | solution.py:376
  62.2 19.3 %collective-permute-start.7 = (bf16[512,512]{1,0:T(8,128)(2,1)S(1)}, bf16[512,512]{1,0:T(8,128)(2,1)S(1)}, u32[]{:S(2)}, u32[]{:S(2)}) collective-permute-start(bf16[512,512]{1,0:T(8,128)(2,1)S(1)} %pick.3), channel_id=1, source_target_pairs={{0,8},{2,10},{4,12},{6,14},{8,0},{10,2},{12,4},{14,6},{1,9},{3,11}... | collective-permute-start | bytes 1572872 | tf_op jit(solution)/shard_map/ppermute | solution.py:371
  81.5 15.1 %copy-start.4 = (bf16[512,512]{1,0:T(8,128)(2,1)}, bf16[512,512]{1,0:T(8,128)(2,1)S(1)}, u32[]{:S(2)}) copy-start(bf16[512,512]{1,0:T(8,128)(2,1)S(1)} %collective-permute-done.7.refs_1_.refs_2_) | copy-start | bytes 1572868
  84.3 6.4 %collective-permute-start.9 = (bf16[256,2176]{1,0:T(8,128)(2,1)S(1)}, bf16[256,2176]{1,0:T(8,128)(2,1)S(1)}, u32[]{:S(2)}, u32[]{:S(2)}) collective-permute-start(bf16[256,2176]{1,0:T(8,128)(2,1)S(1)} %collective-permute-done.2.same_ref), channel_id=1, source_target_pairs={{0,1},{1,0},{2,3},{3,2},{4,5},{5,4},{6,7},{7,6},{8,9},{9,8},{10,11... | collective-permute-start | bytes 3342344 | tf_op jit(solution)/shard_map/ppermute | solution.py:379
  86.3 18.2 %collective-permute-start.10 = (bf16[512,512]{1,0:T(8,128)(2,1)S(1)}, bf16[512,512]{1,0:T(8,128)(2,1)S(1)}, u32[]{:S(2)}, u32[]{:S(2)}) collective-permute-start(bf16[512,512]{1,0:T(8,128)(2,1)S(1)} %collective-permute-done.7.refs_1_.refs_2_), channel_id=1, source_target_pairs={{0,16},{16,0},{1,17},{17,1},{2,18},{18,2},{3,19},{19,3},{4,20},{20... | collective-permute-start | bytes 1572872 | tf_op jit(solution)/shard_map/ppermute | solution.py:382
  87.8 24.4 %collective-permute-start.15 = (bf16[512,512]{1,0:T(8,128)(2,1)S(1)}, bf16[512,512]{1,0:T(8,128)(2,1)S(1)}, u32[]{:S(2)}, u32[]{:S(2)}) collective-permute-start(bf16[512,512]{1,0:T(8,128)(2,1)S(1)} %get-tuple-element.37), channel_id=1, source_target_pairs={{0,2},{1,5},{2,0},{3,7},{4,6},{5,1},{6,4},{7,3},{8,10},{9,13},{10,... | collective-permute-start | bytes 1572872 | tf_op jit(solution)/shard_map/ppermute | solution.py:376
  89.2 28.9 %collective-permute-start.16 = (bf16[512,512]{1,0:T(8,128)(2,1)S(1)}, bf16[512,512]{1,0:T(8,128)(2,1)S(1)}, u32[]{:S(2)}, u32[]{:S(2)}) collective-permute-start(bf16[512,512]{1,0:T(8,128)(2,1)S(1)} %get-tuple-element.40), channel_id=1, source_target_pairs={{0,4},{1,3},{2,6},{3,1},{4,0},{5,7},{6,2},{7,5},{8,12},{9,11},{10,... | collective-permute-start | bytes 1572872 | tf_op jit(solution)/shard_map/ppermute | solution.py:376
  96.0 40.2 %collective-permute-start.17 = (bf16[512,512]{1,0:T(8,128)(2,1)}, bf16[512,512]{1,0:T(8,128)(2,1)}, u32[]{:S(2)}, u32[]{:S(2)}) collective-permute-start(bf16[512,512]{1,0:T(8,128)(2,1)} %get-tuple-element.45), channel_id=1, source_target_pairs={{0,6},{1,7},{2,4},{3,5},{4,2},{5,3},{6,0},{7,1},{8,14},{9,15},{10,... | collective-permute-start | bytes 1572872 | tf_op jit(solution)/shard_map/ppermute | solution.py:376
  103.0 24.3 %collective-permute-start.18 = (bf16[512,256]{1,0:T(8,128)(2,1)S(1)}, bf16[512,256]{1,0:T(8,128)(2,1)S(1)}, u32[]{:S(2)}, u32[]{:S(2)}) collective-permute-start(bf16[512,256]{1,0:T(8,128)(2,1)S(1)} %get-tuple-element.50), channel_id=1, source_target_pairs={{0,2},{1,5},{2,0},{3,7},{4,6},{5,1},{6,4},{7,3},{8,10},{9,13},{10,... | collective-permute-start | bytes 786440 | tf_op jit(solution)/shard_map/ppermute | solution.py:376
  104.5 28.0 %collective-permute-start.19 = (bf16[512,256]{1,0:T(8,128)(2,1)S(1)}, bf16[512,256]{1,0:T(8,128)(2,1)S(1)}, u32[]{:S(2)}, u32[]{:S(2)}) collective-permute-start(bf16[512,256]{1,0:T(8,128)(2,1)S(1)} %get-tuple-element.57), channel_id=1, source_target_pairs={{0,4},{1,3},{2,6},{3,1},{4,0},{5,7},{6,2},{7,5},{8,12},{9,11},{10,... | collective-permute-start | bytes 786440 | tf_op jit(solution)/shard_map/ppermute | solution.py:376
  112.3 21.2 %collective-permute-start.20 = (bf16[512,256]{1,0:T(8,128)(2,1)S(1)}, bf16[512,256]{1,0:T(8,128)(2,1)S(1)}, u32[]{:S(2)}, u32[]{:S(2)}) collective-permute-start(bf16[512,256]{1,0:T(8,128)(2,1)S(1)} %get-tuple-element.58), channel_id=1, source_target_pairs={{0,6},{1,7},{2,4},{3,5},{4,2},{5,3},{6,0},{7,1},{8,14},{9,15},{10,... | collective-permute-start | bytes 786440 | tf_op jit(solution)/shard_map/ppermute | solution.py:376
  118.1 14.4 %copy-start.11 = (bf16[512,512]{1,0:T(8,128)(2,1)}, bf16[512,512]{1,0:T(8,128)(2,1)S(1)}, u32[]{:S(2)}) copy-start(bf16[512,512]{1,0:T(8,128)(2,1)S(1)} %collective-permute-done.16.refs_2_) | copy-start | bytes 1572868
  118.1 31.6 %collective-permute-start.11 = (bf16[512,256]{1,0:T(8,128)(2,1)}, bf16[512,256]{1,0:T(8,128)(2,1)}, u32[]{:S(2)}, u32[]{:S(2)}) collective-permute-start(bf16[512,256]{1,0:T(8,128)(2,1)} %get-tuple-element.52), channel_id=1, source_target_pairs={{0,4},{1,3},{2,6},{3,1},{4,0},{5,7},{6,2},{7,5},{8,12},{9,11},{10,... | collective-permute-start | bytes 786440 | tf_op jit(solution)/shard_map/ppermute | solution.py:376
  127.4 22.3 %collective-permute-start.12 = (bf16[512,256]{1,0:T(8,128)(2,1)}, bf16[512,256]{1,0:T(8,128)(2,1)}, u32[]{:S(2)}, u32[]{:S(2)}) collective-permute-start(bf16[512,256]{1,0:T(8,128)(2,1)} %get-tuple-element.53), channel_id=1, source_target_pairs={{0,6},{1,7},{2,4},{3,5},{4,2},{5,3},{6,0},{7,1},{8,14},{9,15},{10,... | collective-permute-start | bytes 786440 | tf_op jit(solution)/shard_map/ppermute | solution.py:376
  133.2 16.4 %collective-permute-start.13 = (bf16[512,128]{1,0:T(8,128)(2,1)}, bf16[512,128]{1,0:T(8,128)(2,1)S(1)}, u32[]{:S(2)}, u32[]{:S(2)}) collective-permute-start(bf16[512,128]{1,0:T(8,128)(2,1)} %get-tuple-element.55), channel_id=1, source_target_pairs={{0,2},{1,5},{2,0},{3,7},{4,6},{5,1},{6,4},{7,3},{8,10},{9,13},{10,... | collective-permute-start | bytes 393224 | tf_op jit(solution)/shard_map/ppermute | solution.py:376
  134.1 15.5 %collective-permute-start.14 = (bf16[512,128]{1,0:T(8,128)(2,1)}, bf16[512,128]{1,0:T(8,128)(2,1)}, u32[]{:S(2)}, u32[]{:S(2)}) collective-permute-start(bf16[512,128]{1,0:T(8,128)(2,1)} %get-tuple-element.56), channel_id=1, source_target_pairs={{0,2},{1,5},{2,0},{3,7},{4,6},{5,1},{6,4},{7,3},{8,10},{9,13},{10,... | collective-permute-start | bytes 393224 | tf_op jit(solution)/shard_map/ppermute | solution.py:376
  (19 other events, 49.5 us)

commit v12 on v9

--- a/solution.py
+++ b/solution.py
@@ -461,7 +461,9 @@
         pairs.append(other_part(far_pair))
         numbers += [(1 - side) * per_part + index for index in range(per_part)]
     late, gates = [], []
-    for distances in (list(range(half_places // 2, half_places)), list(range(1, half_places // 2)) + [0]):
+    for distances in (list(range(half_places // 2, half_places)), list(range(1, half_places // 2)), [0]):
+        if not distances:
+            continue
         parts_of = [share if 0 < distance < half_places // 2 else 1 for distance in distances]
         mixed_some = attend_far(
             (len(numbers), *sizes),
@@ -475,13 +477,13 @@
             pairs,
             [joined[distance] for distance in distances],
         )
-        mixed, gates = mixed_some[0][0], arrived[1:]
+        mixed, gates = mixed_some[0][0], [] if gates else arrived[1:]
         for distance, pieces in zip(distances, mixed_some):
             base = (away(distance) ^ half_places) * block_width
             each = len(numbers) // len(pieces)
             for index, piece in enumerate(pieces):
                 spans = [base + number * value_width for number in numbers[index * each : (index + 1) * each]]
-                late.append((across(piece, distance) if distance else piece, spans))
+                (late if distance else placed).append((across(piece, distance) if distance else piece, spans))
     held = flush(None)
     placed.extend(late)
     held = flush(held)

time: 138 us -> 141 us (1.022)
  local copies, waits for them, and re-layouts: 3.33 us -> 14.2 us
  waiting for transfers between devices: 67.6 us -> 57.3 us
    unnamed x19 -> x41, local copies, waits for them, and re-layouts: 3.06 us -> 14 us
    ppermute x10, waiting for transfers between devices: 10.6 us -> 3.58 us  [across(): return lax.ppermute(value, ('seq', 'head'), pairs)]
    ppermute x2, waiting for transfers between devices: 50 us -> 46.6 us  [opposite(): lax.ppermute(value, 'seq', [(s, s ^ half_places) for s in range(places)])]
    pallas_call x2 -> x3, Pallas kernels: 17.4 us -> 18.7 us  [attend_far(): pl.pallas_call(partial(far_kernel, sizes, slot_count, numbers, half_place...]
  transfers between devices with their start and end apart: 18 -> 18, of which waited for: 9 -> 6; matrix products, arithmetic and copies ran while one was open for 1% -> 2% of each run, Pallas kernels for 28% -> 29%
where the time goes in v12:
time: 141 us; the launch traced here: 140 us
  waiting for transfers between devices  57.3 us (41%)
  Pallas kernels  43.2 us (31%)
  starting transfers between devices  24.1 us (17%)
  local copies, waits for them, and re-layouts  14.2 us (10%)
    ppermute x2, waiting for transfers between devices, opposite(): lax.ppermute(value, 'seq', [(s, s ^ half_places) for s in range(places)])  46.6 us
    pallas_call x3, Pallas kernels, attend_far(): pl.pallas_call(partial(far_kernel, sizes, slot_count, numbers, half_place...  18.7 us
    pallas_call x4, Pallas kernels, attend_near(): pl.pallas_call(partial(near_kernel, sizes, slot_count, slot, half_places)...  18.2 us
    unnamed x41, local copies, waits for them, and re-layouts  14 us
    ppermute x10, starting transfers between devices, across(): return lax.ppermute(value, ('seq', 'head'), pairs)  13.6 us
    ppermute x2, waiting for transfers between devices, other_part(): return lax.ppermute(value, 'parts', [(p, p ^ 1) for p in range(parts)])  7.01 us
    ppermute x2, starting transfers between devices, opposite(): lax.ppermute(value, 'seq', [(s, s ^ half_places) for s in range(places)])  4.81 us
    pallas_call x2, Pallas kernels, place_pieces(): pl.pallas_call(partial(place_kernel, width, count), out_shape=jax.ShapeDt...  4.78 us
  transfers between devices with their start and end apart: 18, of which 6 were waited for; matrix products, arithmetic and copies ran while one was open for 2% of the time, Pallas kernels for 29%

profile of v12, /device:TPU:0, one launch (start us, length us, event | category | flops | bytes accessed | tf_op | source)
XLA Modules:
  0.0 140.3 jit_solution(10985342440923761978)
XLA Ops:
  0.0 1.7 %copy-done = bf16[1,1536,4,192]{1,3,2,0:T(8,128)(2,1)S(1)} copy-done((bf16[1,1536,4,192]{1,3,2,0:T(8,128)(2,1)S(1)}, bf16[1,1536,4,192]{1,3,2,0:T(8,128)(2,1)}, u32[]{:S(2)}) %copy-start) | copy-done | bytes 2359320
  1.8 4.1 %collective-permute-start.4 = (bf16[2,192,1536]{2,1,0:T(8,128)(2,1)S(1)}, bf16[2,192,1536]{2,1,0:T(8,128)(2,1)S(1)}, u32[]{:S(2)}, u32[]{:S(2)}) collective-permute-start(bf16[2,192,1536]{2,1,0:T(8,128)(2,1)S(1)} %pick.2), channel_id=1, source_target_pairs={{0,8},{2,10},{4,12},{6,14},{8,0},{10,2},{12,4},{14,6},{1,9},{3,11}... | collective-permute-start | bytes 3538952 | tf_op jit(solution)/shard_map/ppermute | solution.py:371
  8.7 1.6 %collective-permute-start = (bf16[256,2176]{1,0:T(8,128)(2,1)S(1)}, bf16[256,2176]{1,0:T(8,128)(2,1)S(1)}, u32[]{:S(2)}, u32[]{:S(2)}) collective-permute-start(bf16[256,2176]{1,0:T(8,128)(2,1)S(1)} %prepare.1.same_ref), channel_id=1, source_target_pairs={{0,4},{1,3},{2,6},{3,1},{4,0},{5,7},{6,2},{7,5},{8,12},{9,11},{10,... | collective-permute-start | bytes 3342344 | tf_op jit(solution)/shard_map/ppermute | solution.py:376
  10.4 1.5 %collective-permute-start.3 = (bf16[256,2176]{1,0:T(8,128)(2,1)S(1)}, bf16[256,2176]{1,0:T(8,128)(2,1)S(1)}, u32[]{:S(2)}, u32[]{:S(2)}) collective-permute-start(bf16[256,2176]{1,0:T(8,128)(2,1)S(1)} %prepare.1.same_ref), channel_id=1, source_target_pairs={{0,2},{1,5},{2,0},{3,7},{4,6},{5,1},{6,4},{7,3},{8,10},{9,13},{10,... | collective-permute-start | bytes 3342344 | tf_op jit(solution)/shard_map/ppermute | solution.py:376
  11.9 1.6 %copy.8 = bf16[64,8,4,256]{3,1,2,0:T(8,128)(2,1)S(1)} copy(bf16[64,8,4,256]{3,2,1,0:T(4,128)(2,1)} %bitcast.55) | data formatting | bytes 2097152
  14.6 4.5 %attend_near.4 = (bf16[512,512]{1,0:T(8,128)(2,1)S(1)}, bf16[512,2176]{1,0:T(8,128)(2,1)S(1)}) custom-call(s32[66]{0:T(128)S(1)} %pad_add_fusion.place_ref, f32[512,256]{1,0:T(8,128)S(1)} %pad_maximum_fusion.table_ref, bf16[4,192,1536]{2,1,0:T(8,128)(2,1)S(1)} %bitcast.44, bf16[512,1024]{1,0:T(8,128)(2,1)S(1)} %bitcast.48, ...), custom_call_target="tpu_custom_call" | custom-call | flops 1024 | bytes 1024 | tf_op jit(solution)/shard_map/attend_near/pallas_call | solution.py:276
  19.9 37.3 %collective-permute-done.4.refs_0_ = bf16[2,192,1536]{2,1,0:T(8,128)(2,1)S(1)} collective-permute-done((bf16[2,192,1536]{2,1,0:T(8,128)(2,1)S(1)}, bf16[2,192,1536]{2,1,0:T(8,128)(2,1)S(1)}, u32[]{:S(2)}, u32[]{:S(2)}) %collective-permute-start.4) | collective-permute-done | bytes 1179680 | tf_op jit(solution)/shard_map/ppermute | solution.py:371
  57.2 1.5 %collective-permute-start.8 = (bf16[2,192,1536]{2,1,0:T(8,128)(2,1)S(1)}, bf16[2,192,1536]{2,1,0:T(8,128)(2,1)S(1)}, u32[]{:S(2)}, u32[]{:S(2)}) collective-permute-start(bf16[2,192,1536]{2,1,0:T(8,128)(2,1)S(1)} %collective-permute-done.4.refs_0_), channel_id=1, source_target_pairs={{0,16},{16,0},{1,17},{17,1},{2,18},{18,2},{3,19},{19,3},{4,20},{20... | collective-permute-start | bytes 3538952 | tf_op jit(solution)/shard_map/ppermute | solution.py:382
  60.2 1.9 %collective-permute-start.2 = (bf16[256,2176]{1,0:T(8,128)(2,1)S(1)}, bf16[256,2176]{1,0:T(8,128)(2,1)S(1)}, u32[]{:S(2)}, u32[]{:S(2)}) collective-permute-start(bf16[256,2176]{1,0:T(8,128)(2,1)S(1)} %collective-permute-done.same_ref), channel_id=1, source_target_pairs={{0,2},{1,5},{2,0},{3,7},{4,6},{5,1},{6,4},{7,3},{8,10},{9,13},{10,... | collective-permute-start | bytes 3342344 | tf_op jit(solution)/shard_map/ppermute | solution.py:376
  62.9 4.5 %attend_near.5 = (bf16[512,512]{1,0:T(8,128)(2,1)S(1)}, bf16[512,2176]{1,0:T(8,128)(2,1)S(1)}) custom-call(s32[66]{0:T(128)S(1)} %pad_add_fusion.place_ref, f32[512,256]{1,0:T(8,128)S(1)} %pad_maximum_fusion.table_ref, bf16[4,192,1536]{2,1,0:T(8,128)(2,1)S(1)} %bitcast.45, bf16[512,1024]{1,0:T(8,128)(2,1)S(1)} %bitcast.50, ...), custom_call_target="tpu_custom_call" | custom-call | flops 1024 | bytes 1024 | tf_op jit(solution)/shard_map/attend_near/pallas_call | solution.py:276
  67.4 4.7 %attend_near.6 = (bf16[512,512]{1,0:T(8,128)(2,1)S(1)}, bf16[512,2176]{1,0:T(8,128)(2,1)S(1)}) custom-call(s32[66]{0:T(128)S(1)} %pad_add_fusion.place_ref, f32[512,256]{1,0:T(8,128)S(1)} %pad_maximum_fusion.table_ref, bf16[4,192,1536]{2,1,0:T(8,128)(2,1)S(1)} %bitcast.46, bf16[512,1024]{1,0:T(8,128)(2,1)S(1)} %bitcast.51, ...), custom_call_target="tpu_custom_call" | custom-call | flops 1024 | bytes 1024 | tf_op jit(solution)/shard_map/attend_near/pallas_call | solution.py:276
  72.1 9.4 %collective-permute-done.7.refs_2_ = bf16[512,512]{1,0:T(8,128)(2,1)S(1)} collective-permute-done((bf16[512,512]{1,0:T(8,128)(2,1)S(1)}, bf16[512,512]{1,0:T(8,128)(2,1)S(1)}, u32[]{:S(2)}, u32[]{:S(2)}) %collective-permute-start.7) | collective-permute-done | bytes 524320 | tf_op jit(solution)/shard_map/ppermute | solution.py:371
  81.5 2.8 %collective-permute-done.8.refs_1_ = bf16[2,192,1536]{2,1,0:T(8,128)(2,1)S(1)} collective-permute-done((bf16[2,192,1536]{2,1,0:T(8,128)(2,1)S(1)}, bf16[2,192,1536]{2,1,0:T(8,128)(2,1)S(1)}, u32[]{:S(2)}, u32[]{:S(2)}) %collective-permute-start.8) | collective-permute-done | bytes 1179680 | tf_op jit(solution)/shard_map/ppermute | solution.py:382
  84.3 2.0 %collective-permute-start.9 = (bf16[256,2176]{1,0:T(8,128)(2,1)S(1)}, bf16[256,2176]{1,0:T(8,128)(2,1)S(1)}, u32[]{:S(2)}, u32[]{:S(2)}) collective-permute-start(bf16[256,2176]{1,0:T(8,128)(2,1)S(1)} %collective-permute-done.2.same_ref), channel_id=1, source_target_pairs={{0,1},{1,0},{2,3},{3,2},{4,5},{5,4},{6,7},{7,6},{8,9},{9,8},{10,11... | collective-permute-start | bytes 3342344 | tf_op jit(solution)/shard_map/ppermute | solution.py:379
  86.3 1.5 %collective-permute-start.10 = (bf16[512,512]{1,0:T(8,128)(2,1)S(1)}, bf16[512,512]{1,0:T(8,128)(2,1)S(1)}, u32[]{:S(2)}, u32[]{:S(2)}) collective-permute-start(bf16[512,512]{1,0:T(8,128)(2,1)S(1)} %collective-permute-done.7.refs_2_), channel_id=1, source_target_pairs={{0,16},{16,0},{1,17},{17,1},{2,18},{18,2},{3,19},{19,3},{4,20},{20... | collective-permute-start | bytes 1572872 | tf_op jit(solution)/shard_map/ppermute | solution.py:382
  90.6 4.5 %attend_near.7 = (bf16[512,512]{1,0:T(8,128)(2,1)S(1)}, bf16[512,2176]{1,0:T(8,128)(2,1)S(1)}) custom-call(s32[66]{0:T(128)S(1)} %pad_add_fusion.place_ref, f32[512,256]{1,0:T(8,128)S(1)} %pad_maximum_fusion.table_ref, bf16[4,192,1536]{2,1,0:T(8,128)(2,1)S(1)} %bitcast.47, bf16[512,1024]{1,0:T(8,128)(2,1)S(1)} %bitcast.52, ...), custom_call_target="tpu_custom_call" | custom-call | flops 1024 | bytes 1024 | tf_op jit(solution)/shard_map/attend_near/pallas_call | solution.py:276
  95.9 4.2 %collective-permute-done.10.refs_3_ = bf16[512,512]{1,0:T(8,128)(2,1)S(1)} collective-permute-done((bf16[512,512]{1,0:T(8,128)(2,1)S(1)}, bf16[512,512]{1,0:T(8,128)(2,1)S(1)}, u32[]{:S(2)}, u32[]{:S(2)}) %collective-permute-start.10) | collective-permute-done | bytes 524320 | tf_op jit(solution)/shard_map/ppermute | solution.py:382
  100.1 8.9 %attend_far.3 = (bf16[512,512]{1,0:T(8,128)(2,1)}, bf16[512,512]{1,0:T(8,128)(2,1)}) custom-call(s32[66]{0:T(128)S(1)} %pad_add_fusion.place_ref, f32[512,256]{1,0:T(8,128)S(1)} %pad_maximum_fusion.table_ref, bf16[2,192,1536]{2,1,0:T(8,128)(2,1)S(1)} %collective-permute-done.4.refs_0_, bf16[2,192,1536]{2,1,0:T(8,128)(2,1)S(1)} %collective-permute-done.8.refs_1_, ...), custom_call_target="tpu_custom_call" | custom-call | flops 1024 | bytes 1024 | tf_op jit(solution)/shard_map/attend_far/pallas_call | solution.py:297
  112.0 2.6 %collective-permute-done.15.refs_3_ = bf16[512,512]{1,0:T(8,128)(2,1)S(1)} collective-permute-done((bf16[512,512]{1,0:T(8,128)(2,1)S(1)}, bf16[512,512]{1,0:T(8,128)(2,1)S(1)}, u32[]{:S(2)}, u32[]{:S(2)}) %collective-permute-start.15) | collective-permute-done | bytes 524320 | tf_op jit(solution)/shard_map/ppermute | solution.py:376
  114.6 5.4 %attend_far.4 = (bf16[512,256]{1,0:T(8,128)(2,1)}, bf16[512,256]{1,0:T(8,128)(2,1)}) custom-call(s32[66]{0:T(128)S(1)} %pad_add_fusion.place_ref, f32[512,256]{1,0:T(8,128)S(1)} %pad_maximum_fusion.table_ref, bf16[2,192,1536]{2,1,0:T(8,128)(2,1)S(1)} %collective-permute-done.4.refs_0_, bf16[2,192,1536]{2,1,0:T(8,128)(2,1)S(1)} %collective-permute-done.8.refs_1_, ...), custom_call_target="tpu_custom_call" | custom-call | flops 1024 | bytes 1024 | tf_op jit(solution)/shard_map/attend_far/pallas_call | solution.py:297
  123.2 1.6 %copy-done.5 = bf16[512,2176]{1,0:T(8,128)(2,1)S(1)} copy-done((bf16[512,2176]{1,0:T(8,128)(2,1)S(1)}, bf16[512,2176]{1,0:T(8,128)(2,1)}, u32[]{:S(2)}) %copy-start.5) | copy-done | bytes 2228248
  124.8 4.4 %attend_far.5.refs_4_ = bf16[512,512]{1,0:T(8,128)(2,1)S(1)} custom-call(s32[66]{0:T(128)S(1)} %pad_add_fusion.place_ref, f32[512,256]{1,0:T(8,128)S(1)} %pad_maximum_fusion.table_ref, bf16[2,192,1536]{2,1,0:T(8,128)(2,1)S(1)} %collective-permute-done.4.refs_0_, bf16[2,192,1536]{2,1,0:T(8,128)(2,1)S(1)} %collective-permute-done.8.refs_1_, ...), custom_call_target="tpu_custom_call" | custom-call | flops 1024 | bytes 1024 | tf_op jit(solution)/shard_map/attend_far/pallas_call | solution.py:297
  135.3 2.2 %place_pieces.2.refs_4_ = bf16[512,4096]{1,0:T(8,128)(2,1)} custom-call(s32[20]{0:T(128)S(1)} %stack.143.offsets_ref, bf16[512,512]{1,0:T(8,128)(2,1)S(1)} %copy-done.10, bf16[512,512]{1,0:T(8,128)(2,1)S(1)} %copy-done.14, bf16[512,512]{1,0:T(8,128)(2,1)S(1)} %copy-done.12, bf16[512,512]{1,0:T(8,128)(2,1)S(1)} %copy-done.16, bf16[512,512]{1,0:T(8,128)(2,1)S(1)} %copy-done.7), custom_call_target="tpu_custom_call" | custom-call | flops 1024 | bytes 1024 | tf_op jit(solution)/shard_map/place_pieces/pallas_call | solution.py:333
  137.6 2.6 %place_pieces.3 = bf16[512,4096]{1,0:T(8,128)(2,1)} custom-call(s32[12]{0:T(128)S(1)} %stack.120.offsets_ref, bf16[512,512]{1,0:T(8,128)(2,1)} %collective-permute-done.11.refs_0_, bf16[512,512]{1,0:T(8,128)(2,1)} %collective-permute-done.12.refs_1_, bf16[512,256]{1,0:T(8,128)(2,1)} %collective-permute-done.16.refs_2_, ...), custom_call_target="tpu_custom_call", output_to_operand_aliasing={{}: (5, {})} | custom-call | flops 1024 | bytes 1024 | tf_op jit(solution)/shard_map/place_pieces/pallas_call | solution.py:333
  (74 shorter events, 22.8 us)
Async XLA Ops:
  1.7 4.3 %copy-start.19 = (f32[512]{0:T(512)S(1)}, f32[512]{0:T(512)}, u32[]{:S(2)}) copy-start(f32[512]{0:T(512)} %param.8) | copy-start | bytes 6148
  1.8 55.5 %collective-permute-start.4 = (bf16[2,192,1536]{2,1,0:T(8,128)(2,1)S(1)}, bf16[2,192,1536]{2,1,0:T(8,128)(2,1)S(1)}, u32[]{:S(2)}, u32[]{:S(2)}) collective-permute-start(bf16[2,192,1536]{2,1,0:T(8,128)(2,1)S(1)} %pick.2), channel_id=1, source_target_pairs={{0,8},{2,10},{4,12},{6,14},{8,0},{10,2},{12,4},{14,6},{1,9},{3,11}... | collective-permute-start | bytes 3538952 | tf_op jit(solution)/shard_map/ppermute | solution.py:371
  8.7 5.9 %collective-permute-start.1 = (bf16[256,2176]{1,0:T(8,128)(2,1)S(1)}, bf16[256,2176]{1,0:T(8,128)(2,1)S(1)}, u32[]{:S(2)}, u32[]{:S(2)}) collective-permute-start(bf16[256,2176]{1,0:T(8,128)(2,1)S(1)} %prepare.1.same_ref), channel_id=1, source_target_pairs={{0,1},{1,0},{2,3},{3,2},{4,5},{5,4},{6,7},{7,6},{8,9},{9,8},{10,11... | collective-permute-start | bytes 3342344 | tf_op jit(solution)/shard_map/ppermute | solution.py:379
  8.7 51.0 %collective-permute-start = (bf16[256,2176]{1,0:T(8,128)(2,1)S(1)}, bf16[256,2176]{1,0:T(8,128)(2,1)S(1)}, u32[]{:S(2)}, u32[]{:S(2)}) collective-permute-start(bf16[256,2176]{1,0:T(8,128)(2,1)S(1)} %prepare.1.same_ref), channel_id=1, source_target_pairs={{0,4},{1,3},{2,6},{3,1},{4,0},{5,7},{6,2},{7,5},{8,12},{9,11},{10,... | collective-permute-start | bytes 3342344 | tf_op jit(solution)/shard_map/ppermute | solution.py:376
  10.4 49.3 %collective-permute-start.3 = (bf16[256,2176]{1,0:T(8,128)(2,1)S(1)}, bf16[256,2176]{1,0:T(8,128)(2,1)S(1)}, u32[]{:S(2)}, u32[]{:S(2)}) collective-permute-start(bf16[256,2176]{1,0:T(8,128)(2,1)S(1)} %prepare.1.same_ref), channel_id=1, source_target_pairs={{0,2},{1,5},{2,0},{3,7},{4,6},{5,1},{6,4},{7,3},{8,10},{9,13},{10,... | collective-permute-start | bytes 3342344 | tf_op jit(solution)/shard_map/ppermute | solution.py:376
  19.9 47.5 %copy-start.4 = (bf16[512,2176]{1,0:T(8,128)(2,1)}, bf16[512,2176]{1,0:T(8,128)(2,1)S(1)}, u32[]{:S(2)}) copy-start(bf16[512,2176]{1,0:T(8,128)(2,1)S(1)} %get-tuple-element.52.refs_4_) | copy-start | bytes 6684676
  57.2 27.1 %collective-permute-start.8 = (bf16[2,192,1536]{2,1,0:T(8,128)(2,1)S(1)}, bf16[2,192,1536]{2,1,0:T(8,128)(2,1)S(1)}, u32[]{:S(2)}, u32[]{:S(2)}) collective-permute-start(bf16[2,192,1536]{2,1,0:T(8,128)(2,1)S(1)} %collective-permute-done.4.refs_0_), channel_id=1, source_target_pairs={{0,16},{16,0},{1,17},{17,1},{2,18},{18,2},{3,19},{19,3},{4,20},{20... | collective-permute-start | bytes 3538952 | tf_op jit(solution)/shard_map/ppermute | solution.py:382
  59.7 3.2 %collective-permute-start.5 = (bf16[256,2176]{1,0:T(8,128)(2,1)S(1)}, bf16[256,2176]{1,0:T(8,128)(2,1)S(1)}, u32[]{:S(2)}, u32[]{:S(2)}) collective-permute-start(bf16[256,2176]{1,0:T(8,128)(2,1)S(1)} %collective-permute-done.same_ref), channel_id=1, source_target_pairs={{0,1},{1,0},{2,3},{3,2},{4,5},{5,4},{6,7},{7,6},{8,9},{9,8},{10,11... | collective-permute-start | bytes 3342344 | tf_op jit(solution)/shard_map/ppermute | solution.py:379
  60.2 7.2 %collective-permute-start.6 = (bf16[256,2176]{1,0:T(8,128)(2,1)S(1)}, bf16[256,2176]{1,0:T(8,128)(2,1)S(1)}, u32[]{:S(2)}, u32[]{:S(2)}) collective-permute-start(bf16[256,2176]{1,0:T(8,128)(2,1)S(1)} %collective-permute-done.3.same_ref), channel_id=1, source_target_pairs={{0,1},{1,0},{2,3},{3,2},{4,5},{5,4},{6,7},{7,6},{8,9},{9,8},{10,11... | collective-permute-start | bytes 3342344 | tf_op jit(solution)/shard_map/ppermute | solution.py:379
  60.2 21.3 %collective-permute-start.2 = (bf16[256,2176]{1,0:T(8,128)(2,1)S(1)}, bf16[256,2176]{1,0:T(8,128)(2,1)S(1)}, u32[]{:S(2)}, u32[]{:S(2)}) collective-permute-start(bf16[256,2176]{1,0:T(8,128)(2,1)S(1)} %collective-permute-done.same_ref), channel_id=1, source_target_pairs={{0,2},{1,5},{2,0},{3,7},{4,6},{5,1},{6,4},{7,3},{8,10},{9,13},{10,... | collective-permute-start | bytes 3342344 | tf_op jit(solution)/shard_map/ppermute | solution.py:376
  62.2 19.3 %collective-permute-start.7 = (bf16[512,512]{1,0:T(8,128)(2,1)S(1)}, bf16[512,512]{1,0:T(8,128)(2,1)S(1)}, u32[]{:S(2)}, u32[]{:S(2)}) collective-permute-start(bf16[512,512]{1,0:T(8,128)(2,1)S(1)} %pick.3), channel_id=1, source_target_pairs={{0,8},{2,10},{4,12},{6,14},{8,0},{10,2},{12,4},{14,6},{1,9},{3,11}... | collective-permute-start | bytes 1572872 | tf_op jit(solution)/shard_map/ppermute | solution.py:371
  84.3 6.3 %collective-permute-start.9 = (bf16[256,2176]{1,0:T(8,128)(2,1)S(1)}, bf16[256,2176]{1,0:T(8,128)(2,1)S(1)}, u32[]{:S(2)}, u32[]{:S(2)}) collective-permute-start(bf16[256,2176]{1,0:T(8,128)(2,1)S(1)} %collective-permute-done.2.same_ref), channel_id=1, source_target_pairs={{0,1},{1,0},{2,3},{3,2},{4,5},{5,4},{6,7},{7,6},{8,9},{9,8},{10,11... | collective-permute-start | bytes 3342344 | tf_op jit(solution)/shard_map/ppermute | solution.py:379
  86.3 13.8 %collective-permute-start.10 = (bf16[512,512]{1,0:T(8,128)(2,1)S(1)}, bf16[512,512]{1,0:T(8,128)(2,1)S(1)}, u32[]{:S(2)}, u32[]{:S(2)}) collective-permute-start(bf16[512,512]{1,0:T(8,128)(2,1)S(1)} %collective-permute-done.7.refs_2_), channel_id=1, source_target_pairs={{0,16},{16,0},{1,17},{17,1},{2,18},{18,2},{3,19},{19,3},{4,20},{20... | collective-permute-start | bytes 1572872 | tf_op jit(solution)/shard_map/ppermute | solution.py:382
  87.8 24.1 %collective-permute-start.14 = (bf16[512,512]{1,0:T(8,128)(2,1)S(1)}, bf16[512,512]{1,0:T(8,128)(2,1)S(1)}, u32[]{:S(2)}, u32[]{:S(2)}) collective-permute-start(bf16[512,512]{1,0:T(8,128)(2,1)S(1)} %get-tuple-element.36), channel_id=1, source_target_pairs={{0,4},{1,3},{2,6},{3,1},{4,0},{5,7},{6,2},{7,5},{8,12},{9,11},{10,... | collective-permute-start | bytes 1572872 | tf_op jit(solution)/shard_map/ppermute | solution.py:376
  89.2 22.8 %collective-permute-start.13 = (bf16[512,512]{1,0:T(8,128)(2,1)S(1)}, bf16[512,512]{1,0:T(8,128)(2,1)S(1)}, u32[]{:S(2)}, u32[]{:S(2)}) collective-permute-start(bf16[512,512]{1,0:T(8,128)(2,1)S(1)} %get-tuple-element.33), channel_id=1, source_target_pairs={{0,2},{1,5},{2,0},{3,7},{4,6},{5,1},{6,4},{7,3},{8,10},{9,13},{10,... | collective-permute-start | bytes 1572872 | tf_op jit(solution)/shard_map/ppermute | solution.py:376
  95.1 19.5 %collective-permute-start.15 = (bf16[512,512]{1,0:T(8,128)(2,1)S(1)}, bf16[512,512]{1,0:T(8,128)(2,1)S(1)}, u32[]{:S(2)}, u32[]{:S(2)}) collective-permute-start(bf16[512,512]{1,0:T(8,128)(2,1)S(1)} %get-tuple-element.41), channel_id=1, source_target_pairs={{0,6},{1,7},{2,4},{3,5},{4,2},{5,3},{6,0},{7,1},{8,14},{9,15},{10,... | collective-permute-start | bytes 1572872 | tf_op jit(solution)/shard_map/ppermute | solution.py:376
  100.1 14.5 %copy-start.2 = (bf16[512,512]{1,0:T(8,128)(2,1)}, bf16[512,512]{1,0:T(8,128)(2,1)S(1)}, u32[]{:S(2)}) copy-start(bf16[512,512]{1,0:T(8,128)(2,1)S(1)} %collective-permute-done.10.refs_3_) | copy-start | bytes 1572868
  109.1 28.5 %collective-permute-start.11 = (bf16[512,512]{1,0:T(8,128)(2,1)}, bf16[512,512]{1,0:T(8,128)(2,1)}, u32[]{:S(2)}, u32[]{:S(2)}) collective-permute-start(bf16[512,512]{1,0:T(8,128)(2,1)} %get-tuple-element.45), channel_id=1, source_target_pairs={{0,4},{1,3},{2,6},{3,1},{4,0},{5,7},{6,2},{7,5},{8,12},{9,11},{10,... | collective-permute-start | bytes 1572872 | tf_op jit(solution)/shard_map/ppermute | solution.py:376
  110.6 27.0 %collective-permute-start.12 = (bf16[512,512]{1,0:T(8,128)(2,1)}, bf16[512,512]{1,0:T(8,128)(2,1)}, u32[]{:S(2)}, u32[]{:S(2)}) collective-permute-start(bf16[512,512]{1,0:T(8,128)(2,1)} %get-tuple-element.46), channel_id=1, source_target_pairs={{0,6},{1,7},{2,4},{3,5},{4,2},{5,3},{6,0},{7,1},{8,14},{9,15},{10,... | collective-permute-start | bytes 1572872 | tf_op jit(solution)/shard_map/ppermute | solution.py:376
  112.0 8.0 %copy-start.11 = (bf16[512,512]{1,0:T(8,128)(2,1)}, bf16[512,512]{1,0:T(8,128)(2,1)S(1)}, u32[]{:S(2)}) copy-start(bf16[512,512]{1,0:T(8,128)(2,1)S(1)} %collective-permute-done.14.refs_2_) | copy-start | bytes 1572868
  112.0 8.0 %copy-start.13 = (bf16[512,512]{1,0:T(8,128)(2,1)}, bf16[512,512]{1,0:T(8,128)(2,1)S(1)}, u32[]{:S(2)}) copy-start(bf16[512,512]{1,0:T(8,128)(2,1)S(1)} %collective-permute-done.13.refs_1_) | copy-start | bytes 1572868
  114.6 5.4 %copy-start.15 = (bf16[512,512]{1,0:T(8,128)(2,1)}, bf16[512,512]{1,0:T(8,128)(2,1)S(1)}, u32[]{:S(2)}) copy-start(bf16[512,512]{1,0:T(8,128)(2,1)S(1)} %collective-permute-done.15.refs_3_) | copy-start | bytes 1572868
  120.0 17.6 %collective-permute-start.16 = (bf16[512,256]{1,0:T(8,128)(2,1)}, bf16[512,256]{1,0:T(8,128)(2,1)}, u32[]{:S(2)}, u32[]{:S(2)}) collective-permute-start(bf16[512,256]{1,0:T(8,128)(2,1)} %get-tuple-element.49), channel_id=1, source_target_pairs={{0,2},{1,5},{2,0},{3,7},{4,6},{5,1},{6,4},{7,3},{8,10},{9,13},{10,... | collective-permute-start | bytes 786440 | tf_op jit(solution)/shard_map/ppermute | solution.py:376
  120.8 16.7 %collective-permute-start.17 = (bf16[512,256]{1,0:T(8,128)(2,1)}, bf16[512,256]{1,0:T(8,128)(2,1)}, u32[]{:S(2)}, u32[]{:S(2)}) collective-permute-start(bf16[512,256]{1,0:T(8,128)(2,1)} %get-tuple-element.50), channel_id=1, source_target_pairs={{0,2},{1,5},{2,0},{3,7},{4,6},{5,1},{6,4},{7,3},{8,10},{9,13},{10,... | collective-permute-start | bytes 786440 | tf_op jit(solution)/shard_map/ppermute | solution.py:376
  (14 other events, 23.5 us)

commit v13 on v12

--- a/solution.py
+++ b/solution.py
@@ -9,7 +9,8 @@
 from jax.sharding import PartitionSpec as P
 
 epsilon = 1e-06
-VMEM_LIMIT = 32 * 1024 * 1024
+VMEM_LIMIT = 14 * 1024 * 1024
+VMEM_SMALL = 8 * 1024 * 1024
 LIGHT = pl.CostEstimate(flops=1024, bytes_accessed=1024, transcendentals=0)
 FAR = -(2.0**100)
 NT = (((1,), (1,)), ((), ()))
@@ -72,7 +73,7 @@
         out_shape=jax.ShapeDtypeStruct((rows, width), jnp.bfloat16),
         in_specs=[pl.BlockSpec(memory_space=pltpu.SMEM), vmem, vmem],
         out_specs=vmem,
-        compiler_params=pltpu.CompilerParams(vmem_limit_bytes=VMEM_LIMIT),
+        compiler_params=pltpu.CompilerParams(vmem_limit_bytes=VMEM_SMALL),
         cost_estimate=LIGHT,
         name="prepare",
     )(place, jnp.transpose(latents), gains[None, :])
@@ -96,7 +97,7 @@
             out_specs=pl.BlockSpec(tuple(out_shape), lambda step, index_ref: (0,) * len(out_shape)),
         ),
         out_shape=jax.ShapeDtypeStruct(tuple(out_shape), source.dtype),
-        compiler_params=pltpu.CompilerParams(vmem_limit_bytes=VMEM_LIMIT),
+        compiler_params=pltpu.CompilerParams(vmem_limit_bytes=VMEM_SMALL),
         cost_estimate=LIGHT,
         name="pick",
     )(jnp.reshape(index, (1,)).astype(jnp.int32), source)
@@ -337,7 +338,7 @@
         out_specs=any_space,
         scratch_shapes=[pltpu.SemaphoreType.DMA((len(offsets),))],
         input_output_aliases=aliases,
-        compiler_params=pltpu.CompilerParams(vmem_limit_bytes=VMEM_LIMIT),
+        compiler_params=pltpu.CompilerParams(vmem_limit_bytes=VMEM_SMALL),
         cost_estimate=LIGHT,
         name="place_pieces",
     )(*operands)

time: 141 us -> 141 us (level)
  no operation moved by 1% of the time
where the time goes in v13:
time: 141 us; the launch traced here: 140 us
  waiting for transfers between devices  57.3 us (41%)
  Pallas kernels  43.2 us (31%)
  starting transfers between devices  24.1 us (17%)
  local copies, waits for them, and re-layouts  14.2 us (10%)
    ppermute x2, waiting for transfers between devices, opposite(): lax.ppermute(value, 'seq', [(s, s ^ half_places) for s in range(places)])  46.6 us
    pallas_call x3, Pallas kernels, attend_far(): pl.pallas_call(partial(far_kernel, sizes, slot_count, numbers, half_place...  18.7 us
    pallas_call x4, Pallas kernels, attend_near(): pl.pallas_call(partial(near_kernel, sizes, slot_count, slot, half_places)...  18.2 us
    unnamed x41, local copies, waits for them, and re-layouts  14 us
    ppermute x10, starting transfers between devices, across(): return lax.ppermute(value, ('seq', 'head'), pairs)  13.6 us
    ppermute x2, waiting for transfers between devices, other_part(): return lax.ppermute(value, 'parts', [(p, p ^ 1) for p in range(parts)])  7.01 us
    ppermute x2, starting transfers between devices, opposite(): lax.ppermute(value, 'seq', [(s, s ^ half_places) for s in range(places)])  4.81 us
    pallas_call x2, Pallas kernels, place_pieces(): pl.pallas_call(partial(place_kernel, width, count), out_shape=jax.ShapeDt...  4.78 us
  transfers between devices with their start and end apart: 18, of which 6 were waited for; matrix products, arithmetic and copies ran while one was open for 2% of the time, Pallas kernels for 29%

profile of v13, /device:TPU:0, one launch (start us, length us, event | category | flops | bytes accessed | tf_op | source)
XLA Modules:
  0.0 140.3 jit_solution(10132069092946033291)
XLA Ops:
  0.0 1.7 %copy-done = bf16[1,1536,4,192]{1,3,2,0:T(8,128)(2,1)S(1)} copy-done((bf16[1,1536,4,192]{1,3,2,0:T(8,128)(2,1)S(1)}, bf16[1,1536,4,192]{1,3,2,0:T(8,128)(2,1)}, u32[]{:S(2)}) %copy-start) | copy-done | bytes 2359320
  1.8 4.1 %collective-permute-start.4 = (bf16[2,192,1536]{2,1,0:T(8,128)(2,1)S(1)}, bf16[2,192,1536]{2,1,0:T(8,128)(2,1)S(1)}, u32[]{:S(2)}, u32[]{:S(2)}) collective-permute-start(bf16[2,192,1536]{2,1,0:T(8,128)(2,1)S(1)} %pick.2), channel_id=1, source_target_pairs={{0,8},{2,10},{4,12},{6,14},{8,0},{10,2},{12,4},{14,6},{1,9},{3,11}... | collective-permute-start | bytes 3538952 | tf_op jit(solution)/shard_map/ppermute | solution.py:372
  8.7 1.6 %collective-permute-start = (bf16[256,2176]{1,0:T(8,128)(2,1)S(1)}, bf16[256,2176]{1,0:T(8,128)(2,1)S(1)}, u32[]{:S(2)}, u32[]{:S(2)}) collective-permute-start(bf16[256,2176]{1,0:T(8,128)(2,1)S(1)} %prepare.1.same_ref), channel_id=1, source_target_pairs={{0,4},{1,3},{2,6},{3,1},{4,0},{5,7},{6,2},{7,5},{8,12},{9,11},{10,... | collective-permute-start | bytes 3342344 | tf_op jit(solution)/shard_map/ppermute | solution.py:377
  10.4 1.5 %collective-permute-start.3 = (bf16[256,2176]{1,0:T(8,128)(2,1)S(1)}, bf16[256,2176]{1,0:T(8,128)(2,1)S(1)}, u32[]{:S(2)}, u32[]{:S(2)}) collective-permute-start(bf16[256,2176]{1,0:T(8,128)(2,1)S(1)} %prepare.1.same_ref), channel_id=1, source_target_pairs={{0,2},{1,5},{2,0},{3,7},{4,6},{5,1},{6,4},{7,3},{8,10},{9,13},{10,... | collective-permute-start | bytes 3342344 | tf_op jit(solution)/shard_map/ppermute | solution.py:377
  11.9 1.6 %copy.8 = bf16[64,8,4,256]{3,1,2,0:T(8,128)(2,1)S(1)} copy(bf16[64,8,4,256]{3,2,1,0:T(4,128)(2,1)} %bitcast.55) | data formatting | bytes 2097152
  14.6 4.5 %attend_near.4 = (bf16[512,512]{1,0:T(8,128)(2,1)S(1)}, bf16[512,2176]{1,0:T(8,128)(2,1)S(1)}) custom-call(s32[66]{0:T(128)S(1)} %pad_add_fusion.place_ref, f32[512,256]{1,0:T(8,128)S(1)} %pad_maximum_fusion.table_ref, bf16[4,192,1536]{2,1,0:T(8,128)(2,1)S(1)} %bitcast.44, bf16[512,1024]{1,0:T(8,128)(2,1)S(1)} %bitcast.48, ...), custom_call_target="tpu_custom_call" | custom-call | flops 1024 | bytes 1024 | tf_op jit(solution)/shard_map/attend_near/pallas_call | solution.py:277
  19.9 37.3 %collective-permute-done.4.refs_0_ = bf16[2,192,1536]{2,1,0:T(8,128)(2,1)S(1)} collective-permute-done((bf16[2,192,1536]{2,1,0:T(8,128)(2,1)S(1)}, bf16[2,192,1536]{2,1,0:T(8,128)(2,1)S(1)}, u32[]{:S(2)}, u32[]{:S(2)}) %collective-permute-start.4) | collective-permute-done | bytes 1179680 | tf_op jit(solution)/shard_map/ppermute | solution.py:372
  57.2 1.5 %collective-permute-start.8 = (bf16[2,192,1536]{2,1,0:T(8,128)(2,1)S(1)}, bf16[2,192,1536]{2,1,0:T(8,128)(2,1)S(1)}, u32[]{:S(2)}, u32[]{:S(2)}) collective-permute-start(bf16[2,192,1536]{2,1,0:T(8,128)(2,1)S(1)} %collective-permute-done.4.refs_0_), channel_id=1, source_target_pairs={{0,16},{16,0},{1,17},{17,1},{2,18},{18,2},{3,19},{19,3},{4,20},{20... | collective-permute-start | bytes 3538952 | tf_op jit(solution)/shard_map/ppermute | solution.py:383
  60.2 1.9 %collective-permute-start.2 = (bf16[256,2176]{1,0:T(8,128)(2,1)S(1)}, bf16[256,2176]{1,0:T(8,128)(2,1)S(1)}, u32[]{:S(2)}, u32[]{:S(2)}) collective-permute-start(bf16[256,2176]{1,0:T(8,128)(2,1)S(1)} %collective-permute-done.same_ref), channel_id=1, source_target_pairs={{0,2},{1,5},{2,0},{3,7},{4,6},{5,1},{6,4},{7,3},{8,10},{9,13},{10,... | collective-permute-start | bytes 3342344 | tf_op jit(solution)/shard_map/ppermute | solution.py:377
  62.9 4.5 %attend_near.5 = (bf16[512,512]{1,0:T(8,128)(2,1)S(1)}, bf16[512,2176]{1,0:T(8,128)(2,1)S(1)}) custom-call(s32[66]{0:T(128)S(1)} %pad_add_fusion.place_ref, f32[512,256]{1,0:T(8,128)S(1)} %pad_maximum_fusion.table_ref, bf16[4,192,1536]{2,1,0:T(8,128)(2,1)S(1)} %bitcast.45, bf16[512,1024]{1,0:T(8,128)(2,1)S(1)} %bitcast.50, ...), custom_call_target="tpu_custom_call" | custom-call | flops 1024 | bytes 1024 | tf_op jit(solution)/shard_map/attend_near/pallas_call | solution.py:277
  67.4 4.7 %attend_near.6 = (bf16[512,512]{1,0:T(8,128)(2,1)S(1)}, bf16[512,2176]{1,0:T(8,128)(2,1)S(1)}) custom-call(s32[66]{0:T(128)S(1)} %pad_add_fusion.place_ref, f32[512,256]{1,0:T(8,128)S(1)} %pad_maximum_fusion.table_ref, bf16[4,192,1536]{2,1,0:T(8,128)(2,1)S(1)} %bitcast.46, bf16[512,1024]{1,0:T(8,128)(2,1)S(1)} %bitcast.51, ...), custom_call_target="tpu_custom_call" | custom-call | flops 1024 | bytes 1024 | tf_op jit(solution)/shard_map/attend_near/pallas_call | solution.py:277
  72.1 9.4 %collective-permute-done.7.refs_2_ = bf16[512,512]{1,0:T(8,128)(2,1)S(1)} collective-permute-done((bf16[512,512]{1,0:T(8,128)(2,1)S(1)}, bf16[512,512]{1,0:T(8,128)(2,1)S(1)}, u32[]{:S(2)}, u32[]{:S(2)}) %collective-permute-start.7) | collective-permute-done | bytes 524320 | tf_op jit(solution)/shard_map/ppermute | solution.py:372
  81.5 2.8 %collective-permute-done.8.refs_1_ = bf16[2,192,1536]{2,1,0:T(8,128)(2,1)S(1)} collective-permute-done((bf16[2,192,1536]{2,1,0:T(8,128)(2,1)S(1)}, bf16[2,192,1536]{2,1,0:T(8,128)(2,1)S(1)}, u32[]{:S(2)}, u32[]{:S(2)}) %collective-permute-start.8) | collective-permute-done | bytes 1179680 | tf_op jit(solution)/shard_map/ppermute | solution.py:383
  84.3 2.0 %collective-permute-start.9 = (bf16[256,2176]{1,0:T(8,128)(2,1)S(1)}, bf16[256,2176]{1,0:T(8,128)(2,1)S(1)}, u32[]{:S(2)}, u32[]{:S(2)}) collective-permute-start(bf16[256,2176]{1,0:T(8,128)(2,1)S(1)} %collective-permute-done.2.same_ref), channel_id=1, source_target_pairs={{0,1},{1,0},{2,3},{3,2},{4,5},{5,4},{6,7},{7,6},{8,9},{9,8},{10,11... | collective-permute-start | bytes 3342344 | tf_op jit(solution)/shard_map/ppermute | solution.py:380
  86.3 1.5 %collective-permute-start.10 = (bf16[512,512]{1,0:T(8,128)(2,1)S(1)}, bf16[512,512]{1,0:T(8,128)(2,1)S(1)}, u32[]{:S(2)}, u32[]{:S(2)}) collective-permute-start(bf16[512,512]{1,0:T(8,128)(2,1)S(1)} %collective-permute-done.7.refs_2_), channel_id=1, source_target_pairs={{0,16},{16,0},{1,17},{17,1},{2,18},{18,2},{3,19},{19,3},{4,20},{20... | collective-permute-start | bytes 1572872 | tf_op jit(solution)/shard_map/ppermute | solution.py:383
  90.6 4.5 %attend_near.7 = (bf16[512,512]{1,0:T(8,128)(2,1)S(1)}, bf16[512,2176]{1,0:T(8,128)(2,1)S(1)}) custom-call(s32[66]{0:T(128)S(1)} %pad_add_fusion.place_ref, f32[512,256]{1,0:T(8,128)S(1)} %pad_maximum_fusion.table_ref, bf16[4,192,1536]{2,1,0:T(8,128)(2,1)S(1)} %bitcast.47, bf16[512,1024]{1,0:T(8,128)(2,1)S(1)} %bitcast.52, ...), custom_call_target="tpu_custom_call" | custom-call | flops 1024 | bytes 1024 | tf_op jit(solution)/shard_map/attend_near/pallas_call | solution.py:277
  95.9 4.2 %collective-permute-done.10.refs_3_ = bf16[512,512]{1,0:T(8,128)(2,1)S(1)} collective-permute-done((bf16[512,512]{1,0:T(8,128)(2,1)S(1)}, bf16[512,512]{1,0:T(8,128)(2,1)S(1)}, u32[]{:S(2)}, u32[]{:S(2)}) %collective-permute-start.10) | collective-permute-done | bytes 524320 | tf_op jit(solution)/shard_map/ppermute | solution.py:383
  100.1 8.9 %attend_far.3 = (bf16[512,512]{1,0:T(8,128)(2,1)}, bf16[512,512]{1,0:T(8,128)(2,1)}) custom-call(s32[66]{0:T(128)S(1)} %pad_add_fusion.place_ref, f32[512,256]{1,0:T(8,128)S(1)} %pad_maximum_fusion.table_ref, bf16[2,192,1536]{2,1,0:T(8,128)(2,1)S(1)} %collective-permute-done.4.refs_0_, bf16[2,192,1536]{2,1,0:T(8,128)(2,1)S(1)} %collective-permute-done.8.refs_1_, ...), custom_call_target="tpu_custom_call" | custom-call | flops 1024 | bytes 1024 | tf_op jit(solution)/shard_map/attend_far/pallas_call | solution.py:298
  112.0 2.6 %collective-permute-done.15.refs_3_ = bf16[512,512]{1,0:T(8,128)(2,1)S(1)} collective-permute-done((bf16[512,512]{1,0:T(8,128)(2,1)S(1)}, bf16[512,512]{1,0:T(8,128)(2,1)S(1)}, u32[]{:S(2)}, u32[]{:S(2)}) %collective-permute-start.15) | collective-permute-done | bytes 524320 | tf_op jit(solution)/shard_map/ppermute | solution.py:377
  114.6 5.4 %attend_far.4 = (bf16[512,256]{1,0:T(8,128)(2,1)}, bf16[512,256]{1,0:T(8,128)(2,1)}) custom-call(s32[66]{0:T(128)S(1)} %pad_add_fusion.place_ref, f32[512,256]{1,0:T(8,128)S(1)} %pad_maximum_fusion.table_ref, bf16[2,192,1536]{2,1,0:T(8,128)(2,1)S(1)} %collective-permute-done.4.refs_0_, bf16[2,192,1536]{2,1,0:T(8,128)(2,1)S(1)} %collective-permute-done.8.refs_1_, ...), custom_call_target="tpu_custom_call" | custom-call | flops 1024 | bytes 1024 | tf_op jit(solution)/shard_map/attend_far/pallas_call | solution.py:298
  123.2 1.6 %copy-done.5 = bf16[512,2176]{1,0:T(8,128)(2,1)S(1)} copy-done((bf16[512,2176]{1,0:T(8,128)(2,1)S(1)}, bf16[512,2176]{1,0:T(8,128)(2,1)}, u32[]{:S(2)}) %copy-start.5) | copy-done | bytes 2228248
  124.8 4.4 %attend_far.5.refs_4_ = bf16[512,512]{1,0:T(8,128)(2,1)S(1)} custom-call(s32[66]{0:T(128)S(1)} %pad_add_fusion.place_ref, f32[512,256]{1,0:T(8,128)S(1)} %pad_maximum_fusion.table_ref, bf16[2,192,1536]{2,1,0:T(8,128)(2,1)S(1)} %collective-permute-done.4.refs_0_, bf16[2,192,1536]{2,1,0:T(8,128)(2,1)S(1)} %collective-permute-done.8.refs_1_, ...), custom_call_target="tpu_custom_call" | custom-call | flops 1024 | bytes 1024 | tf_op jit(solution)/shard_map/attend_far/pallas_call | solution.py:298
  135.3 2.2 %place_pieces.2.refs_4_ = bf16[512,4096]{1,0:T(8,128)(2,1)} custom-call(s32[20]{0:T(128)S(1)} %stack.143.offsets_ref, bf16[512,512]{1,0:T(8,128)(2,1)S(1)} %copy-done.10, bf16[512,512]{1,0:T(8,128)(2,1)S(1)} %copy-done.14, bf16[512,512]{1,0:T(8,128)(2,1)S(1)} %copy-done.12, bf16[512,512]{1,0:T(8,128)(2,1)S(1)} %copy-done.16, bf16[512,512]{1,0:T(8,128)(2,1)S(1)} %copy-done.7), custom_call_target="tpu_custom_call" | custom-call | flops 1024 | bytes 1024 | tf_op jit(solution)/shard_map/place_pieces/pallas_call | solution.py:334
  137.6 2.6 %place_pieces.3 = bf16[512,4096]{1,0:T(8,128)(2,1)} custom-call(s32[12]{0:T(128)S(1)} %stack.120.offsets_ref, bf16[512,512]{1,0:T(8,128)(2,1)} %collective-permute-done.11.refs_0_, bf16[512,512]{1,0:T(8,128)(2,1)} %collective-permute-done.12.refs_1_, bf16[512,256]{1,0:T(8,128)(2,1)} %collective-permute-done.16.refs_2_, ...), custom_call_target="tpu_custom_call", output_to_operand_aliasing={{}: (5, {})} | custom-call | flops 1024 | bytes 1024 | tf_op jit(solution)/shard_map/place_pieces/pallas_call | solution.py:334
  (74 shorter events, 22.8 us)
Async XLA Ops:
  1.7 4.3 %copy-start.19 = (f32[512]{0:T(512)S(1)}, f32[512]{0:T(512)}, u32[]{:S(2)}) copy-start(f32[512]{0:T(512)} %param.8) | copy-start | bytes 6148
  1.8 55.5 %collective-permute-start.4 = (bf16[2,192,1536]{2,1,0:T(8,128)(2,1)S(1)}, bf16[2,192,1536]{2,1,0:T(8,128)(2,1)S(1)}, u32[]{:S(2)}, u32[]{:S(2)}) collective-permute-start(bf16[2,192,1536]{2,1,0:T(8,128)(2,1)S(1)} %pick.2), channel_id=1, source_target_pairs={{0,8},{2,10},{4,12},{6,14},{8,0},{10,2},{12,4},{14,6},{1,9},{3,11}... | collective-permute-start | bytes 3538952 | tf_op jit(solution)/shard_map/ppermute | solution.py:372
  8.7 5.9 %collective-permute-start.1 = (bf16[256,2176]{1,0:T(8,128)(2,1)S(1)}, bf16[256,2176]{1,0:T(8,128)(2,1)S(1)}, u32[]{:S(2)}, u32[]{:S(2)}) collective-permute-start(bf16[256,2176]{1,0:T(8,128)(2,1)S(1)} %prepare.1.same_ref), channel_id=1, source_target_pairs={{0,1},{1,0},{2,3},{3,2},{4,5},{5,4},{6,7},{7,6},{8,9},{9,8},{10,11... | collective-permute-start | bytes 3342344 | tf_op jit(solution)/shard_map/ppermute | solution.py:380
  8.7 51.0 %collective-permute-start = (bf16[256,2176]{1,0:T(8,128)(2,1)S(1)}, bf16[256,2176]{1,0:T(8,128)(2,1)S(1)}, u32[]{:S(2)}, u32[]{:S(2)}) collective-permute-start(bf16[256,2176]{1,0:T(8,128)(2,1)S(1)} %prepare.1.same_ref), channel_id=1, source_target_pairs={{0,4},{1,3},{2,6},{3,1},{4,0},{5,7},{6,2},{7,5},{8,12},{9,11},{10,... | collective-permute-start | bytes 3342344 | tf_op jit(solution)/shard_map/ppermute | solution.py:377
  10.4 49.3 %collective-permute-start.3 = (bf16[256,2176]{1,0:T(8,128)(2,1)S(1)}, bf16[256,2176]{1,0:T(8,128)(2,1)S(1)}, u32[]{:S(2)}, u32[]{:S(2)}) collective-permute-start(bf16[256,2176]{1,0:T(8,128)(2,1)S(1)} %prepare.1.same_ref), channel_id=1, source_target_pairs={{0,2},{1,5},{2,0},{3,7},{4,6},{5,1},{6,4},{7,3},{8,10},{9,13},{10,... | collective-permute-start | bytes 3342344 | tf_op jit(solution)/shard_map/ppermute | solution.py:377
  19.9 47.5 %copy-start.4 = (bf16[512,2176]{1,0:T(8,128)(2,1)}, bf16[512,2176]{1,0:T(8,128)(2,1)S(1)}, u32[]{:S(2)}) copy-start(bf16[512,2176]{1,0:T(8,128)(2,1)S(1)} %get-tuple-element.52.refs_4_) | copy-start | bytes 6684676
  57.2 27.1 %collective-permute-start.8 = (bf16[2,192,1536]{2,1,0:T(8,128)(2,1)S(1)}, bf16[2,192,1536]{2,1,0:T(8,128)(2,1)S(1)}, u32[]{:S(2)}, u32[]{:S(2)}) collective-permute-start(bf16[2,192,1536]{2,1,0:T(8,128)(2,1)S(1)} %collective-permute-done.4.refs_0_), channel_id=1, source_target_pairs={{0,16},{16,0},{1,17},{17,1},{2,18},{18,2},{3,19},{19,3},{4,20},{20... | collective-permute-start | bytes 3538952 | tf_op jit(solution)/shard_map/ppermute | solution.py:383
  59.7 3.2 %collective-permute-start.5 = (bf16[256,2176]{1,0:T(8,128)(2,1)S(1)}, bf16[256,2176]{1,0:T(8,128)(2,1)S(1)}, u32[]{:S(2)}, u32[]{:S(2)}) collective-permute-start(bf16[256,2176]{1,0:T(8,128)(2,1)S(1)} %collective-permute-done.same_ref), channel_id=1, source_target_pairs={{0,1},{1,0},{2,3},{3,2},{4,5},{5,4},{6,7},{7,6},{8,9},{9,8},{10,11... | collective-permute-start | bytes 3342344 | tf_op jit(solution)/shard_map/ppermute | solution.py:380
  60.2 7.2 %collective-permute-start.6 = (bf16[256,2176]{1,0:T(8,128)(2,1)S(1)}, bf16[256,2176]{1,0:T(8,128)(2,1)S(1)}, u32[]{:S(2)}, u32[]{:S(2)}) collective-permute-start(bf16[256,2176]{1,0:T(8,128)(2,1)S(1)} %collective-permute-done.3.same_ref), channel_id=1, source_target_pairs={{0,1},{1,0},{2,3},{3,2},{4,5},{5,4},{6,7},{7,6},{8,9},{9,8},{10,11... | collective-permute-start | bytes 3342344 | tf_op jit(solution)/shard_map/ppermute | solution.py:380
  60.2 21.3 %collective-permute-start.2 = (bf16[256,2176]{1,0:T(8,128)(2,1)S(1)}, bf16[256,2176]{1,0:T(8,128)(2,1)S(1)}, u32[]{:S(2)}, u32[]{:S(2)}) collective-permute-start(bf16[256,2176]{1,0:T(8,128)(2,1)S(1)} %collective-permute-done.same_ref), channel_id=1, source_target_pairs={{0,2},{1,5},{2,0},{3,7},{4,6},{5,1},{6,4},{7,3},{8,10},{9,13},{10,... | collective-permute-start | bytes 3342344 | tf_op jit(solution)/shard_map/ppermute | solution.py:377
  62.2 19.3 %collective-permute-start.7 = (bf16[512,512]{1,0:T(8,128)(2,1)S(1)}, bf16[512,512]{1,0:T(8,128)(2,1)S(1)}, u32[]{:S(2)}, u32[]{:S(2)}) collective-permute-start(bf16[512,512]{1,0:T(8,128)(2,1)S(1)} %pick.3), channel_id=1, source_target_pairs={{0,8},{2,10},{4,12},{6,14},{8,0},{10,2},{12,4},{14,6},{1,9},{3,11}... | collective-permute-start | bytes 1572872 | tf_op jit(solution)/shard_map/ppermute | solution.py:372
  84.3 6.3 %collective-permute-start.9 = (bf16[256,2176]{1,0:T(8,128)(2,1)S(1)}, bf16[256,2176]{1,0:T(8,128)(2,1)S(1)}, u32[]{:S(2)}, u32[]{:S(2)}) collective-permute-start(bf16[256,2176]{1,0:T(8,128)(2,1)S(1)} %collective-permute-done.2.same_ref), channel_id=1, source_target_pairs={{0,1},{1,0},{2,3},{3,2},{4,5},{5,4},{6,7},{7,6},{8,9},{9,8},{10,11... | collective-permute-start | bytes 3342344 | tf_op jit(solution)/shard_map/ppermute | solution.py:380
  86.3 13.8 %collective-permute-start.10 = (bf16[512,512]{1,0:T(8,128)(2,1)S(1)}, bf16[512,512]{1,0:T(8,128)(2,1)S(1)}, u32[]{:S(2)}, u32[]{:S(2)}) collective-permute-start(bf16[512,512]{1,0:T(8,128)(2,1)S(1)} %collective-permute-done.7.refs_2_), channel_id=1, source_target_pairs={{0,16},{16,0},{1,17},{17,1},{2,18},{18,2},{3,19},{19,3},{4,20},{20... | collective-permute-start | bytes 1572872 | tf_op jit(solution)/shard_map/ppermute | solution.py:383
  87.8 24.1 %collective-permute-start.14 = (bf16[512,512]{1,0:T(8,128)(2,1)S(1)}, bf16[512,512]{1,0:T(8,128)(2,1)S(1)}, u32[]{:S(2)}, u32[]{:S(2)}) collective-permute-start(bf16[512,512]{1,0:T(8,128)(2,1)S(1)} %get-tuple-element.36), channel_id=1, source_target_pairs={{0,4},{1,3},{2,6},{3,1},{4,0},{5,7},{6,2},{7,5},{8,12},{9,11},{10,... | collective-permute-start | bytes 1572872 | tf_op jit(solution)/shard_map/ppermute | solution.py:377
  89.2 22.8 %collective-permute-start.13 = (bf16[512,512]{1,0:T(8,128)(2,1)S(1)}, bf16[512,512]{1,0:T(8,128)(2,1)S(1)}, u32[]{:S(2)}, u32[]{:S(2)}) collective-permute-start(bf16[512,512]{1,0:T(8,128)(2,1)S(1)} %get-tuple-element.33), channel_id=1, source_target_pairs={{0,2},{1,5},{2,0},{3,7},{4,6},{5,1},{6,4},{7,3},{8,10},{9,13},{10,... | collective-permute-start | bytes 1572872 | tf_op jit(solution)/shard_map/ppermute | solution.py:377
  95.1 19.5 %collective-permute-start.15 = (bf16[512,512]{1,0:T(8,128)(2,1)S(1)}, bf16[512,512]{1,0:T(8,128)(2,1)S(1)}, u32[]{:S(2)}, u32[]{:S(2)}) collective-permute-start(bf16[512,512]{1,0:T(8,128)(2,1)S(1)} %get-tuple-element.41), channel_id=1, source_target_pairs={{0,6},{1,7},{2,4},{3,5},{4,2},{5,3},{6,0},{7,1},{8,14},{9,15},{10,... | collective-permute-start | bytes 1572872 | tf_op jit(solution)/shard_map/ppermute | solution.py:377
  100.1 14.5 %copy-start.2 = (bf16[512,512]{1,0:T(8,128)(2,1)}, bf16[512,512]{1,0:T(8,128)(2,1)S(1)}, u32[]{:S(2)}) copy-start(bf16[512,512]{1,0:T(8,128)(2,1)S(1)} %collective-permute-done.10.refs_3_) | copy-start | bytes 1572868
  109.1 28.5 %collective-permute-start.11 = (bf16[512,512]{1,0:T(8,128)(2,1)}, bf16[512,512]{1,0:T(8,128)(2,1)}, u32[]{:S(2)}, u32[]{:S(2)}) collective-permute-start(bf16[512,512]{1,0:T(8,128)(2,1)} %get-tuple-element.45), channel_id=1, source_target_pairs={{0,4},{1,3},{2,6},{3,1},{4,0},{5,7},{6,2},{7,5},{8,12},{9,11},{10,... | collective-permute-start | bytes 1572872 | tf_op jit(solution)/shard_map/ppermute | solution.py:377
  110.6 27.0 %collective-permute-start.12 = (bf16[512,512]{1,0:T(8,128)(2,1)}, bf16[512,512]{1,0:T(8,128)(2,1)}, u32[]{:S(2)}, u32[]{:S(2)}) collective-permute-start(bf16[512,512]{1,0:T(8,128)(2,1)} %get-tuple-element.46), channel_id=1, source_target_pairs={{0,6},{1,7},{2,4},{3,5},{4,2},{5,3},{6,0},{7,1},{8,14},{9,15},{10,... | collective-permute-start | bytes 1572872 | tf_op jit(solution)/shard_map/ppermute | solution.py:377
  112.0 8.0 %copy-start.11 = (bf16[512,512]{1,0:T(8,128)(2,1)}, bf16[512,512]{1,0:T(8,128)(2,1)S(1)}, u32[]{:S(2)}) copy-start(bf16[512,512]{1,0:T(8,128)(2,1)S(1)} %collective-permute-done.14.refs_2_) | copy-start | bytes 1572868
  112.0 8.0 %copy-start.13 = (bf16[512,512]{1,0:T(8,128)(2,1)}, bf16[512,512]{1,0:T(8,128)(2,1)S(1)}, u32[]{:S(2)}) copy-start(bf16[512,512]{1,0:T(8,128)(2,1)S(1)} %collective-permute-done.13.refs_1_) | copy-start | bytes 1572868
  114.6 5.4 %copy-start.15 = (bf16[512,512]{1,0:T(8,128)(2,1)}, bf16[512,512]{1,0:T(8,128)(2,1)S(1)}, u32[]{:S(2)}) copy-start(bf16[512,512]{1,0:T(8,128)(2,1)S(1)} %collective-permute-done.15.refs_3_) | copy-start | bytes 1572868
  120.0 17.6 %collective-permute-start.16 = (bf16[512,256]{1,0:T(8,128)(2,1)}, bf16[512,256]{1,0:T(8,128)(2,1)}, u32[]{:S(2)}, u32[]{:S(2)}) collective-permute-start(bf16[512,256]{1,0:T(8,128)(2,1)} %get-tuple-element.49), channel_id=1, source_target_pairs={{0,2},{1,5},{2,0},{3,7},{4,6},{5,1},{6,4},{7,3},{8,10},{9,13},{10,... | collective-permute-start | bytes 786440 | tf_op jit(solution)/shard_map/ppermute | solution.py:377
  120.8 16.7 %collective-permute-start.17 = (bf16[512,256]{1,0:T(8,128)(2,1)}, bf16[512,256]{1,0:T(8,128)(2,1)}, u32[]{:S(2)}, u32[]{:S(2)}) collective-permute-start(bf16[512,256]{1,0:T(8,128)(2,1)} %get-tuple-element.50), channel_id=1, source_target_pairs={{0,2},{1,5},{2,0},{3,7},{4,6},{5,1},{6,4},{7,3},{8,10},{9,13},{10,... | collective-permute-start | bytes 786440 | tf_op jit(solution)/shard_map/ppermute | solution.py:377
  (14 other events, 23.5 us)

commit v14 on v9

--- a/solution.py
+++ b/solution.py
@@ -229,7 +229,8 @@
         turn_ref[index * block : (index + 1) * block, :] = table_ref[pl.ds(position, block), :]
 
 
-def near_kernel(sizes, slot_count, slot, half_places, place_ref, table_ref, query_weight_ref, pair_weight_ref, same_ref, other_ref, out_ref, tokens_ref, *scratch):
+def near_kernel(sizes, slot_count, slot, half_places, parts, place_ref, table_ref, query_weight_ref, pair_weight_ref, same_ref, other_ref, *refs):
+    out_refs, tokens_ref, scratch = refs[:parts], refs[parts], refs[parts + 1 :]
     core = place_ref[1]
     group = place_ref[0] ^ distance_of(slot, core, half_places)
     rows = same_ref.shape[0]
@@ -238,7 +239,7 @@
     set_up(scratch)
     set_turn(group, slot_count, place_ref, table_ref, scratch[3])
     chosen = [(query_weight_ref, pair_weight_ref, head) for head in range(sizes[0])]
-    attend_groups([attend_group(sizes, chosen, tokens_ref, scratch, [out_ref])])
+    attend_groups([attend_group(sizes, chosen, tokens_ref, scratch, out_refs)])
 
 
 def far_kernel(sizes, slot_count, numbers, half_places, parts, arrays, place_ref, table_ref, *refs):
@@ -269,18 +270,16 @@
     ]
 
 
-def attend_near(sizes, slot_count, slot, half_places, place, table, query_weight, pair_weight, same, other):
+def attend_near(sizes, slot_count, slot, half_places, parts, place, table, query_weight, pair_weight, same, other):
     rows, width = same.shape
     heads, value_width = sizes[0], sizes[-1]
     vmem = pl.BlockSpec(memory_space=pltpu.VMEM)
     return pl.pallas_call(
-        partial(near_kernel, sizes, slot_count, slot, half_places),
-        out_shape=[
-            jax.ShapeDtypeStruct((2 * rows, heads * value_width), jnp.bfloat16),
-            jax.ShapeDtypeStruct((2 * rows, width), jnp.bfloat16),
-        ],
+        partial(near_kernel, sizes, slot_count, slot, half_places, parts),
+        out_shape=[jax.ShapeDtypeStruct((2 * rows, heads // parts * value_width), jnp.bfloat16)] * parts
+        + [jax.ShapeDtypeStruct((2 * rows, width), jnp.bfloat16)],
         in_specs=[pl.BlockSpec(memory_space=pltpu.SMEM)] + [vmem] * 5,
-        out_specs=[vmem, vmem],
+        out_specs=[vmem] * (parts + 1),
         scratch_shapes=scratch_for(sizes, 2 * rows),
         compiler_params=pltpu.CompilerParams(vmem_limit_bytes=VMEM_LIMIT),
         cost_estimate=LIGHT,
@@ -308,13 +307,18 @@
 
 
 def place_kernel(width, count, offsets_ref, *refs):
-    pieces, out_ref, sems = refs[:count], refs[-2], refs[-1]
-    copies = []
-    for piece in pieces:
-        for low in range(0, piece.shape[1], width):
+    pieces, out_ref, held, in_sems, out_sems = refs[:count], refs[-3 - count], refs[-2 - count : -2], refs[-2], refs[-1]
+    fetches, copies = [], []
+    for index, (piece, held_ref) in enumerate(zip(pieces, held)):
+        fetches.append(pltpu.make_async_copy(piece, held_ref, in_sems.at[index]))
+        fetches[-1].start()
+    for fetch, held_ref in zip(fetches, held):
+        fetch.wait()
+        for low in range(0, held_ref.shape[1], width):
             index = len(copies)
             columns = pl.ds(pl.multiple_of(offsets_ref[index], 128), width)
-            copies.append(pltpu.make_async_copy(piece.at[:, low : low + width], out_ref.at[:, columns], sems.at[index]))
+            source = held_ref.at[:, low : low + width]
+            copies.append(pltpu.make_async_copy(source, out_ref.at[:, columns], out_sems.at[index]))
             copies[-1].start()
     for copy in copies:
         copy.wait()
@@ -324,18 +328,17 @@
     count = len(pieces)
     any_space = pl.BlockSpec(memory_space=pl.ANY)
     operands = [jnp.stack(offsets).astype(jnp.int32), *pieces]
-    specs = [pl.BlockSpec(memory_space=pltpu.SMEM)] + [pl.BlockSpec(memory_space=pltpu.VMEM)] * count
     aliases = {}
     if held is not None:
         aliases = {len(operands): 0}
         operands.append(held)
-        specs.append(any_space)
     return pl.pallas_call(
         partial(place_kernel, width, count),
         out_shape=jax.ShapeDtypeStruct((pieces[0].shape[0], out_width), pieces[0].dtype),
-        in_specs=specs,
+        in_specs=[pl.BlockSpec(memory_space=pltpu.SMEM)] + [any_space] * (len(operands) - 1),
         out_specs=any_space,
-        scratch_shapes=[pltpu.SemaphoreType.DMA((len(offsets),))],
+        scratch_shapes=[pltpu.VMEM(piece.shape, piece.dtype) for piece in pieces]
+        + [pltpu.SemaphoreType.DMA((count,)), pltpu.SemaphoreType.DMA((len(offsets),))],
         input_output_aliases=aliases,
         compiler_params=pltpu.CompilerParams(vmem_limit_bytes=VMEM_LIMIT),
         cost_estimate=LIGHT,
@@ -407,11 +410,13 @@
     joined = []
 
     def near(distance, *earlier):
-        mixed, tokens_joined = attend_near(
+        parts_of = share if distance == 1 else 1
+        *mixed, tokens_joined = attend_near(
             (local_heads, *sizes),
             slot_count,
             distance,
             half_places,
+            parts_of,
             spot,
             table,
             own_query,
@@ -424,6 +429,7 @@
 
     mixed = near(0)
     arrived = [mixed]
+    mixed = mixed[0]
     direct = [entry for entry in same[1:] if entry is not None]
     partner = [slot if half_places < 4 else swapped_bits(slot) for slot in range(half_places)]
     for distance in range(1, half_places):
@@ -438,13 +444,17 @@
     crossed_query = [other_part(after(far_query, mixed))] if share == 2 else []
     for distance in range(1, half_places):
         if other[distance] is None:
-            other[distance] = sibling(after(same[partner[distance]], mixed, far_pair, *crossed_query))
-        mixed = near(distance, mixed)
-        arrived.append(across(mixed, distance))
+            other[distance] = sibling(after(same[partner[distance]], mixed, far_pair, *crossed_query, *early))
+        pieces = near(distance, mixed)
+        mixed = pieces[-1]
+        arrived.append([across(piece, distance) for piece in pieces])
+        early = arrived[1]
     placed = []
     for distance in range(half_places):
         base = away(distance) * block_width
-        placed.append((arrived[distance], [base + head * value_width for head in range(local_heads)]))
+        each = local_heads // len(arrived[distance])
+        for index, piece in enumerate(arrived[distance]):
+            placed.append((piece, [base + (index * each + head) * value_width for head in range(each)]))
 
     out_width = places * block_width
 
@@ -475,7 +485,7 @@
             pairs,
             [joined[distance] for distance in distances],
         )
-        mixed, gates = mixed_some[0][0], arrived[1:]
+        mixed, gates = mixed_some[0][0], [piece for pieces in arrived[1:] for piece in pieces]
         for distance, pieces in zip(distances, mixed_some):
             base = (away(distance) ^ half_places) * block_width
             each = len(numbers) // len(pieces)

time: 138 us -> 146 us (1.058)
  local copies, waits for them, and re-layouts: 3.33 us -> 6.63 us
  waiting for transfers between devices: 67.6 us -> 69.9 us
  starting transfers between devices: 23.7 us -> 25.4 us
    ppermute x2, waiting for transfers between devices: 50 us -> 6.97 us  [opposite(): lax.ppermute(value, 'seq', [(s, s ^ half_places) for s in range(places)])]
    ppermute x10 -> x11, waiting for transfers between devices: 10.6 us -> 50.3 us  [across(): return lax.ppermute(value, ('seq', 'head'), pairs)]
    ppermute x2, waiting for transfers between devices: 6.97 us -> 11.1 us  [other_part(): return lax.ppermute(value, 'parts', [(p, p ^ 1) for p in range(parts)])]
    unnamed x19 -> x27, local copies, waits for them, and re-layouts: 3.06 us -> 6.37 us
    ppermute x4, starting transfers between devices: 1.34 us -> 4.46 us  [sibling(): return lax.ppermute(value, 'head', [(0, 1), (1, 0)])]
    ppermute x4, waiting for transfers between devices: 0.01 us -> 1.58 us  [sibling(): return lax.ppermute(value, 'head', [(0, 1), (1, 0)])]
    ppermute x10 -> x11, starting transfers between devices: 14.1 us -> 13.7 us  [across(): return lax.ppermute(value, ('seq', 'head'), pairs)]
  transfers between devices with their start and end apart: 18 -> 19, of which waited for: 9 -> 7; matrix products, arithmetic and copies ran while one was open for 1% -> 1% of each run, Pallas kernels for 28% -> 27%
where the time goes in v14:
time: 146 us
  waiting for transfers between devices  69.9 us (48%)
  Pallas kernels  42.4 us (29%)
  starting transfers between devices  25.4 us (17%)
  local copies, waits for them, and re-layouts  6.63 us (5%)
    ppermute x11, waiting for transfers between devices, across(): return lax.ppermute(value, ('seq', 'head'), pairs)  50.3 us
    pallas_call x4, Pallas kernels, attend_near(): pl.pallas_call(partial(near_kernel, sizes, slot_count, slot, half_places,...  18.3 us
    pallas_call x2, Pallas kernels, attend_far(): pl.pallas_call(partial(far_kernel, sizes, slot_count, numbers, half_place...  17.4 us
    ppermute x11, starting transfers between devices, across(): return lax.ppermute(value, ('seq', 'head'), pairs)  13.7 us
    ppermute x2, waiting for transfers between devices, other_part(): return lax.ppermute(value, 'parts', [(p, p ^ 1) for p in range(parts)])  11.1 us
    ppermute x2, waiting for transfers between devices, opposite(): lax.ppermute(value, 'seq', [(s, s ^ half_places) for s in range(places)])  6.97 us
    unnamed x27, local copies, waits for them, and re-layouts  6.37 us
    pallas_call x2, Pallas kernels, place_pieces(): pl.pallas_call(partial(place_kernel, width, count), out_shape=jax.ShapeDt...  5.26 us
  transfers between devices with their start and end apart: 19, of which 7 were waited for; matrix products, arithmetic and copies ran while one was open for 1% of the time, Pallas kernels for 27%

profile of v14, /device:TPU:0, one launch (start us, length us, event | category | flops | bytes accessed | tf_op | source)
XLA Modules:
  0.0 145.9 jit_solution(572916941516081526)
XLA Ops:
  0.0 1.7 %copy-done = bf16[1,1536,4,192]{1,3,2,0:T(8,128)(2,1)S(1)} copy-done((bf16[1,1536,4,192]{1,3,2,0:T(8,128)(2,1)S(1)}, bf16[1,1536,4,192]{1,3,2,0:T(8,128)(2,1)}, u32[]{:S(2)}) %copy-start) | copy-done | bytes 2359320
  1.8 4.1 %collective-permute-start.4 = (bf16[2,192,1536]{2,1,0:T(8,128)(2,1)S(1)}, bf16[2,192,1536]{2,1,0:T(8,128)(2,1)S(1)}, u32[]{:S(2)}, u32[]{:S(2)}) collective-permute-start(bf16[2,192,1536]{2,1,0:T(8,128)(2,1)S(1)} %pick.2), channel_id=1, source_target_pairs={{0,8},{2,10},{4,12},{6,14},{8,0},{10,2},{12,4},{14,6},{1,9},{3,11}... | collective-permute-start | bytes 3538952 | tf_op jit(solution)/shard_map/ppermute | solution.py:374
  7.5 1.6 %collective-permute-start = (bf16[256,2176]{1,0:T(8,128)(2,1)S(1)}, bf16[256,2176]{1,0:T(8,128)(2,1)S(1)}, u32[]{:S(2)}, u32[]{:S(2)}) collective-permute-start(bf16[256,2176]{1,0:T(8,128)(2,1)S(1)} %prepare.1.same_ref), channel_id=1, source_target_pairs={{0,4},{1,3},{2,6},{3,1},{4,0},{5,7},{6,2},{7,5},{8,12},{9,11},{10,... | collective-permute-start | bytes 3342344 | tf_op jit(solution)/shard_map/ppermute | solution.py:379
  9.2 1.5 %collective-permute-start.3 = (bf16[256,2176]{1,0:T(8,128)(2,1)S(1)}, bf16[256,2176]{1,0:T(8,128)(2,1)S(1)}, u32[]{:S(2)}, u32[]{:S(2)}) collective-permute-start(bf16[256,2176]{1,0:T(8,128)(2,1)S(1)} %prepare.1.same_ref), channel_id=1, source_target_pairs={{0,2},{1,5},{2,0},{3,7},{4,6},{5,1},{6,4},{7,3},{8,10},{9,13},{10,... | collective-permute-start | bytes 3342344 | tf_op jit(solution)/shard_map/ppermute | solution.py:379
  12.4 4.5 %attend_near.4 = (bf16[512,512]{1,0:T(8,128)(2,1)S(1)}, bf16[512,2176]{1,0:T(8,128)(2,1)S(1)}) custom-call(s32[66]{0:T(128)S(1)} %pad_add_fusion.place_ref, f32[512,256]{1,0:T(8,128)S(1)} %pad_maximum_fusion.table_ref, bf16[4,192,1536]{2,1,0:T(8,128)(2,1)S(1)} %bitcast.44, bf16[512,1024]{1,0:T(8,128)(2,1)S(1)} %bitcast.48, ...), custom_call_target="tpu_custom_call" | custom-call | flops 1024 | bytes 1024 | tf_op jit(solution)/shard_map/attend_near/pallas_call | solution.py:277
  16.9 41.6 %collective-permute-done.same_ref = bf16[256,2176]{1,0:T(8,128)(2,1)S(1)} collective-permute-done((bf16[256,2176]{1,0:T(8,128)(2,1)S(1)}, bf16[256,2176]{1,0:T(8,128)(2,1)S(1)}, u32[]{:S(2)}, u32[]{:S(2)}) %collective-permute-start) | collective-permute-done | bytes 1114144 | tf_op jit(solution)/shard_map/ppermute | solution.py:379
  59.0 1.5 %collective-permute-start.8 = (bf16[2,192,1536]{2,1,0:T(8,128)(2,1)S(1)}, bf16[2,192,1536]{2,1,0:T(8,128)(2,1)S(1)}, u32[]{:S(2)}, u32[]{:S(2)}) collective-permute-start(bf16[2,192,1536]{2,1,0:T(8,128)(2,1)S(1)} %collective-permute-done.4.refs_0_), channel_id=1, source_target_pairs={{0,16},{16,0},{1,17},{17,1},{2,18},{18,2},{3,19},{19,3},{4,20},{20... | collective-permute-start | bytes 3538952 | tf_op jit(solution)/shard_map/ppermute | solution.py:385
  60.6 1.9 %collective-permute-start.2 = (bf16[256,2176]{1,0:T(8,128)(2,1)S(1)}, bf16[256,2176]{1,0:T(8,128)(2,1)S(1)}, u32[]{:S(2)}, u32[]{:S(2)}) collective-permute-start(bf16[256,2176]{1,0:T(8,128)(2,1)S(1)} %collective-permute-done.same_ref), channel_id=1, source_target_pairs={{0,2},{1,5},{2,0},{3,7},{4,6},{5,1},{6,4},{7,3},{8,10},{9,13},{10,... | collective-permute-start | bytes 3342344 | tf_op jit(solution)/shard_map/ppermute | solution.py:379
  63.6 4.5 %attend_near.5 = (bf16[512,256]{1,0:T(8,128)(2,1)S(1)}, bf16[512,256]{1,0:T(8,128)(2,1)S(1)}, bf16[512,2176]{1,0:T(8,128)(2,1)S(1)}) custom-call(s32[66]{0:T(128)S(1)} %pad_add_fusion.place_ref, f32[512,256]{1,0:T(8,128)S(1)} %pad_maximum_fusion.table_ref, bf16[4,192,1536]{2,1,0:T(8,128)(2,1)S(1)} %bitcast.45, bf16[512,1024]{1,0:T(8,128)(2,1)S(1)} %bitcast.50, ...), custom_call_target="tpu_custom_call" | custom-call | flops 1024 | bytes 1024 | tf_op jit(solution)/shard_map/attend_near/pallas_call | solution.py:277
  68.6 1.6 %collective-permute-start.10 = (bf16[512,256]{1,0:T(8,128)(2,1)S(1)}, bf16[512,256]{1,0:T(8,128)(2,1)S(1)}, u32[]{:S(2)}, u32[]{:S(2)}) collective-permute-start(bf16[512,256]{1,0:T(8,128)(2,1)S(1)} %get-tuple-element.34), channel_id=1, source_target_pairs={{0,2},{1,5},{2,0},{3,7},{4,6},{5,1},{6,4},{7,3},{8,10},{9,13},{10,... | collective-permute-start | bytes 786440 | tf_op jit(solution)/shard_map/ppermute | solution.py:379
  70.2 4.7 %attend_near.6 = (bf16[512,512]{1,0:T(8,128)(2,1)S(1)}, bf16[512,2176]{1,0:T(8,128)(2,1)S(1)}) custom-call(s32[66]{0:T(128)S(1)} %pad_add_fusion.place_ref, f32[512,256]{1,0:T(8,128)S(1)} %pad_maximum_fusion.table_ref, bf16[4,192,1536]{2,1,0:T(8,128)(2,1)S(1)} %bitcast.46, bf16[512,1024]{1,0:T(8,128)(2,1)S(1)} %bitcast.51, ...), custom_call_target="tpu_custom_call" | custom-call | flops 1024 | bytes 1024 | tf_op jit(solution)/shard_map/attend_near/pallas_call | solution.py:277
  74.9 7.0 %collective-permute-done.7.refs_2_ = bf16[512,512]{1,0:T(8,128)(2,1)S(1)} collective-permute-done((bf16[512,512]{1,0:T(8,128)(2,1)S(1)}, bf16[512,512]{1,0:T(8,128)(2,1)S(1)}, u32[]{:S(2)}, u32[]{:S(2)}) %collective-permute-start.7) | collective-permute-done | bytes 524320 | tf_op jit(solution)/shard_map/ppermute | solution.py:374
  81.9 5.5 %collective-permute-done.8.refs_1_ = bf16[2,192,1536]{2,1,0:T(8,128)(2,1)S(1)} collective-permute-done((bf16[2,192,1536]{2,1,0:T(8,128)(2,1)S(1)}, bf16[2,192,1536]{2,1,0:T(8,128)(2,1)S(1)}, u32[]{:S(2)}, u32[]{:S(2)}) %collective-permute-start.8) | collective-permute-done | bytes 1179680 | tf_op jit(solution)/shard_map/ppermute | solution.py:385
  88.8 3.9 %collective-permute-start.11 = (bf16[256,2176]{1,0:T(8,128)(2,1)S(1)}, bf16[256,2176]{1,0:T(8,128)(2,1)S(1)}, u32[]{:S(2)}, u32[]{:S(2)}) collective-permute-start(bf16[256,2176]{1,0:T(8,128)(2,1)S(1)} %collective-permute-done.2.same_ref), channel_id=1, source_target_pairs={{0,1},{1,0},{2,3},{3,2},{4,5},{5,4},{6,7},{7,6},{8,9},{9,8},{10,11... | collective-permute-start | bytes 3342344 | tf_op jit(solution)/shard_map/ppermute | solution.py:382
  93.5 1.6 %collective-permute-done.11.other_ref = bf16[256,2176]{1,0:T(8,128)(2,1)S(1)} collective-permute-done((bf16[256,2176]{1,0:T(8,128)(2,1)S(1)}, bf16[256,2176]{1,0:T(8,128)(2,1)S(1)}, u32[]{:S(2)}, u32[]{:S(2)}) %collective-permute-start.11) | collective-permute-done | bytes 1114144 | tf_op jit(solution)/shard_map/ppermute | solution.py:382
  95.0 4.5 %attend_near.7 = (bf16[512,512]{1,0:T(8,128)(2,1)S(1)}, bf16[512,2176]{1,0:T(8,128)(2,1)S(1)}) custom-call(s32[66]{0:T(128)S(1)} %pad_add_fusion.place_ref, f32[512,256]{1,0:T(8,128)S(1)} %pad_maximum_fusion.table_ref, bf16[4,192,1536]{2,1,0:T(8,128)(2,1)S(1)} %bitcast.47, bf16[512,1024]{1,0:T(8,128)(2,1)S(1)} %bitcast.52, ...), custom_call_target="tpu_custom_call" | custom-call | flops 1024 | bytes 1024 | tf_op jit(solution)/shard_map/attend_near/pallas_call | solution.py:277
  100.9 5.6 %collective-permute-done.12.refs_3_ = bf16[512,512]{1,0:T(8,128)(2,1)S(1)} collective-permute-done((bf16[512,512]{1,0:T(8,128)(2,1)S(1)}, bf16[512,512]{1,0:T(8,128)(2,1)S(1)}, u32[]{:S(2)}, u32[]{:S(2)}) %collective-permute-start.12) | collective-permute-done | bytes 524320 | tf_op jit(solution)/shard_map/ppermute | solution.py:385
  106.5 9.0 %attend_far.2 = (bf16[512,512]{1,0:T(8,128)(2,1)}, bf16[512,512]{1,0:T(8,128)(2,1)}) custom-call(s32[66]{0:T(128)S(1)} %pad_add_fusion.place_ref, f32[512,256]{1,0:T(8,128)S(1)} %pad_maximum_fusion.table_ref, bf16[2,192,1536]{2,1,0:T(8,128)(2,1)S(1)} %collective-permute-done.4.refs_0_, bf16[2,192,1536]{2,1,0:T(8,128)(2,1)S(1)} %collective-permute-done.8.refs_1_, ...), custom_call_target="tpu_custom_call" | custom-call | flops 1024 | bytes 1024 | tf_op jit(solution)/shard_map/attend_far/pallas_call | solution.py:296
  115.8 2.6 %collective-permute-start.14 = (bf16[512,512]{1,0:T(8,128)(2,1)}, bf16[512,512]{1,0:T(8,128)(2,1)}, u32[]{:S(2)}, u32[]{:S(2)}) collective-permute-start(bf16[512,512]{1,0:T(8,128)(2,1)} %get-tuple-element.48), channel_id=1, source_target_pairs={{0,6},{1,7},{2,4},{3,5},{4,2},{5,3},{6,0},{7,1},{8,14},{9,15},{10,... | collective-permute-start | bytes 1572872 | tf_op jit(solution)/shard_map/ppermute | solution.py:379
  118.4 8.4 %attend_far.3 = (bf16[512,256]{1,0:T(8,128)(2,1)}, bf16[512,256]{1,0:T(8,128)(2,1)}, bf16[512,512]{1,0:T(8,128)(2,1)S(1)}) custom-call(s32[66]{0:T(128)S(1)} %pad_add_fusion.place_ref, f32[512,256]{1,0:T(8,128)S(1)} %pad_maximum_fusion.table_ref, bf16[2,192,1536]{2,1,0:T(8,128)(2,1)S(1)} %collective-permute-done.4.refs_0_, ...), custom_call_target="tpu_custom_call" | custom-call | flops 1024 | bytes 1024 | tf_op jit(solution)/shard_map/attend_far/pallas_call | solution.py:296
  128.2 1.5 %collective-permute-start.18 = (bf16[512,256]{1,0:T(8,128)(2,1)}, bf16[512,256]{1,0:T(8,128)(2,1)S(1)}, u32[]{:S(2)}, u32[]{:S(2)}) collective-permute-start(bf16[512,256]{1,0:T(8,128)(2,1)} %get-tuple-element.53), channel_id=1, source_target_pairs={{0,2},{1,5},{2,0},{3,7},{4,6},{5,1},{6,4},{7,3},{8,10},{9,13},{10,... | collective-permute-start | bytes 786440 | tf_op jit(solution)/shard_map/ppermute | solution.py:379
  131.7 2.2 %place_pieces.2.refs_5_ = bf16[512,4096]{1,0:T(8,128)(2,1)} custom-call(s32[16]{0:T(128)S(1)} %stack.143.offsets_ref, bf16[512,512]{1,0:T(8,128)(2,1)S(1)} %get-tuple-element.30.refs_0_, bf16[512,256]{1,0:T(8,128)(2,1)S(1)} %copy-done.6, bf16[512,256]{1,0:T(8,128)(2,1)S(1)} %copy-done.8, bf16[512,512]{1,0:T(8,128)(2,1)S(1)} %collective-permute-done.15.refs_3_, ...), custom_call_target="tpu_custom_call" | custom-call | flops 1024 | bytes 1024 | tf_op jit(solution)/shard_map/place_pieces/pallas_call | solution.py:335
  133.9 8.3 %collective-permute-done.14.refs_1_ = bf16[512,512]{1,0:T(8,128)(2,1)} collective-permute-done((bf16[512,512]{1,0:T(8,128)(2,1)}, bf16[512,512]{1,0:T(8,128)(2,1)}, u32[]{:S(2)}, u32[]{:S(2)}) %collective-permute-start.14) | collective-permute-done | bytes 524320 | tf_op jit(solution)/shard_map/ppermute | solution.py:379
  142.6 3.1 %place_pieces.3 = bf16[512,4096]{1,0:T(8,128)(2,1)} custom-call(s32[16]{0:T(128)S(1)} %stack.124.offsets_ref, bf16[512,512]{1,0:T(8,128)(2,1)S(1)} %collective-permute-done.13.refs_0_, bf16[512,512]{1,0:T(8,128)(2,1)} %collective-permute-done.14.refs_1_, bf16[512,256]{1,0:T(8,128)(2,1)S(1)} %collective-permute-done.17.refs_2_, ...), custom_call_target="tpu_custom_call", output_to_operand_aliasing={{}: (6, {})} | custom-call | flops 1024 | bytes 1024 | tf_op jit(solution)/shard_map/place_pieces/pallas_call | solution.py:335
  (61 shorter events, 13.2 us)
Async XLA Ops:
  1.7 4.3 %copy-start.10 = (f32[1536]{0:T(1024)S(1)}, f32[1536]{0:T(1024)}, u32[]{:S(2)}) copy-start(f32[1536]{0:T(1024)} %param.7) | copy-start | bytes 18436
  1.7 4.3 %copy-start.12 = (f32[512]{0:T(512)S(1)}, f32[512]{0:T(512)}, u32[]{:S(2)}) copy-start(f32[512]{0:T(512)} %param.8) | copy-start | bytes 6148
  1.7 4.4 %copy-start.2 = (bf16[256,2112]{0,1:T(8,128)(2,1)S(1)}, bf16[256,2112]{0,1:T(8,128)(2,1)}, u32[]{:S(2)}) copy-start(bf16[256,2112]{0,1:T(8,128)(2,1)} %param.6) | copy-start | bytes 3244036
  1.8 56.7 %collective-permute-start.4 = (bf16[2,192,1536]{2,1,0:T(8,128)(2,1)S(1)}, bf16[2,192,1536]{2,1,0:T(8,128)(2,1)S(1)}, u32[]{:S(2)}, u32[]{:S(2)}) collective-permute-start(bf16[2,192,1536]{2,1,0:T(8,128)(2,1)S(1)} %pick.2), channel_id=1, source_target_pairs={{0,8},{2,10},{4,12},{6,14},{8,0},{10,2},{12,4},{14,6},{1,9},{3,11}... | collective-permute-start | bytes 3538952 | tf_op jit(solution)/shard_map/ppermute | solution.py:374
  6.0 4.7 %copy-start.9 = (bf16[1,512,4,256]{3,2,1,0:T(4,128)(2,1)S(1)}, bf16[1,512,4,256]{3,2,1,0:T(4,128)(2,1)}, u32[]{:S(2)}) copy-start(bf16[1,512,4,256]{3,2,1,0:T(4,128)(2,1)} %param.10) | copy-start | bytes 3145732
  7.5 4.5 %collective-permute-start.1 = (bf16[256,2176]{1,0:T(8,128)(2,1)S(1)}, bf16[256,2176]{1,0:T(8,128)(2,1)S(1)}, u32[]{:S(2)}, u32[]{:S(2)}) collective-permute-start(bf16[256,2176]{1,0:T(8,128)(2,1)S(1)} %prepare.1.same_ref), channel_id=1, source_target_pairs={{0,1},{1,0},{2,3},{3,2},{4,5},{5,4},{6,7},{7,6},{8,9},{9,8},{10,11... | collective-permute-start | bytes 3342344 | tf_op jit(solution)/shard_map/ppermute | solution.py:382
  7.5 51.0 %collective-permute-start = (bf16[256,2176]{1,0:T(8,128)(2,1)S(1)}, bf16[256,2176]{1,0:T(8,128)(2,1)S(1)}, u32[]{:S(2)}, u32[]{:S(2)}) collective-permute-start(bf16[256,2176]{1,0:T(8,128)(2,1)S(1)} %prepare.1.same_ref), channel_id=1, source_target_pairs={{0,4},{1,3},{2,6},{3,1},{4,0},{5,7},{6,2},{7,5},{8,12},{9,11},{10,... | collective-permute-start | bytes 3342344 | tf_op jit(solution)/shard_map/ppermute | solution.py:379
  9.2 49.3 %collective-permute-start.3 = (bf16[256,2176]{1,0:T(8,128)(2,1)S(1)}, bf16[256,2176]{1,0:T(8,128)(2,1)S(1)}, u32[]{:S(2)}, u32[]{:S(2)}) collective-permute-start(bf16[256,2176]{1,0:T(8,128)(2,1)S(1)} %prepare.1.same_ref), channel_id=1, source_target_pairs={{0,2},{1,5},{2,0},{3,7},{4,6},{5,1},{6,4},{7,3},{8,10},{9,13},{10,... | collective-permute-start | bytes 3342344 | tf_op jit(solution)/shard_map/ppermute | solution.py:379
  58.5 5.1 %collective-permute-start.5 = (bf16[256,2176]{1,0:T(8,128)(2,1)S(1)}, bf16[256,2176]{1,0:T(8,128)(2,1)S(1)}, u32[]{:S(2)}, u32[]{:S(2)}) collective-permute-start(bf16[256,2176]{1,0:T(8,128)(2,1)S(1)} %collective-permute-done.same_ref), channel_id=1, source_target_pairs={{0,1},{1,0},{2,3},{3,2},{4,5},{5,4},{6,7},{7,6},{8,9},{9,8},{10,11... | collective-permute-start | bytes 3342344 | tf_op jit(solution)/shard_map/ppermute | solution.py:382
  59.0 9.6 %collective-permute-start.6 = (bf16[256,2176]{1,0:T(8,128)(2,1)S(1)}, bf16[256,2176]{1,0:T(8,128)(2,1)S(1)}, u32[]{:S(2)}, u32[]{:S(2)}) collective-permute-start(bf16[256,2176]{1,0:T(8,128)(2,1)S(1)} %collective-permute-done.3.same_ref), channel_id=1, source_target_pairs={{0,1},{1,0},{2,3},{3,2},{4,5},{5,4},{6,7},{7,6},{8,9},{9,8},{10,11... | collective-permute-start | bytes 3342344 | tf_op jit(solution)/shard_map/ppermute | solution.py:382
  59.0 28.3 %collective-permute-start.8 = (bf16[2,192,1536]{2,1,0:T(8,128)(2,1)S(1)}, bf16[2,192,1536]{2,1,0:T(8,128)(2,1)S(1)}, u32[]{:S(2)}, u32[]{:S(2)}) collective-permute-start(bf16[2,192,1536]{2,1,0:T(8,128)(2,1)S(1)} %collective-permute-done.4.refs_0_), channel_id=1, source_target_pairs={{0,16},{16,0},{1,17},{17,1},{2,18},{18,2},{3,19},{19,3},{4,20},{20... | collective-permute-start | bytes 3538952 | tf_op jit(solution)/shard_map/ppermute | solution.py:385
  60.6 21.3 %collective-permute-start.2 = (bf16[256,2176]{1,0:T(8,128)(2,1)S(1)}, bf16[256,2176]{1,0:T(8,128)(2,1)S(1)}, u32[]{:S(2)}, u32[]{:S(2)}) collective-permute-start(bf16[256,2176]{1,0:T(8,128)(2,1)S(1)} %collective-permute-done.same_ref), channel_id=1, source_target_pairs={{0,2},{1,5},{2,0},{3,7},{4,6},{5,1},{6,4},{7,3},{8,10},{9,13},{10,... | collective-permute-start | bytes 3342344 | tf_op jit(solution)/shard_map/ppermute | solution.py:379
  62.5 19.4 %collective-permute-start.7 = (bf16[512,512]{1,0:T(8,128)(2,1)S(1)}, bf16[512,512]{1,0:T(8,128)(2,1)S(1)}, u32[]{:S(2)}, u32[]{:S(2)}) collective-permute-start(bf16[512,512]{1,0:T(8,128)(2,1)S(1)} %pick.3), channel_id=1, source_target_pairs={{0,8},{2,10},{4,12},{6,14},{8,0},{10,2},{12,4},{14,6},{1,9},{3,11}... | collective-permute-start | bytes 1572872 | tf_op jit(solution)/shard_map/ppermute | solution.py:374
  68.1 19.3 %collective-permute-start.9 = (bf16[512,256]{1,0:T(8,128)(2,1)S(1)}, bf16[512,256]{1,0:T(8,128)(2,1)S(1)}, u32[]{:S(2)}, u32[]{:S(2)}) collective-permute-start(bf16[512,256]{1,0:T(8,128)(2,1)S(1)} %get-tuple-element.41), channel_id=1, source_target_pairs={{0,2},{1,5},{2,0},{3,7},{4,6},{5,1},{6,4},{7,3},{8,10},{9,13},{10,... | collective-permute-start | bytes 786440 | tf_op jit(solution)/shard_map/ppermute | solution.py:379
  68.6 19.5 %collective-permute-start.10 = (bf16[512,256]{1,0:T(8,128)(2,1)S(1)}, bf16[512,256]{1,0:T(8,128)(2,1)S(1)}, u32[]{:S(2)}, u32[]{:S(2)}) collective-permute-start(bf16[512,256]{1,0:T(8,128)(2,1)S(1)} %get-tuple-element.34), channel_id=1, source_target_pairs={{0,2},{1,5},{2,0},{3,7},{4,6},{5,1},{6,4},{7,3},{8,10},{9,13},{10,... | collective-permute-start | bytes 786440 | tf_op jit(solution)/shard_map/ppermute | solution.py:379
  88.8 6.3 %collective-permute-start.11 = (bf16[256,2176]{1,0:T(8,128)(2,1)S(1)}, bf16[256,2176]{1,0:T(8,128)(2,1)S(1)}, u32[]{:S(2)}, u32[]{:S(2)}) collective-permute-start(bf16[256,2176]{1,0:T(8,128)(2,1)S(1)} %collective-permute-done.2.same_ref), channel_id=1, source_target_pairs={{0,1},{1,0},{2,3},{3,2},{4,5},{5,4},{6,7},{7,6},{8,9},{9,8},{10,11... | collective-permute-start | bytes 3342344 | tf_op jit(solution)/shard_map/ppermute | solution.py:382
  92.7 13.8 %collective-permute-start.12 = (bf16[512,512]{1,0:T(8,128)(2,1)S(1)}, bf16[512,512]{1,0:T(8,128)(2,1)S(1)}, u32[]{:S(2)}, u32[]{:S(2)}) collective-permute-start(bf16[512,512]{1,0:T(8,128)(2,1)S(1)} %collective-permute-done.7.refs_2_), channel_id=1, source_target_pairs={{0,16},{16,0},{1,17},{17,1},{2,18},{18,2},{3,19},{19,3},{4,20},{20... | collective-permute-start | bytes 1572872 | tf_op jit(solution)/shard_map/ppermute | solution.py:385
  93.2 25.2 %collective-permute-start.15 = (bf16[512,512]{1,0:T(8,128)(2,1)S(1)}, bf16[512,512]{1,0:T(8,128)(2,1)S(1)}, u32[]{:S(2)}, u32[]{:S(2)}) collective-permute-start(bf16[512,512]{1,0:T(8,128)(2,1)S(1)} %get-tuple-element.37), channel_id=1, source_target_pairs={{0,4},{1,3},{2,6},{3,1},{4,0},{5,7},{6,2},{7,5},{8,12},{9,11},{10,... | collective-permute-start | bytes 1572872 | tf_op jit(solution)/shard_map/ppermute | solution.py:379
  99.6 18.8 %collective-permute-start.16 = (bf16[512,512]{1,0:T(8,128)(2,1)S(1)}, bf16[512,512]{1,0:T(8,128)(2,1)S(1)}, u32[]{:S(2)}, u32[]{:S(2)}) collective-permute-start(bf16[512,512]{1,0:T(8,128)(2,1)S(1)} %get-tuple-element.43), channel_id=1, source_target_pairs={{0,6},{1,7},{2,4},{3,5},{4,2},{5,3},{6,0},{7,1},{8,14},{9,15},{10,... | collective-permute-start | bytes 1572872 | tf_op jit(solution)/shard_map/ppermute | solution.py:379
  115.5 18.4 %collective-permute-start.13 = (bf16[512,512]{1,0:T(8,128)(2,1)}, bf16[512,512]{1,0:T(8,128)(2,1)S(1)}, u32[]{:S(2)}, u32[]{:S(2)}) collective-permute-start(bf16[512,512]{1,0:T(8,128)(2,1)} %get-tuple-element.47), channel_id=1, source_target_pairs={{0,4},{1,3},{2,6},{3,1},{4,0},{5,7},{6,2},{7,5},{8,12},{9,11},{10,... | collective-permute-start | bytes 1572872 | tf_op jit(solution)/shard_map/ppermute | solution.py:379
  115.8 26.4 %collective-permute-start.14 = (bf16[512,512]{1,0:T(8,128)(2,1)}, bf16[512,512]{1,0:T(8,128)(2,1)}, u32[]{:S(2)}, u32[]{:S(2)}) collective-permute-start(bf16[512,512]{1,0:T(8,128)(2,1)} %get-tuple-element.48), channel_id=1, source_target_pairs={{0,6},{1,7},{2,4},{3,5},{4,2},{5,3},{6,0},{7,1},{8,14},{9,15},{10,... | collective-permute-start | bytes 1572872 | tf_op jit(solution)/shard_map/ppermute | solution.py:379
  127.6 14.6 %collective-permute-start.17 = (bf16[512,256]{1,0:T(8,128)(2,1)}, bf16[512,256]{1,0:T(8,128)(2,1)S(1)}, u32[]{:S(2)}, u32[]{:S(2)}) collective-permute-start(bf16[512,256]{1,0:T(8,128)(2,1)} %get-tuple-element.52), channel_id=1, source_target_pairs={{0,2},{1,5},{2,0},{3,7},{4,6},{5,1},{6,4},{7,3},{8,10},{9,13},{10,... | collective-permute-start | bytes 786440 | tf_op jit(solution)/shard_map/ppermute | solution.py:379
  128.2 14.4 %collective-permute-start.18 = (bf16[512,256]{1,0:T(8,128)(2,1)}, bf16[512,256]{1,0:T(8,128)(2,1)S(1)}, u32[]{:S(2)}, u32[]{:S(2)}) collective-permute-start(bf16[512,256]{1,0:T(8,128)(2,1)} %get-tuple-element.53), channel_id=1, source_target_pairs={{0,2},{1,5},{2,0},{3,7},{4,6},{5,1},{6,4},{7,3},{8,10},{9,13},{10,... | collective-permute-start | bytes 786440 | tf_op jit(solution)/shard_map/ppermute | solution.py:379
  131.7 10.9 %copy-start.4 = (bf16[512,512]{1,0:T(8,128)(2,1)S(1)}, bf16[512,512]{1,0:T(8,128)(2,1)}, u32[]{:S(2)}) copy-start(bf16[512,512]{1,0:T(8,128)(2,1)} %copy-done.3) | copy-start | bytes 1572868
  (8 other events, 11.7 us)

commit v15 on v9

--- a/solution.py
+++ b/solution.py
@@ -438,8 +438,8 @@
     crossed_query = [other_part(after(far_query, mixed))] if share == 2 else []
     for distance in range(1, half_places):
         if other[distance] is None:
-            other[distance] = sibling(after(same[partner[distance]], mixed, far_pair, *crossed_query))
-        mixed = near(distance, mixed)
+            other[distance] = sibling(after(same[partner[distance]], mixed, far_pair))
+        mixed = near(distance, mixed, *(crossed_query if distance + 1 == half_places else []))
         arrived.append(across(mixed, distance))
     placed = []
     for distance in range(half_places):
@@ -481,7 +481,7 @@
             each = len(numbers) // len(pieces)
             for index, piece in enumerate(pieces):
                 spans = [base + number * value_width for number in numbers[index * each : (index + 1) * each]]
-                late.append((across(piece, distance) if distance else piece, spans))
+                (late if distance else placed).append((across(piece, distance) if distance else piece, spans))
     held = flush(None)
     placed.extend(late)
     held = flush(held)

time: 138 us -> 139 us (level)
  waiting for transfers between devices: 67.6 us -> 62.1 us
  starting transfers between devices: 23.7 us -> 27.4 us
  local copies, waits for them, and re-layouts: 3.33 us -> 6.46 us
    ppermute x2, waiting for transfers between devices: 50 us -> 7.85 us  [opposite(): lax.ppermute(value, 'seq', [(s, s ^ half_places) for s in range(places)])]
    ppermute x10, waiting for transfers between devices: 10.6 us -> 49 us  [across(): return lax.ppermute(value, ('seq', 'head'), pairs)]
    ppermute x4, starting transfers between devices: 1.34 us -> 5.27 us  [sibling(): return lax.ppermute(value, 'head', [(0, 1), (1, 0)])]
    unnamed x19 -> x27, local copies, waits for them, and re-layouts: 3.06 us -> 6.19 us
    ppermute x2, waiting for transfers between devices: 6.97 us -> 5.23 us  [other_part(): return lax.ppermute(value, 'parts', [(p, p ^ 1) for p in range(parts)])]
  transfers between devices with their start and end apart: 18 -> 18, of which waited for: 9 -> 7; matrix products, arithmetic and copies ran while one was open for 1% -> 1% of each run, Pallas kernels for 28% -> 28%
where the time goes in v15:
time: 139 us
  waiting for transfers between devices  62.1 us (45%)
  Pallas kernels  41.1 us (30%)
  starting transfers between devices  27.4 us (20%)
  local copies, waits for them, and re-layouts  6.46 us (5%)
    ppermute x10, waiting for transfers between devices, across(): return lax.ppermute(value, ('seq', 'head'), pairs)  49 us
    pallas_call x4, Pallas kernels, attend_near(): pl.pallas_call(partial(near_kernel, sizes, slot_count, slot, half_places)...  18.3 us
    pallas_call x2, Pallas kernels, attend_far(): pl.pallas_call(partial(far_kernel, sizes, slot_count, numbers, half_place...  17.4 us
    ppermute x10, starting transfers between devices, across(): return lax.ppermute(value, ('seq', 'head'), pairs)  13.9 us
    ppermute x2, waiting for transfers between devices, opposite(): lax.ppermute(value, 'seq', [(s, s ^ half_places) for s in range(places)])  7.85 us
    unnamed x27, local copies, waits for them, and re-layouts  6.19 us
    ppermute x4, starting transfers between devices, sibling(): return lax.ppermute(value, 'head', [(0, 1), (1, 0)])  5.27 us
    ppermute x2, waiting for transfers between devices, other_part(): return lax.ppermute(value, 'parts', [(p, p ^ 1) for p in range(parts)])  5.23 us
  transfers between devices with their start and end apart: 18, of which 7 were waited for; matrix products, arithmetic and copies ran while one was open for 1% of the time, Pallas kernels for 28%

profile of v15, /device:TPU:0, one launch (start us, length us, event | category | flops | bytes accessed | tf_op | source)
XLA Modules:
  0.0 138.6 jit_solution(2029957110747308684)
XLA Ops:
  0.0 1.7 %copy-done = bf16[1,1536,4,192]{1,3,2,0:T(8,128)(2,1)S(1)} copy-done((bf16[1,1536,4,192]{1,3,2,0:T(8,128)(2,1)S(1)}, bf16[1,1536,4,192]{1,3,2,0:T(8,128)(2,1)}, u32[]{:S(2)}) %copy-start) | copy-done | bytes 2359320
  1.8 4.1 %collective-permute-start.4 = (bf16[2,192,1536]{2,1,0:T(8,128)(2,1)S(1)}, bf16[2,192,1536]{2,1,0:T(8,128)(2,1)S(1)}, u32[]{:S(2)}, u32[]{:S(2)}) collective-permute-start(bf16[2,192,1536]{2,1,0:T(8,128)(2,1)S(1)} %pick.2), channel_id=1, source_target_pairs={{0,8},{2,10},{4,12},{6,14},{8,0},{10,2},{12,4},{14,6},{1,9},{3,11}... | collective-permute-start | bytes 3538952 | tf_op jit(solution)/shard_map/ppermute | solution.py:371
  7.5 1.6 %collective-permute-start = (bf16[256,2176]{1,0:T(8,128)(2,1)S(1)}, bf16[256,2176]{1,0:T(8,128)(2,1)S(1)}, u32[]{:S(2)}, u32[]{:S(2)}) collective-permute-start(bf16[256,2176]{1,0:T(8,128)(2,1)S(1)} %prepare.1.same_ref), channel_id=1, source_target_pairs={{0,4},{1,3},{2,6},{3,1},{4,0},{5,7},{6,2},{7,5},{8,12},{9,11},{10,... | collective-permute-start | bytes 3342344 | tf_op jit(solution)/shard_map/ppermute | solution.py:376
  9.2 1.5 %collective-permute-start.3 = (bf16[256,2176]{1,0:T(8,128)(2,1)S(1)}, bf16[256,2176]{1,0:T(8,128)(2,1)S(1)}, u32[]{:S(2)}, u32[]{:S(2)}) collective-permute-start(bf16[256,2176]{1,0:T(8,128)(2,1)S(1)} %prepare.1.same_ref), channel_id=1, source_target_pairs={{0,2},{1,5},{2,0},{3,7},{4,6},{5,1},{6,4},{7,3},{8,10},{9,13},{10,... | collective-permute-start | bytes 3342344 | tf_op jit(solution)/shard_map/ppermute | solution.py:376
  12.4 4.5 %attend_near.4 = (bf16[512,512]{1,0:T(8,128)(2,1)S(1)}, bf16[512,2176]{1,0:T(8,128)(2,1)S(1)}) custom-call(s32[66]{0:T(128)S(1)} %pad_add_fusion.place_ref, f32[512,256]{1,0:T(8,128)S(1)} %pad_maximum_fusion.table_ref, bf16[4,192,1536]{2,1,0:T(8,128)(2,1)S(1)} %bitcast.44, bf16[512,1024]{1,0:T(8,128)(2,1)S(1)} %bitcast.48, ...), custom_call_target="tpu_custom_call" | custom-call | flops 1024 | bytes 1024 | tf_op jit(solution)/shard_map/attend_near/pallas_call | solution.py:276
  16.9 41.6 %collective-permute-done.same_ref = bf16[256,2176]{1,0:T(8,128)(2,1)S(1)} collective-permute-done((bf16[256,2176]{1,0:T(8,128)(2,1)S(1)}, bf16[256,2176]{1,0:T(8,128)(2,1)S(1)}, u32[]{:S(2)}, u32[]{:S(2)}) %collective-permute-start) | collective-permute-done | bytes 1114144 | tf_op jit(solution)/shard_map/ppermute | solution.py:376
  59.0 1.9 %collective-permute-start.2 = (bf16[256,2176]{1,0:T(8,128)(2,1)S(1)}, bf16[256,2176]{1,0:T(8,128)(2,1)S(1)}, u32[]{:S(2)}, u32[]{:S(2)}) collective-permute-start(bf16[256,2176]{1,0:T(8,128)(2,1)S(1)} %collective-permute-done.same_ref), channel_id=1, source_target_pairs={{0,2},{1,5},{2,0},{3,7},{4,6},{5,1},{6,4},{7,3},{8,10},{9,13},{10,... | collective-permute-start | bytes 3342344 | tf_op jit(solution)/shard_map/ppermute | solution.py:376
  62.1 1.5 %collective-permute-start.7 = (bf16[2,192,1536]{2,1,0:T(8,128)(2,1)S(1)}, bf16[2,192,1536]{2,1,0:T(8,128)(2,1)S(1)}, u32[]{:S(2)}, u32[]{:S(2)}) collective-permute-start(bf16[2,192,1536]{2,1,0:T(8,128)(2,1)S(1)} %collective-permute-done.4.refs_0_), channel_id=1, source_target_pairs={{0,16},{16,0},{1,17},{17,1},{2,18},{18,2},{3,19},{19,3},{4,20},{20... | collective-permute-start | bytes 3538952 | tf_op jit(solution)/shard_map/ppermute | solution.py:382
  63.6 4.5 %attend_near.5 = (bf16[512,512]{1,0:T(8,128)(2,1)S(1)}, bf16[512,2176]{1,0:T(8,128)(2,1)S(1)}) custom-call(s32[66]{0:T(128)S(1)} %pad_add_fusion.place_ref, f32[512,256]{1,0:T(8,128)S(1)} %pad_maximum_fusion.table_ref, bf16[4,192,1536]{2,1,0:T(8,128)(2,1)S(1)} %bitcast.45, bf16[512,1024]{1,0:T(8,128)(2,1)S(1)} %bitcast.50, ...), custom_call_target="tpu_custom_call" | custom-call | flops 1024 | bytes 1024 | tf_op jit(solution)/shard_map/attend_near/pallas_call | solution.py:276
  68.1 4.7 %attend_near.6 = (bf16[512,512]{1,0:T(8,128)(2,1)S(1)}, bf16[512,2176]{1,0:T(8,128)(2,1)S(1)}) custom-call(s32[66]{0:T(128)S(1)} %pad_add_fusion.place_ref, f32[512,256]{1,0:T(8,128)S(1)} %pad_maximum_fusion.table_ref, bf16[4,192,1536]{2,1,0:T(8,128)(2,1)S(1)} %bitcast.46, bf16[512,1024]{1,0:T(8,128)(2,1)S(1)} %bitcast.51, ...), custom_call_target="tpu_custom_call" | custom-call | flops 1024 | bytes 1024 | tf_op jit(solution)/shard_map/attend_near/pallas_call | solution.py:276
  72.8 7.8 %collective-permute-done.8.refs_2_ = bf16[512,512]{1,0:T(8,128)(2,1)S(1)} collective-permute-done((bf16[512,512]{1,0:T(8,128)(2,1)S(1)}, bf16[512,512]{1,0:T(8,128)(2,1)S(1)}, u32[]{:S(2)}, u32[]{:S(2)}) %collective-permute-start.8) | collective-permute-done | bytes 524320 | tf_op jit(solution)/shard_map/ppermute | solution.py:371
  80.7 4.7 %collective-permute-start.9 = (bf16[256,2176]{1,0:T(8,128)(2,1)S(1)}, bf16[256,2176]{1,0:T(8,128)(2,1)S(1)}, u32[]{:S(2)}, u32[]{:S(2)}) collective-permute-start(bf16[256,2176]{1,0:T(8,128)(2,1)S(1)} %collective-permute-done.2.same_ref), channel_id=1, source_target_pairs={{0,1},{1,0},{2,3},{3,2},{4,5},{5,4},{6,7},{7,6},{8,9},{9,8},{10,11... | collective-permute-start | bytes 3342344 | tf_op jit(solution)/shard_map/ppermute | solution.py:379
  85.4 1.5 %collective-permute-start.10 = (bf16[512,512]{1,0:T(8,128)(2,1)S(1)}, bf16[512,512]{1,0:T(8,128)(2,1)S(1)}, u32[]{:S(2)}, u32[]{:S(2)}) collective-permute-start(bf16[512,512]{1,0:T(8,128)(2,1)S(1)} %collective-permute-done.8.refs_2_), channel_id=1, source_target_pairs={{0,16},{16,0},{1,17},{17,1},{2,18},{18,2},{3,19},{19,3},{4,20},{20... | collective-permute-start | bytes 1572872 | tf_op jit(solution)/shard_map/ppermute | solution.py:382
  86.9 1.5 %collective-permute-start.14 = (bf16[512,512]{1,0:T(8,128)(2,1)S(1)}, bf16[512,512]{1,0:T(8,128)(2,1)S(1)}, u32[]{:S(2)}, u32[]{:S(2)}) collective-permute-start(bf16[512,512]{1,0:T(8,128)(2,1)S(1)} %get-tuple-element.36), channel_id=1, source_target_pairs={{0,4},{1,3},{2,6},{3,1},{4,0},{5,7},{6,2},{7,5},{8,12},{9,11},{10,... | collective-permute-start | bytes 1572872 | tf_op jit(solution)/shard_map/ppermute | solution.py:376
  90.8 4.5 %attend_near.7 = (bf16[512,512]{1,0:T(8,128)(2,1)S(1)}, bf16[512,2176]{1,0:T(8,128)(2,1)S(1)}) custom-call(s32[66]{0:T(128)S(1)} %pad_add_fusion.place_ref, f32[512,256]{1,0:T(8,128)S(1)} %pad_maximum_fusion.table_ref, bf16[4,192,1536]{2,1,0:T(8,128)(2,1)S(1)} %bitcast.47, bf16[512,1024]{1,0:T(8,128)(2,1)S(1)} %bitcast.52, ...), custom_call_target="tpu_custom_call" | custom-call | flops 1024 | bytes 1024 | tf_op jit(solution)/shard_map/attend_near/pallas_call | solution.py:276
  95.4 2.1 %collective-permute-start.15 = (bf16[512,512]{1,0:T(8,128)(2,1)S(1)}, bf16[512,512]{1,0:T(8,128)(2,1)S(1)}, u32[]{:S(2)}, u32[]{:S(2)}) collective-permute-start(bf16[512,512]{1,0:T(8,128)(2,1)S(1)} %get-tuple-element.41), channel_id=1, source_target_pairs={{0,6},{1,7},{2,4},{3,5},{4,2},{5,3},{6,0},{7,1},{8,14},{9,15},{10,... | collective-permute-start | bytes 1572872 | tf_op jit(solution)/shard_map/ppermute | solution.py:376
  97.4 4.3 %collective-permute-done.10.refs_3_ = bf16[512,512]{1,0:T(8,128)(2,1)S(1)} collective-permute-done((bf16[512,512]{1,0:T(8,128)(2,1)S(1)}, bf16[512,512]{1,0:T(8,128)(2,1)S(1)}, u32[]{:S(2)}, u32[]{:S(2)}) %collective-permute-start.10) | collective-permute-done | bytes 524320 | tf_op jit(solution)/shard_map/ppermute | solution.py:382
  101.7 9.0 %attend_far.2 = (bf16[512,512]{1,0:T(8,128)(2,1)}, bf16[512,512]{1,0:T(8,128)(2,1)}) custom-call(s32[66]{0:T(128)S(1)} %pad_add_fusion.place_ref, f32[512,256]{1,0:T(8,128)S(1)} %pad_maximum_fusion.table_ref, bf16[2,192,1536]{2,1,0:T(8,128)(2,1)S(1)} %collective-permute-done.4.refs_0_, bf16[2,192,1536]{2,1,0:T(8,128)(2,1)S(1)} %collective-permute-done.7.refs_1_, ...), custom_call_target="tpu_custom_call" | custom-call | flops 1024 | bytes 1024 | tf_op jit(solution)/shard_map/attend_far/pallas_call | solution.py:297
  111.0 1.5 %collective-permute-start.12 = (bf16[512,512]{1,0:T(8,128)(2,1)}, bf16[512,512]{1,0:T(8,128)(2,1)S(1)}, u32[]{:S(2)}, u32[]{:S(2)}) collective-permute-start(bf16[512,512]{1,0:T(8,128)(2,1)} %get-tuple-element.46), channel_id=1, source_target_pairs={{0,6},{1,7},{2,4},{3,5},{4,2},{5,3},{6,0},{7,1},{8,14},{9,15},{10,... | collective-permute-start | bytes 1572872 | tf_op jit(solution)/shard_map/ppermute | solution.py:376
  112.9 8.4 %attend_far.3 = (bf16[512,256]{1,0:T(8,128)(2,1)}, bf16[512,256]{1,0:T(8,128)(2,1)}, bf16[512,512]{1,0:T(8,128)(2,1)S(1)}) custom-call(s32[66]{0:T(128)S(1)} %pad_add_fusion.place_ref, f32[512,256]{1,0:T(8,128)S(1)} %pad_maximum_fusion.table_ref, bf16[2,192,1536]{2,1,0:T(8,128)(2,1)S(1)} %collective-permute-done.4.refs_0_, ...), custom_call_target="tpu_custom_call" | custom-call | flops 1024 | bytes 1024 | tf_op jit(solution)/shard_map/attend_far/pallas_call | solution.py:297
  122.1 1.5 %collective-permute-start.16 = (bf16[512,256]{1,0:T(8,128)(2,1)}, bf16[512,256]{1,0:T(8,128)(2,1)S(1)}, u32[]{:S(2)}, u32[]{:S(2)}) collective-permute-start(bf16[512,256]{1,0:T(8,128)(2,1)} %get-tuple-element.50), channel_id=1, source_target_pairs={{0,2},{1,5},{2,0},{3,7},{4,6},{5,1},{6,4},{7,3},{8,10},{9,13},{10,... | collective-permute-start | bytes 786440 | tf_op jit(solution)/shard_map/ppermute | solution.py:376
  127.5 2.2 %place_pieces.2.refs_4_ = bf16[512,4096]{1,0:T(8,128)(2,1)} custom-call(s32[20]{0:T(128)S(1)} %stack.143.offsets_ref, bf16[512,512]{1,0:T(8,128)(2,1)S(1)} %get-tuple-element.29.refs_0_, bf16[512,512]{1,0:T(8,128)(2,1)S(1)} %copy-done.4, bf16[512,512]{1,0:T(8,128)(2,1)S(1)} %collective-permute-done.14.refs_2_, bf16[512,512]{1,0:T(8,128)(2,1)S(1)} %copy-done.6, ...), custom_call_target="tpu_custom_call" | custom-call | flops 1024 | bytes 1024 | tf_op jit(solution)/shard_map/place_pieces/pallas_call | solution.py:333
  129.7 6.1 %collective-permute-done.12.refs_1_ = bf16[512,512]{1,0:T(8,128)(2,1)S(1)} collective-permute-done((bf16[512,512]{1,0:T(8,128)(2,1)}, bf16[512,512]{1,0:T(8,128)(2,1)S(1)}, u32[]{:S(2)}, u32[]{:S(2)}) %collective-permute-start.12) | collective-permute-done | bytes 524320 | tf_op jit(solution)/shard_map/ppermute | solution.py:376
  136.7 1.8 %place_pieces.3 = bf16[512,4096]{1,0:T(8,128)(2,1)} custom-call(s32[12]{0:T(128)S(1)} %stack.120.offsets_ref, bf16[512,512]{1,0:T(8,128)(2,1)S(1)} %collective-permute-done.11.refs_0_, bf16[512,512]{1,0:T(8,128)(2,1)S(1)} %collective-permute-done.12.refs_1_, bf16[512,256]{1,0:T(8,128)(2,1)S(1)} %collective-permute-done.16.refs_2_, ...), custom_call_target="tpu_custom_call", output_to_operand_aliasing={{}: (5, {})} | custom-call | flops 1024 | bytes 1024 | tf_op jit(solution)/shard_map/place_pieces/pallas_call | solution.py:333
  (59 shorter events, 13.7 us)
Async XLA Ops:
  1.7 4.3 %copy-start.10 = (f32[1536]{0:T(1024)S(1)}, f32[1536]{0:T(1024)}, u32[]{:S(2)}) copy-start(f32[1536]{0:T(1024)} %param.7) | copy-start | bytes 18436
  1.7 4.3 %copy-start.12 = (f32[512]{0:T(512)S(1)}, f32[512]{0:T(512)}, u32[]{:S(2)}) copy-start(f32[512]{0:T(512)} %param.8) | copy-start | bytes 6148
  1.7 4.4 %copy-start.2 = (bf16[256,2112]{0,1:T(8,128)(2,1)S(1)}, bf16[256,2112]{0,1:T(8,128)(2,1)}, u32[]{:S(2)}) copy-start(bf16[256,2112]{0,1:T(8,128)(2,1)} %param.6) | copy-start | bytes 3244036
  1.8 56.7 %collective-permute-start.4 = (bf16[2,192,1536]{2,1,0:T(8,128)(2,1)S(1)}, bf16[2,192,1536]{2,1,0:T(8,128)(2,1)S(1)}, u32[]{:S(2)}, u32[]{:S(2)}) collective-permute-start(bf16[2,192,1536]{2,1,0:T(8,128)(2,1)S(1)} %pick.2), channel_id=1, source_target_pairs={{0,8},{2,10},{4,12},{6,14},{8,0},{10,2},{12,4},{14,6},{1,9},{3,11}... | collective-permute-start | bytes 3538952 | tf_op jit(solution)/shard_map/ppermute | solution.py:371
  6.0 4.7 %copy-start.9 = (bf16[1,512,4,256]{3,2,1,0:T(4,128)(2,1)S(1)}, bf16[1,512,4,256]{3,2,1,0:T(4,128)(2,1)}, u32[]{:S(2)}) copy-start(bf16[1,512,4,256]{3,2,1,0:T(4,128)(2,1)} %param.10) | copy-start | bytes 3145732
  7.5 4.5 %collective-permute-start.1 = (bf16[256,2176]{1,0:T(8,128)(2,1)S(1)}, bf16[256,2176]{1,0:T(8,128)(2,1)S(1)}, u32[]{:S(2)}, u32[]{:S(2)}) collective-permute-start(bf16[256,2176]{1,0:T(8,128)(2,1)S(1)} %prepare.1.same_ref), channel_id=1, source_target_pairs={{0,1},{1,0},{2,3},{3,2},{4,5},{5,4},{6,7},{7,6},{8,9},{9,8},{10,11... | collective-permute-start | bytes 3342344 | tf_op jit(solution)/shard_map/ppermute | solution.py:379
  7.5 51.0 %collective-permute-start = (bf16[256,2176]{1,0:T(8,128)(2,1)S(1)}, bf16[256,2176]{1,0:T(8,128)(2,1)S(1)}, u32[]{:S(2)}, u32[]{:S(2)}) collective-permute-start(bf16[256,2176]{1,0:T(8,128)(2,1)S(1)} %prepare.1.same_ref), channel_id=1, source_target_pairs={{0,4},{1,3},{2,6},{3,1},{4,0},{5,7},{6,2},{7,5},{8,12},{9,11},{10,... | collective-permute-start | bytes 3342344 | tf_op jit(solution)/shard_map/ppermute | solution.py:376
  9.2 49.3 %collective-permute-start.3 = (bf16[256,2176]{1,0:T(8,128)(2,1)S(1)}, bf16[256,2176]{1,0:T(8,128)(2,1)S(1)}, u32[]{:S(2)}, u32[]{:S(2)}) collective-permute-start(bf16[256,2176]{1,0:T(8,128)(2,1)S(1)} %prepare.1.same_ref), channel_id=1, source_target_pairs={{0,2},{1,5},{2,0},{3,7},{4,6},{5,1},{6,4},{7,3},{8,10},{9,13},{10,... | collective-permute-start | bytes 3342344 | tf_op jit(solution)/shard_map/ppermute | solution.py:376
  58.5 5.1 %collective-permute-start.5 = (bf16[256,2176]{1,0:T(8,128)(2,1)S(1)}, bf16[256,2176]{1,0:T(8,128)(2,1)S(1)}, u32[]{:S(2)}, u32[]{:S(2)}) collective-permute-start(bf16[256,2176]{1,0:T(8,128)(2,1)S(1)} %collective-permute-done.same_ref), channel_id=1, source_target_pairs={{0,1},{1,0},{2,3},{3,2},{4,5},{5,4},{6,7},{7,6},{8,9},{9,8},{10,11... | collective-permute-start | bytes 3342344 | tf_op jit(solution)/shard_map/ppermute | solution.py:379
  59.0 9.1 %collective-permute-start.6 = (bf16[256,2176]{1,0:T(8,128)(2,1)S(1)}, bf16[256,2176]{1,0:T(8,128)(2,1)S(1)}, u32[]{:S(2)}, u32[]{:S(2)}) collective-permute-start(bf16[256,2176]{1,0:T(8,128)(2,1)S(1)} %collective-permute-done.3.same_ref), channel_id=1, source_target_pairs={{0,1},{1,0},{2,3},{3,2},{4,5},{5,4},{6,7},{7,6},{8,9},{9,8},{10,11... | collective-permute-start | bytes 3342344 | tf_op jit(solution)/shard_map/ppermute | solution.py:379
  59.0 21.7 %collective-permute-start.2 = (bf16[256,2176]{1,0:T(8,128)(2,1)S(1)}, bf16[256,2176]{1,0:T(8,128)(2,1)S(1)}, u32[]{:S(2)}, u32[]{:S(2)}) collective-permute-start(bf16[256,2176]{1,0:T(8,128)(2,1)S(1)} %collective-permute-done.same_ref), channel_id=1, source_target_pairs={{0,2},{1,5},{2,0},{3,7},{4,6},{5,1},{6,4},{7,3},{8,10},{9,13},{10,... | collective-permute-start | bytes 3342344 | tf_op jit(solution)/shard_map/ppermute | solution.py:376
  61.0 19.7 %collective-permute-start.8 = (bf16[512,512]{1,0:T(8,128)(2,1)S(1)}, bf16[512,512]{1,0:T(8,128)(2,1)S(1)}, u32[]{:S(2)}, u32[]{:S(2)}) collective-permute-start(bf16[512,512]{1,0:T(8,128)(2,1)S(1)} %pick.3), channel_id=1, source_target_pairs={{0,8},{2,10},{4,12},{6,14},{8,0},{10,2},{12,4},{14,6},{1,9},{3,11}... | collective-permute-start | bytes 1572872 | tf_op jit(solution)/shard_map/ppermute | solution.py:371
  62.1 28.8 %collective-permute-start.7 = (bf16[2,192,1536]{2,1,0:T(8,128)(2,1)S(1)}, bf16[2,192,1536]{2,1,0:T(8,128)(2,1)S(1)}, u32[]{:S(2)}, u32[]{:S(2)}) collective-permute-start(bf16[2,192,1536]{2,1,0:T(8,128)(2,1)S(1)} %collective-permute-done.4.refs_0_), channel_id=1, source_target_pairs={{0,16},{16,0},{1,17},{17,1},{2,18},{18,2},{3,19},{19,3},{4,20},{20... | collective-permute-start | bytes 3538952 | tf_op jit(solution)/shard_map/ppermute | solution.py:382
  80.7 10.1 %collective-permute-start.9 = (bf16[256,2176]{1,0:T(8,128)(2,1)S(1)}, bf16[256,2176]{1,0:T(8,128)(2,1)S(1)}, u32[]{:S(2)}, u32[]{:S(2)}) collective-permute-start(bf16[256,2176]{1,0:T(8,128)(2,1)S(1)} %collective-permute-done.2.same_ref), channel_id=1, source_target_pairs={{0,1},{1,0},{2,3},{3,2},{4,5},{5,4},{6,7},{7,6},{8,9},{9,8},{10,11... | collective-permute-start | bytes 3342344 | tf_op jit(solution)/shard_map/ppermute | solution.py:379
  85.4 16.3 %collective-permute-start.10 = (bf16[512,512]{1,0:T(8,128)(2,1)S(1)}, bf16[512,512]{1,0:T(8,128)(2,1)S(1)}, u32[]{:S(2)}, u32[]{:S(2)}) collective-permute-start(bf16[512,512]{1,0:T(8,128)(2,1)S(1)} %collective-permute-done.8.refs_2_), channel_id=1, source_target_pairs={{0,16},{16,0},{1,17},{17,1},{2,18},{18,2},{3,19},{19,3},{4,20},{20... | collective-permute-start | bytes 1572872 | tf_op jit(solution)/shard_map/ppermute | solution.py:382
  86.9 25.5 %collective-permute-start.14 = (bf16[512,512]{1,0:T(8,128)(2,1)S(1)}, bf16[512,512]{1,0:T(8,128)(2,1)S(1)}, u32[]{:S(2)}, u32[]{:S(2)}) collective-permute-start(bf16[512,512]{1,0:T(8,128)(2,1)S(1)} %get-tuple-element.36), channel_id=1, source_target_pairs={{0,4},{1,3},{2,6},{3,1},{4,0},{5,7},{6,2},{7,5},{8,12},{9,11},{10,... | collective-permute-start | bytes 1572872 | tf_op jit(solution)/shard_map/ppermute | solution.py:376
  88.4 24.1 %collective-permute-start.13 = (bf16[512,512]{1,0:T(8,128)(2,1)S(1)}, bf16[512,512]{1,0:T(8,128)(2,1)S(1)}, u32[]{:S(2)}, u32[]{:S(2)}) collective-permute-start(bf16[512,512]{1,0:T(8,128)(2,1)S(1)} %get-tuple-element.33), channel_id=1, source_target_pairs={{0,2},{1,5},{2,0},{3,7},{4,6},{5,1},{6,4},{7,3},{8,10},{9,13},{10,... | collective-permute-start | bytes 1572872 | tf_op jit(solution)/shard_map/ppermute | solution.py:376
  95.4 17.5 %collective-permute-start.15 = (bf16[512,512]{1,0:T(8,128)(2,1)S(1)}, bf16[512,512]{1,0:T(8,128)(2,1)S(1)}, u32[]{:S(2)}, u32[]{:S(2)}) collective-permute-start(bf16[512,512]{1,0:T(8,128)(2,1)S(1)} %get-tuple-element.41), channel_id=1, source_target_pairs={{0,6},{1,7},{2,4},{3,5},{4,2},{5,3},{6,0},{7,1},{8,14},{9,15},{10,... | collective-permute-start | bytes 1572872 | tf_op jit(solution)/shard_map/ppermute | solution.py:376
  110.7 19.0 %collective-permute-start.11 = (bf16[512,512]{1,0:T(8,128)(2,1)}, bf16[512,512]{1,0:T(8,128)(2,1)S(1)}, u32[]{:S(2)}, u32[]{:S(2)}) collective-permute-start(bf16[512,512]{1,0:T(8,128)(2,1)} %get-tuple-element.45), channel_id=1, source_target_pairs={{0,4},{1,3},{2,6},{3,1},{4,0},{5,7},{6,2},{7,5},{8,12},{9,11},{10,... | collective-permute-start | bytes 1572872 | tf_op jit(solution)/shard_map/ppermute | solution.py:376
  111.0 24.8 %collective-permute-start.12 = (bf16[512,512]{1,0:T(8,128)(2,1)}, bf16[512,512]{1,0:T(8,128)(2,1)S(1)}, u32[]{:S(2)}, u32[]{:S(2)}) collective-permute-start(bf16[512,512]{1,0:T(8,128)(2,1)} %get-tuple-element.46), channel_id=1, source_target_pairs={{0,6},{1,7},{2,4},{3,5},{4,2},{5,3},{6,0},{7,1},{8,14},{9,15},{10,... | collective-permute-start | bytes 1572872 | tf_op jit(solution)/shard_map/ppermute | solution.py:376
  112.5 8.8 %copy-start.3 = (bf16[512,512]{1,0:T(8,128)(2,1)}, bf16[512,512]{1,0:T(8,128)(2,1)S(1)}, u32[]{:S(2)}) copy-start(bf16[512,512]{1,0:T(8,128)(2,1)S(1)} %collective-permute-done.13.refs_1_) | copy-start | bytes 1572868
  112.9 8.4 %copy-start.5 = (bf16[512,512]{1,0:T(8,128)(2,1)}, bf16[512,512]{1,0:T(8,128)(2,1)S(1)}, u32[]{:S(2)}) copy-start(bf16[512,512]{1,0:T(8,128)(2,1)S(1)} %collective-permute-done.15.refs_3_) | copy-start | bytes 1572868
  122.1 13.7 %collective-permute-start.16 = (bf16[512,256]{1,0:T(8,128)(2,1)}, bf16[512,256]{1,0:T(8,128)(2,1)S(1)}, u32[]{:S(2)}, u32[]{:S(2)}) collective-permute-start(bf16[512,256]{1,0:T(8,128)(2,1)} %get-tuple-element.50), channel_id=1, source_target_pairs={{0,2},{1,5},{2,0},{3,7},{4,6},{5,1},{6,4},{7,3},{8,10},{9,13},{10,... | collective-permute-start | bytes 786440 | tf_op jit(solution)/shard_map/ppermute | solution.py:376
  123.6 13.1 %collective-permute-start.17 = (bf16[512,256]{1,0:T(8,128)(2,1)}, bf16[512,256]{1,0:T(8,128)(2,1)S(1)}, u32[]{:S(2)}, u32[]{:S(2)}) collective-permute-start(bf16[512,256]{1,0:T(8,128)(2,1)} %get-tuple-element.51), channel_id=1, source_target_pairs={{0,2},{1,5},{2,0},{3,7},{4,6},{5,1},{6,4},{7,3},{8,10},{9,13},{10,... | collective-permute-start | bytes 786440 | tf_op jit(solution)/shard_map/ppermute | solution.py:376
  (7 other events, 11.5 us)

commit v16 on v9

--- a/solution.py
+++ b/solution.py
@@ -121,28 +121,34 @@
     def dot(left, right, dims):
         return lax.dot_general(left, right, dims, preferred_element_type=jnp.float32)
 
+    def query(low, high, picked):
+        parts = [query_weight_ref[number, low:high, :] for query_weight_ref, _, number in picked]
+        return dot(tokens_ref[:, :q_width], jnp.concatenate(parts, axis=0), NT)
+
+    def turn_all():
+        picked = list(chosen)
+        while len(picked) % group_heads:
+            picked.append(picked[-1])
+        ropes = query(nope_width, query_width, picked)
+        for first in range(0, heads, group_heads):
+            rope = ropes[:, first * rope_width : (first + group_heads) * rope_width]
+            swapped = jnp.where(is_first, pltpu.roll(rope, nope_width - half_width, 1), pltpu.roll(rope, half_width, 1))
+            turned = (rope * turn_ref[:, :nope_width] + swapped * turn_ref[:, nope_width:]) * score_scale
+            for index in range(min(group_heads, heads - first)):
+                low = (2 * (first + index) + 1) * nope_width
+                moved = pltpu.roll(turned, nope_width - index * rope_width, 1) if index else turned
+                query_ref[:, low : low + nope_width] = jnp.where(is_rope, moved, apart).astype(jnp.bfloat16)
+
     def project(some):
         picked = [chosen[head] for head in some]
-        while len(picked) < group_heads:
-            picked.append(picked[-1])
-
-        def query(low, high, picked):
-            parts = [query_weight_ref[number, low:high, :] for query_weight_ref, _, number in picked]
-            return dot(tokens_ref[:, :q_width], jnp.concatenate(parts, axis=0), NT)
-
-        rope = query(nope_width, query_width, picked)
-        nope = query(0, nope_width, picked[: len(some)])
+        nope = query(0, nope_width, picked)
         latent = tokens_ref[:, q_width:rope_low]
         pairs = [weight_ref[:, number * pair_width : (number + 1) * pair_width] for _, weight_ref, number in picked]
-        pair = dot(latent, jnp.concatenate(pairs[: len(some)], axis=1), NN)
-        swapped = jnp.where(is_first, pltpu.roll(rope, nope_width - half_width, 1), pltpu.roll(rope, half_width, 1))
-        turned = (rope * turn_ref[:, :nope_width] + swapped * turn_ref[:, nope_width:]) * score_scale
+        pair = dot(latent, jnp.concatenate(pairs, axis=1), NN)
         for index, head in enumerate(some):
             low = 2 * head * nope_width
             part = nope[:, index * nope_width : (index + 1) * nope_width]
             query_ref[:, low : low + nope_width] = (part * score_scale).astype(jnp.bfloat16)
-            moved = pltpu.roll(turned, nope_width - index * rope_width, 1) if index else turned
-            query_ref[:, low + nope_width : low + 2 * nope_width] = jnp.where(is_rope, moved, apart).astype(jnp.bfloat16)
             both = pair[:, index * pair_width : (index + 1) * pair_width].astype(jnp.bfloat16)
             key_ref[:, head * nope_width : (head + 1) * nope_width] = both[:, :nope_width]
             value_ref[head, :, :value_width] = both[:, nope_width:]
@@ -169,6 +175,7 @@
         ).astype(jnp.bfloat16)
 
     batches = [list(range(heads))[low : low + group_heads] for low in range(0, heads, group_heads)]
+    turn_all()
     project(batches[0])
     yield
     terms = None
@@ -481,7 +488,7 @@
             each = len(numbers) // len(pieces)
             for index, piece in enumerate(pieces):
                 spans = [base + number * value_width for number in numbers[index * each : (index + 1) * each]]
-                late.append((across(piece, distance) if distance else piece, spans))
+                (late if distance else placed).append((across(piece, distance) if distance else piece, spans))
     held = flush(None)
     placed.extend(late)
     held = flush(held)

time: 138 us -> 138 us (level)
  Pallas kernels: 41.8 us -> 37.9 us
  local copies, waits for them, and re-layouts: 3.33 us -> 6.46 us
    unnamed x19 -> x27, local copies, waits for them, and re-layouts: 3.06 us -> 6.19 us
    pallas_call x4, Pallas kernels: 18.3 us -> 16.7 us  [attend_near(): pl.pallas_call(partial(near_kernel, sizes, slot_count, slot, half_places)...]
    pallas_call x2, Pallas kernels: 17.4 us -> 15.7 us  [attend_far(): pl.pallas_call(partial(far_kernel, sizes, slot_count, numbers, half_place...]
  transfers between devices with their start and end apart: 18 -> 18, of which waited for: 9 -> 7; matrix products, arithmetic and copies ran while one was open for 1% -> 1% of each run, Pallas kernels for 28% -> 26%
where the time goes in v16:
time: 138 us
  waiting for transfers between devices  68 us (49%)
  Pallas kernels  37.9 us (27%)
  starting transfers between devices  23.7 us (17%)
  local copies, waits for them, and re-layouts  6.46 us (5%)
    ppermute x2, waiting for transfers between devices, opposite(): lax.ppermute(value, 'seq', [(s, s ^ half_places) for s in range(places)])  51.3 us
    pallas_call x4, Pallas kernels, attend_near(): pl.pallas_call(partial(near_kernel, sizes, slot_count, slot, half_places)...  16.7 us
    pallas_call x2, Pallas kernels, attend_far(): pl.pallas_call(partial(far_kernel, sizes, slot_count, numbers, half_place...  15.7 us
    ppermute x10, starting transfers between devices, across(): return lax.ppermute(value, ('seq', 'head'), pairs)  14.1 us
    ppermute x10, waiting for transfers between devices, across(): return lax.ppermute(value, ('seq', 'head'), pairs)  9.36 us
    ppermute x2, waiting for transfers between devices, other_part(): return lax.ppermute(value, 'parts', [(p, p ^ 1) for p in range(parts)])  7.37 us
    unnamed x27, local copies, waits for them, and re-layouts  6.19 us
    ppermute x2, starting transfers between devices, opposite(): lax.ppermute(value, 'seq', [(s, s ^ half_places) for s in range(places)])  5.19 us
  transfers between devices with their start and end apart: 18, of which 7 were waited for; matrix products, arithmetic and copies ran while one was open for 1% of the time, Pallas kernels for 26%

profile of v16, /device:TPU:0, one launch (start us, length us, event | category | flops | bytes accessed | tf_op | source)
XLA Modules:
  0.0 137.6 jit_solution(12532883426485845369)
XLA Ops:
  0.0 1.7 %copy-done = bf16[1,1536,4,192]{1,3,2,0:T(8,128)(2,1)S(1)} copy-done((bf16[1,1536,4,192]{1,3,2,0:T(8,128)(2,1)S(1)}, bf16[1,1536,4,192]{1,3,2,0:T(8,128)(2,1)}, u32[]{:S(2)}) %copy-start) | copy-done | bytes 2359320
  1.8 4.1 %collective-permute-start.4 = (bf16[2,192,1536]{2,1,0:T(8,128)(2,1)S(1)}, bf16[2,192,1536]{2,1,0:T(8,128)(2,1)S(1)}, u32[]{:S(2)}, u32[]{:S(2)}) collective-permute-start(bf16[2,192,1536]{2,1,0:T(8,128)(2,1)S(1)} %pick.2), channel_id=1, source_target_pairs={{0,8},{2,10},{4,12},{6,14},{8,0},{10,2},{12,4},{14,6},{1,9},{3,11}... | collective-permute-start | bytes 3538952 | tf_op jit(solution)/shard_map/ppermute | solution.py:378
  7.5 1.6 %collective-permute-start = (bf16[256,2176]{1,0:T(8,128)(2,1)S(1)}, bf16[256,2176]{1,0:T(8,128)(2,1)S(1)}, u32[]{:S(2)}, u32[]{:S(2)}) collective-permute-start(bf16[256,2176]{1,0:T(8,128)(2,1)S(1)} %prepare.1.same_ref), channel_id=1, source_target_pairs={{0,4},{1,3},{2,6},{3,1},{4,0},{5,7},{6,2},{7,5},{8,12},{9,11},{10,... | collective-permute-start | bytes 3342344 | tf_op jit(solution)/shard_map/ppermute | solution.py:383
  9.2 1.5 %collective-permute-start.3 = (bf16[256,2176]{1,0:T(8,128)(2,1)S(1)}, bf16[256,2176]{1,0:T(8,128)(2,1)S(1)}, u32[]{:S(2)}, u32[]{:S(2)}) collective-permute-start(bf16[256,2176]{1,0:T(8,128)(2,1)S(1)} %prepare.1.same_ref), channel_id=1, source_target_pairs={{0,2},{1,5},{2,0},{3,7},{4,6},{5,1},{6,4},{7,3},{8,10},{9,13},{10,... | collective-permute-start | bytes 3342344 | tf_op jit(solution)/shard_map/ppermute | solution.py:383
  12.4 4.1 %attend_near.4 = (bf16[512,512]{1,0:T(8,128)(2,1)S(1)}, bf16[512,2176]{1,0:T(8,128)(2,1)S(1)}) custom-call(s32[66]{0:T(128)S(1)} %pad_add_fusion.place_ref, f32[512,256]{1,0:T(8,128)S(1)} %pad_maximum_fusion.table_ref, bf16[4,192,1536]{2,1,0:T(8,128)(2,1)S(1)} %bitcast.44, bf16[512,1024]{1,0:T(8,128)(2,1)S(1)} %bitcast.48, ...), custom_call_target="tpu_custom_call" | custom-call | flops 1024 | bytes 1024 | tf_op jit(solution)/shard_map/attend_near/pallas_call | solution.py:283
  16.5 40.7 %collective-permute-done.4.refs_0_ = bf16[2,192,1536]{2,1,0:T(8,128)(2,1)S(1)} collective-permute-done((bf16[2,192,1536]{2,1,0:T(8,128)(2,1)S(1)}, bf16[2,192,1536]{2,1,0:T(8,128)(2,1)S(1)}, u32[]{:S(2)}, u32[]{:S(2)}) %collective-permute-start.4) | collective-permute-done | bytes 1179680 | tf_op jit(solution)/shard_map/ppermute | solution.py:378
  57.2 1.5 %collective-permute-start.8 = (bf16[2,192,1536]{2,1,0:T(8,128)(2,1)S(1)}, bf16[2,192,1536]{2,1,0:T(8,128)(2,1)S(1)}, u32[]{:S(2)}, u32[]{:S(2)}) collective-permute-start(bf16[2,192,1536]{2,1,0:T(8,128)(2,1)S(1)} %collective-permute-done.4.refs_0_), channel_id=1, source_target_pairs={{0,16},{16,0},{1,17},{17,1},{2,18},{18,2},{3,19},{19,3},{4,20},{20... | collective-permute-start | bytes 3538952 | tf_op jit(solution)/shard_map/ppermute | solution.py:389
  59.3 1.6 %collective-permute-start.2 = (bf16[256,2176]{1,0:T(8,128)(2,1)S(1)}, bf16[256,2176]{1,0:T(8,128)(2,1)S(1)}, u32[]{:S(2)}, u32[]{:S(2)}) collective-permute-start(bf16[256,2176]{1,0:T(8,128)(2,1)S(1)} %collective-permute-done.same_ref), channel_id=1, source_target_pairs={{0,2},{1,5},{2,0},{3,7},{4,6},{5,1},{6,4},{7,3},{8,10},{9,13},{10,... | collective-permute-start | bytes 3342344 | tf_op jit(solution)/shard_map/ppermute | solution.py:383
  62.1 4.1 %attend_near.5 = (bf16[512,512]{1,0:T(8,128)(2,1)S(1)}, bf16[512,2176]{1,0:T(8,128)(2,1)S(1)}) custom-call(s32[66]{0:T(128)S(1)} %pad_add_fusion.place_ref, f32[512,256]{1,0:T(8,128)S(1)} %pad_maximum_fusion.table_ref, bf16[4,192,1536]{2,1,0:T(8,128)(2,1)S(1)} %bitcast.45, bf16[512,1024]{1,0:T(8,128)(2,1)S(1)} %bitcast.50, ...), custom_call_target="tpu_custom_call" | custom-call | flops 1024 | bytes 1024 | tf_op jit(solution)/shard_map/attend_near/pallas_call | solution.py:283
  66.2 4.3 %attend_near.6 = (bf16[512,512]{1,0:T(8,128)(2,1)S(1)}, bf16[512,2176]{1,0:T(8,128)(2,1)S(1)}) custom-call(s32[66]{0:T(128)S(1)} %pad_add_fusion.place_ref, f32[512,256]{1,0:T(8,128)S(1)} %pad_maximum_fusion.table_ref, bf16[4,192,1536]{2,1,0:T(8,128)(2,1)S(1)} %bitcast.46, bf16[512,1024]{1,0:T(8,128)(2,1)S(1)} %bitcast.51, ...), custom_call_target="tpu_custom_call" | custom-call | flops 1024 | bytes 1024 | tf_op jit(solution)/shard_map/attend_near/pallas_call | solution.py:283
  70.5 10.5 %collective-permute-done.7.refs_2_ = bf16[512,512]{1,0:T(8,128)(2,1)S(1)} collective-permute-done((bf16[512,512]{1,0:T(8,128)(2,1)S(1)}, bf16[512,512]{1,0:T(8,128)(2,1)S(1)}, u32[]{:S(2)}, u32[]{:S(2)}) %collective-permute-start.7) | collective-permute-done | bytes 524320 | tf_op jit(solution)/shard_map/ppermute | solution.py:378
  81.0 3.3 %collective-permute-done.8.refs_1_ = bf16[2,192,1536]{2,1,0:T(8,128)(2,1)S(1)} collective-permute-done((bf16[2,192,1536]{2,1,0:T(8,128)(2,1)S(1)}, bf16[2,192,1536]{2,1,0:T(8,128)(2,1)S(1)}, u32[]{:S(2)}, u32[]{:S(2)}) %collective-permute-start.8) | collective-permute-done | bytes 1179680 | tf_op jit(solution)/shard_map/ppermute | solution.py:389
  85.1 1.5 %collective-permute-start.10 = (bf16[512,512]{1,0:T(8,128)(2,1)S(1)}, bf16[512,512]{1,0:T(8,128)(2,1)S(1)}, u32[]{:S(2)}, u32[]{:S(2)}) collective-permute-start(bf16[512,512]{1,0:T(8,128)(2,1)S(1)} %collective-permute-done.7.refs_2_), channel_id=1, source_target_pairs={{0,16},{16,0},{1,17},{17,1},{2,18},{18,2},{3,19},{19,3},{4,20},{20... | collective-permute-start | bytes 1572872 | tf_op jit(solution)/shard_map/ppermute | solution.py:389
  86.6 1.8 %collective-permute-start.14 = (bf16[512,512]{1,0:T(8,128)(2,1)S(1)}, bf16[512,512]{1,0:T(8,128)(2,1)S(1)}, u32[]{:S(2)}, u32[]{:S(2)}) collective-permute-start(bf16[512,512]{1,0:T(8,128)(2,1)S(1)} %get-tuple-element.36), channel_id=1, source_target_pairs={{0,4},{1,3},{2,6},{3,1},{4,0},{5,7},{6,2},{7,5},{8,12},{9,11},{10,... | collective-permute-start | bytes 1572872 | tf_op jit(solution)/shard_map/ppermute | solution.py:383
  88.4 1.4 %collective-permute-start.13 = (bf16[512,512]{1,0:T(8,128)(2,1)S(1)}, bf16[512,512]{1,0:T(8,128)(2,1)S(1)}, u32[]{:S(2)}, u32[]{:S(2)}) collective-permute-start(bf16[512,512]{1,0:T(8,128)(2,1)S(1)} %get-tuple-element.33), channel_id=1, source_target_pairs={{0,2},{1,5},{2,0},{3,7},{4,6},{5,1},{6,4},{7,3},{8,10},{9,13},{10,... | collective-permute-start | bytes 1572872 | tf_op jit(solution)/shard_map/ppermute | solution.py:383
  89.8 4.1 %attend_near.7 = (bf16[512,512]{1,0:T(8,128)(2,1)S(1)}, bf16[512,2176]{1,0:T(8,128)(2,1)S(1)}) custom-call(s32[66]{0:T(128)S(1)} %pad_add_fusion.place_ref, f32[512,256]{1,0:T(8,128)S(1)} %pad_maximum_fusion.table_ref, bf16[4,192,1536]{2,1,0:T(8,128)(2,1)S(1)} %bitcast.47, bf16[512,1024]{1,0:T(8,128)(2,1)S(1)} %bitcast.52, ...), custom_call_target="tpu_custom_call" | custom-call | flops 1024 | bytes 1024 | tf_op jit(solution)/shard_map/attend_near/pallas_call | solution.py:283
  94.8 4.1 %collective-permute-done.10.refs_3_ = bf16[512,512]{1,0:T(8,128)(2,1)S(1)} collective-permute-done((bf16[512,512]{1,0:T(8,128)(2,1)S(1)}, bf16[512,512]{1,0:T(8,128)(2,1)S(1)}, u32[]{:S(2)}, u32[]{:S(2)}) %collective-permute-start.10) | collective-permute-done | bytes 524320 | tf_op jit(solution)/shard_map/ppermute | solution.py:389
  98.9 8.2 %attend_far.2 = (bf16[512,512]{1,0:T(8,128)(2,1)}, bf16[512,512]{1,0:T(8,128)(2,1)}) custom-call(s32[66]{0:T(128)S(1)} %pad_add_fusion.place_ref, f32[512,256]{1,0:T(8,128)S(1)} %pad_maximum_fusion.table_ref, bf16[2,192,1536]{2,1,0:T(8,128)(2,1)S(1)} %collective-permute-done.4.refs_0_, bf16[2,192,1536]{2,1,0:T(8,128)(2,1)S(1)} %collective-permute-done.8.refs_1_, ...), custom_call_target="tpu_custom_call" | custom-call | flops 1024 | bytes 1024 | tf_op jit(solution)/shard_map/attend_far/pallas_call | solution.py:304
  107.1 2.3 %collective-permute-start.11 = (bf16[512,512]{1,0:T(8,128)(2,1)}, bf16[512,512]{1,0:T(8,128)(2,1)S(1)}, u32[]{:S(2)}, u32[]{:S(2)}) collective-permute-start(bf16[512,512]{1,0:T(8,128)(2,1)} %get-tuple-element.45), channel_id=1, source_target_pairs={{0,4},{1,3},{2,6},{3,1},{4,0},{5,7},{6,2},{7,5},{8,12},{9,11},{10,... | collective-permute-start | bytes 1572872 | tf_op jit(solution)/shard_map/ppermute | solution.py:383
  110.3 3.3 %collective-permute-done.15.refs_3_ = bf16[512,512]{1,0:T(8,128)(2,1)S(1)} collective-permute-done((bf16[512,512]{1,0:T(8,128)(2,1)S(1)}, bf16[512,512]{1,0:T(8,128)(2,1)S(1)}, u32[]{:S(2)}, u32[]{:S(2)}) %collective-permute-start.15) | collective-permute-done | bytes 524320 | tf_op jit(solution)/shard_map/ppermute | solution.py:383
  113.6 7.6 %attend_far.3 = (bf16[512,256]{1,0:T(8,128)(2,1)}, bf16[512,256]{1,0:T(8,128)(2,1)}, bf16[512,512]{1,0:T(8,128)(2,1)S(1)}) custom-call(s32[66]{0:T(128)S(1)} %pad_add_fusion.place_ref, f32[512,256]{1,0:T(8,128)S(1)} %pad_maximum_fusion.table_ref, bf16[2,192,1536]{2,1,0:T(8,128)(2,1)S(1)} %collective-permute-done.4.refs_0_, ...), custom_call_target="tpu_custom_call" | custom-call | flops 1024 | bytes 1024 | tf_op jit(solution)/shard_map/attend_far/pallas_call | solution.py:304
  127.3 2.2 %place_pieces.2.refs_4_ = bf16[512,4096]{1,0:T(8,128)(2,1)} custom-call(s32[20]{0:T(128)S(1)} %stack.143.offsets_ref, bf16[512,512]{1,0:T(8,128)(2,1)S(1)} %get-tuple-element.29.refs_0_, bf16[512,512]{1,0:T(8,128)(2,1)S(1)} %copy-done.4, bf16[512,512]{1,0:T(8,128)(2,1)S(1)} %collective-permute-done.14.refs_2_, bf16[512,512]{1,0:T(8,128)(2,1)S(1)} %copy-done.6, ...), custom_call_target="tpu_custom_call" | custom-call | flops 1024 | bytes 1024 | tf_op jit(solution)/shard_map/place_pieces/pallas_call | solution.py:340
  129.5 5.0 %collective-permute-done.12.refs_1_ = bf16[512,512]{1,0:T(8,128)(2,1)S(1)} collective-permute-done((bf16[512,512]{1,0:T(8,128)(2,1)}, bf16[512,512]{1,0:T(8,128)(2,1)S(1)}, u32[]{:S(2)}, u32[]{:S(2)}) %collective-permute-start.12) | collective-permute-done | bytes 524320 | tf_op jit(solution)/shard_map/ppermute | solution.py:383
  135.6 1.8 %place_pieces.3 = bf16[512,4096]{1,0:T(8,128)(2,1)} custom-call(s32[12]{0:T(128)S(1)} %stack.120.offsets_ref, bf16[512,512]{1,0:T(8,128)(2,1)S(1)} %collective-permute-done.11.refs_0_, bf16[512,512]{1,0:T(8,128)(2,1)S(1)} %collective-permute-done.12.refs_1_, bf16[512,256]{1,0:T(8,128)(2,1)S(1)} %collective-permute-done.16.refs_2_, ...), custom_call_target="tpu_custom_call", output_to_operand_aliasing={{}: (5, {})} | custom-call | flops 1024 | bytes 1024 | tf_op jit(solution)/shard_map/place_pieces/pallas_call | solution.py:340
  (59 shorter events, 14.9 us)
Async XLA Ops:
  1.7 4.3 %copy-start.10 = (f32[1536]{0:T(1024)S(1)}, f32[1536]{0:T(1024)}, u32[]{:S(2)}) copy-start(f32[1536]{0:T(1024)} %param.7) | copy-start | bytes 18436
  1.7 4.3 %copy-start.12 = (f32[512]{0:T(512)S(1)}, f32[512]{0:T(512)}, u32[]{:S(2)}) copy-start(f32[512]{0:T(512)} %param.8) | copy-start | bytes 6148
  1.7 4.4 %copy-start.2 = (bf16[256,2112]{0,1:T(8,128)(2,1)S(1)}, bf16[256,2112]{0,1:T(8,128)(2,1)}, u32[]{:S(2)}) copy-start(bf16[256,2112]{0,1:T(8,128)(2,1)} %param.6) | copy-start | bytes 3244036
  1.8 55.5 %collective-permute-start.4 = (bf16[2,192,1536]{2,1,0:T(8,128)(2,1)S(1)}, bf16[2,192,1536]{2,1,0:T(8,128)(2,1)S(1)}, u32[]{:S(2)}, u32[]{:S(2)}) collective-permute-start(bf16[2,192,1536]{2,1,0:T(8,128)(2,1)S(1)} %pick.2), channel_id=1, source_target_pairs={{0,8},{2,10},{4,12},{6,14},{8,0},{10,2},{12,4},{14,6},{1,9},{3,11}... | collective-permute-start | bytes 3538952 | tf_op jit(solution)/shard_map/ppermute | solution.py:378
  6.0 4.7 %copy-start.9 = (bf16[1,512,4,256]{3,2,1,0:T(4,128)(2,1)S(1)}, bf16[1,512,4,256]{3,2,1,0:T(4,128)(2,1)}, u32[]{:S(2)}) copy-start(bf16[1,512,4,256]{3,2,1,0:T(4,128)(2,1)} %param.10) | copy-start | bytes 3145732
  7.5 4.5 %collective-permute-start.1 = (bf16[256,2176]{1,0:T(8,128)(2,1)S(1)}, bf16[256,2176]{1,0:T(8,128)(2,1)S(1)}, u32[]{:S(2)}, u32[]{:S(2)}) collective-permute-start(bf16[256,2176]{1,0:T(8,128)(2,1)S(1)} %prepare.1.same_ref), channel_id=1, source_target_pairs={{0,1},{1,0},{2,3},{3,2},{4,5},{5,4},{6,7},{7,6},{8,9},{9,8},{10,11... | collective-permute-start | bytes 3342344 | tf_op jit(solution)/shard_map/ppermute | solution.py:386
  7.5 51.2 %collective-permute-start = (bf16[256,2176]{1,0:T(8,128)(2,1)S(1)}, bf16[256,2176]{1,0:T(8,128)(2,1)S(1)}, u32[]{:S(2)}, u32[]{:S(2)}) collective-permute-start(bf16[256,2176]{1,0:T(8,128)(2,1)S(1)} %prepare.1.same_ref), channel_id=1, source_target_pairs={{0,4},{1,3},{2,6},{3,1},{4,0},{5,7},{6,2},{7,5},{8,12},{9,11},{10,... | collective-permute-start | bytes 3342344 | tf_op jit(solution)/shard_map/ppermute | solution.py:383
  9.2 49.6 %collective-permute-start.3 = (bf16[256,2176]{1,0:T(8,128)(2,1)S(1)}, bf16[256,2176]{1,0:T(8,128)(2,1)S(1)}, u32[]{:S(2)}, u32[]{:S(2)}) collective-permute-start(bf16[256,2176]{1,0:T(8,128)(2,1)S(1)} %prepare.1.same_ref), channel_id=1, source_target_pairs={{0,2},{1,5},{2,0},{3,7},{4,6},{5,1},{6,4},{7,3},{8,10},{9,13},{10,... | collective-permute-start | bytes 3342344 | tf_op jit(solution)/shard_map/ppermute | solution.py:383
  57.2 27.1 %collective-permute-start.8 = (bf16[2,192,1536]{2,1,0:T(8,128)(2,1)S(1)}, bf16[2,192,1536]{2,1,0:T(8,128)(2,1)S(1)}, u32[]{:S(2)}, u32[]{:S(2)}) collective-permute-start(bf16[2,192,1536]{2,1,0:T(8,128)(2,1)S(1)} %collective-permute-done.4.refs_0_), channel_id=1, source_target_pairs={{0,16},{16,0},{1,17},{17,1},{2,18},{18,2},{3,19},{19,3},{4,20},{20... | collective-permute-start | bytes 3538952 | tf_op jit(solution)/shard_map/ppermute | solution.py:389
  58.8 3.3 %collective-permute-start.5 = (bf16[256,2176]{1,0:T(8,128)(2,1)S(1)}, bf16[256,2176]{1,0:T(8,128)(2,1)S(1)}, u32[]{:S(2)}, u32[]{:S(2)}) collective-permute-start(bf16[256,2176]{1,0:T(8,128)(2,1)S(1)} %collective-permute-done.same_ref), channel_id=1, source_target_pairs={{0,1},{1,0},{2,3},{3,2},{4,5},{5,4},{6,7},{7,6},{8,9},{9,8},{10,11... | collective-permute-start | bytes 3342344 | tf_op jit(solution)/shard_map/ppermute | solution.py:386
  59.0 7.2 %collective-permute-start.6 = (bf16[256,2176]{1,0:T(8,128)(2,1)S(1)}, bf16[256,2176]{1,0:T(8,128)(2,1)S(1)}, u32[]{:S(2)}, u32[]{:S(2)}) collective-permute-start(bf16[256,2176]{1,0:T(8,128)(2,1)S(1)} %collective-permute-done.3.same_ref), channel_id=1, source_target_pairs={{0,1},{1,0},{2,3},{3,2},{4,5},{5,4},{6,7},{7,6},{8,9},{9,8},{10,11... | collective-permute-start | bytes 3342344 | tf_op jit(solution)/shard_map/ppermute | solution.py:386
  59.3 21.8 %collective-permute-start.2 = (bf16[256,2176]{1,0:T(8,128)(2,1)S(1)}, bf16[256,2176]{1,0:T(8,128)(2,1)S(1)}, u32[]{:S(2)}, u32[]{:S(2)}) collective-permute-start(bf16[256,2176]{1,0:T(8,128)(2,1)S(1)} %collective-permute-done.same_ref), channel_id=1, source_target_pairs={{0,2},{1,5},{2,0},{3,7},{4,6},{5,1},{6,4},{7,3},{8,10},{9,13},{10,... | collective-permute-start | bytes 3342344 | tf_op jit(solution)/shard_map/ppermute | solution.py:383
  61.0 20.1 %collective-permute-start.7 = (bf16[512,512]{1,0:T(8,128)(2,1)S(1)}, bf16[512,512]{1,0:T(8,128)(2,1)S(1)}, u32[]{:S(2)}, u32[]{:S(2)}) collective-permute-start(bf16[512,512]{1,0:T(8,128)(2,1)S(1)} %pick.3), channel_id=1, source_target_pairs={{0,8},{2,10},{4,12},{6,14},{8,0},{10,2},{12,4},{14,6},{1,9},{3,11}... | collective-permute-start | bytes 1572872 | tf_op jit(solution)/shard_map/ppermute | solution.py:378
  84.3 5.5 %collective-permute-start.9 = (bf16[256,2176]{1,0:T(8,128)(2,1)S(1)}, bf16[256,2176]{1,0:T(8,128)(2,1)S(1)}, u32[]{:S(2)}, u32[]{:S(2)}) collective-permute-start(bf16[256,2176]{1,0:T(8,128)(2,1)S(1)} %collective-permute-done.2.same_ref), channel_id=1, source_target_pairs={{0,1},{1,0},{2,3},{3,2},{4,5},{5,4},{6,7},{7,6},{8,9},{9,8},{10,11... | collective-permute-start | bytes 3342344 | tf_op jit(solution)/shard_map/ppermute | solution.py:386
  85.1 13.8 %collective-permute-start.10 = (bf16[512,512]{1,0:T(8,128)(2,1)S(1)}, bf16[512,512]{1,0:T(8,128)(2,1)S(1)}, u32[]{:S(2)}, u32[]{:S(2)}) collective-permute-start(bf16[512,512]{1,0:T(8,128)(2,1)S(1)} %collective-permute-done.7.refs_2_), channel_id=1, source_target_pairs={{0,16},{16,0},{1,17},{17,1},{2,18},{18,2},{3,19},{19,3},{4,20},{20... | collective-permute-start | bytes 1572872 | tf_op jit(solution)/shard_map/ppermute | solution.py:389
  86.6 23.7 %collective-permute-start.14 = (bf16[512,512]{1,0:T(8,128)(2,1)S(1)}, bf16[512,512]{1,0:T(8,128)(2,1)S(1)}, u32[]{:S(2)}, u32[]{:S(2)}) collective-permute-start(bf16[512,512]{1,0:T(8,128)(2,1)S(1)} %get-tuple-element.36), channel_id=1, source_target_pairs={{0,4},{1,3},{2,6},{3,1},{4,0},{5,7},{6,2},{7,5},{8,12},{9,11},{10,... | collective-permute-start | bytes 1572872 | tf_op jit(solution)/shard_map/ppermute | solution.py:383
  88.4 21.9 %collective-permute-start.13 = (bf16[512,512]{1,0:T(8,128)(2,1)S(1)}, bf16[512,512]{1,0:T(8,128)(2,1)S(1)}, u32[]{:S(2)}, u32[]{:S(2)}) collective-permute-start(bf16[512,512]{1,0:T(8,128)(2,1)S(1)} %get-tuple-element.33), channel_id=1, source_target_pairs={{0,2},{1,5},{2,0},{3,7},{4,6},{5,1},{6,4},{7,3},{8,10},{9,13},{10,... | collective-permute-start | bytes 1572872 | tf_op jit(solution)/shard_map/ppermute | solution.py:383
  93.9 19.6 %collective-permute-start.15 = (bf16[512,512]{1,0:T(8,128)(2,1)S(1)}, bf16[512,512]{1,0:T(8,128)(2,1)S(1)}, u32[]{:S(2)}, u32[]{:S(2)}) collective-permute-start(bf16[512,512]{1,0:T(8,128)(2,1)S(1)} %get-tuple-element.41), channel_id=1, source_target_pairs={{0,6},{1,7},{2,4},{3,5},{4,2},{5,3},{6,0},{7,1},{8,14},{9,15},{10,... | collective-permute-start | bytes 1572872 | tf_op jit(solution)/shard_map/ppermute | solution.py:383
  107.1 22.4 %collective-permute-start.11 = (bf16[512,512]{1,0:T(8,128)(2,1)}, bf16[512,512]{1,0:T(8,128)(2,1)S(1)}, u32[]{:S(2)}, u32[]{:S(2)}) collective-permute-start(bf16[512,512]{1,0:T(8,128)(2,1)} %get-tuple-element.45), channel_id=1, source_target_pairs={{0,4},{1,3},{2,6},{3,1},{4,0},{5,7},{6,2},{7,5},{8,12},{9,11},{10,... | collective-permute-start | bytes 1572872 | tf_op jit(solution)/shard_map/ppermute | solution.py:383
  109.3 25.2 %collective-permute-start.12 = (bf16[512,512]{1,0:T(8,128)(2,1)}, bf16[512,512]{1,0:T(8,128)(2,1)S(1)}, u32[]{:S(2)}, u32[]{:S(2)}) collective-permute-start(bf16[512,512]{1,0:T(8,128)(2,1)} %get-tuple-element.46), channel_id=1, source_target_pairs={{0,6},{1,7},{2,4},{3,5},{4,2},{5,3},{6,0},{7,1},{8,14},{9,15},{10,... | collective-permute-start | bytes 1572872 | tf_op jit(solution)/shard_map/ppermute | solution.py:383
  110.3 10.8 %copy-start.3 = (bf16[512,512]{1,0:T(8,128)(2,1)}, bf16[512,512]{1,0:T(8,128)(2,1)S(1)}, u32[]{:S(2)}) copy-start(bf16[512,512]{1,0:T(8,128)(2,1)S(1)} %collective-permute-done.13.refs_1_) | copy-start | bytes 1572868
  113.6 7.6 %copy-start.5 = (bf16[512,512]{1,0:T(8,128)(2,1)}, bf16[512,512]{1,0:T(8,128)(2,1)S(1)}, u32[]{:S(2)}) copy-start(bf16[512,512]{1,0:T(8,128)(2,1)S(1)} %collective-permute-done.15.refs_3_) | copy-start | bytes 1572868
  122.0 12.5 %collective-permute-start.16 = (bf16[512,256]{1,0:T(8,128)(2,1)}, bf16[512,256]{1,0:T(8,128)(2,1)S(1)}, u32[]{:S(2)}, u32[]{:S(2)}) collective-permute-start(bf16[512,256]{1,0:T(8,128)(2,1)} %get-tuple-element.50), channel_id=1, source_target_pairs={{0,2},{1,5},{2,0},{3,7},{4,6},{5,1},{6,4},{7,3},{8,10},{9,13},{10,... | collective-permute-start | bytes 786440 | tf_op jit(solution)/shard_map/ppermute | solution.py:383
  122.6 13.0 %collective-permute-start.17 = (bf16[512,256]{1,0:T(8,128)(2,1)}, bf16[512,256]{1,0:T(8,128)(2,1)S(1)}, u32[]{:S(2)}, u32[]{:S(2)}) collective-permute-start(bf16[512,256]{1,0:T(8,128)(2,1)} %get-tuple-element.51), channel_id=1, source_target_pairs={{0,2},{1,5},{2,0},{3,7},{4,6},{5,1},{6,4},{7,3},{8,10},{9,13},{10,... | collective-permute-start | bytes 786440 | tf_op jit(solution)/shard_map/ppermute | solution.py:383
  (7 other events, 11.5 us)

commit v17 on v16

--- a/solution.py
+++ b/solution.py
@@ -445,8 +445,8 @@
     crossed_query = [other_part(after(far_query, mixed))] if share == 2 else []
     for distance in range(1, half_places):
         if other[distance] is None:
-            other[distance] = sibling(after(same[partner[distance]], mixed, far_pair, *crossed_query))
-        mixed = near(distance, mixed)
+            other[distance] = sibling(after(same[partner[distance]], mixed, far_pair))
+        mixed = near(distance, mixed, *(crossed_query if distance + 1 == half_places else []))
         arrived.append(across(mixed, distance))
     placed = []
     for distance in range(half_places):

time: 138 us -> 138 us (level)
  starting transfers between devices: 23.7 us -> 27.4 us
  waiting for transfers between devices: 68 us -> 64.6 us
    ppermute x2, waiting for transfers between devices: 51.3 us -> 8.68 us  [opposite(): lax.ppermute(value, 'seq', [(s, s ^ half_places) for s in range(places)])]
    ppermute x10, waiting for transfers between devices: 9.36 us -> 50.3 us  [across(): return lax.ppermute(value, ('seq', 'head'), pairs)]
    ppermute x4, starting transfers between devices: 1.34 us -> 5.27 us  [sibling(): return lax.ppermute(value, 'head', [(0, 1), (1, 0)])]
    ppermute x2, waiting for transfers between devices: 7.37 us -> 5.63 us  [other_part(): return lax.ppermute(value, 'parts', [(p, p ^ 1) for p in range(parts)])]
where the time goes in v17:
time: 138 us
  waiting for transfers between devices  64.6 us (47%)
  Pallas kernels  37.9 us (27%)
  starting transfers between devices  27.4 us (20%)
  local copies, waits for them, and re-layouts  6.46 us (5%)
    ppermute x10, waiting for transfers between devices, across(): return lax.ppermute(value, ('seq', 'head'), pairs)  50.3 us
    pallas_call x4, Pallas kernels, attend_near(): pl.pallas_call(partial(near_kernel, sizes, slot_count, slot, half_places)...  16.7 us
    pallas_call x2, Pallas kernels, attend_far(): pl.pallas_call(partial(far_kernel, sizes, slot_count, numbers, half_place...  15.7 us
    ppermute x10, starting transfers between devices, across(): return lax.ppermute(value, ('seq', 'head'), pairs)  13.9 us
    ppermute x2, waiting for transfers between devices, opposite(): lax.ppermute(value, 'seq', [(s, s ^ half_places) for s in range(places)])  8.68 us
    unnamed x27, local copies, waits for them, and re-layouts  6.19 us
    ppermute x2, waiting for transfers between devices, other_part(): return lax.ppermute(value, 'parts', [(p, p ^ 1) for p in range(parts)])  5.63 us
    ppermute x4, starting transfers between devices, sibling(): return lax.ppermute(value, 'head', [(0, 1), (1, 0)])  5.27 us
  transfers between devices with their start and end apart: 18, of which 7 were waited for; matrix products, arithmetic and copies ran while one was open for 1% of the time, Pallas kernels for 26%

profile of v17, /device:TPU:0, one launch (start us, length us, event | category | flops | bytes accessed | tf_op | source)
XLA Modules:
  0.0 137.8 jit_solution(15850629223022676651)
XLA Ops:
  0.0 1.7 %copy-done = bf16[1,1536,4,192]{1,3,2,0:T(8,128)(2,1)S(1)} copy-done((bf16[1,1536,4,192]{1,3,2,0:T(8,128)(2,1)S(1)}, bf16[1,1536,4,192]{1,3,2,0:T(8,128)(2,1)}, u32[]{:S(2)}) %copy-start) | copy-done | bytes 2359320
  1.8 4.1 %collective-permute-start.4 = (bf16[2,192,1536]{2,1,0:T(8,128)(2,1)S(1)}, bf16[2,192,1536]{2,1,0:T(8,128)(2,1)S(1)}, u32[]{:S(2)}, u32[]{:S(2)}) collective-permute-start(bf16[2,192,1536]{2,1,0:T(8,128)(2,1)S(1)} %pick.2), channel_id=1, source_target_pairs={{0,8},{2,10},{4,12},{6,14},{8,0},{10,2},{12,4},{14,6},{1,9},{3,11}... | collective-permute-start | bytes 3538952 | tf_op jit(solution)/shard_map/ppermute | solution.py:378
  7.5 1.6 %collective-permute-start = (bf16[256,2176]{1,0:T(8,128)(2,1)S(1)}, bf16[256,2176]{1,0:T(8,128)(2,1)S(1)}, u32[]{:S(2)}, u32[]{:S(2)}) collective-permute-start(bf16[256,2176]{1,0:T(8,128)(2,1)S(1)} %prepare.1.same_ref), channel_id=1, source_target_pairs={{0,4},{1,3},{2,6},{3,1},{4,0},{5,7},{6,2},{7,5},{8,12},{9,11},{10,... | collective-permute-start | bytes 3342344 | tf_op jit(solution)/shard_map/ppermute | solution.py:383
  9.2 1.5 %collective-permute-start.3 = (bf16[256,2176]{1,0:T(8,128)(2,1)S(1)}, bf16[256,2176]{1,0:T(8,128)(2,1)S(1)}, u32[]{:S(2)}, u32[]{:S(2)}) collective-permute-start(bf16[256,2176]{1,0:T(8,128)(2,1)S(1)} %prepare.1.same_ref), channel_id=1, source_target_pairs={{0,2},{1,5},{2,0},{3,7},{4,6},{5,1},{6,4},{7,3},{8,10},{9,13},{10,... | collective-permute-start | bytes 3342344 | tf_op jit(solution)/shard_map/ppermute | solution.py:383
  12.4 4.1 %attend_near.4 = (bf16[512,512]{1,0:T(8,128)(2,1)S(1)}, bf16[512,2176]{1,0:T(8,128)(2,1)S(1)}) custom-call(s32[66]{0:T(128)S(1)} %pad_add_fusion.place_ref, f32[512,256]{1,0:T(8,128)S(1)} %pad_maximum_fusion.table_ref, bf16[4,192,1536]{2,1,0:T(8,128)(2,1)S(1)} %bitcast.44, bf16[512,1024]{1,0:T(8,128)(2,1)S(1)} %bitcast.48, ...), custom_call_target="tpu_custom_call" | custom-call | flops 1024 | bytes 1024 | tf_op jit(solution)/shard_map/attend_near/pallas_call | solution.py:283
  16.5 42.0 %collective-permute-done.same_ref = bf16[256,2176]{1,0:T(8,128)(2,1)S(1)} collective-permute-done((bf16[256,2176]{1,0:T(8,128)(2,1)S(1)}, bf16[256,2176]{1,0:T(8,128)(2,1)S(1)}, u32[]{:S(2)}, u32[]{:S(2)}) %collective-permute-start) | collective-permute-done | bytes 1114144 | tf_op jit(solution)/shard_map/ppermute | solution.py:383
  59.0 1.9 %collective-permute-start.2 = (bf16[256,2176]{1,0:T(8,128)(2,1)S(1)}, bf16[256,2176]{1,0:T(8,128)(2,1)S(1)}, u32[]{:S(2)}, u32[]{:S(2)}) collective-permute-start(bf16[256,2176]{1,0:T(8,128)(2,1)S(1)} %collective-permute-done.same_ref), channel_id=1, source_target_pairs={{0,2},{1,5},{2,0},{3,7},{4,6},{5,1},{6,4},{7,3},{8,10},{9,13},{10,... | collective-permute-start | bytes 3342344 | tf_op jit(solution)/shard_map/ppermute | solution.py:383
  62.1 1.5 %collective-permute-start.7 = (bf16[2,192,1536]{2,1,0:T(8,128)(2,1)S(1)}, bf16[2,192,1536]{2,1,0:T(8,128)(2,1)S(1)}, u32[]{:S(2)}, u32[]{:S(2)}) collective-permute-start(bf16[2,192,1536]{2,1,0:T(8,128)(2,1)S(1)} %collective-permute-done.4.refs_0_), channel_id=1, source_target_pairs={{0,16},{16,0},{1,17},{17,1},{2,18},{18,2},{3,19},{19,3},{4,20},{20... | collective-permute-start | bytes 3538952 | tf_op jit(solution)/shard_map/ppermute | solution.py:389
  63.6 4.1 %attend_near.5 = (bf16[512,512]{1,0:T(8,128)(2,1)S(1)}, bf16[512,2176]{1,0:T(8,128)(2,1)S(1)}) custom-call(s32[66]{0:T(128)S(1)} %pad_add_fusion.place_ref, f32[512,256]{1,0:T(8,128)S(1)} %pad_maximum_fusion.table_ref, bf16[4,192,1536]{2,1,0:T(8,128)(2,1)S(1)} %bitcast.45, bf16[512,1024]{1,0:T(8,128)(2,1)S(1)} %bitcast.50, ...), custom_call_target="tpu_custom_call" | custom-call | flops 1024 | bytes 1024 | tf_op jit(solution)/shard_map/attend_near/pallas_call | solution.py:283
  67.7 4.3 %attend_near.6 = (bf16[512,512]{1,0:T(8,128)(2,1)S(1)}, bf16[512,2176]{1,0:T(8,128)(2,1)S(1)}) custom-call(s32[66]{0:T(128)S(1)} %pad_add_fusion.place_ref, f32[512,256]{1,0:T(8,128)S(1)} %pad_maximum_fusion.table_ref, bf16[4,192,1536]{2,1,0:T(8,128)(2,1)S(1)} %bitcast.46, bf16[512,1024]{1,0:T(8,128)(2,1)S(1)} %bitcast.51, ...), custom_call_target="tpu_custom_call" | custom-call | flops 1024 | bytes 1024 | tf_op jit(solution)/shard_map/attend_near/pallas_call | solution.py:283
  72.0 8.7 %collective-permute-done.8.refs_2_ = bf16[512,512]{1,0:T(8,128)(2,1)S(1)} collective-permute-done((bf16[512,512]{1,0:T(8,128)(2,1)S(1)}, bf16[512,512]{1,0:T(8,128)(2,1)S(1)}, u32[]{:S(2)}, u32[]{:S(2)}) %collective-permute-start.8) | collective-permute-done | bytes 524320 | tf_op jit(solution)/shard_map/ppermute | solution.py:378
  80.7 4.7 %collective-permute-start.9 = (bf16[256,2176]{1,0:T(8,128)(2,1)S(1)}, bf16[256,2176]{1,0:T(8,128)(2,1)S(1)}, u32[]{:S(2)}, u32[]{:S(2)}) collective-permute-start(bf16[256,2176]{1,0:T(8,128)(2,1)S(1)} %collective-permute-done.2.same_ref), channel_id=1, source_target_pairs={{0,1},{1,0},{2,3},{3,2},{4,5},{5,4},{6,7},{7,6},{8,9},{9,8},{10,11... | collective-permute-start | bytes 3342344 | tf_op jit(solution)/shard_map/ppermute | solution.py:386
  85.4 1.5 %collective-permute-start.10 = (bf16[512,512]{1,0:T(8,128)(2,1)S(1)}, bf16[512,512]{1,0:T(8,128)(2,1)S(1)}, u32[]{:S(2)}, u32[]{:S(2)}) collective-permute-start(bf16[512,512]{1,0:T(8,128)(2,1)S(1)} %collective-permute-done.8.refs_2_), channel_id=1, source_target_pairs={{0,16},{16,0},{1,17},{17,1},{2,18},{18,2},{3,19},{19,3},{4,20},{20... | collective-permute-start | bytes 1572872 | tf_op jit(solution)/shard_map/ppermute | solution.py:389
  86.9 1.5 %collective-permute-start.14 = (bf16[512,512]{1,0:T(8,128)(2,1)S(1)}, bf16[512,512]{1,0:T(8,128)(2,1)S(1)}, u32[]{:S(2)}, u32[]{:S(2)}) collective-permute-start(bf16[512,512]{1,0:T(8,128)(2,1)S(1)} %get-tuple-element.36), channel_id=1, source_target_pairs={{0,4},{1,3},{2,6},{3,1},{4,0},{5,7},{6,2},{7,5},{8,12},{9,11},{10,... | collective-permute-start | bytes 1572872 | tf_op jit(solution)/shard_map/ppermute | solution.py:383
  90.8 4.1 %attend_near.7 = (bf16[512,512]{1,0:T(8,128)(2,1)S(1)}, bf16[512,2176]{1,0:T(8,128)(2,1)S(1)}) custom-call(s32[66]{0:T(128)S(1)} %pad_add_fusion.place_ref, f32[512,256]{1,0:T(8,128)S(1)} %pad_maximum_fusion.table_ref, bf16[4,192,1536]{2,1,0:T(8,128)(2,1)S(1)} %bitcast.47, bf16[512,1024]{1,0:T(8,128)(2,1)S(1)} %bitcast.52, ...), custom_call_target="tpu_custom_call" | custom-call | flops 1024 | bytes 1024 | tf_op jit(solution)/shard_map/attend_near/pallas_call | solution.py:283
  95.0 2.1 %collective-permute-start.15 = (bf16[512,512]{1,0:T(8,128)(2,1)S(1)}, bf16[512,512]{1,0:T(8,128)(2,1)S(1)}, u32[]{:S(2)}, u32[]{:S(2)}) collective-permute-start(bf16[512,512]{1,0:T(8,128)(2,1)S(1)} %get-tuple-element.41), channel_id=1, source_target_pairs={{0,6},{1,7},{2,4},{3,5},{4,2},{5,3},{6,0},{7,1},{8,14},{9,15},{10,... | collective-permute-start | bytes 1572872 | tf_op jit(solution)/shard_map/ppermute | solution.py:383
  97.0 4.7 %collective-permute-done.10.refs_3_ = bf16[512,512]{1,0:T(8,128)(2,1)S(1)} collective-permute-done((bf16[512,512]{1,0:T(8,128)(2,1)S(1)}, bf16[512,512]{1,0:T(8,128)(2,1)S(1)}, u32[]{:S(2)}, u32[]{:S(2)}) %collective-permute-start.10) | collective-permute-done | bytes 524320 | tf_op jit(solution)/shard_map/ppermute | solution.py:389
  101.7 8.2 %attend_far.2 = (bf16[512,512]{1,0:T(8,128)(2,1)}, bf16[512,512]{1,0:T(8,128)(2,1)}) custom-call(s32[66]{0:T(128)S(1)} %pad_add_fusion.place_ref, f32[512,256]{1,0:T(8,128)S(1)} %pad_maximum_fusion.table_ref, bf16[2,192,1536]{2,1,0:T(8,128)(2,1)S(1)} %collective-permute-done.4.refs_0_, bf16[2,192,1536]{2,1,0:T(8,128)(2,1)S(1)} %collective-permute-done.7.refs_1_, ...), custom_call_target="tpu_custom_call" | custom-call | flops 1024 | bytes 1024 | tf_op jit(solution)/shard_map/attend_far/pallas_call | solution.py:304
  110.2 1.5 %collective-permute-start.12 = (bf16[512,512]{1,0:T(8,128)(2,1)}, bf16[512,512]{1,0:T(8,128)(2,1)S(1)}, u32[]{:S(2)}, u32[]{:S(2)}) collective-permute-start(bf16[512,512]{1,0:T(8,128)(2,1)} %get-tuple-element.46), channel_id=1, source_target_pairs={{0,6},{1,7},{2,4},{3,5},{4,2},{5,3},{6,0},{7,1},{8,14},{9,15},{10,... | collective-permute-start | bytes 1572872 | tf_op jit(solution)/shard_map/ppermute | solution.py:383
  112.9 7.6 %attend_far.3 = (bf16[512,256]{1,0:T(8,128)(2,1)}, bf16[512,256]{1,0:T(8,128)(2,1)}, bf16[512,512]{1,0:T(8,128)(2,1)S(1)}) custom-call(s32[66]{0:T(128)S(1)} %pad_add_fusion.place_ref, f32[512,256]{1,0:T(8,128)S(1)} %pad_maximum_fusion.table_ref, bf16[2,192,1536]{2,1,0:T(8,128)(2,1)S(1)} %collective-permute-done.4.refs_0_, ...), custom_call_target="tpu_custom_call" | custom-call | flops 1024 | bytes 1024 | tf_op jit(solution)/shard_map/attend_far/pallas_call | solution.py:304
  121.3 1.5 %collective-permute-start.16 = (bf16[512,256]{1,0:T(8,128)(2,1)}, bf16[512,256]{1,0:T(8,128)(2,1)S(1)}, u32[]{:S(2)}, u32[]{:S(2)}) collective-permute-start(bf16[512,256]{1,0:T(8,128)(2,1)} %get-tuple-element.50), channel_id=1, source_target_pairs={{0,2},{1,5},{2,0},{3,7},{4,6},{5,1},{6,4},{7,3},{8,10},{9,13},{10,... | collective-permute-start | bytes 786440 | tf_op jit(solution)/shard_map/ppermute | solution.py:383
  126.7 2.2 %place_pieces.2.refs_4_ = bf16[512,4096]{1,0:T(8,128)(2,1)} custom-call(s32[20]{0:T(128)S(1)} %stack.143.offsets_ref, bf16[512,512]{1,0:T(8,128)(2,1)S(1)} %get-tuple-element.29.refs_0_, bf16[512,512]{1,0:T(8,128)(2,1)S(1)} %copy-done.4, bf16[512,512]{1,0:T(8,128)(2,1)S(1)} %collective-permute-done.14.refs_2_, bf16[512,512]{1,0:T(8,128)(2,1)S(1)} %copy-done.6, ...), custom_call_target="tpu_custom_call" | custom-call | flops 1024 | bytes 1024 | tf_op jit(solution)/shard_map/place_pieces/pallas_call | solution.py:340
  128.9 6.1 %collective-permute-done.12.refs_1_ = bf16[512,512]{1,0:T(8,128)(2,1)S(1)} collective-permute-done((bf16[512,512]{1,0:T(8,128)(2,1)}, bf16[512,512]{1,0:T(8,128)(2,1)S(1)}, u32[]{:S(2)}, u32[]{:S(2)}) %collective-permute-start.12) | collective-permute-done | bytes 524320 | tf_op jit(solution)/shard_map/ppermute | solution.py:383
  135.9 1.8 %place_pieces.3 = bf16[512,4096]{1,0:T(8,128)(2,1)} custom-call(s32[12]{0:T(128)S(1)} %stack.120.offsets_ref, bf16[512,512]{1,0:T(8,128)(2,1)S(1)} %collective-permute-done.11.refs_0_, bf16[512,512]{1,0:T(8,128)(2,1)S(1)} %collective-permute-done.12.refs_1_, bf16[512,256]{1,0:T(8,128)(2,1)S(1)} %collective-permute-done.16.refs_2_, ...), custom_call_target="tpu_custom_call", output_to_operand_aliasing={{}: (5, {})} | custom-call | flops 1024 | bytes 1024 | tf_op jit(solution)/shard_map/place_pieces/pallas_call | solution.py:340
  (59 shorter events, 14.5 us)
Async XLA Ops:
  1.7 4.3 %copy-start.10 = (f32[1536]{0:T(1024)S(1)}, f32[1536]{0:T(1024)}, u32[]{:S(2)}) copy-start(f32[1536]{0:T(1024)} %param.7) | copy-start | bytes 18436
  1.7 4.3 %copy-start.12 = (f32[512]{0:T(512)S(1)}, f32[512]{0:T(512)}, u32[]{:S(2)}) copy-start(f32[512]{0:T(512)} %param.8) | copy-start | bytes 6148
  1.7 4.4 %copy-start.2 = (bf16[256,2112]{0,1:T(8,128)(2,1)S(1)}, bf16[256,2112]{0,1:T(8,128)(2,1)}, u32[]{:S(2)}) copy-start(bf16[256,2112]{0,1:T(8,128)(2,1)} %param.6) | copy-start | bytes 3244036
  1.8 56.7 %collective-permute-start.4 = (bf16[2,192,1536]{2,1,0:T(8,128)(2,1)S(1)}, bf16[2,192,1536]{2,1,0:T(8,128)(2,1)S(1)}, u32[]{:S(2)}, u32[]{:S(2)}) collective-permute-start(bf16[2,192,1536]{2,1,0:T(8,128)(2,1)S(1)} %pick.2), channel_id=1, source_target_pairs={{0,8},{2,10},{4,12},{6,14},{8,0},{10,2},{12,4},{14,6},{1,9},{3,11}... | collective-permute-start | bytes 3538952 | tf_op jit(solution)/shard_map/ppermute | solution.py:378
  6.0 4.7 %copy-start.9 = (bf16[1,512,4,256]{3,2,1,0:T(4,128)(2,1)S(1)}, bf16[1,512,4,256]{3,2,1,0:T(4,128)(2,1)}, u32[]{:S(2)}) copy-start(bf16[1,512,4,256]{3,2,1,0:T(4,128)(2,1)} %param.10) | copy-start | bytes 3145732
  7.5 4.5 %collective-permute-start.1 = (bf16[256,2176]{1,0:T(8,128)(2,1)S(1)}, bf16[256,2176]{1,0:T(8,128)(2,1)S(1)}, u32[]{:S(2)}, u32[]{:S(2)}) collective-permute-start(bf16[256,2176]{1,0:T(8,128)(2,1)S(1)} %prepare.1.same_ref), channel_id=1, source_target_pairs={{0,1},{1,0},{2,3},{3,2},{4,5},{5,4},{6,7},{7,6},{8,9},{9,8},{10,11... | collective-permute-start | bytes 3342344 | tf_op jit(solution)/shard_map/ppermute | solution.py:386
  7.5 51.0 %collective-permute-start = (bf16[256,2176]{1,0:T(8,128)(2,1)S(1)}, bf16[256,2176]{1,0:T(8,128)(2,1)S(1)}, u32[]{:S(2)}, u32[]{:S(2)}) collective-permute-start(bf16[256,2176]{1,0:T(8,128)(2,1)S(1)} %prepare.1.same_ref), channel_id=1, source_target_pairs={{0,4},{1,3},{2,6},{3,1},{4,0},{5,7},{6,2},{7,5},{8,12},{9,11},{10,... | collective-permute-start | bytes 3342344 | tf_op jit(solution)/shard_map/ppermute | solution.py:383
  9.2 49.3 %collective-permute-start.3 = (bf16[256,2176]{1,0:T(8,128)(2,1)S(1)}, bf16[256,2176]{1,0:T(8,128)(2,1)S(1)}, u32[]{:S(2)}, u32[]{:S(2)}) collective-permute-start(bf16[256,2176]{1,0:T(8,128)(2,1)S(1)} %prepare.1.same_ref), channel_id=1, source_target_pairs={{0,2},{1,5},{2,0},{3,7},{4,6},{5,1},{6,4},{7,3},{8,10},{9,13},{10,... | collective-permute-start | bytes 3342344 | tf_op jit(solution)/shard_map/ppermute | solution.py:383
  58.5 5.1 %collective-permute-start.5 = (bf16[256,2176]{1,0:T(8,128)(2,1)S(1)}, bf16[256,2176]{1,0:T(8,128)(2,1)S(1)}, u32[]{:S(2)}, u32[]{:S(2)}) collective-permute-start(bf16[256,2176]{1,0:T(8,128)(2,1)S(1)} %collective-permute-done.same_ref), channel_id=1, source_target_pairs={{0,1},{1,0},{2,3},{3,2},{4,5},{5,4},{6,7},{7,6},{8,9},{9,8},{10,11... | collective-permute-start | bytes 3342344 | tf_op jit(solution)/shard_map/ppermute | solution.py:386
  59.0 8.7 %collective-permute-start.6 = (bf16[256,2176]{1,0:T(8,128)(2,1)S(1)}, bf16[256,2176]{1,0:T(8,128)(2,1)S(1)}, u32[]{:S(2)}, u32[]{:S(2)}) collective-permute-start(bf16[256,2176]{1,0:T(8,128)(2,1)S(1)} %collective-permute-done.3.same_ref), channel_id=1, source_target_pairs={{0,1},{1,0},{2,3},{3,2},{4,5},{5,4},{6,7},{7,6},{8,9},{9,8},{10,11... | collective-permute-start | bytes 3342344 | tf_op jit(solution)/shard_map/ppermute | solution.py:386
  59.0 21.7 %collective-permute-start.2 = (bf16[256,2176]{1,0:T(8,128)(2,1)S(1)}, bf16[256,2176]{1,0:T(8,128)(2,1)S(1)}, u32[]{:S(2)}, u32[]{:S(2)}) collective-permute-start(bf16[256,2176]{1,0:T(8,128)(2,1)S(1)} %collective-permute-done.same_ref), channel_id=1, source_target_pairs={{0,2},{1,5},{2,0},{3,7},{4,6},{5,1},{6,4},{7,3},{8,10},{9,13},{10,... | collective-permute-start | bytes 3342344 | tf_op jit(solution)/shard_map/ppermute | solution.py:383
  61.0 19.7 %collective-permute-start.8 = (bf16[512,512]{1,0:T(8,128)(2,1)S(1)}, bf16[512,512]{1,0:T(8,128)(2,1)S(1)}, u32[]{:S(2)}, u32[]{:S(2)}) collective-permute-start(bf16[512,512]{1,0:T(8,128)(2,1)S(1)} %pick.3), channel_id=1, source_target_pairs={{0,8},{2,10},{4,12},{6,14},{8,0},{10,2},{12,4},{14,6},{1,9},{3,11}... | collective-permute-start | bytes 1572872 | tf_op jit(solution)/shard_map/ppermute | solution.py:378
  62.1 28.8 %collective-permute-start.7 = (bf16[2,192,1536]{2,1,0:T(8,128)(2,1)S(1)}, bf16[2,192,1536]{2,1,0:T(8,128)(2,1)S(1)}, u32[]{:S(2)}, u32[]{:S(2)}) collective-permute-start(bf16[2,192,1536]{2,1,0:T(8,128)(2,1)S(1)} %collective-permute-done.4.refs_0_), channel_id=1, source_target_pairs={{0,16},{16,0},{1,17},{17,1},{2,18},{18,2},{3,19},{19,3},{4,20},{20... | collective-permute-start | bytes 3538952 | tf_op jit(solution)/shard_map/ppermute | solution.py:389
  80.7 10.1 %collective-permute-start.9 = (bf16[256,2176]{1,0:T(8,128)(2,1)S(1)}, bf16[256,2176]{1,0:T(8,128)(2,1)S(1)}, u32[]{:S(2)}, u32[]{:S(2)}) collective-permute-start(bf16[256,2176]{1,0:T(8,128)(2,1)S(1)} %collective-permute-done.2.same_ref), channel_id=1, source_target_pairs={{0,1},{1,0},{2,3},{3,2},{4,5},{5,4},{6,7},{7,6},{8,9},{9,8},{10,11... | collective-permute-start | bytes 3342344 | tf_op jit(solution)/shard_map/ppermute | solution.py:386
  85.4 16.3 %collective-permute-start.10 = (bf16[512,512]{1,0:T(8,128)(2,1)S(1)}, bf16[512,512]{1,0:T(8,128)(2,1)S(1)}, u32[]{:S(2)}, u32[]{:S(2)}) collective-permute-start(bf16[512,512]{1,0:T(8,128)(2,1)S(1)} %collective-permute-done.8.refs_2_), channel_id=1, source_target_pairs={{0,16},{16,0},{1,17},{17,1},{2,18},{18,2},{3,19},{19,3},{4,20},{20... | collective-permute-start | bytes 1572872 | tf_op jit(solution)/shard_map/ppermute | solution.py:389
  86.9 24.7 %collective-permute-start.14 = (bf16[512,512]{1,0:T(8,128)(2,1)S(1)}, bf16[512,512]{1,0:T(8,128)(2,1)S(1)}, u32[]{:S(2)}, u32[]{:S(2)}) collective-permute-start(bf16[512,512]{1,0:T(8,128)(2,1)S(1)} %get-tuple-element.36), channel_id=1, source_target_pairs={{0,4},{1,3},{2,6},{3,1},{4,0},{5,7},{6,2},{7,5},{8,12},{9,11},{10,... | collective-permute-start | bytes 1572872 | tf_op jit(solution)/shard_map/ppermute | solution.py:383
  88.4 23.3 %collective-permute-start.13 = (bf16[512,512]{1,0:T(8,128)(2,1)S(1)}, bf16[512,512]{1,0:T(8,128)(2,1)S(1)}, u32[]{:S(2)}, u32[]{:S(2)}) collective-permute-start(bf16[512,512]{1,0:T(8,128)(2,1)S(1)} %get-tuple-element.33), channel_id=1, source_target_pairs={{0,2},{1,5},{2,0},{3,7},{4,6},{5,1},{6,4},{7,3},{8,10},{9,13},{10,... | collective-permute-start | bytes 1572872 | tf_op jit(solution)/shard_map/ppermute | solution.py:383
  95.0 18.0 %collective-permute-start.15 = (bf16[512,512]{1,0:T(8,128)(2,1)S(1)}, bf16[512,512]{1,0:T(8,128)(2,1)S(1)}, u32[]{:S(2)}, u32[]{:S(2)}) collective-permute-start(bf16[512,512]{1,0:T(8,128)(2,1)S(1)} %get-tuple-element.41), channel_id=1, source_target_pairs={{0,6},{1,7},{2,4},{3,5},{4,2},{5,3},{6,0},{7,1},{8,14},{9,15},{10,... | collective-permute-start | bytes 1572872 | tf_op jit(solution)/shard_map/ppermute | solution.py:383
  109.9 19.0 %collective-permute-start.11 = (bf16[512,512]{1,0:T(8,128)(2,1)}, bf16[512,512]{1,0:T(8,128)(2,1)S(1)}, u32[]{:S(2)}, u32[]{:S(2)}) collective-permute-start(bf16[512,512]{1,0:T(8,128)(2,1)} %get-tuple-element.45), channel_id=1, source_target_pairs={{0,4},{1,3},{2,6},{3,1},{4,0},{5,7},{6,2},{7,5},{8,12},{9,11},{10,... | collective-permute-start | bytes 1572872 | tf_op jit(solution)/shard_map/ppermute | solution.py:383
  110.2 24.9 %collective-permute-start.12 = (bf16[512,512]{1,0:T(8,128)(2,1)}, bf16[512,512]{1,0:T(8,128)(2,1)S(1)}, u32[]{:S(2)}, u32[]{:S(2)}) collective-permute-start(bf16[512,512]{1,0:T(8,128)(2,1)} %get-tuple-element.46), channel_id=1, source_target_pairs={{0,6},{1,7},{2,4},{3,5},{4,2},{5,3},{6,0},{7,1},{8,14},{9,15},{10,... | collective-permute-start | bytes 1572872 | tf_op jit(solution)/shard_map/ppermute | solution.py:383
  111.7 8.9 %copy-start.3 = (bf16[512,512]{1,0:T(8,128)(2,1)}, bf16[512,512]{1,0:T(8,128)(2,1)S(1)}, u32[]{:S(2)}) copy-start(bf16[512,512]{1,0:T(8,128)(2,1)S(1)} %collective-permute-done.13.refs_1_) | copy-start | bytes 1572868
  112.9 7.6 %copy-start.5 = (bf16[512,512]{1,0:T(8,128)(2,1)}, bf16[512,512]{1,0:T(8,128)(2,1)S(1)}, u32[]{:S(2)}) copy-start(bf16[512,512]{1,0:T(8,128)(2,1)S(1)} %collective-permute-done.15.refs_3_) | copy-start | bytes 1572868
  121.3 13.7 %collective-permute-start.16 = (bf16[512,256]{1,0:T(8,128)(2,1)}, bf16[512,256]{1,0:T(8,128)(2,1)S(1)}, u32[]{:S(2)}, u32[]{:S(2)}) collective-permute-start(bf16[512,256]{1,0:T(8,128)(2,1)} %get-tuple-element.50), channel_id=1, source_target_pairs={{0,2},{1,5},{2,0},{3,7},{4,6},{5,1},{6,4},{7,3},{8,10},{9,13},{10,... | collective-permute-start | bytes 786440 | tf_op jit(solution)/shard_map/ppermute | solution.py:383
  122.8 13.0 %collective-permute-start.17 = (bf16[512,256]{1,0:T(8,128)(2,1)}, bf16[512,256]{1,0:T(8,128)(2,1)S(1)}, u32[]{:S(2)}, u32[]{:S(2)}) collective-permute-start(bf16[512,256]{1,0:T(8,128)(2,1)} %get-tuple-element.51), channel_id=1, source_target_pairs={{0,2},{1,5},{2,0},{3,7},{4,6},{5,1},{6,4},{7,3},{8,10},{9,13},{10,... | collective-permute-start | bytes 786440 | tf_op jit(solution)/shard_map/ppermute | solution.py:383
  (7 other events, 11.5 us)
